TPU v7x, 32 devices: a whole 2x2x4 slice. The times are simulated.
32 devices in a mesh: ctx: 8 (over y, x, core), tp: 4 (over z).
Axes of the slice: x: 2, y: 2, z: 4, core: 2. Of those that a mesh axis runs over, the one named last changes fastest.
Arguments:
- hyena_inputs: bfloat16 [3, 1024, 4096], P(None, 'ctx', 'tp'), may hold values from -6 to 6
- filters: float32 [128, 4096], P('tp'), may hold values from -1.25 to 1.25
- skip_bias: float32 [4096], P('tp'), may hold values from -4 to 4
- queries: bfloat16 [1024, 4096], P('ctx', 'tp'), may hold values from -8 to 8
- keys_values: bfloat16 [2, 1024, 4096], P(None, 'ctx', 'tp'), may hold values from -8 to 8
- doc_start: int32 [1024], P('ctx'), may hold values from 0 to 1023, as said below
Outputs:
- hyena_out: bfloat16 [1024, 4096], P('ctx', 'tp')
- attention_out: bfloat16 [1024, 4096], P('ctx', 'tp')
- log_totals: float32 [32, 1024], P('tp', 'ctx')
Inputs may be any that keep to these rules, and one draw needn't show every extreme that they name: doc_start[t] <= t; doc_start is non-decreasing, equal within a document and equal to t at a document's first base; no document is longer than 896 bases and one has exactly 896; the last base forms a document of its own.
All inputs are finite; a program needn't handle non-finite values.
Results may differ from a plain program's by a relative error of at most 0.009.
Values may be sent and summed in bfloat16 or wider, within the bound.
No kernel may reach another device: no remote copies, remote signals or barrier semaphores. Data moves between devices by JAX's collectives and lax.ppermute only.
A program may use at most 128 MiB of HBM per device.

v0:
```python
import math

import jax
import jax.numpy as jnp
from jax import lax
from jax.sharding import PartitionSpec as P

HD = 128
FLEN = 128
HOPS = 7


def shifted_2(shard, axis, by):
    peers = lax.axis_size(axis)
    pairs = [(i, i + by) for i in range(peers) if 0 <= i + by < peers]
    return lax.ppermute(shard, axis, pairs)


def local(hyena_inputs, filters, skip_bias, queries, keys_values, doc_start):
    row_count = hyena_inputs.shape[1]
    cycle_index = lax.axis_index("ctx")
    first_row = cycle_index * row_count
    places = first_row + jnp.arange(row_count, dtype=jnp.int32)
    kv_product = (hyena_inputs[1].astype(jnp.float32) * hyena_inputs[2].astype(jnp.float32)).astype(
        jnp.bfloat16
    )
    panel_taps = lax.all_to_all(
        filters.astype(jnp.bfloat16), "tp", split_axis=1, concat_axis=0, tiled=True
    ).astype(filters.dtype)
    left_rim = shifted_2(kv_product[row_count - (FLEN - 1) :], "ctx", 1)
    extended = jnp.concatenate([left_rim, kv_product], axis=0)
    channel_count = kv_product.shape[1]
    reach = (places - doc_start)[:, None]
    convolved = jnp.zeros((row_count, channel_count), jnp.float32)
    for lag in range(FLEN):
        shifted = extended[FLEN - 1 - lag : FLEN - 1 - lag + row_count].astype(jnp.float32)
        convolved = convolved + jnp.where(reach >= lag, shifted * panel_taps[lag][None, :], 0.0)
    hyena_out = (
        hyena_inputs[0].astype(jnp.float32)
        * (skip_bias[None, :] * kv_product.astype(jnp.float32) + convolved)
    ).astype(jnp.bfloat16)
    head_count = queries.shape[1] // HD
    query_heads = queries.reshape(row_count, head_count, HD)
    score_scale = 1.0 / math.sqrt(HD)
    pieces = [keys_values]
    for distance in range(1, HOPS + 1):
        pieces.append(shifted_2(pieces[-1], "ctx", 1))
    carried = (
        jnp.full((head_count, row_count), -jnp.inf, jnp.float32),
        jnp.zeros((head_count, row_count), jnp.float32),
        jnp.zeros((head_count, row_count, HD), jnp.float32),
    )
    for pair_index in range((HOPS + 1) // 2):
        block = jnp.concatenate([pieces[2 * pair_index + 1], pieces[2 * pair_index]], axis=1)
        key_first = (cycle_index - 2 * pair_index - 1) * row_count
        add_row_top, add_denominator, add_accumulated = carried
        key_rows = block[0].reshape(2 * row_count, head_count, HD)
        value_rows = block[1].reshape(2 * row_count, head_count, HD)
        scores = (
            jnp.einsum("thd,khd->htk", query_heads, key_rows, preferred_element_type=jnp.float32)
            * score_scale
        )
        key_places = key_first + jnp.arange(2 * row_count, dtype=jnp.int32)
        allowed = (key_places[None, :] >= doc_start[:, None]) & (
            key_places[None, :] <= places[:, None]
        )
        scores = jnp.where(allowed[None], scores, -jnp.inf)
        new_top = jnp.maximum(add_row_top, jnp.max(scores, axis=2))
        weights = jnp.exp(scores - new_top[:, :, None])
        rescale = jnp.exp(add_row_top - new_top)
        add_denominator = add_denominator * rescale + jnp.sum(weights, axis=2)
        add_accumulated = add_accumulated * rescale[:, :, None] + jnp.einsum(
            "htk,khd->htd",
            weights.astype(jnp.bfloat16),
            value_rows,
            preferred_element_type=jnp.float32,
        )
        carried = (new_top, add_denominator, add_accumulated)
    row_top, denominator, accumulated = carried
    attention_out = (
        (accumulated / denominator[:, :, None])
        .transpose(1, 0, 2)
        .reshape(row_count, head_count * HD)
        .astype(jnp.bfloat16)
    )
    log_totals = row_top + jnp.log(denominator)
    return (hyena_out, attention_out, log_totals)


def solution(mesh):
    in_specs = (
        P(None, "ctx", "tp"),
        P("tp", None),
        P("tp"),
        P("ctx", "tp"),
        P(None, "ctx", "tp"),
        P("ctx"),
    )
    out_specs = (P("ctx", "tp"), P("ctx", "tp"), P("tp", "ctx"))
    return jax.shard_map(local, mesh=mesh, in_specs=in_specs, out_specs=out_specs, check_vma=False)
```

profile of v0, /device:TPU:12, one launch (start us, length us, event | category | flops | bytes accessed | tf_op | source)
XLA Modules:
  0.0 237.3 jit_solution(11087094952165187453)
XLA Ops:
  0.7 1.2 convert_element_type.445
  1.8 0.7 copy.104
  2.5 5.3 %all-to-all-start = ((bf16[32,4,1024]{2,0,1:T(8,128)(2,1)}), bf16[32,4,1024]{2,0,1:T(8,128)(2,1)}, u32[]{:S(2)}, u32[]{:S(2)}) async-start(bf16[32,4,1024]{2,0,1:T(8,128)(2,1)} %bitcast.294), calls=%async_computation | async-start | bytes 524288 | tf_op jit(solution)/shard_map/all_to_all | solution.py:27
  8.0 2.1 collective-permute-start
  10.4 3.5 %collective-permute-start.1 = (bf16[2,128,1024]{1,2,0:T(8,128)(2,1)S(1)}, bf16[2,128,1024]{1,2,0:T(8,128)(2,1)}, u32[]{:S(2)}, u32[]{:S(2)}) collective-permute-start(bf16[2,128,1024]{1,2,0:T(8,128)(2,1)S(1)} %copy.54), channel_id=1, source_target_pairs={{0,4},{4,8},{8,12},{12,16},{16,20},{20,24},{24,28},{1,5},{5,9},{9,... | collective-permute-start | bytes 1572872 | tf_op jit(solution)/shard_map/ppermute | solution.py:16
  13.9 0.6 copy-done.43
  15.3 1.5 broadcast_compare_fusion.81
  16.9 1.5 fusion.107
  18.4 1.5 fusion.179
  19.9 1.6 fusion.152
  21.5 1.6 fusion.170
  23.1 1.6 fusion.161
  24.7 1.6 fusion.134
  26.3 1.5 fusion.116
  27.8 1.6 fusion.125
  29.4 1.6 fusion.143
  31.1 1.1 convert_element_type.585
  32.3 1.9 collective-permute-start.2
  34.5 9.5 %collective-permute-done.2 = bf16[2,128,1024]{1,2,0:T(8,128)(2,1)S(1)} collective-permute-done((bf16[2,128,1024]{1,2,0:T(8,128)(2,1)}, bf16[2,128,1024]{1,2,0:T(8,128)(2,1)S(1)}, u32[]{:S(2)}, u32[]{:S(2)}) %collective-permute-start.2) | collective-permute-done | bytes 524320 | tf_op jit(solution)/shard_map/ppermute | solution.py:16
  43.9 1.9 collective-permute-start.3
  46.4 8.9 %collective-permute-done.3 = bf16[2,128,1024]{1,2,0:T(8,128)(2,1)S(1)} collective-permute-done((bf16[2,128,1024]{1,2,0:T(8,128)(2,1)S(1)}, bf16[2,128,1024]{1,2,0:T(8,128)(2,1)S(1)}, u32[]{:S(2)}, u32[]{:S(2)}) %collective-permute-start.3) | collective-permute-done | bytes 524320 | tf_op jit(solution)/shard_map/ppermute | solution.py:16
  55.3 1.9 collective-permute-start.4
  58.3 139.6 %fusion.27 = bf16[128,1024]{1,0:T(8,128)(2,1)} fusion(bf16[128,1024]{1,0:T(8,128)(2,1)S(1)} %get-tuple-element.242, bf16[128,1024]{1,0:T(8,128)(2,1)S(1)} %get-tuple-element.241, bf16[128,1024]{1,0:T(8,128)(2,1)} %get-tuple-element.240, bf16[128,1024]{1,0:T(8,128)(2,1)} %get-tuple-element.239, bf16[128,1024]{1,0:T(8,128)(2,1)S(1)} %copy-done.15, ...), kind=kLoop, calls=%fused_computation.295 | loop fusion | flops 84279296 | bytes 24131456 | tf_op jit(solution)/shard_map/convert_element_type | solution.py:41
  197.9 1.1 fusion.57
  199.1 1.9 collective-permute-start.5
  201.8 8.7 %collective-permute-done.5 = bf16[2,128,1024]{1,2,0:T(8,128)(2,1)S(1)} collective-permute-done((bf16[2,128,1024]{1,2,0:T(8,128)(2,1)S(1)}, bf16[2,128,1024]{1,2,0:T(8,128)(2,1)S(1)}, u32[]{:S(2)}, u32[]{:S(2)}) %collective-permute-start.5) | collective-permute-done | bytes 524320 | tf_op jit(solution)/shard_map/ppermute | solution.py:16
  210.5 1.9 collective-permute-start.6
  213.1 8.8 %collective-permute-done.6 = bf16[2,128,1024]{1,2,0:T(8,128)(2,1)S(1)} collective-permute-done((bf16[2,128,1024]{1,2,0:T(8,128)(2,1)S(1)}, bf16[2,128,1024]{1,2,0:T(8,128)(2,1)S(1)}, u32[]{:S(2)}, u32[]{:S(2)}) %collective-permute-start.6) | collective-permute-done | bytes 524320 | tf_op jit(solution)/shard_map/ppermute | solution.py:16
  221.9 2.1 collective-permute-start.7
  224.4 8.8 %collective-permute-done.7 = bf16[2,128,1024]{1,2,0:T(8,128)(2,1)S(1)} collective-permute-done((bf16[2,128,1024]{1,2,0:T(8,128)(2,1)S(1)}, bf16[2,128,1024]{1,2,0:T(8,128)(2,1)S(1)}, u32[]{:S(2)}, u32[]{:S(2)}) %collective-permute-start.7) | collective-permute-done | bytes 524320 | tf_op jit(solution)/shard_map/ppermute | solution.py:16
  234.5 0.6 log_add_fusion
  236.4 0.9 copy.68
  (132 shorter events, 7.0 us)
Async XLA Ops:
  0.6 200.4 %copy-start = (bf16[128,1024]{1,0:T(8,128)(2,1)S(1)}, bf16[128,1024]{1,0:T(8,128)(2,1)}, u32[]{:S(2)}) copy-start(bf16[128,1024]{1,0:T(8,128)(2,1)} %param.9) | copy-start | bytes 786436
  2.5 28.5 %all-to-all-start = ((bf16[32,4,1024]{2,0,1:T(8,128)(2,1)}), bf16[32,4,1024]{2,0,1:T(8,128)(2,1)}, u32[]{:S(2)}, u32[]{:S(2)}) async-start(bf16[32,4,1024]{2,0,1:T(8,128)(2,1)} %bitcast.294), calls=%async_computation | async-start | bytes 524288 | tf_op jit(solution)/shard_map/all_to_all | solution.py:27
  8.0 8.9 %collective-permute-start = (bf16[127,1024]{1,0:T(8,128)(2,1)S(1)}, bf16[127,1024]{1,0:T(8,128)(2,1)S(1)}, u32[]{:S(2)}, u32[]{:S(2)}) collective-permute-start(bf16[127,1024]{1,0:T(8,128)(2,1)S(1)} %slice_bitcast_fusion), channel_id=1, source_target_pairs={{0,4},{4,8},{8,12},{12,16},{16,20},{20,24},{24,28},{1,5},{5,9},{9,... | collective-permute-start | bytes 780296 | tf_op jit(solution)/shard_map/ppermute | solution.py:16
  10.4 22.0 %collective-permute-start.1 = (bf16[2,128,1024]{1,2,0:T(8,128)(2,1)S(1)}, bf16[2,128,1024]{1,2,0:T(8,128)(2,1)}, u32[]{:S(2)}, u32[]{:S(2)}) collective-permute-start(bf16[2,128,1024]{1,2,0:T(8,128)(2,1)S(1)} %copy.54), channel_id=1, source_target_pairs={{0,4},{4,8},{8,12},{12,16},{16,20},{20,24},{24,28},{1,5},{5,9},{9,... | collective-permute-start | bytes 1572872 | tf_op jit(solution)/shard_map/ppermute | solution.py:16
  31.1 26.2 %copy-start.13 = (bf16[128,1024]{1,0:T(8,128)(2,1)S(1)}, bf16[128,1024]{1,0:T(8,128)(2,1)}, u32[]{:S(2)}) copy-start(bf16[128,1024]{1,0:T(8,128)(2,1)} %get-tuple-element.236) | copy-start | bytes 786436
  31.1 26.2 %copy-start.14 = (bf16[128,1024]{1,0:T(8,128)(2,1)S(1)}, bf16[128,1024]{1,0:T(8,128)(2,1)}, u32[]{:S(2)}) copy-start(bf16[128,1024]{1,0:T(8,128)(2,1)} %get-tuple-element.237) | copy-start | bytes 786436
  31.1 26.2 %copy-start.15 = (bf16[128,1024]{1,0:T(8,128)(2,1)S(1)}, bf16[128,1024]{1,0:T(8,128)(2,1)}, u32[]{:S(2)}) copy-start(bf16[128,1024]{1,0:T(8,128)(2,1)} %get-tuple-element.238) | copy-start | bytes 786436
  32.2 25.1 %copy-start.12 = (bf16[128,1024]{1,0:T(8,128)(2,1)S(1)}, bf16[128,1024]{1,0:T(8,128)(2,1)}, u32[]{:S(2)}) copy-start(bf16[128,1024]{1,0:T(8,128)(2,1)} %get-tuple-element.235) | copy-start | bytes 786436
  32.3 11.6 %collective-permute-start.2 = (bf16[2,128,1024]{1,2,0:T(8,128)(2,1)}, bf16[2,128,1024]{1,2,0:T(8,128)(2,1)S(1)}, u32[]{:S(2)}, u32[]{:S(2)}) collective-permute-start(bf16[2,128,1024]{1,2,0:T(8,128)(2,1)} %collective-permute-done.1), channel_id=1, source_target_pairs={{0,4},{4,8},{8,12},{12,16},{16,20},{20,24},{24,28},{1,5},{5,9},{9,... | collective-permute-start | bytes 1572872 | tf_op jit(solution)/shard_map/ppermute | solution.py:16
  34.2 23.1 %copy-start.11 = (bf16[128,1024]{1,0:T(8,128)(2,1)S(1)}, bf16[128,1024]{1,0:T(8,128)(2,1)}, u32[]{:S(2)}) copy-start(bf16[128,1024]{1,0:T(8,128)(2,1)} %get-tuple-element.234) | copy-start | bytes 786436
  34.4 11.6 %copy-start.42 = (pred[128]{0:T(512)(128)(4,1)S(1)}, pred[128]{0:T(512)(128)(4,1)}, u32[]{:S(2)}) copy-start(pred[128]{0:T(512)(128)(4,1)} %get-tuple-element.330) | copy-start | bytes 388
  34.4 22.9 %copy-start.10 = (bf16[128,1024]{1,0:T(8,128)(2,1)S(1)}, bf16[128,1024]{1,0:T(8,128)(2,1)}, u32[]{:S(2)}) copy-start(bf16[128,1024]{1,0:T(8,128)(2,1)} %get-tuple-element.233) | copy-start | bytes 786436
  43.9 11.4 %collective-permute-start.3 = (bf16[2,128,1024]{1,2,0:T(8,128)(2,1)S(1)}, bf16[2,128,1024]{1,2,0:T(8,128)(2,1)S(1)}, u32[]{:S(2)}, u32[]{:S(2)}) collective-permute-start(bf16[2,128,1024]{1,2,0:T(8,128)(2,1)S(1)} %collective-permute-done.2), channel_id=1, source_target_pairs={{0,4},{4,8},{8,12},{12,16},{16,20},{20,24},{24,28},{1,5},{5,9},{9,... | collective-permute-start | bytes 1572872 | tf_op jit(solution)/shard_map/ppermute | solution.py:16
  45.9 11.4 %copy-start.9 = (bf16[128,1024]{1,0:T(8,128)(2,1)S(1)}, bf16[128,1024]{1,0:T(8,128)(2,1)}, u32[]{:S(2)}) copy-start(bf16[128,1024]{1,0:T(8,128)(2,1)} %get-tuple-element.232) | copy-start | bytes 786436
  46.0 11.4 %copy-start.5 = (bf16[128,1024]{1,0:T(8,128)(2,1)S(1)}, bf16[128,1024]{1,0:T(8,128)(2,1)}, u32[]{:S(2)}) copy-start(bf16[128,1024]{1,0:T(8,128)(2,1)} %get-tuple-element.165) | copy-start | bytes 786436
  46.0 11.4 %copy-start.6 = (bf16[128,1024]{1,0:T(8,128)(2,1)S(1)}, bf16[128,1024]{1,0:T(8,128)(2,1)}, u32[]{:S(2)}) copy-start(bf16[128,1024]{1,0:T(8,128)(2,1)} %get-tuple-element.166) | copy-start | bytes 786436
  46.0 11.4 %copy-start.7 = (bf16[128,1024]{1,0:T(8,128)(2,1)S(1)}, bf16[128,1024]{1,0:T(8,128)(2,1)}, u32[]{:S(2)}) copy-start(bf16[128,1024]{1,0:T(8,128)(2,1)} %get-tuple-element.167) | copy-start | bytes 786436
  46.0 11.4 %copy-start.8 = (bf16[128,1024]{1,0:T(8,128)(2,1)S(1)}, bf16[128,1024]{1,0:T(8,128)(2,1)}, u32[]{:S(2)}) copy-start(bf16[128,1024]{1,0:T(8,128)(2,1)} %get-tuple-element.168) | copy-start | bytes 786436
  46.0 11.4 %copy-start.17 = (f32[1024]{0:T(1024)S(1)}, f32[1024]{0:T(1024)}, u32[]{:S(2)}) copy-start(f32[1024]{0:T(1024)} %param.8) | copy-start | bytes 12292
  46.0 11.3 %copy-start.18 = (pred[128]{0:T(512)(128)(4,1)S(1)}, pred[128]{0:T(512)(128)(4,1)}, u32[]{:S(2)}) copy-start(pred[128]{0:T(512)(128)(4,1)} %get-tuple-element.252) | copy-start | bytes 388
  46.0 11.3 %copy-start.19 = (pred[128]{0:T(512)(128)(4,1)S(1)}, pred[128]{0:T(512)(128)(4,1)}, u32[]{:S(2)}) copy-start(pred[128]{0:T(512)(128)(4,1)} %get-tuple-element.253) | copy-start | bytes 388
  46.1 11.3 %copy-start.20 = (pred[128]{0:T(512)(128)(4,1)S(1)}, pred[128]{0:T(512)(128)(4,1)}, u32[]{:S(2)}) copy-start(pred[128]{0:T(512)(128)(4,1)} %get-tuple-element.254) | copy-start | bytes 388
  46.1 11.3 %copy-start.21 = (pred[128]{0:T(512)(128)(4,1)S(1)}, pred[128]{0:T(512)(128)(4,1)}, u32[]{:S(2)}) copy-start(pred[128]{0:T(512)(128)(4,1)} %get-tuple-element.255) | copy-start | bytes 388
  46.1 11.3 %copy-start.22 = (pred[128]{0:T(512)(128)(4,1)S(1)}, pred[128]{0:T(512)(128)(4,1)}, u32[]{:S(2)}) copy-start(pred[128]{0:T(512)(128)(4,1)} %get-tuple-element.256) | copy-start | bytes 388
  46.1 11.3 %copy-start.23 = (pred[128]{0:T(512)(128)(4,1)S(1)}, pred[128]{0:T(512)(128)(4,1)}, u32[]{:S(2)}) copy-start(pred[128]{0:T(512)(128)(4,1)} %get-tuple-element.257) | copy-start | bytes 388
  46.1 11.3 %copy-start.24 = (pred[128]{0:T(512)(128)(4,1)S(1)}, pred[128]{0:T(512)(128)(4,1)}, u32[]{:S(2)}) copy-start(pred[128]{0:T(512)(128)(4,1)} %get-tuple-element.258) | copy-start | bytes 388
  46.1 11.3 %copy-start.25 = (pred[128]{0:T(512)(128)(4,1)S(1)}, pred[128]{0:T(512)(128)(4,1)}, u32[]{:S(2)}) copy-start(pred[128]{0:T(512)(128)(4,1)} %get-tuple-element.259) | copy-start | bytes 388
  46.1 11.3 %copy-start.26 = (pred[128]{0:T(512)(128)(4,1)S(1)}, pred[128]{0:T(512)(128)(4,1)}, u32[]{:S(2)}) copy-start(pred[128]{0:T(512)(128)(4,1)} %get-tuple-element.260) | copy-start | bytes 388
  55.3 143.8 %collective-permute-start.4 = (bf16[2,128,1024]{1,2,0:T(8,128)(2,1)S(1)}, bf16[2,128,1024]{1,2,0:T(8,128)(2,1)S(1)}, u32[]{:S(2)}, u32[]{:S(2)}) collective-permute-start(bf16[2,128,1024]{1,2,0:T(8,128)(2,1)S(1)} %collective-permute-done.3), channel_id=1, source_target_pairs={{0,4},{4,8},{8,12},{12,16},{16,20},{20,24},{24,28},{1,5},{5,9},{9,... | collective-permute-start | bytes 1572872 | tf_op jit(solution)/shard_map/ppermute | solution.py:16
  199.1 11.4 %collective-permute-start.5 = (bf16[2,128,1024]{1,2,0:T(8,128)(2,1)S(1)}, bf16[2,128,1024]{1,2,0:T(8,128)(2,1)S(1)}, u32[]{:S(2)}, u32[]{:S(2)}) collective-permute-start(bf16[2,128,1024]{1,2,0:T(8,128)(2,1)S(1)} %collective-permute-done.4), channel_id=1, source_target_pairs={{0,4},{4,8},{8,12},{12,16},{16,20},{20,24},{24,28},{1,5},{5,9},{9,... | collective-permute-start | bytes 1572872 | tf_op jit(solution)/shard_map/ppermute | solution.py:16
  210.5 11.4 %collective-permute-start.6 = (bf16[2,128,1024]{1,2,0:T(8,128)(2,1)S(1)}, bf16[2,128,1024]{1,2,0:T(8,128)(2,1)S(1)}, u32[]{:S(2)}, u32[]{:S(2)}) collective-permute-start(bf16[2,128,1024]{1,2,0:T(8,128)(2,1)S(1)} %collective-permute-done.5), channel_id=1, source_target_pairs={{0,4},{4,8},{8,12},{12,16},{16,20},{20,24},{24,28},{1,5},{5,9},{9,... | collective-permute-start | bytes 1572872 | tf_op jit(solution)/shard_map/ppermute | solution.py:16
  221.9 11.4 %collective-permute-start.7 = (bf16[2,128,1024]{1,2,0:T(8,128)(2,1)S(1)}, bf16[2,128,1024]{1,2,0:T(8,128)(2,1)S(1)}, u32[]{:S(2)}, u32[]{:S(2)}) collective-permute-start(bf16[2,128,1024]{1,2,0:T(8,128)(2,1)S(1)} %collective-permute-done.6), channel_id=1, source_target_pairs={{0,4},{4,8},{8,12},{12,16},{16,20},{20,24},{24,28},{1,5},{5,9},{9,... | collective-permute-start | bytes 1572872 | tf_op jit(solution)/shard_map/ppermute | solution.py:16
  (21 other events, 183.4 us)
where the time goes:
time: 238 us; the launch traced here: 237 us
  other arithmetic  161 us (68%)
  waiting for transfers between devices  44.7 us (19%)
  starting transfers between devices  22.5 us (9%)
  local copies, waits for them, and re-layouts  4.72 us (2%)
  matrix products  2.74 us (1%)
    convert_element_type x1, other arithmetic, local(): hyena_out = (hyena_inputs[0].astype(jnp.float32) * (skip_bias[None, :] *...  140 us
    ppermute x8, waiting for transfers between devices, shifted_2(): return lax.ppermute(shard, axis, pairs)  44.7 us
    ppermute x8, starting transfers between devices, shifted_2(): return lax.ppermute(shard, axis, pairs)  17.2 us
    concatenate x10, other arithmetic, local(): extended = jnp.concatenate([left_rim, kv_product], axis=0)  14.2 us
    all_to_all x1, starting transfers between devices, local(): lax.all_to_all(filters.astype(jnp.bfloat16), 'tp', split_axis=1, concat_a...  5.32 us
  transfers between devices with their start and end apart: 9, of which 5 were waited for; matrix products, arithmetic and copies ran while one was open for 68% of the time, Pallas kernels for 0%

commit v1 on v0

v1 whole, which is shorter than its diff:
```python
import functools
import math

import jax
import jax.numpy as jnp
import numpy as np
from jax import lax
from jax.experimental import pallas as pl
from jax.experimental.pallas import tpu as pltpu
from jax.sharding import PartitionSpec as P

HD = 128
FLEN = 128
DIGIT = 256
NOTE_ROWS = 16
MASKED = -1e30
VMEM_LIMIT = 16 * 1024 * 1024


def vmem():
    return pl.BlockSpec(memory_space=pltpu.VMEM)


def hbm():
    return pl.BlockSpec(memory_space=pltpu.HBM)


def call(kernel, out_shape, args, flops, nbytes, scratch=(), specs=None):
    return pl.pallas_call(
        kernel,
        out_shape=out_shape,
        in_specs=specs or [vmem() for _ in args],
        out_specs=jax.tree.map(lambda _: vmem(), out_shape),
        scratch_shapes=list(scratch),
        compiler_params=pltpu.CompilerParams(vmem_limit_bytes=VMEM_LIMIT),
        cost_estimate=pl.CostEstimate(flops=flops, bytes_accessed=nbytes, transcendentals=0),
    )(*args)


def crossed(array, axis, bits):
    return lax.ppermute(array, axis, [(i, i ^ bits) for i in range(lax.axis_size(axis))])


def place(heads):
    index = lax.axis_index("ctx")
    member = lax.rem(index, heads)
    return index // heads, member // 2, lax.rem(member, 2)


def pack_heads(heads, extra, queries_ref, keys_values_ref, starts_ref, *refs):
    extras, refs = refs[:extra], refs[extra:]
    *outs, held_ref, start_sem, extra_sem, sem = refs
    outs, brought = outs[:-extra], outs[-extra:]
    rows = queries_ref.shape[0]
    _, pair, _ = place(heads)
    first = pltpu.make_async_copy(starts_ref, held_ref, start_sem)
    first.start()
    copies = []
    for step, out in enumerate(outs):
        columns = pl.ds(pl.multiple_of((pair ^ step) * (2 * HD), 2 * HD), 2 * HD)
        for part, source in enumerate(
            (queries_ref, keys_values_ref.at[0], keys_values_ref.at[1])
        ):
            copies.append(
                pltpu.make_async_copy(
                    source.at[:, columns], out.at[pl.ds(part * rows, rows)], sem.at[step, part]
                )
            )
    for index, (source, out) in enumerate(zip(extras, brought)):
        copies.append(pltpu.make_async_copy(source, out, extra_sem.at[index]))
    for copy in copies:
        copy.start()
    first.wait()
    starts = held_ref[...]
    high = (starts // DIGIT).astype(jnp.float32)
    low = (starts % DIGIT).astype(jnp.float32)
    line = lax.broadcasted_iota(jnp.int32, (NOTE_ROWS, rows), 0)
    note = jnp.where(line == 0, high, jnp.where(line == 1, low, 0.0)).astype(jnp.bfloat16)
    for out in outs:
        out[3 * rows :, :HD] = note
        out[3 * rows :, HD:] = note
    for copy in copies:
        copy.wait()


def split(matrix):
    high = matrix.astype(jnp.bfloat16)
    low = (matrix - high.astype(jnp.float32)).astype(jnp.bfloat16)
    return jnp.concatenate([high, low], axis=1)


def pack_hyena(
    hyena_ref, filters_ref, ahead_ref, wide_back_ref,
    product_ref, own_ref, far_ref, near_ref, early_ref, late_ref, back_ref,
):
    product_ref[...] = (hyena_ref[1].astype(jnp.float32) * hyena_ref[2].astype(jnp.float32)).astype(
        jnp.bfloat16
    )
    width = own_ref.shape[1]
    panel = lax.axis_index("tp")
    parity = lax.rem(lax.axis_index("ctx"), 2)

    def taps(target):
        columns = pl.ds(pl.multiple_of(target * width, width), width)
        return filters_ref[:, columns].astype(jnp.bfloat16)

    own_ref[...] = taps(panel)
    far_ref[...] = taps(panel ^ (2 + parity))
    near_ref[...] = taps(panel ^ 1)
    rows = product_ref.shape[0]
    early_ref[...] = split(ahead_ref[:, :rows])
    late_ref[...] = split(ahead_ref[:, rows:])
    back_ref[...] = wide_back_ref[...].astype(jnp.bfloat16)


def columns_of(ref, rows, index):
    return ref[rows, index * 2 * HD : (index + 1) * 2 * HD]


def sort_heads(heads, *refs):
    count = heads // 2
    far_ref, near_ref, product_ref, query_ref, side_ref = refs[-5:]
    rows = (refs[0].shape[0] - NOTE_ROWS) // 3
    _, pair, _ = place(heads)
    for step in range(count):
        source = pair ^ step
        query_ref[source, :rows] = refs[step][:rows]
        query_ref[source, rows:] = refs[step][3 * rows :]
        side_ref[2 * source] = refs[step][rows : 2 * rows]
        side_ref[2 * source + 1] = refs[step][2 * rows : 3 * rows]
    height, width = far_ref.shape
    parts = width // (2 * HD)
    for part in range(parts):
        line = slice(part * height, (part + 1) * height)
        side_ref[heads, line] = columns_of(far_ref, slice(None), part)
        side_ref[heads + 1, line] = columns_of(near_ref, slice(None), part)
        side_ref[heads + 2 + part] = columns_of(product_ref, slice(None), part)


UNIT = 2


def key_set(ref, blocks, head, origin, parity, own):
    columns = slice(head * HD, (head + 1) * HD)
    rows = ref.shape[1]
    key = jnp.concatenate([ref[2 * block, :, columns] for block in range(blocks)], axis=0)
    value = jnp.concatenate([ref[2 * block + 1, :, columns] for block in range(blocks)], axis=0)
    firsts = [((2 * block + parity) * rows + origin, block >= own) for block in range(blocks)]
    return key, value, firsts


def masked_scores(sets, query, start, own):
    blocks = []
    for key, _, firsts in sets:
        scores = lax.dot_general(
            key, query, (((1,), (1,)), ((), ())), preferred_element_type=jnp.float32
        )
        rows = key.shape[0] // len(firsts)
        line = lax.broadcasted_iota(jnp.int32, (rows, query.shape[0]), 0)
        for index, (first, causal) in enumerate(firsts):
            allowed = line >= start - first
            if causal:
                allowed &= line <= own - first
            blocks.append(jnp.where(allowed, scores[index * rows : (index + 1) * rows], MASKED))
    return blocks


def highest(blocks):
    return jnp.max(functools.reduce(jnp.maximum, blocks), axis=0, keepdims=True)


def weigh(sets, blocks, top):
    weights = [jnp.exp2((block - top) * FACTOR) for block in blocks]
    total = jnp.sum(functools.reduce(jnp.add, weights), axis=0, keepdims=True)
    value = jnp.concatenate([one[1] for one in sets], axis=0)
    rounded = jnp.concatenate([each.astype(jnp.bfloat16) for each in weights], axis=0)
    return total, dot(value.T, rounded)


def unit_rows(heads, query_ref, head, begin):
    rows = query_ref.shape[1] - NOTE_ROWS
    group, _, parity = place(heads)
    query = query_ref[begin : begin + UNIT, :rows, head * HD : (head + 1) * HD]
    starts = []
    for block in range(begin, begin + UNIT):
        note = query_ref[block, rows:, :HD].astype(jnp.float32)
        starts.append(note[0:1] * float(DIGIT) + note[1:2])
    start = jnp.concatenate(starts, axis=1).astype(jnp.int32) - group * (heads * rows)
    line = lax.broadcasted_iota(jnp.int32, (1, UNIT * rows), 1)
    own = line // rows * rows + line + (2 * begin + parity) * rows
    return query.reshape(UNIT * rows, HD), start, own


FACTOR = math.log2(math.e) / math.sqrt(HD)


def attend_first(heads, query_ref, key_value_ref, top_ref, total_ref, mixed_ref):
    rows = query_ref.shape[1] - NOTE_ROWS
    _, _, parity = place(heads)
    for head in range(2):
        for unit in range(heads // 2 // UNIT):
            begin = unit * UNIT
            query, start, own = unit_rows(heads, query_ref, head, begin)
            sets = [key_set(key_value_ref, begin + UNIT, head, 0, parity, begin)]
            blocks = masked_scores(sets, query, start, own)
            top = highest(blocks)
            top_ref[head, unit] = top
            total_ref[head, unit], mixed_ref[head, unit] = weigh(sets, blocks, top)


def attend_second(heads, *refs):
    count = heads // 2
    query_ref, top_ref, total_ref, mixed_ref, other_ref, *more = refs[: -count - 1]
    outs, held_ref = refs[-count - 1 : -1], refs[-1]
    rows = query_ref.shape[1] - NOTE_ROWS
    _, pair, parity = place(heads)
    for head in range(2):
        columns = slice(head * HD, (head + 1) * HD)
        for unit in range(count // UNIT):
            begin = unit * UNIT
            query, start, own = unit_rows(heads, query_ref, head, begin)
            sets = [key_set(other_ref, begin + UNIT, head, 0, 1 - parity, begin)]
            for ref, side in zip(more, (parity, 1 - parity)):
                sets.append(key_set(ref, count, head, -heads * rows, side, count))
            blocks = masked_scores(sets, query, start, own)
            before = top_ref[head, unit]
            top = jnp.maximum(before, highest(blocks))
            scale = jnp.exp2((before - top) * FACTOR)
            total, mixed = weigh(sets, blocks, top)
            total = total_ref[head, unit] * scale + total
            mixed = mixed_ref[head, unit] * scale + mixed
            mixed = (mixed / total).T.astype(jnp.bfloat16)
            logs = top * (1.0 / math.sqrt(HD)) + jnp.log(total)
            high = logs.astype(jnp.bfloat16).astype(jnp.float32)
            middle = (logs - high).astype(jnp.bfloat16).astype(jnp.float32)
            low = logs - high - middle
            line = lax.broadcasted_iota(jnp.int32, (NOTE_ROWS, UNIT * rows), 0)
            note = jnp.where(
                line == 0, high, jnp.where(line == 1, middle, jnp.where(line == 2, low, 0.0))
            ).astype(jnp.bfloat16)
            for index in range(UNIT):
                span = slice(index * rows, (index + 1) * rows)
                held_ref[begin + index, :rows, columns] = mixed[span]
                held_ref[begin + index, rows:, columns] = note[:, span]
    for step, out in enumerate(outs):
        out[...] = held_ref[pair ^ step]


def unpack_heads(heads, *refs):
    *sources, out_ref, logs_ref = refs
    rows = out_ref.shape[0]
    _, pair, _ = place(heads)
    for step, source in enumerate(sources):
        owner = pair ^ step
        out_ref[:, pl.ds(pl.multiple_of(owner * (2 * HD), 2 * HD), 2 * HD)] = source[:rows]
        note = source[rows:].astype(jnp.float32)
        logs = note[0:1] + note[1:2] + note[2:3]
        for head in range(2):
            logs_ref[pl.ds(owner * 2 + head, 1), :] = logs[:, head * HD : (head + 1) * HD]


def dot(left, right):
    return jnp.dot(left, right, preferred_element_type=jnp.float32)


def twice(array):
    return jnp.concatenate([array, array], axis=0)


def document_starts(starts_ref, rows):
    return jnp.maximum(starts_ref[...] - lax.axis_index("ctx") * rows, -rows)


def filtered(spectrum, filter_ref, back_ref):
    half = spectrum.shape[0] // 2
    even, odd = spectrum[:half], spectrum[half:]
    tap_even, tap_odd = filter_ref[:half], filter_ref[half:]
    real = (even * tap_even - odd * tap_odd).astype(jnp.bfloat16)
    imag = (even * tap_odd + odd * tap_even).astype(jnp.bfloat16)
    return dot(back_ref[...], jnp.concatenate([real, imag], axis=0))


def convolve(
    heads, other_ref, mine_ref, before_ref, own_taps_ref, starts_ref, product_ref, gate_ref, skip_ref,
    early_ref, late_ref, back_ref, out_ref, taps_ref, halo_ref, filter_ref, sum_ref,
):
    rows = product_ref.shape[0]
    height, width = own_taps_ref.shape
    panel = lax.axis_index("tp")
    even = lax.rem(lax.axis_index("ctx"), 2) == 0
    everything = slice(None)

    def store(step, part, value):
        line = pl.ds(pl.multiple_of((panel ^ step) * height, height), height)
        taps_ref[line, part * 2 * HD : (part + 1) * 2 * HD] = value

    for part in range(width // (2 * HD)):
        line = slice(part * height, (part + 1) * height)
        mine_far, other_far = mine_ref[heads, line], other_ref[heads, line]
        store(0, part, columns_of(own_taps_ref, everything, part))
        store(1, part, jnp.where(even, mine_ref[heads + 1, line], other_ref[heads + 1, line]))
        store(2, part, jnp.where(even, mine_far, other_far))
        store(3, part, jnp.where(even, other_far, mine_far))
        halo_ref[:, part * 2 * HD : (part + 1) * 2 * HD] = jnp.where(
            even, columns_of(before_ref, everything, part), other_ref[heads + 2 + part]
        )
    filter_ref[...] = dot(early_ref[...], twice(taps_ref[...]))
    starts = document_starts(starts_ref, rows)
    line = lax.broadcasted_iota(jnp.int32, (rows, 1), 0)
    zero = jnp.zeros((), jnp.bfloat16)

    begin = jnp.min(starts)
    past = jnp.where(line - rows >= begin, halo_ref[...], zero)
    here = jnp.where(line >= begin, product_ref[...], zero)
    spectrum = dot(early_ref[...], twice(past)) + dot(late_ref[...], twice(here))
    sum_ref[...] = filtered(spectrum, filter_ref, back_ref)

    def one_document(begin):
        here = jnp.where(line >= begin, product_ref[...], zero)
        result = filtered(dot(late_ref[...], twice(here)), filter_ref, back_ref)
        sum_ref[...] = jnp.where(line >= begin, result, sum_ref[...])
        return jnp.min(jnp.where(starts > begin, starts, rows))

    second = jnp.min(jnp.where(starts > begin, starts, rows))
    lax.while_loop(lambda begin: begin < rows, one_document, second)
    out_ref[...] = (
        gate_ref[0].astype(jnp.float32)
        * (skip_ref[...] * product_ref[...].astype(jnp.float32) + sum_ref[...])
    ).astype(jnp.bfloat16)


def twiddles(rows):
    window = 2 * rows
    order = np.arange(rows)[:, None] * 2 + 1
    angle = np.pi * ((order * np.arange(window)[None, :]) % (2 * window)) / window
    ahead = np.concatenate([np.cos(angle), -np.sin(angle)], axis=0)
    back = ahead.T[rows:] / rows
    return jnp.asarray(ahead, jnp.float32), jnp.asarray(back, jnp.float32)


def taps_pairs(peers, panels):
    assert panels == 4
    far, near = [], []
    for peer in range(peers):
        for panel in range(panels):
            here = peer * panels + panel
            far.append((here, peer * panels + (panel ^ (2 + peer % 2))))
            if peer % 2 == 0:
                near.append((here, peer * panels + (panel ^ 1)))
    return far, near


def local(hyena_inputs, filters, skip_bias, queries, keys_values, doc_start):
    rows = queries.shape[0]
    channels = hyena_inputs.shape[2]
    heads = queries.shape[1] // HD
    count = heads // 2
    peers = lax.axis_size("ctx")
    bf16, f32 = jnp.bfloat16, jnp.float32
    shape = jax.ShapeDtypeStruct
    starts = doc_start.reshape(1, rows)

    extras = (filters, *twiddles(rows))
    *packed, near_filters, ahead, back = call(
        functools.partial(pack_heads, heads, len(extras)),
        (shape((3 * rows + NOTE_ROWS, 2 * HD), bf16),) * count
        + tuple(shape(x.shape, x.dtype) for x in extras),
        [
            pltpu.with_memory_space_constraint(x, pltpu.HBM)
            for x in (queries, keys_values, starts, *extras)
        ],
        0,
        4 * queries.size * 3,
        scratch=(
            pltpu.VMEM((1, rows), jnp.int32),
            pltpu.SemaphoreType.DMA,
            pltpu.SemaphoreType.DMA((len(extras),)),
            pltpu.SemaphoreType.DMA((count, 3)),
        ),
        specs=[hbm()] * (3 + len(extras)),
    )
    arrived = [packed[0]] + [None] * (count - 1)
    for step in reversed(range(1, count)):
        arrived[step] = crossed(packed[step], "ctx", 2 * step)
    product, own_taps, far_taps, near_taps, early, late, back = call(
        pack_hyena,
        (shape((rows, channels), bf16),)
        + (shape((filters.shape[0], channels), bf16),) * 3
        + (shape((2 * rows, 2 * rows), bf16),) * 2
        + (shape((rows, 2 * rows), bf16),),
        (hyena_inputs, near_filters, ahead, back),
        0,
        4 * queries.size * 3,
    )
    axes = ("ctx", "tp")
    far_pairs, near_pairs = taps_pairs(peers, lax.axis_size("tp"))
    far_taps = lax.ppermute(far_taps, axes, far_pairs)
    near_taps = lax.ppermute(near_taps, axes, near_pairs)
    before = lax.ppermute(product, "ctx", [(i, i + 1) for i in range(1, peers - 1, 2)])
    query, key_value = call(
        functools.partial(sort_heads, heads),
        (
            shape((count, rows + NOTE_ROWS, 2 * HD), bf16),
            shape((heads + 2 + channels // (2 * HD), rows, 2 * HD), bf16),
        ),
        (*arrived, far_taps, near_taps, product),
        0,
        4 * queries.size * 3,
    )
    other = crossed(key_value, "ctx", 1)
    units = count // UNIT
    partial = call(
        functools.partial(attend_first, heads),
        (
            shape((2, units, 1, UNIT * rows), f32),
            shape((2, units, 1, UNIT * rows), f32),
            shape((2, units, HD, UNIT * rows), f32),
        ),
        (query, key_value),
        2 * (heads * rows) ** 2 * HD,
        4 * queries.size * 4,
    )
    operands = [query, *partial, other]
    if peers > heads:
        pairs = [(i, i + heads) for i in range(peers - heads)]
        operands += [lax.ppermute(each, "ctx", pairs) for each in (key_value, other)]
    mixed = call(
        functools.partial(attend_second, heads),
        (shape((rows + NOTE_ROWS, 2 * HD), bf16),) * count,
        operands,
        2 * (heads * rows) ** 2 * HD,
        4 * queries.size * 4,
        scratch=(pltpu.VMEM((count, rows + NOTE_ROWS, 2 * HD), bf16),),
    )
    returned = [mixed[0]] + [None] * (count - 1)
    for step in reversed(range(1, count)):
        returned[step] = crossed(mixed[step], "ctx", 2 * step)
    hyena_out = call(
        functools.partial(convolve, heads),
        shape((rows, channels), bf16),
        (
            other, key_value, before, own_taps, starts, product, hyena_inputs,
            skip_bias.reshape(1, channels), early, late, back,
        ),
        2 * 4 * 256 * 256 * channels,
        4 * queries.size * 4,
        scratch=(
            pltpu.VMEM((FLEN, channels), bf16),
            pltpu.VMEM((rows, channels), bf16),
            pltpu.VMEM((2 * rows, channels), f32),
            pltpu.VMEM((rows, channels), f32),
        ),
    )
    attention_out, log_totals = call(
        functools.partial(unpack_heads, heads),
        (shape((rows, heads * HD), bf16), shape((heads, rows), f32)),
        returned,
        0,
        4 * queries.size,
    )
    return (hyena_out, attention_out, log_totals)


def solution(mesh):
    in_specs = (
        P(None, "ctx", "tp"),
        P("tp", None),
        P("tp"),
        P("ctx", "tp"),
        P(None, "ctx", "tp"),
        P("ctx"),
    )
    out_specs = (P("ctx", "tp"), P("ctx", "tp"), P("tp", "ctx"))
    return jax.shard_map(local, mesh=mesh, in_specs=in_specs, out_specs=out_specs, check_vma=False)
```

time: 238 us -> 30.2 us (0.13)
  the two profiles are of different devices: /device:TPU:12 before, /device:TPU:0 now
where the time goes in v1:
time: 30.2 us; the launch traced here: 30 us
  starting transfers between devices  15.4 us (51%)
  Pallas kernels  8.28 us (27%)
  waiting for transfers between devices  4.89 us (16%)
  between operations  0.72 us (2%)
  local copies, waits for them, and re-layouts  0.69 us (2%)
    pallas_call x7, Pallas kernels, call(): pl.pallas_call(kernel, out_shape=out_shape, in_specs=specs or [vmem() for...  8.28 us
    ppermute x7, starting transfers between devices, crossed(): lax.ppermute(array, axis, [(i, i ^ bits) for i in range(lax.axis_size(axi...  8.17 us
    ppermute x1, starting transfers between devices, local(): near_taps = lax.ppermute(near_taps, axes, near_pairs)  3.47 us
    ppermute x1, starting transfers between devices, local(): far_taps = lax.ppermute(far_taps, axes, far_pairs)  3.11 us
    ppermute x1, waiting for transfers between devices, local(): near_taps = lax.ppermute(near_taps, axes, near_pairs)  2.66 us
    ppermute x7, waiting for transfers between devices, crossed(): lax.ppermute(array, axis, [(i, i ^ bits) for i in range(lax.axis_size(axi...  2.23 us
    unnamed x6, local copies, waits for them, and re-layouts  0.69 us
    ppermute x1, starting transfers between devices, local(): lax.ppermute(product, 'ctx', [(i, i + 1) for i in range(1, peers - 1, 2)])  0.68 us
  transfers between devices with their start and end apart: 10, of which 3 were waited for; matrix products, arithmetic and copies ran while one was open for 0% of the time, Pallas kernels for 19%

profile of v1, /device:TPU:0, one launch (start us, length us, event | category | flops | bytes accessed | tf_op | source)
XLA Modules:
  0.0 30.0 jit_solution(5961325298243109280)
XLA Ops:
  0.6 0.0 copy-start
  0.6 1.6 %shard_map.103 = (bf16[400,256]{1,0:T(8,128)(2,1)S(1)}, bf16[400,256]{1,0:T(8,128)(2,1)S(1)}, bf16[400,256]{1,0:T(8,128)(2,1)S(1)}, bf16[400,256]{1,0:T(8,128)(2...) custom-call(bf16[128,1024]{1,0:T(8,128)(2,1)} %queries_ref.1, ...), custom_call_target="tpu_custom_call" | custom-call | bytes 1572864 | tf_op jit(solution)/shard_map/pallas_call | solution.py:29
  2.3 3.0 %collective-permute-start = (bf16[400,256]{1,0:T(8,128)(2,1)S(1)}, bf16[400,256]{1,0:T(8,128)(2,1)S(1)}, u32[]{:S(2)}, u32[]{:S(2)}) collective-permute-start(bf16[400,256]{1,0:T(8,128)(2,1)S(1)} %get-tuple-element.29), channel_id=1, source_target_pairs={{0,8},{4,12},{8,0},{12,4},{16,24},{20,28},{24,16},{28,20},{1,9},{5... | collective-permute-start | bytes 614408 | tf_op jit(solution)/shard_map/ppermute | solution.py:41
  5.3 1.5 %collective-permute-start.1 = (bf16[400,256]{1,0:T(8,128)(2,1)S(1)}, bf16[400,256]{1,0:T(8,128)(2,1)S(1)}, u32[]{:S(2)}, u32[]{:S(2)}) collective-permute-start(bf16[400,256]{1,0:T(8,128)(2,1)S(1)} %get-tuple-element.30), channel_id=1, source_target_pairs={{0,16},{4,20},{8,24},{12,28},{16,0},{20,4},{24,8},{28,12},{1,17},{... | collective-permute-start | bytes 614408 | tf_op jit(solution)/shard_map/ppermute | solution.py:41
  6.8 0.0 collective-permute-start.2
  6.8 0.0 copy-done
  6.8 0.1 shard_map.104
  6.9 3.1 %collective-permute-start.3 = (bf16[32,1024]{1,0:T(8,128)(2,1)S(1)}, bf16[32,1024]{1,0:T(8,128)(2,1)S(1)}, u32[]{:S(2)}, u32[]{:S(2)}) collective-permute-start(bf16[32,1024]{1,0:T(8,128)(2,1)S(1)} %get-tuple-element.35), channel_id=1, source_target_pairs={{0,2},{1,3},{2,0},{3,1},{4,7},{5,6},{6,5},{7,4},{8,10},{9,11},{10,... | collective-permute-start | bytes 196616 | tf_op jit(solution)/shard_map/ppermute | solution.py:397
  10.0 3.5 %collective-permute-start.4 = (bf16[32,1024]{1,0:T(8,128)(2,1)S(1)}, bf16[32,1024]{1,0:T(8,128)(2,1)S(1)}, u32[]{:S(2)}, u32[]{:S(2)}) collective-permute-start(bf16[32,1024]{1,0:T(8,128)(2,1)S(1)} %get-tuple-element.36), channel_id=1, source_target_pairs={{0,1},{1,0},{2,3},{3,2},{8,9},{9,8},{10,11},{11,10},{16,17},{17,16... | collective-permute-start | bytes 196616 | tf_op jit(solution)/shard_map/ppermute | solution.py:398
  13.5 0.0 collective-permute-done.3.refs_4_
  13.5 2.7 %collective-permute-done.4.refs_5_ = bf16[32,1024]{1,0:T(8,128)(2,1)S(1)} collective-permute-done((bf16[32,1024]{1,0:T(8,128)(2,1)S(1)}, bf16[32,1024]{1,0:T(8,128)(2,1)S(1)}, u32[]{:S(2)}, u32[]{:S(2)}) %collective-permute-start.4) | collective-permute-done | bytes 65568 | tf_op jit(solution)/shard_map/ppermute | solution.py:398
  16.2 0.0 collective-permute-done.refs_1_
  16.2 0.0 collective-permute-done.1.refs_2_
  16.2 0.0 collective-permute-done.2.refs_3_
  16.2 0.1 shard_map.105
  16.3 0.1 collective-permute-start.5
  16.4 0.7 %collective-permute-start.6 = (bf16[128,1024]{1,0:T(8,128)(2,1)S(1)}, bf16[128,1024]{1,0:T(8,128)(2,1)S(1)}, u32[]{:S(2)}, u32[]{:S(2)}) collective-permute-start(bf16[128,1024]{1,0:T(8,128)(2,1)S(1)} %get-tuple-element.37.refs_6_.product_ref), channel_id=1, source_target_pairs={{4,8},{12,16},{20,24},{5,9},{13,17},{21,25},{6,10},{14,18},{22,26}... | collective-permute-start | bytes 786440 | tf_op jit(solution)/shard_map/ppermute | solution.py:399
  17.1 1.4 %shard_map.107 = (f32[2,2,1,256]{3,2,1,0:T(1,128)S(1)}, f32[2,2,1,256]{3,2,1,0:T(1,128)S(1)}, f32[2,2,128,256]{3,2,1,0:T(8,128)S(1)}) custom-call(bf16[4,144,256]{2,1,0:T(8,128)(2,1)S(1)} %get-tuple-element.43.query_ref.refs_0_, bf16[14,128,256]{2,1,0:T(8,128)(2,1)S(1)} %get-tuple-element.38.mine_ref.key_value_ref), custom_call_target="tpu_custom_call" | custom-call | flops 268435456 | bytes 2097152 | tf_op jit(solution)/shard_map/pallas_call | solution.py:29
  18.4 0.4 %collective-permute-done.5.other_ref.refs_4_ = bf16[14,128,256]{2,1,0:T(8,128)(2,1)S(1)} collective-permute-done((bf16[14,128,256]{2,1,0:T(8,128)(2,1)S(1)}, bf16[14,128,256]{2,1,0:T(8,128)(2,1)S(1)}, u32[]{:S(2)}, u32[]{:S(2)}) %collective-permute-start.5) | collective-permute-done | bytes 917536 | tf_op jit(solution)/shard_map/ppermute | solution.py:41
  18.9 1.5 %shard_map.108 = (bf16[144,256]{1,0:T(8,128)(2,1)S(1)}, bf16[144,256]{1,0:T(8,128)(2,1)S(1)}, bf16[144,256]{1,0:T(8,128)(2,1)S(1)}, bf16[144,256]{1,0:T(8,128)(2,1)S(1)}) custom-call(bf16[4,144,256]{2,1,0:T(8,128)(2,1)S(1)} %get-tuple-element.43.query_ref.refs_0_, f32[2,2,1,256]{3,2,1,0:T(1,128)S(1)} %get-tuple-element.44.refs_1_, ...), custom_call_target="tpu_custom_call" | custom-call | flops 268435456 | bytes 2097152 | tf_op jit(solution)/shard_map/pallas_call | solution.py:29
  20.4 1.8 %collective-permute-start.7 = (bf16[144,256]{1,0:T(8,128)(2,1)S(1)}, bf16[144,256]{1,0:T(8,128)(2,1)S(1)}, u32[]{:S(2)}, u32[]{:S(2)}) collective-permute-start(bf16[144,256]{1,0:T(8,128)(2,1)S(1)} %get-tuple-element.48), channel_id=1, source_target_pairs={{0,8},{4,12},{8,0},{12,4},{16,24},{20,28},{24,16},{28,20},{1,9},{5... | collective-permute-start | bytes 221192 | tf_op jit(solution)/shard_map/ppermute | solution.py:41
  22.1 1.5 %collective-permute-start.8 = (bf16[144,256]{1,0:T(8,128)(2,1)S(1)}, bf16[144,256]{1,0:T(8,128)(2,1)S(1)}, u32[]{:S(2)}, u32[]{:S(2)}) collective-permute-start(bf16[144,256]{1,0:T(8,128)(2,1)S(1)} %get-tuple-element.49), channel_id=1, source_target_pairs={{0,16},{4,20},{8,24},{12,28},{16,0},{20,4},{24,8},{28,12},{1,17},{... | collective-permute-start | bytes 221192 | tf_op jit(solution)/shard_map/ppermute | solution.py:41
  23.7 0.3 collective-permute-start.9
  23.9 0.0 collective-permute-done.6.before_ref
  23.9 0.0 copy-start.1
  23.9 0.7 %copy-done.1 = f32[1024]{0:T(1024)S(1)} copy-done((f32[1024]{0:T(1024)S(1)}, f32[1024]{0:T(1024)}, u32[]{:S(2)}) %copy-start.1) | copy-done | bytes 4120
  24.6 0.0 copy-done.2
  24.6 2.9 %shard_map.106 = bf16[128,1024]{1,0:T(8,128)(2,1)} custom-call(bf16[14,128,256]{2,1,0:T(8,128)(2,1)S(1)} %collective-permute-done.5.other_ref.refs_4_, bf16[14,128,256]{2,1,0:T(8,128)(2,1)S(1)} %get-tuple-element.38.mine_ref.key_value_ref, bf16[128,1024]{1,0:T(8,128)(2,1)S(1)} %collective-permute-done.6.before_ref, ...), custom_call_target="tpu_custom_call" | custom-call | flops 536870912 | bytes 2097152 | tf_op jit(solution)/shard_map/pallas_call | solution.py:29
  27.5 0.0 collective-permute-done.7.refs_1_
  27.5 0.0 collective-permute-done.8.refs_2_
  27.5 1.8 %collective-permute-done.9.refs_3_ = bf16[144,256]{1,0:T(8,128)(2,1)S(1)} collective-permute-done((bf16[144,256]{1,0:T(8,128)(2,1)S(1)}, bf16[144,256]{1,0:T(8,128)(2,1)S(1)}, u32[]{:S(2)}, u32[]{:S(2)}) %collective-permute-start.9) | collective-permute-done | bytes 73760 | tf_op jit(solution)/shard_map/ppermute | solution.py:41
  29.3 0.7 %shard_map.109 = (bf16[128,1024]{1,0:T(8,128)(2,1)}, f32[8,128]{1,0:T(8,128)}) custom-call(bf16[144,256]{1,0:T(8,128)(2,1)S(1)} %get-tuple-element.47.refs_0_, bf16[144,256]{1,0:T(8,128)(2,1)S(1)} %collective-permute-done.7.refs_1_, bf16[144,256]{1,0:T(8,128)(2,1)S(1)} %collective-permute-done.8.refs_2_, bf16[144,256]{1,0:T(8,128)(2,1)S(1)} %collective-permute-done.9.refs_3_), custom_call_target="tpu_custom_call" | custom-call | bytes 524288 | tf_op jit(solution)/shard_map/pallas_call | solution.py:29
  (1 shorter events, 0.0 us)
Async XLA Ops:
  0.6 6.2 %copy-start = (bf16[3,128,1024]{2,1,0:T(8,128)(2,1)S(1)}, bf16[3,128,1024]{2,1,0:T(8,128)(2,1)}, u32[]{:S(2)}) copy-start(bf16[3,128,1024]{2,1,0:T(8,128)(2,1)} %gate_ref.1) | copy-start | bytes 2359300
  2.3 13.9 %collective-permute-start = (bf16[400,256]{1,0:T(8,128)(2,1)S(1)}, bf16[400,256]{1,0:T(8,128)(2,1)S(1)}, u32[]{:S(2)}, u32[]{:S(2)}) collective-permute-start(bf16[400,256]{1,0:T(8,128)(2,1)S(1)} %get-tuple-element.29), channel_id=1, source_target_pairs={{0,8},{4,12},{8,0},{12,4},{16,24},{20,28},{24,16},{28,20},{1,9},{5... | collective-permute-start | bytes 614408 | tf_op jit(solution)/shard_map/ppermute | solution.py:41
  5.3 10.9 %collective-permute-start.1 = (bf16[400,256]{1,0:T(8,128)(2,1)S(1)}, bf16[400,256]{1,0:T(8,128)(2,1)S(1)}, u32[]{:S(2)}, u32[]{:S(2)}) collective-permute-start(bf16[400,256]{1,0:T(8,128)(2,1)S(1)} %get-tuple-element.30), channel_id=1, source_target_pairs={{0,16},{4,20},{8,24},{12,28},{16,0},{20,4},{24,8},{28,12},{1,17},{... | collective-permute-start | bytes 614408 | tf_op jit(solution)/shard_map/ppermute | solution.py:41
  6.8 9.4 %collective-permute-start.2 = (bf16[400,256]{1,0:T(8,128)(2,1)S(1)}, bf16[400,256]{1,0:T(8,128)(2,1)S(1)}, u32[]{:S(2)}, u32[]{:S(2)}) collective-permute-start(bf16[400,256]{1,0:T(8,128)(2,1)S(1)} %get-tuple-element.31), channel_id=1, source_target_pairs={{0,24},{4,28},{8,16},{12,20},{16,8},{20,12},{24,0},{28,4},{1,25},{... | collective-permute-start | bytes 614408 | tf_op jit(solution)/shard_map/ppermute | solution.py:41
  6.9 6.6 %collective-permute-start.3 = (bf16[32,1024]{1,0:T(8,128)(2,1)S(1)}, bf16[32,1024]{1,0:T(8,128)(2,1)S(1)}, u32[]{:S(2)}, u32[]{:S(2)}) collective-permute-start(bf16[32,1024]{1,0:T(8,128)(2,1)S(1)} %get-tuple-element.35), channel_id=1, source_target_pairs={{0,2},{1,3},{2,0},{3,1},{4,7},{5,6},{6,5},{7,4},{8,10},{9,11},{10,... | collective-permute-start | bytes 196616 | tf_op jit(solution)/shard_map/ppermute | solution.py:397
  10.0 6.1 %collective-permute-start.4 = (bf16[32,1024]{1,0:T(8,128)(2,1)S(1)}, bf16[32,1024]{1,0:T(8,128)(2,1)S(1)}, u32[]{:S(2)}, u32[]{:S(2)}) collective-permute-start(bf16[32,1024]{1,0:T(8,128)(2,1)S(1)} %get-tuple-element.36), channel_id=1, source_target_pairs={{0,1},{1,0},{2,3},{3,2},{8,9},{9,8},{10,11},{11,10},{16,17},{17,16... | collective-permute-start | bytes 196616 | tf_op jit(solution)/shard_map/ppermute | solution.py:398
  16.3 2.5 %collective-permute-start.5 = (bf16[14,128,256]{2,1,0:T(8,128)(2,1)S(1)}, bf16[14,128,256]{2,1,0:T(8,128)(2,1)S(1)}, u32[]{:S(2)}, u32[]{:S(2)}) collective-permute-start(bf16[14,128,256]{2,1,0:T(8,128)(2,1)S(1)} %get-tuple-element.38.mine_ref.key_value_ref), channel_id=1, source_target_pairs={{0,4},{4,0},{8,12},{12,8},{16,20},{20,16},{24,28},{28,24},{1,5},{5... | collective-permute-start | bytes 2752520 | tf_op jit(solution)/shard_map/ppermute | solution.py:41
  16.4 7.5 %collective-permute-start.6 = (bf16[128,1024]{1,0:T(8,128)(2,1)S(1)}, bf16[128,1024]{1,0:T(8,128)(2,1)S(1)}, u32[]{:S(2)}, u32[]{:S(2)}) collective-permute-start(bf16[128,1024]{1,0:T(8,128)(2,1)S(1)} %get-tuple-element.37.refs_6_.product_ref), channel_id=1, source_target_pairs={{4,8},{12,16},{20,24},{5,9},{13,17},{21,25},{6,10},{14,18},{22,26}... | collective-permute-start | bytes 786440 | tf_op jit(solution)/shard_map/ppermute | solution.py:399
  20.4 7.1 %collective-permute-start.7 = (bf16[144,256]{1,0:T(8,128)(2,1)S(1)}, bf16[144,256]{1,0:T(8,128)(2,1)S(1)}, u32[]{:S(2)}, u32[]{:S(2)}) collective-permute-start(bf16[144,256]{1,0:T(8,128)(2,1)S(1)} %get-tuple-element.48), channel_id=1, source_target_pairs={{0,8},{4,12},{8,0},{12,4},{16,24},{20,28},{24,16},{28,20},{1,9},{5... | collective-permute-start | bytes 221192 | tf_op jit(solution)/shard_map/ppermute | solution.py:41
  22.1 5.3 %collective-permute-start.8 = (bf16[144,256]{1,0:T(8,128)(2,1)S(1)}, bf16[144,256]{1,0:T(8,128)(2,1)S(1)}, u32[]{:S(2)}, u32[]{:S(2)}) collective-permute-start(bf16[144,256]{1,0:T(8,128)(2,1)S(1)} %get-tuple-element.49), channel_id=1, source_target_pairs={{0,16},{4,20},{8,24},{12,28},{16,0},{20,4},{24,8},{28,12},{1,17},{... | collective-permute-start | bytes 221192 | tf_op jit(solution)/shard_map/ppermute | solution.py:41
  23.7 5.6 %collective-permute-start.9 = (bf16[144,256]{1,0:T(8,128)(2,1)S(1)}, bf16[144,256]{1,0:T(8,128)(2,1)S(1)}, u32[]{:S(2)}, u32[]{:S(2)}) collective-permute-start(bf16[144,256]{1,0:T(8,128)(2,1)S(1)} %get-tuple-element.50), channel_id=1, source_target_pairs={{0,24},{4,28},{8,16},{12,20},{16,8},{20,12},{24,0},{28,4},{1,25},{... | collective-permute-start | bytes 221192 | tf_op jit(solution)/shard_map/ppermute | solution.py:41
  23.9 0.7 %copy-start.1 = (f32[1024]{0:T(1024)S(1)}, f32[1024]{0:T(1024)}, u32[]{:S(2)}) copy-start(f32[1024]{0:T(1024)} %param.10) | copy-start | bytes 12292
  23.9 0.7 %copy-start.2 = (s32[128]{0:T(128)S(1)}, s32[128]{0:T(128)}, u32[]{:S(2)}) copy-start(s32[128]{0:T(128)} %param.13) | copy-start | bytes 1540

commit v2 on v1

--- a/solution.py
+++ b/solution.py
@@ -47,10 +47,8 @@
     return index // heads, member // 2, lax.rem(member, 2)
 
 
-def pack_heads(heads, extra, queries_ref, keys_values_ref, starts_ref, *refs):
-    extras, refs = refs[:extra], refs[extra:]
-    *outs, held_ref, start_sem, extra_sem, sem = refs
-    outs, brought = outs[:-extra], outs[-extra:]
+def pack_heads(heads, queries_ref, keys_values_ref, starts_ref, *refs):
+    *outs, held_ref, start_sem, sem = refs
     rows = queries_ref.shape[0]
     _, pair, _ = place(heads)
     first = pltpu.make_async_copy(starts_ref, held_ref, start_sem)
@@ -66,8 +64,6 @@
                     source.at[:, columns], out.at[pl.ds(part * rows, rows)], sem.at[step, part]
                 )
             )
-    for index, (source, out) in enumerate(zip(extras, brought)):
-        copies.append(pltpu.make_async_copy(source, out, extra_sem.at[index]))
     for copy in copies:
         copy.start()
     first.wait()
@@ -90,27 +86,36 @@
 
 
 def pack_hyena(
-    hyena_ref, filters_ref, ahead_ref, wide_back_ref,
-    product_ref, own_ref, far_ref, near_ref, early_ref, late_ref, back_ref,
+    hyena_ref, filters_ref, ahead_ref, back_ref, starts_ref, skip_ref,
+    product_ref, own_ref, far_ref, near_ref, early_ref, late_ref, back_out, starts_out, skip_out,
+    taps_ref, ahead_held, back_held, sem,
 ):
-    product_ref[...] = (hyena_ref[1].astype(jnp.float32) * hyena_ref[2].astype(jnp.float32)).astype(
-        jnp.bfloat16
-    )
     width = own_ref.shape[1]
     panel = lax.axis_index("tp")
     parity = lax.rem(lax.axis_index("ctx"), 2)
-
-    def taps(target):
+    targets = (panel, panel ^ (3 - parity), panel ^ 1)
+    pairs = [(ahead_ref, ahead_held), (back_ref, back_held)]
+    pairs += [(starts_ref, starts_out), (skip_ref, skip_out)]
+    for index, target in enumerate(targets):
         columns = pl.ds(pl.multiple_of(target * width, width), width)
-        return filters_ref[:, columns].astype(jnp.bfloat16)
-
-    own_ref[...] = taps(panel)
-    far_ref[...] = taps(panel ^ (2 + parity))
-    near_ref[...] = taps(panel ^ 1)
+        pairs.append((filters_ref.at[:, columns], taps_ref.at[index]))
+    copies = [
+        pltpu.make_async_copy(source, out, sem.at[index])
+        for index, (source, out) in enumerate(pairs)
+    ]
+    for copy in copies:
+        copy.start()
+    product_ref[...] = (hyena_ref[1].astype(jnp.float32) * hyena_ref[2].astype(jnp.float32)).astype(
+        jnp.bfloat16
+    )
+    for copy in copies:
+        copy.wait()
+    for index, out in enumerate((own_ref, far_ref, near_ref)):
+        out[...] = taps_ref[index].astype(jnp.bfloat16)
     rows = product_ref.shape[0]
-    early_ref[...] = split(ahead_ref[:, :rows])
-    late_ref[...] = split(ahead_ref[:, rows:])
-    back_ref[...] = wide_back_ref[...].astype(jnp.bfloat16)
+    early_ref[...] = split(ahead_held[:, :rows])
+    late_ref[...] = split(ahead_held[:, rows:])
+    back_out[...] = back_held[...].astype(jnp.bfloat16)
 
 
 def columns_of(ref, rows, index):
@@ -140,47 +145,66 @@
 UNIT = 2
 
 
-def key_set(ref, blocks, head, origin, parity, own):
+def key_set(ref, blocks, head, origin, parity, causal):
     columns = slice(head * HD, (head + 1) * HD)
     rows = ref.shape[1]
     key = jnp.concatenate([ref[2 * block, :, columns] for block in range(blocks)], axis=0)
     value = jnp.concatenate([ref[2 * block + 1, :, columns] for block in range(blocks)], axis=0)
-    firsts = [((2 * block + parity) * rows + origin, block >= own) for block in range(blocks)]
-    return key, value, firsts
-
-
-def masked_scores(sets, query, start, own):
-    blocks = []
-    for key, _, firsts in sets:
+    return key, value, [(2 * block + parity) * rows + origin for block in range(blocks)], causal
+
+
+def masked_scores(sets, query, start, own, begin):
+    held = [[] for _ in range(UNIT)]
+    for key, _, firsts, causal in sets:
         scores = lax.dot_general(
             key, query, (((1,), (1,)), ((), ())), preferred_element_type=jnp.float32
         )
         rows = key.shape[0] // len(firsts)
-        line = lax.broadcasted_iota(jnp.int32, (rows, query.shape[0]), 0)
-        for index, (first, causal) in enumerate(firsts):
-            allowed = line >= start - first
-            if causal:
-                allowed &= line <= own - first
-            blocks.append(jnp.where(allowed, scores[index * rows : (index + 1) * rows], MASKED))
-    return blocks
-
-
-def highest(blocks):
-    return jnp.max(functools.reduce(jnp.maximum, blocks), axis=0, keepdims=True)
-
-
-def weigh(sets, blocks, top):
-    weights = [jnp.exp2((block - top) * FACTOR) for block in blocks]
-    total = jnp.sum(functools.reduce(jnp.add, weights), axis=0, keepdims=True)
-    value = jnp.concatenate([one[1] for one in sets], axis=0)
-    rounded = jnp.concatenate([each.astype(jnp.bfloat16) for each in weights], axis=0)
-    return total, dot(value.T, rounded)
-
-
-def unit_rows(heads, query_ref, head, begin):
+        line = lax.broadcasted_iota(jnp.int32, (rows, rows), 0)
+        for block, first in enumerate(firsts):
+            for index in range(UNIT):
+                if causal and block > begin + index:
+                    held[index].append(None)
+                    continue
+                lanes = slice(index * rows, (index + 1) * rows)
+                allowed = line >= start[:, lanes] - first
+                if causal and block == begin + index:
+                    allowed &= line <= own[:, lanes] - first
+                part = scores[block * rows : (block + 1) * rows, lanes]
+                held[index].append(jnp.where(allowed, part, MASKED))
+    return held
+
+
+def highest(held):
+    tops = [functools.reduce(jnp.maximum, [x for x in parts if x is not None]) for parts in held]
+    return jnp.concatenate([jnp.max(top, axis=0, keepdims=True) for top in tops], axis=1)
+
+
+def weigh(held, top):
+    totals, rounded = [], []
+    for index, parts in enumerate(held):
+        rows = next(x for x in parts if x is not None).shape[1]
+        here = top[:, index * rows : (index + 1) * rows]
+        weights = [None if x is None else jnp.exp2((x - here) * FACTOR) for x in parts]
+        total = functools.reduce(jnp.add, [x for x in weights if x is not None])
+        totals.append(jnp.sum(total, axis=0, keepdims=True))
+        rounded.append(
+            [
+                jnp.zeros((rows, rows), jnp.bfloat16) if x is None else x.astype(jnp.bfloat16)
+                for x in weights
+            ]
+        )
+    lines = [jnp.concatenate(line, axis=1) for line in zip(*rounded)]
+    return jnp.concatenate(totals, axis=1), jnp.concatenate(lines, axis=0)
+
+
+def mix(sets, rounded):
+    return dot(jnp.concatenate([one[1] for one in sets], axis=0).T, rounded)
+
+
+def unit_rows(heads, query_ref, begin):
     rows = query_ref.shape[1] - NOTE_ROWS
     group, _, parity = place(heads)
-    query = query_ref[begin : begin + UNIT, :rows, head * HD : (head + 1) * HD]
     starts = []
     for block in range(begin, begin + UNIT):
         note = query_ref[block, rows:, :HD].astype(jnp.float32)
@@ -188,48 +212,66 @@
     start = jnp.concatenate(starts, axis=1).astype(jnp.int32) - group * (heads * rows)
     line = lax.broadcasted_iota(jnp.int32, (1, UNIT * rows), 1)
     own = line // rows * rows + line + (2 * begin + parity) * rows
-    return query.reshape(UNIT * rows, HD), start, own
+    return start, own
+
+
+def unit_queries(query_ref, head, begin):
+    rows = query_ref.shape[1] - NOTE_ROWS
+    blocks = range(begin, begin + UNIT)
+    columns = slice(head * HD, (head + 1) * HD)
+    return jnp.concatenate([query_ref[block, :rows, columns] for block in blocks], axis=0)
 
 
 FACTOR = math.log2(math.e) / math.sqrt(HD)
 
 
 def attend_first(heads, query_ref, key_value_ref, top_ref, total_ref, mixed_ref):
-    rows = query_ref.shape[1] - NOTE_ROWS
     _, _, parity = place(heads)
-    for head in range(2):
-        for unit in range(heads // 2 // UNIT):
-            begin = unit * UNIT
-            query, start, own = unit_rows(heads, query_ref, head, begin)
-            sets = [key_set(key_value_ref, begin + UNIT, head, 0, parity, begin)]
-            blocks = masked_scores(sets, query, start, own)
-            top = highest(blocks)
-            top_ref[head, unit] = top
-            total_ref[head, unit], mixed_ref[head, unit] = weigh(sets, blocks, top)
-
-
-def attend_second(heads, *refs):
+    for unit in range(heads // 2 // UNIT):
+        begin = unit * UNIT
+        start, own = unit_rows(heads, query_ref, begin)
+        sets = [[key_set(key_value_ref, begin + UNIT, head, 0, parity, True)] for head in range(2)]
+        held = [
+            masked_scores(sets[head], unit_queries(query_ref, head, begin), start, own, begin)
+            for head in range(2)
+        ]
+        tops = [highest(each) for each in held]
+        weights = [weigh(each, top) for each, top in zip(held, tops)]
+        for head, (total, rounded) in enumerate(weights):
+            top_ref[head, unit] = tops[head]
+            total_ref[head, unit] = total
+            mixed_ref[head, unit] = mix(sets[head], rounded)
+
+
+def attend_second(heads, mine, *refs):
     count = heads // 2
-    query_ref, top_ref, total_ref, mixed_ref, other_ref, *more = refs[: -count - 1]
-    outs, held_ref = refs[-count - 1 : -1], refs[-1]
+    query_ref, top_ref, total_ref, mixed_ref, other_ref, *more = refs[: -UNIT - 1]
+    outs, held_ref = refs[-UNIT - 1 : -1], refs[-1]
+    more = more[: len(more) // 2 * 2]
     rows = query_ref.shape[1] - NOTE_ROWS
     _, pair, parity = place(heads)
-    for head in range(2):
-        columns = slice(head * HD, (head + 1) * HD)
-        for unit in range(count // UNIT):
-            begin = unit * UNIT
-            query, start, own = unit_rows(heads, query_ref, head, begin)
-            sets = [key_set(other_ref, begin + UNIT, head, 0, 1 - parity, begin)]
+    here = pair // UNIT
+
+    def one_unit(unit):
+        begin = unit * UNIT
+        start, own = unit_rows(heads, query_ref, begin)
+        sets, held, tops = [], [], []
+        for head in range(2):
+            sets.append([key_set(other_ref, begin + UNIT, head, 0, 1 - parity, True)])
             for ref, side in zip(more, (parity, 1 - parity)):
-                sets.append(key_set(ref, count, head, -heads * rows, side, count))
-            blocks = masked_scores(sets, query, start, own)
-            before = top_ref[head, unit]
-            top = jnp.maximum(before, highest(blocks))
-            scale = jnp.exp2((before - top) * FACTOR)
-            total, mixed = weigh(sets, blocks, top)
+                sets[head].append(key_set(ref, count, head, -heads * rows, side, False))
+            query = unit_queries(query_ref, head, begin)
+            held.append(masked_scores(sets[head], query, start, own, begin))
+        for head in range(2):
+            tops.append(jnp.maximum(top_ref[head, unit], highest(held[head])))
+        weights = [weigh(each, top) for each, top in zip(held, tops)]
+        for head, (total, rounded) in enumerate(weights):
+            columns = slice(head * HD, (head + 1) * HD)
+            top = tops[head]
+            scale = jnp.exp2((top_ref[head, unit] - top) * FACTOR)
             total = total_ref[head, unit] * scale + total
-            mixed = mixed_ref[head, unit] * scale + mixed
-            mixed = (mixed / total).T.astype(jnp.bfloat16)
+            mixed = mixed_ref[head, unit] * scale + mix(sets[head], rounded)
+            mixed = (mixed * (1.0 / total)).astype(jnp.bfloat16).T
             logs = top * (1.0 / math.sqrt(HD)) + jnp.log(total)
             high = logs.astype(jnp.bfloat16).astype(jnp.float32)
             middle = (logs - high).astype(jnp.bfloat16).astype(jnp.float32)
@@ -240,17 +282,24 @@
             ).astype(jnp.bfloat16)
             for index in range(UNIT):
                 span = slice(index * rows, (index + 1) * rows)
-                held_ref[begin + index, :rows, columns] = mixed[span]
-                held_ref[begin + index, rows:, columns] = note[:, span]
+                held_ref[index, :rows, columns] = mixed[span]
+                held_ref[index, rows:, columns] = note[:, span]
+
+    for unit in range(count // UNIT):
+
+        @pl.when((here == unit) if mine else (here != unit))
+        def _():
+            one_unit(unit)
+
     for step, out in enumerate(outs):
-        out[...] = held_ref[pair ^ step]
-
-
-def unpack_heads(heads, *refs):
+        out[...] = held_ref[lax.rem(pair, UNIT) ^ step]
+
+
+def unpack_heads(heads, steps, *refs):
     *sources, out_ref, logs_ref = refs
     rows = out_ref.shape[0]
     _, pair, _ = place(heads)
-    for step, source in enumerate(sources):
+    for step, source in zip(steps, sources):
         owner = pair ^ step
         out_ref[:, pl.ds(pl.multiple_of(owner * (2 * HD), 2 * HD), 2 * HD)] = source[:rows]
         note = source[rows:].astype(jnp.float32)
@@ -298,9 +347,9 @@
         line = slice(part * height, (part + 1) * height)
         mine_far, other_far = mine_ref[heads, line], other_ref[heads, line]
         store(0, part, columns_of(own_taps_ref, everything, part))
-        store(1, part, jnp.where(even, mine_ref[heads + 1, line], other_ref[heads + 1, line]))
-        store(2, part, jnp.where(even, mine_far, other_far))
-        store(3, part, jnp.where(even, other_far, mine_far))
+        store(1, part, jnp.where(even, other_ref[heads + 1, line], mine_ref[heads + 1, line]))
+        store(2, part, jnp.where(even, other_far, mine_far))
+        store(3, part, jnp.where(even, mine_far, other_far))
         halo_ref[:, part * 2 * HD : (part + 1) * 2 * HD] = jnp.where(
             even, columns_of(before_ref, everything, part), other_ref[heads + 2 + part]
         )
@@ -344,8 +393,8 @@
     for peer in range(peers):
         for panel in range(panels):
             here = peer * panels + panel
-            far.append((here, peer * panels + (panel ^ (2 + peer % 2))))
-            if peer % 2 == 0:
+            far.append((here, peer * panels + (panel ^ (3 - peer % 2))))
+            if peer % 2 == 1:
                 near.append((here, peer * panels + (panel ^ 1)))
     return far, near
 
@@ -360,37 +409,45 @@
     shape = jax.ShapeDtypeStruct
     starts = doc_start.reshape(1, rows)
 
-    extras = (filters, *twiddles(rows))
-    *packed, near_filters, ahead, back = call(
-        functools.partial(pack_heads, heads, len(extras)),
-        (shape((3 * rows + NOTE_ROWS, 2 * HD), bf16),) * count
-        + tuple(shape(x.shape, x.dtype) for x in extras),
-        [
-            pltpu.with_memory_space_constraint(x, pltpu.HBM)
-            for x in (queries, keys_values, starts, *extras)
-        ],
+    packed = call(
+        functools.partial(pack_heads, heads),
+        (shape((3 * rows + NOTE_ROWS, 2 * HD), bf16),) * count,
+        [pltpu.with_memory_space_constraint(x, pltpu.HBM) for x in (queries, keys_values, starts)],
         0,
         4 * queries.size * 3,
         scratch=(
             pltpu.VMEM((1, rows), jnp.int32),
             pltpu.SemaphoreType.DMA,
-            pltpu.SemaphoreType.DMA((len(extras),)),
             pltpu.SemaphoreType.DMA((count, 3)),
         ),
-        specs=[hbm()] * (3 + len(extras)),
+        specs=[hbm()] * 3,
     )
     arrived = [packed[0]] + [None] * (count - 1)
     for step in reversed(range(1, count)):
         arrived[step] = crossed(packed[step], "ctx", 2 * step)
-    product, own_taps, far_taps, near_taps, early, late, back = call(
+    height = filters.shape[0]
+    ahead, back = twiddles(rows)
+    near_hbm = [
+        pltpu.with_memory_space_constraint(x, pltpu.HBM)
+        for x in (filters, ahead, back, starts, skip_bias.reshape(1, channels))
+    ]
+    product, own_taps, far_taps, near_taps, early, late, back, near_starts, skip = call(
         pack_hyena,
         (shape((rows, channels), bf16),)
-        + (shape((filters.shape[0], channels), bf16),) * 3
+        + (shape((height, channels), bf16),) * 3
         + (shape((2 * rows, 2 * rows), bf16),) * 2
-        + (shape((rows, 2 * rows), bf16),),
-        (hyena_inputs, near_filters, ahead, back),
+        + (shape((rows, 2 * rows), bf16),)
+        + (shape((1, rows), jnp.int32), shape((1, channels), f32)),
+        (hyena_inputs, *near_hbm),
         0,
         4 * queries.size * 3,
+        scratch=(
+            pltpu.VMEM((3, height, channels), f32),
+            pltpu.VMEM((2 * rows, 2 * rows), f32),
+            pltpu.VMEM((rows, 2 * rows), f32),
+            pltpu.SemaphoreType.DMA((7,)),
+        ),
+        specs=[vmem()] + [hbm()] * 5,
     )
     axes = ("ctx", "tp")
     far_pairs, near_pairs = taps_pairs(peers, lax.axis_size("tp"))
@@ -424,23 +481,29 @@
     if peers > heads:
         pairs = [(i, i + heads) for i in range(peers - heads)]
         operands += [lax.ppermute(each, "ctx", pairs) for each in (key_value, other)]
-    mixed = call(
-        functools.partial(attend_second, heads),
-        (shape((rows + NOTE_ROWS, 2 * HD), bf16),) * count,
-        operands,
-        2 * (heads * rows) ** 2 * HD,
-        4 * queries.size * 4,
-        scratch=(pltpu.VMEM((count, rows + NOTE_ROWS, 2 * HD), bf16),),
-    )
-    returned = [mixed[0]] + [None] * (count - 1)
-    for step in reversed(range(1, count)):
-        returned[step] = crossed(mixed[step], "ctx", 2 * step)
+    assert count == 2 * UNIT
+    message = shape((rows + NOTE_ROWS, 2 * HD), bf16)
+
+    def second(mine, *more):
+        return call(
+            functools.partial(attend_second, heads, mine),
+            (message,) * UNIT,
+            (*operands, *more),
+            (heads * rows) ** 2 * HD,
+            4 * queries.size * 4,
+            scratch=(pltpu.VMEM((UNIT, rows + NOTE_ROWS, 2 * HD), bf16),),
+        )
+
+    theirs = second(False)
+    own = second(True, theirs[0])
+    returned = [own[0], crossed(theirs[0], "ctx", 4), crossed(theirs[1], "ctx", 6)]
+    returned.append(crossed(own[1], "ctx", 2))
     hyena_out = call(
         functools.partial(convolve, heads),
         shape((rows, channels), bf16),
         (
-            other, key_value, before, own_taps, starts, product, hyena_inputs,
-            skip_bias.reshape(1, channels), early, late, back,
+            other, key_value, before, own_taps, near_starts, product, hyena_inputs,
+            skip, early, late, back,
         ),
         2 * 4 * 256 * 256 * channels,
         4 * queries.size * 4,
@@ -452,7 +515,7 @@
         ),
     )
     attention_out, log_totals = call(
-        functools.partial(unpack_heads, heads),
+        functools.partial(unpack_heads, heads, (0, 2, 3, 1)),
         (shape((rows, heads * HD), bf16), shape((heads, rows), f32)),
         returned,
         0,

time: 30.2 us -> 28.3 us (0.937)
  starting transfers between devices: 15.4 us -> 13.7 us
  local copies, waits for them, and re-layouts: 0.69 us -> 0.01 us
  waiting for transfers between devices: 4.89 us -> 5.53 us
    ppermute x1, starting transfers between devices: 3.47 us -> 0.65 us  [local(): near_taps = lax.ppermute(near_taps, axes, near_pairs)]
    ppermute x1, waiting for transfers between devices: 2.66 us -> 0.01 us  [local(): near_taps = lax.ppermute(near_taps, axes, near_pairs)]
    ppermute x1, waiting for transfers between devices: 0.01 us -> 2 us  [local(): far_taps = lax.ppermute(far_taps, axes, far_pairs)]
    ppermute x7, waiting for transfers between devices: 2.23 us -> 3.53 us  [crossed(): lax.ppermute(array, axis, [(i, i ^ bits) for i in range(lax.axis_size(axi...]
    ppermute x1, starting transfers between devices: 3.11 us -> 4.12 us  [local(): far_taps = lax.ppermute(far_taps, axes, far_pairs)]
    unnamed x6 -> x2, local copies, waits for them, and re-layouts: 0.69 us -> 0.01 us
    pallas_call x7 -> x8, Pallas kernels: 8.28 us -> 8.07 us  [call(): pl.pallas_call(kernel, out_shape=out_shape, in_specs=specs or [vmem() for...]
  transfers between devices with their start and end apart: 10 -> 10, of which waited for: 3 -> 5; matrix products, arithmetic and copies ran while one was open for 0% -> 0% of each run, Pallas kernels for 19% -> 21%
where the time goes in v2:
time: 28.3 us; the launch traced here: 28 us
  starting transfers between devices  13.7 us (48%)
  Pallas kernels  8.07 us (29%)
  waiting for transfers between devices  5.53 us (20%)
  between operations  0.71 us (3%)
    ppermute x7, starting transfers between devices, crossed(): lax.ppermute(array, axis, [(i, i ^ bits) for i in range(lax.axis_size(axi...  8.25 us
    pallas_call x8, Pallas kernels, call(): pl.pallas_call(kernel, out_shape=out_shape, in_specs=specs or [vmem() for...  8.07 us
    ppermute x1, starting transfers between devices, local(): far_taps = lax.ppermute(far_taps, axes, far_pairs)  4.12 us
    ppermute x7, waiting for transfers between devices, crossed(): lax.ppermute(array, axis, [(i, i ^ bits) for i in range(lax.axis_size(axi...  3.53 us
    ppermute x1, waiting for transfers between devices, local(): far_taps = lax.ppermute(far_taps, axes, far_pairs)  2 us
    ppermute x1, starting transfers between devices, local(): lax.ppermute(product, 'ctx', [(i, i + 1) for i in range(1, peers - 1, 2)])  0.68 us
    ppermute x1, starting transfers between devices, local(): near_taps = lax.ppermute(near_taps, axes, near_pairs)  0.65 us
  transfers between devices with their start and end apart: 10, of which 5 were waited for; matrix products, arithmetic and copies ran while one was open for 0% of the time, Pallas kernels for 21%

profile of v2, /device:TPU:0, one launch (start us, length us, event | category | flops | bytes accessed | tf_op | source)
XLA Modules:
  0.0 28.0 jit_solution(898624668179070960)
XLA Ops:
  0.6 0.0 copy-start
  0.6 1.4 %shard_map.103 = (bf16[400,256]{1,0:T(8,128)(2,1)S(1)}, bf16[400,256]{1,0:T(8,128)(2,1)S(1)}, bf16[400,256]{1,0:T(8,128)(2,1)S(1)}, bf16[400,256]{1,0:T(8,128)(2,1)S(1)}) custom-call(bf16[128,1024]{1,0:T(8,128)(2,1)} %queries_ref.1, bf16[2,128,1024]{2,1,0:T(8,128)(2,1)} %keys_values_ref.1, s32[1,128]{1,0:T(1,128)} %bitcast.3), custom_call_target="tpu_custom_call" | custom-call | bytes 1572864 | tf_op jit(solution)/shard_map/pallas_call | solution.py:29
  2.0 3.0 %collective-permute-start = (bf16[400,256]{1,0:T(8,128)(2,1)S(1)}, bf16[400,256]{1,0:T(8,128)(2,1)S(1)}, u32[]{:S(2)}, u32[]{:S(2)}) collective-permute-start(bf16[400,256]{1,0:T(8,128)(2,1)S(1)} %get-tuple-element.28), channel_id=1, source_target_pairs={{0,8},{4,12},{8,0},{12,4},{16,24},{20,28},{24,16},{28,20},{1,9},{5... | collective-permute-start | bytes 614408 | tf_op jit(solution)/shard_map/ppermute | solution.py:41
  5.0 1.5 %collective-permute-start.1 = (bf16[400,256]{1,0:T(8,128)(2,1)S(1)}, bf16[400,256]{1,0:T(8,128)(2,1)S(1)}, u32[]{:S(2)}, u32[]{:S(2)}) collective-permute-start(bf16[400,256]{1,0:T(8,128)(2,1)S(1)} %get-tuple-element.29), channel_id=1, source_target_pairs={{0,16},{4,20},{8,24},{12,28},{16,0},{20,4},{24,8},{28,12},{1,17},{... | collective-permute-start | bytes 614408 | tf_op jit(solution)/shard_map/ppermute | solution.py:41
  6.5 0.0 collective-permute-start.2
  6.6 0.0 copy-done
  6.6 1.3 %shard_map.104 = (bf16[128,1024]{1,0:T(8,128)(2,1)S(1)}, bf16[32,1024]{1,0:T(8,128)(2,1)S(1)}, bf16[32,1024]{1,0:T(8,128)(2,1)S(1)}, bf16[32,1024]{1,0:T(8,128)(...) custom-call(bf16[3,128,1024]{2,1,0:T(8,128)(2,1)S(1)} %copy-done, ...), custom_call_target="tpu_custom_call" | custom-call | bytes 1572864 | tf_op jit(solution)/shard_map/pallas_call | solution.py:29
  7.9 4.1 %collective-permute-start.3 = (bf16[32,1024]{1,0:T(8,128)(2,1)S(1)}, bf16[32,1024]{1,0:T(8,128)(2,1)S(1)}, u32[]{:S(2)}, u32[]{:S(2)}) collective-permute-start(bf16[32,1024]{1,0:T(8,128)(2,1)S(1)} %get-tuple-element.31), channel_id=1, source_target_pairs={{0,3},{1,2},{2,1},{3,0},{4,6},{5,7},{6,4},{7,5},{8,11},{9,10},{10,... | collective-permute-start | bytes 196616 | tf_op jit(solution)/shard_map/ppermute | solution.py:454
  12.0 0.7 %collective-permute-start.4 = (bf16[32,1024]{1,0:T(8,128)(2,1)S(1)}, bf16[32,1024]{1,0:T(8,128)(2,1)S(1)}, u32[]{:S(2)}, u32[]{:S(2)}) collective-permute-start(bf16[32,1024]{1,0:T(8,128)(2,1)S(1)} %get-tuple-element.32), channel_id=1, source_target_pairs={{4,5},{5,4},{6,7},{7,6},{12,13},{13,12},{14,15},{15,14},{20,21},{2... | collective-permute-start | bytes 196616 | tf_op jit(solution)/shard_map/ppermute | solution.py:455
  12.7 2.0 %collective-permute-done.3.refs_4_ = bf16[32,1024]{1,0:T(8,128)(2,1)S(1)} collective-permute-done((bf16[32,1024]{1,0:T(8,128)(2,1)S(1)}, bf16[32,1024]{1,0:T(8,128)(2,1)S(1)}, u32[]{:S(2)}, u32[]{:S(2)}) %collective-permute-start.3) | collective-permute-done | bytes 65568 | tf_op jit(solution)/shard_map/ppermute | solution.py:454
  14.7 0.0 collective-permute-done.4.refs_5_
  14.7 0.0 collective-permute-done.refs_1_
  14.7 1.3 %collective-permute-done.1.refs_2_ = bf16[400,256]{1,0:T(8,128)(2,1)S(1)} collective-permute-done((bf16[400,256]{1,0:T(8,128)(2,1)S(1)}, bf16[400,256]{1,0:T(8,128)(2,1)S(1)}, u32[]{:S(2)}, u32[]{:S(2)}) %collective-permute-start.1) | collective-permute-done | bytes 204832 | tf_op jit(solution)/shard_map/ppermute | solution.py:41
  15.9 0.0 collective-permute-done.2.refs_3_
  15.9 0.1 shard_map.105
  16.1 0.1 collective-permute-start.5
  16.1 0.7 %collective-permute-start.6 = (bf16[128,1024]{1,0:T(8,128)(2,1)S(1)}, bf16[128,1024]{1,0:T(8,128)(2,1)S(1)}, u32[]{:S(2)}, u32[]{:S(2)}) collective-permute-start(bf16[128,1024]{1,0:T(8,128)(2,1)S(1)} %get-tuple-element.33.refs_6_.product_ref), channel_id=1, source_target_pairs={{4,8},{12,16},{20,24},{5,9},{13,17},{21,25},{6,10},{14,18},{22,26}... | collective-permute-start | bytes 786440 | tf_op jit(solution)/shard_map/ppermute | solution.py:456
  16.8 1.0 %shard_map.107 = (f32[2,2,1,256]{3,2,1,0:T(1,128)S(1)}, f32[2,2,1,256]{3,2,1,0:T(1,128)S(1)}, f32[2,2,128,256]{3,2,1,0:T(8,128)S(1)}) custom-call(bf16[4,144,256]{2,1,0:T(8,128)(2,1)S(1)} %get-tuple-element.41.query_ref.refs_0_, bf16[14,128,256]{2,1,0:T(8,128)(2,1)S(1)} %get-tuple-element.34.mine_ref.key_value_ref), custom_call_target="tpu_custom_call" | custom-call | flops 268435456 | bytes 2097152 | tf_op jit(solution)/shard_map/pallas_call | solution.py:29
  17.8 0.8 %collective-permute-done.5.other_ref.refs_4_ = bf16[14,128,256]{2,1,0:T(8,128)(2,1)S(1)} collective-permute-done((bf16[14,128,256]{2,1,0:T(8,128)(2,1)S(1)}, bf16[14,128,256]{2,1,0:T(8,128)(2,1)S(1)}, u32[]{:S(2)}, u32[]{:S(2)}) %collective-permute-start.5) | collective-permute-done | bytes 917536 | tf_op jit(solution)/shard_map/ppermute | solution.py:41
  18.6 0.8 %shard_map.108 = (bf16[144,256]{1,0:T(8,128)(2,1)S(1)}, bf16[144,256]{1,0:T(8,128)(2,1)S(1)}) custom-call(bf16[4,144,256]{2,1,0:T(8,128)(2,1)S(1)} %get-tuple-element.41.query_ref.refs_0_, f32[2,2,1,256]{3,2,1,0:T(1,128)S(1)} %get-tuple-element.42.refs_1_, f32[2,2,1,256]{3,2,1,0:T(1,128)S(1)} %get-tuple-element.43.refs_2_, ...), custom_call_target="tpu_custom_call" | custom-call | flops 134217728 | bytes 2097152 | tf_op jit(solution)/shard_map/pallas_call | solution.py:29
  19.4 1.4 %collective-permute-start.7 = (bf16[144,256]{1,0:T(8,128)(2,1)S(1)}, bf16[144,256]{1,0:T(8,128)(2,1)S(1)}, u32[]{:S(2)}, u32[]{:S(2)}) collective-permute-start(bf16[144,256]{1,0:T(8,128)(2,1)S(1)} %get-tuple-element.45.refs_5_), channel_id=1, source_target_pairs={{0,16},{4,20},{8,24},{12,28},{16,0},{20,4},{24,8},{28,12},{1,17},{... | collective-permute-start | bytes 221192 | tf_op jit(solution)/shard_map/ppermute | solution.py:41
  20.8 1.4 %collective-permute-start.8 = (bf16[144,256]{1,0:T(8,128)(2,1)S(1)}, bf16[144,256]{1,0:T(8,128)(2,1)S(1)}, u32[]{:S(2)}, u32[]{:S(2)}) collective-permute-start(bf16[144,256]{1,0:T(8,128)(2,1)S(1)} %get-tuple-element.47), channel_id=1, source_target_pairs={{0,24},{4,28},{8,16},{12,20},{16,8},{20,12},{24,0},{28,4},{1,25},{... | collective-permute-start | bytes 221192 | tf_op jit(solution)/shard_map/ppermute | solution.py:41
  22.1 0.6 %shard_map.109 = (bf16[144,256]{1,0:T(8,128)(2,1)S(1)}, bf16[144,256]{1,0:T(8,128)(2,1)S(1)}) custom-call(bf16[4,144,256]{2,1,0:T(8,128)(2,1)S(1)} %get-tuple-element.41.query_ref.refs_0_, f32[2,2,1,256]{3,2,1,0:T(1,128)S(1)} %get-tuple-element.42.refs_1_, f32[2,2,1,256]{3,2,1,0:T(1,128)S(1)} %get-tuple-element.43.refs_2_, ...), custom_call_target="tpu_custom_call" | custom-call | flops 134217728 | bytes 2097152 | tf_op jit(solution)/shard_map/pallas_call | solution.py:29
  22.7 0.9 %collective-permute-start.9 = (bf16[144,256]{1,0:T(8,128)(2,1)S(1)}, bf16[144,256]{1,0:T(8,128)(2,1)S(1)}, u32[]{:S(2)}, u32[]{:S(2)}) collective-permute-start(bf16[144,256]{1,0:T(8,128)(2,1)S(1)} %get-tuple-element.48), channel_id=1, source_target_pairs={{0,8},{4,12},{8,0},{12,4},{16,24},{20,28},{24,16},{28,20},{1,9},{5... | collective-permute-start | bytes 221192 | tf_op jit(solution)/shard_map/ppermute | solution.py:41
  23.6 0.0 collective-permute-done.6.before_ref
  23.6 2.3 %shard_map.106 = bf16[128,1024]{1,0:T(8,128)(2,1)} custom-call(bf16[14,128,256]{2,1,0:T(8,128)(2,1)S(1)} %collective-permute-done.5.other_ref.refs_4_, bf16[14,128,256]{2,1,0:T(8,128)(2,1)S(1)} %get-tuple-element.34.mine_ref.key_value_ref, bf16[128,1024]{1,0:T(8,128)(2,1)S(1)} %collective-permute-done.6.before_ref, ...), custom_call_target="tpu_custom_call" | custom-call | flops 536870912 | bytes 2097152 | tf_op jit(solution)/shard_map/pallas_call | solution.py:29
  25.8 1.1 %collective-permute-done.7.refs_1_ = bf16[144,256]{1,0:T(8,128)(2,1)S(1)} collective-permute-done((bf16[144,256]{1,0:T(8,128)(2,1)S(1)}, bf16[144,256]{1,0:T(8,128)(2,1)S(1)}, u32[]{:S(2)}, u32[]{:S(2)}) %collective-permute-start.7) | collective-permute-done | bytes 73760 | tf_op jit(solution)/shard_map/ppermute | solution.py:41
  26.9 0.0 collective-permute-done.8.refs_2_
  26.9 0.4 %collective-permute-done.9.refs_3_ = bf16[144,256]{1,0:T(8,128)(2,1)S(1)} collective-permute-done((bf16[144,256]{1,0:T(8,128)(2,1)S(1)}, bf16[144,256]{1,0:T(8,128)(2,1)S(1)}, u32[]{:S(2)}, u32[]{:S(2)}) %collective-permute-start.9) | collective-permute-done | bytes 73760 | tf_op jit(solution)/shard_map/ppermute | solution.py:41
  27.3 0.7 %shard_map.110 = (bf16[128,1024]{1,0:T(8,128)(2,1)}, f32[8,128]{1,0:T(8,128)}) custom-call(bf16[144,256]{1,0:T(8,128)(2,1)S(1)} %get-tuple-element.46.refs_0_, bf16[144,256]{1,0:T(8,128)(2,1)S(1)} %collective-permute-done.7.refs_1_, bf16[144,256]{1,0:T(8,128)(2,1)S(1)} %collective-permute-done.8.refs_2_, bf16[144,256]{1,0:T(8,128)(2,1)S(1)} %collective-permute-done.9.refs_3_), custom_call_target="tpu_custom_call" | custom-call | bytes 524288 | tf_op jit(solution)/shard_map/pallas_call | solution.py:29
Async XLA Ops:
  0.6 5.9 %copy-start = (bf16[3,128,1024]{2,1,0:T(8,128)(2,1)S(1)}, bf16[3,128,1024]{2,1,0:T(8,128)(2,1)}, u32[]{:S(2)}) copy-start(bf16[3,128,1024]{2,1,0:T(8,128)(2,1)} %gate_ref.1) | copy-start | bytes 2359300
  2.0 12.6 %collective-permute-start = (bf16[400,256]{1,0:T(8,128)(2,1)S(1)}, bf16[400,256]{1,0:T(8,128)(2,1)S(1)}, u32[]{:S(2)}, u32[]{:S(2)}) collective-permute-start(bf16[400,256]{1,0:T(8,128)(2,1)S(1)} %get-tuple-element.28), channel_id=1, source_target_pairs={{0,8},{4,12},{8,0},{12,4},{16,24},{20,28},{24,16},{28,20},{1,9},{5... | collective-permute-start | bytes 614408 | tf_op jit(solution)/shard_map/ppermute | solution.py:41
  5.0 10.9 %collective-permute-start.1 = (bf16[400,256]{1,0:T(8,128)(2,1)S(1)}, bf16[400,256]{1,0:T(8,128)(2,1)S(1)}, u32[]{:S(2)}, u32[]{:S(2)}) collective-permute-start(bf16[400,256]{1,0:T(8,128)(2,1)S(1)} %get-tuple-element.29), channel_id=1, source_target_pairs={{0,16},{4,20},{8,24},{12,28},{16,0},{20,4},{24,8},{28,12},{1,17},{... | collective-permute-start | bytes 614408 | tf_op jit(solution)/shard_map/ppermute | solution.py:41
  6.5 9.4 %collective-permute-start.2 = (bf16[400,256]{1,0:T(8,128)(2,1)S(1)}, bf16[400,256]{1,0:T(8,128)(2,1)S(1)}, u32[]{:S(2)}, u32[]{:S(2)}) collective-permute-start(bf16[400,256]{1,0:T(8,128)(2,1)S(1)} %get-tuple-element.30), channel_id=1, source_target_pairs={{0,24},{4,28},{8,16},{12,20},{16,8},{20,12},{24,0},{28,4},{1,25},{... | collective-permute-start | bytes 614408 | tf_op jit(solution)/shard_map/ppermute | solution.py:41
  7.9 6.8 %collective-permute-start.3 = (bf16[32,1024]{1,0:T(8,128)(2,1)S(1)}, bf16[32,1024]{1,0:T(8,128)(2,1)S(1)}, u32[]{:S(2)}, u32[]{:S(2)}) collective-permute-start(bf16[32,1024]{1,0:T(8,128)(2,1)S(1)} %get-tuple-element.31), channel_id=1, source_target_pairs={{0,3},{1,2},{2,1},{3,0},{4,6},{5,7},{6,4},{7,5},{8,11},{9,10},{10,... | collective-permute-start | bytes 196616 | tf_op jit(solution)/shard_map/ppermute | solution.py:454
  12.0 2.7 %collective-permute-start.4 = (bf16[32,1024]{1,0:T(8,128)(2,1)S(1)}, bf16[32,1024]{1,0:T(8,128)(2,1)S(1)}, u32[]{:S(2)}, u32[]{:S(2)}) collective-permute-start(bf16[32,1024]{1,0:T(8,128)(2,1)S(1)} %get-tuple-element.32), channel_id=1, source_target_pairs={{4,5},{5,4},{6,7},{7,6},{12,13},{13,12},{14,15},{15,14},{20,21},{2... | collective-permute-start | bytes 196616 | tf_op jit(solution)/shard_map/ppermute | solution.py:455
  16.1 2.5 %collective-permute-start.5 = (bf16[14,128,256]{2,1,0:T(8,128)(2,1)S(1)}, bf16[14,128,256]{2,1,0:T(8,128)(2,1)S(1)}, u32[]{:S(2)}, u32[]{:S(2)}) collective-permute-start(bf16[14,128,256]{2,1,0:T(8,128)(2,1)S(1)} %get-tuple-element.34.mine_ref.key_value_ref), channel_id=1, source_target_pairs={{0,4},{4,0},{8,12},{12,8},{16,20},{20,16},{24,28},{28,24},{1,5},{5... | collective-permute-start | bytes 2752520 | tf_op jit(solution)/shard_map/ppermute | solution.py:41
  16.1 7.4 %collective-permute-start.6 = (bf16[128,1024]{1,0:T(8,128)(2,1)S(1)}, bf16[128,1024]{1,0:T(8,128)(2,1)S(1)}, u32[]{:S(2)}, u32[]{:S(2)}) collective-permute-start(bf16[128,1024]{1,0:T(8,128)(2,1)S(1)} %get-tuple-element.33.refs_6_.product_ref), channel_id=1, source_target_pairs={{4,8},{12,16},{20,24},{5,9},{13,17},{21,25},{6,10},{14,18},{22,26}... | collective-permute-start | bytes 786440 | tf_op jit(solution)/shard_map/ppermute | solution.py:456
  19.4 7.5 %collective-permute-start.7 = (bf16[144,256]{1,0:T(8,128)(2,1)S(1)}, bf16[144,256]{1,0:T(8,128)(2,1)S(1)}, u32[]{:S(2)}, u32[]{:S(2)}) collective-permute-start(bf16[144,256]{1,0:T(8,128)(2,1)S(1)} %get-tuple-element.45.refs_5_), channel_id=1, source_target_pairs={{0,16},{4,20},{8,24},{12,28},{16,0},{20,4},{24,8},{28,12},{1,17},{... | collective-permute-start | bytes 221192 | tf_op jit(solution)/shard_map/ppermute | solution.py:41
  20.8 6.1 %collective-permute-start.8 = (bf16[144,256]{1,0:T(8,128)(2,1)S(1)}, bf16[144,256]{1,0:T(8,128)(2,1)S(1)}, u32[]{:S(2)}, u32[]{:S(2)}) collective-permute-start(bf16[144,256]{1,0:T(8,128)(2,1)S(1)} %get-tuple-element.47), channel_id=1, source_target_pairs={{0,24},{4,28},{8,16},{12,20},{16,8},{20,12},{24,0},{28,4},{1,25},{... | collective-permute-start | bytes 221192 | tf_op jit(solution)/shard_map/ppermute | solution.py:41
  22.7 4.6 %collective-permute-start.9 = (bf16[144,256]{1,0:T(8,128)(2,1)S(1)}, bf16[144,256]{1,0:T(8,128)(2,1)S(1)}, u32[]{:S(2)}, u32[]{:S(2)}) collective-permute-start(bf16[144,256]{1,0:T(8,128)(2,1)S(1)} %get-tuple-element.48), channel_id=1, source_target_pairs={{0,8},{4,12},{8,0},{12,4},{16,24},{20,28},{24,16},{28,20},{1,9},{5... | collective-permute-start | bytes 221192 | tf_op jit(solution)/shard_map/ppermute | solution.py:41

commit v3 on v2

--- a/solution.py
+++ b/solution.py
@@ -47,8 +47,8 @@
     return index // heads, member // 2, lax.rem(member, 2)
 
 
-def pack_heads(heads, queries_ref, keys_values_ref, starts_ref, *refs):
-    *outs, held_ref, start_sem, sem = refs
+def pack_heads(heads, queries_ref, keys_values_ref, starts_ref, filters_ref, *refs):
+    *outs, taps_ref, held_ref, start_sem, taps_sem, sem = refs
     rows = queries_ref.shape[0]
     _, pair, _ = place(heads)
     first = pltpu.make_async_copy(starts_ref, held_ref, start_sem)
@@ -64,6 +64,15 @@
                     source.at[:, columns], out.at[pl.ds(part * rows, rows)], sem.at[step, part]
                 )
             )
+    width = taps_ref.shape[2]
+    panel = lax.axis_index("tp")
+    for index, target in enumerate((panel, panel ^ (3 - lax.rem(lax.axis_index("ctx"), 2)), panel ^ 1)):
+        columns = pl.ds(pl.multiple_of(target * width, width), width)
+        copies.append(
+            pltpu.make_async_copy(
+                filters_ref.at[:, columns], taps_ref.at[index], taps_sem.at[index]
+            )
+        )
     for copy in copies:
         copy.start()
     first.wait()
@@ -85,34 +94,39 @@
     return jnp.concatenate([high, low], axis=1)
 
 
-def pack_hyena(
-    hyena_ref, filters_ref, ahead_ref, back_ref, starts_ref, skip_ref,
-    product_ref, own_ref, far_ref, near_ref, early_ref, late_ref, back_out, starts_out, skip_out,
-    taps_ref, ahead_held, back_held, sem,
+def pack_hyena(hyena_ref, taps_ref, product_ref, own_ref, far_ref, mixed_ref):
+    product_ref[...] = (hyena_ref[1].astype(jnp.float32) * hyena_ref[2].astype(jnp.float32)).astype(
+        jnp.bfloat16
+    )
+    own_ref[...] = taps_ref[0].astype(jnp.bfloat16)
+    far_ref[...] = taps_ref[1].astype(jnp.bfloat16)
+    height, width = own_ref.shape
+    whole = mixed_ref.shape[1]
+    mixed_ref[...] = product_ref[:, :whole]
+
+    @pl.when(lax.rem(lax.axis_index("ctx"), 2) == 1)
+    def _():
+        near = taps_ref[2].astype(jnp.bfloat16)
+        mixed_ref[:height] = near[:, :whole]
+        mixed_ref[height : 2 * height, : width - whole] = near[:, whole:]
+
+
+def prepare(
+    ahead_ref, back_ref, starts_ref, skip_ref, early_ref, late_ref, back_out, starts_out, skip_out,
+    ahead_held, back_held, sem,
 ):
-    width = own_ref.shape[1]
-    panel = lax.axis_index("tp")
-    parity = lax.rem(lax.axis_index("ctx"), 2)
-    targets = (panel, panel ^ (3 - parity), panel ^ 1)
-    pairs = [(ahead_ref, ahead_held), (back_ref, back_held)]
-    pairs += [(starts_ref, starts_out), (skip_ref, skip_out)]
-    for index, target in enumerate(targets):
-        columns = pl.ds(pl.multiple_of(target * width, width), width)
-        pairs.append((filters_ref.at[:, columns], taps_ref.at[index]))
+    pairs = (
+        (ahead_ref, ahead_held), (back_ref, back_held), (starts_ref, starts_out), (skip_ref, skip_out)
+    )
     copies = [
         pltpu.make_async_copy(source, out, sem.at[index])
         for index, (source, out) in enumerate(pairs)
     ]
     for copy in copies:
         copy.start()
-    product_ref[...] = (hyena_ref[1].astype(jnp.float32) * hyena_ref[2].astype(jnp.float32)).astype(
-        jnp.bfloat16
-    )
     for copy in copies:
         copy.wait()
-    for index, out in enumerate((own_ref, far_ref, near_ref)):
-        out[...] = taps_ref[index].astype(jnp.bfloat16)
-    rows = product_ref.shape[0]
+    rows = back_out.shape[0]
     early_ref[...] = split(ahead_held[:, :rows])
     late_ref[...] = split(ahead_held[:, rows:])
     back_out[...] = back_held[...].astype(jnp.bfloat16)
@@ -122,9 +136,16 @@
     return ref[rows, index * 2 * HD : (index + 1) * 2 * HD]
 
 
+def near_strip(came_ref, height, part):
+    parts = came_ref.shape[1] // (2 * HD)
+    line = part // parts
+    return columns_of(came_ref, slice(line * height, (line + 1) * height), part % parts)
+
+
 def sort_heads(heads, *refs):
     count = heads // 2
-    far_ref, near_ref, product_ref, query_ref, side_ref = refs[-5:]
+    far_ref, came_ref, product_ref = refs[count : count + 3]
+    query_ref, side_ref = refs[-2:]
     rows = (refs[0].shape[0] - NOTE_ROWS) // 3
     _, pair, _ = place(heads)
     for step in range(count):
@@ -138,8 +159,8 @@
     for part in range(parts):
         line = slice(part * height, (part + 1) * height)
         side_ref[heads, line] = columns_of(far_ref, slice(None), part)
-        side_ref[heads + 1, line] = columns_of(near_ref, slice(None), part)
-        side_ref[heads + 2 + part] = columns_of(product_ref, slice(None), part)
+        side_ref[heads + 1, line] = near_strip(came_ref, height, part)
+    side_ref[heads + 2] = columns_of(product_ref, slice(None), parts - 1)
 
 
 UNIT = 2
@@ -330,7 +351,7 @@
 
 
 def convolve(
-    heads, other_ref, mine_ref, before_ref, own_taps_ref, starts_ref, product_ref, gate_ref, skip_ref,
+    heads, other_ref, mine_ref, came_ref, before_ref, own_taps_ref, starts_ref, product_ref, gate_ref, skip_ref,
     early_ref, late_ref, back_ref, out_ref, taps_ref, halo_ref, filter_ref, sum_ref,
 ):
     rows = product_ref.shape[0]
@@ -343,15 +364,18 @@
         line = pl.ds(pl.multiple_of((panel ^ step) * height, height), height)
         taps_ref[line, part * 2 * HD : (part + 1) * 2 * HD] = value
 
-    for part in range(width // (2 * HD)):
+    parts = width // (2 * HD)
+    for part in range(parts):
         line = slice(part * height, (part + 1) * height)
         mine_far, other_far = mine_ref[heads, line], other_ref[heads, line]
         store(0, part, columns_of(own_taps_ref, everything, part))
-        store(1, part, jnp.where(even, other_ref[heads + 1, line], mine_ref[heads + 1, line]))
+        store(1, part, jnp.where(even, near_strip(came_ref, height, part), other_ref[heads + 1, line]))
         store(2, part, jnp.where(even, other_far, mine_far))
         store(3, part, jnp.where(even, mine_far, other_far))
         halo_ref[:, part * 2 * HD : (part + 1) * 2 * HD] = jnp.where(
-            even, columns_of(before_ref, everything, part), other_ref[heads + 2 + part]
+            even,
+            columns_of(before_ref, everything, part),
+            other_ref[heads + 2] if part == parts - 1 else columns_of(came_ref, everything, part),
         )
     filter_ref[...] = dot(early_ref[...], twice(taps_ref[...]))
     starts = document_starts(starts_ref, rows)
@@ -387,16 +411,18 @@
     return jnp.asarray(ahead, jnp.float32), jnp.asarray(back, jnp.float32)
 
 
-def taps_pairs(peers, panels):
+def side_pairs(peers, panels):
     assert panels == 4
-    far, near = [], []
+    far, mixed = [], []
     for peer in range(peers):
         for panel in range(panels):
             here = peer * panels + panel
             far.append((here, peer * panels + (panel ^ (3 - peer % 2))))
-            if peer % 2 == 1:
-                near.append((here, peer * panels + (panel ^ 1)))
-    return far, near
+            if peer % 2 == 0:
+                mixed.append((here, here + panels))
+            else:
+                mixed.append((here, (peer - 1) * panels + (panel ^ 1)))
+    return far, mixed
 
 
 def local(hyena_inputs, filters, skip_bias, queries, keys_values, doc_start):
@@ -409,58 +435,63 @@
     shape = jax.ShapeDtypeStruct
     starts = doc_start.reshape(1, rows)
 
-    packed = call(
+    height = filters.shape[0]
+
+    def pinned(*arrays):
+        return [pltpu.with_memory_space_constraint(x, pltpu.HBM) for x in arrays]
+
+    *packed, wide_taps = call(
         functools.partial(pack_heads, heads),
-        (shape((3 * rows + NOTE_ROWS, 2 * HD), bf16),) * count,
-        [pltpu.with_memory_space_constraint(x, pltpu.HBM) for x in (queries, keys_values, starts)],
+        (shape((3 * rows + NOTE_ROWS, 2 * HD), bf16),) * count + (shape((3, height, channels), f32),),
+        pinned(queries, keys_values, starts, filters),
         0,
         4 * queries.size * 3,
         scratch=(
             pltpu.VMEM((1, rows), jnp.int32),
             pltpu.SemaphoreType.DMA,
+            pltpu.SemaphoreType.DMA((3,)),
             pltpu.SemaphoreType.DMA((count, 3)),
         ),
-        specs=[hbm()] * 3,
-    )
-    arrived = [packed[0]] + [None] * (count - 1)
-    for step in reversed(range(1, count)):
-        arrived[step] = crossed(packed[step], "ctx", 2 * step)
-    height = filters.shape[0]
-    ahead, back = twiddles(rows)
-    near_hbm = [
-        pltpu.with_memory_space_constraint(x, pltpu.HBM)
-        for x in (filters, ahead, back, starts, skip_bias.reshape(1, channels))
-    ]
-    product, own_taps, far_taps, near_taps, early, late, back, near_starts, skip = call(
+        specs=[hbm()] * 4,
+    )
+    arrived = [packed[0]] + [crossed(packed[step], "ctx", 2 * step) for step in range(1, count)]
+    product, own_taps, far_taps, mixed_rows = call(
         pack_hyena,
         (shape((rows, channels), bf16),)
-        + (shape((height, channels), bf16),) * 3
-        + (shape((2 * rows, 2 * rows), bf16),) * 2
-        + (shape((rows, 2 * rows), bf16),)
-        + (shape((1, rows), jnp.int32), shape((1, channels), f32)),
-        (hyena_inputs, *near_hbm),
+        + (shape((height, channels), bf16),) * 2
+        + (shape((rows, channels - 2 * HD), bf16),),
+        (hyena_inputs, wide_taps),
         0,
         4 * queries.size * 3,
+    )
+    axes = ("ctx", "tp")
+    far_pairs, mixed_pairs = side_pairs(peers, lax.axis_size("tp"))
+    far_taps = lax.ppermute(far_taps, axes, far_pairs)
+    came = lax.ppermute(mixed_rows, axes, mixed_pairs)
+    before = lax.ppermute(product, "ctx", [(i, i + 1) for i in range(1, peers - 1, 2)])
+    ahead, back = twiddles(rows)
+    early, late, back, near_starts, skip = call(
+        prepare,
+        (shape((2 * rows, 2 * rows), bf16),) * 2
+        + (shape((rows, 2 * rows), bf16), shape((1, rows), jnp.int32), shape((1, channels), f32)),
+        pinned(ahead, back, starts, skip_bias.reshape(1, channels)),
+        0,
+        4 * queries.size,
         scratch=(
-            pltpu.VMEM((3, height, channels), f32),
             pltpu.VMEM((2 * rows, 2 * rows), f32),
             pltpu.VMEM((rows, 2 * rows), f32),
-            pltpu.SemaphoreType.DMA((7,)),
+            pltpu.SemaphoreType.DMA((4,)),
         ),
-        specs=[vmem()] + [hbm()] * 5,
-    )
-    axes = ("ctx", "tp")
-    far_pairs, near_pairs = taps_pairs(peers, lax.axis_size("tp"))
-    far_taps = lax.ppermute(far_taps, axes, far_pairs)
-    near_taps = lax.ppermute(near_taps, axes, near_pairs)
-    before = lax.ppermute(product, "ctx", [(i, i + 1) for i in range(1, peers - 1, 2)])
+        specs=[hbm()] * 4,
+    )
+
     query, key_value = call(
         functools.partial(sort_heads, heads),
         (
             shape((count, rows + NOTE_ROWS, 2 * HD), bf16),
-            shape((heads + 2 + channels // (2 * HD), rows, 2 * HD), bf16),
+            shape((heads + 3, rows, 2 * HD), bf16),
         ),
-        (*arrived, far_taps, near_taps, product),
+        (*arrived, far_taps, came, product, skip),
         0,
         4 * queries.size * 3,
     )
@@ -502,7 +533,7 @@
         functools.partial(convolve, heads),
         shape((rows, channels), bf16),
         (
-            other, key_value, before, own_taps, near_starts, product, hyena_inputs,
+            other, key_value, came, before, own_taps, near_starts, product, hyena_inputs,
             skip, early, late, back,
         ),
         2 * 4 * 256 * 256 * channels,

time: 28.3 us -> 28.5 us (level)
  waiting for transfers between devices: 5.53 us -> 6.18 us
  starting transfers between devices: 13.7 us -> 13.1 us
    ppermute x7, waiting for transfers between devices: 3.53 us -> 4.29 us  [crossed(): lax.ppermute(array, axis, [(i, i ^ bits) for i in range(lax.axis_size(axi...]
    ppermute x1, starting transfers between devices: 0.65 us -> 0.06 us  [local(): came = lax.ppermute(mixed_rows, axes, mixed_pairs)]
    pallas_call x8 -> x9, Pallas kernels: 8.07 us -> 8.16 us  [call(): pl.pallas_call(kernel, out_shape=out_shape, in_specs=specs or [vmem() for...]
  transfers between devices with their start and end apart: 10 -> 10, of which waited for: 5 -> 5; matrix products, arithmetic and copies ran while one was open for 0% -> 0% of each run, Pallas kernels for 21% -> 20%
where the time goes in v3:
time: 28.5 us; the launch traced here: 28.2 us
  starting transfers between devices  13.1 us (46%)
  Pallas kernels  8.16 us (29%)
  waiting for transfers between devices  6.18 us (22%)
  between operations  0.72 us (3%)
    ppermute x7, starting transfers between devices, crossed(): lax.ppermute(array, axis, [(i, i ^ bits) for i in range(lax.axis_size(axi...  8.25 us
    pallas_call x9, Pallas kernels, call(): pl.pallas_call(kernel, out_shape=out_shape, in_specs=specs or [vmem() for...  8.16 us
    ppermute x7, waiting for transfers between devices, crossed(): lax.ppermute(array, axis, [(i, i ^ bits) for i in range(lax.axis_size(axi...  4.29 us
    ppermute x1, starting transfers between devices, local(): far_taps = lax.ppermute(far_taps, axes, far_pairs)  4.12 us
    ppermute x1, waiting for transfers between devices, local(): far_taps = lax.ppermute(far_taps, axes, far_pairs)  1.88 us
    ppermute x1, starting transfers between devices, local(): lax.ppermute(product, 'ctx', [(i, i + 1) for i in range(1, peers - 1, 2)])  0.68 us
  transfers between devices with their start and end apart: 10, of which 5 were waited for; matrix products, arithmetic and copies ran while one was open for 0% of the time, Pallas kernels for 20%

profile of v3, /device:TPU:0, one launch (start us, length us, event | category | flops | bytes accessed | tf_op | source)
XLA Modules:
  0.0 28.2 jit_solution(14743210129463142726)
XLA Ops:
  0.6 0.0 copy-start
  0.6 1.6 %shard_map.103 = (bf16[400,256]{1,0:T(8,128)(2,1)S(1)}, bf16[400,256]{1,0:T(8,128)(2,1)S(1)}, bf16[400,256]{1,0:T(8,128)(2,1)S(1)}, bf16[400,256]{1,0:T(8,128)(2,1)S(1)}, f32[3,32,1024]{2,1,0:T(8,128)S(1)}) custom-call(bf16[128,1024]{1,0:T(8,128)(2,1)} %queries_ref.1, bf16[2,128,1024]{2,1,0:T(8,128)(2,1)} %keys_values_ref.1, s32[1,128]{1,0:T(1,128)} %bitcast.3, ...), custom_call_target="tpu_custom_call" | custom-call | bytes 1572864 | tf_op jit(solution)/shard_map/pallas_call | solution.py:29
  2.2 3.0 %collective-permute-start = (bf16[400,256]{1,0:T(8,128)(2,1)S(1)}, bf16[400,256]{1,0:T(8,128)(2,1)S(1)}, u32[]{:S(2)}, u32[]{:S(2)}) collective-permute-start(bf16[400,256]{1,0:T(8,128)(2,1)S(1)} %get-tuple-element.29), channel_id=1, source_target_pairs={{0,8},{4,12},{8,0},{12,4},{16,24},{20,28},{24,16},{28,20},{1,9},{5... | collective-permute-start | bytes 614408 | tf_op jit(solution)/shard_map/ppermute | solution.py:41
  5.2 1.5 %collective-permute-start.1 = (bf16[400,256]{1,0:T(8,128)(2,1)S(1)}, bf16[400,256]{1,0:T(8,128)(2,1)S(1)}, u32[]{:S(2)}, u32[]{:S(2)}) collective-permute-start(bf16[400,256]{1,0:T(8,128)(2,1)S(1)} %get-tuple-element.30), channel_id=1, source_target_pairs={{0,16},{4,20},{8,24},{12,28},{16,0},{20,4},{24,8},{28,12},{1,17},{... | collective-permute-start | bytes 614408 | tf_op jit(solution)/shard_map/ppermute | solution.py:41
  6.7 0.0 collective-permute-start.2
  6.8 0.0 copy-done
  6.8 0.1 shard_map.104
  6.9 0.1 collective-permute-start.4
  7.0 4.1 %collective-permute-start.3 = (bf16[32,1024]{1,0:T(8,128)(2,1)S(1)}, bf16[32,1024]{1,0:T(8,128)(2,1)S(1)}, u32[]{:S(2)}, u32[]{:S(2)}) collective-permute-start(bf16[32,1024]{1,0:T(8,128)(2,1)S(1)} %get-tuple-element.33), channel_id=1, source_target_pairs={{0,3},{1,2},{2,1},{3,0},{4,6},{5,7},{6,4},{7,5},{8,11},{9,10},{10,... | collective-permute-start | bytes 196616 | tf_op jit(solution)/shard_map/ppermute | solution.py:469
  11.1 1.1 %shard_map.105 = (bf16[256,256]{1,0:T(8,128)(2,1)S(1)}, bf16[256,256]{1,0:T(8,128)(2,1)S(1)}, bf16[128,256]{1,0:T(8,128)(2,1)S(1)}, s32[1,128]{1,0:T(1,128)S(1)}, f32[1,1024]{1,0:T(1,128)S(1)}) custom-call(f32[256,256]{1,0:T(8,128)} %constant.4.clone.ahead_ref, f32[128,256]{1,0:T(8,128)} %constant.5.clone.back_ref, s32[1,128]{1,0:T(1,128)} %bitcast.4, ...), custom_call_target="tpu_custom_call" | custom-call | bytes 524288 | tf_op jit(solution)/shard_map/pallas_call | solution.py:29
  12.2 1.9 %collective-permute-done.3.refs_4_ = bf16[32,1024]{1,0:T(8,128)(2,1)S(1)} collective-permute-done((bf16[32,1024]{1,0:T(8,128)(2,1)S(1)}, bf16[32,1024]{1,0:T(8,128)(2,1)S(1)}, u32[]{:S(2)}, u32[]{:S(2)}) %collective-permute-start.3) | collective-permute-done | bytes 65568 | tf_op jit(solution)/shard_map/ppermute | solution.py:469
  14.0 0.0 collective-permute-done.4.refs_5_.came_ref
  14.0 0.0 collective-permute-done.refs_1_
  14.0 2.1 %collective-permute-done.1.refs_2_ = bf16[400,256]{1,0:T(8,128)(2,1)S(1)} collective-permute-done((bf16[400,256]{1,0:T(8,128)(2,1)S(1)}, bf16[400,256]{1,0:T(8,128)(2,1)S(1)}, u32[]{:S(2)}, u32[]{:S(2)}) %collective-permute-start.1) | collective-permute-done | bytes 204832 | tf_op jit(solution)/shard_map/ppermute | solution.py:41
  16.1 0.0 collective-permute-done.2.refs_3_
  16.1 0.1 shard_map.106
  16.2 0.1 collective-permute-start.5
  16.3 0.7 %collective-permute-start.6 = (bf16[128,1024]{1,0:T(8,128)(2,1)S(1)}, bf16[128,1024]{1,0:T(8,128)(2,1)S(1)}, u32[]{:S(2)}, u32[]{:S(2)}) collective-permute-start(bf16[128,1024]{1,0:T(8,128)(2,1)S(1)} %get-tuple-element.35.refs_6_.product_ref), channel_id=1, source_target_pairs={{4,8},{12,16},{20,24},{5,9},{13,17},{21,25},{6,10},{14,18},{22,26}... | collective-permute-start | bytes 786440 | tf_op jit(solution)/shard_map/ppermute | solution.py:471
  17.0 1.0 %shard_map.108 = (f32[2,2,1,256]{3,2,1,0:T(1,128)S(1)}, f32[2,2,1,256]{3,2,1,0:T(1,128)S(1)}, f32[2,2,128,256]{3,2,1,0:T(8,128)S(1)}) custom-call(bf16[4,144,256]{2,1,0:T(8,128)(2,1)S(1)} %get-tuple-element.43.query_ref.refs_0_, bf16[11,128,256]{2,1,0:T(8,128)(2,1)S(1)} %get-tuple-element.37.mine_ref.key_value_ref), custom_call_target="tpu_custom_call" | custom-call | flops 268435456 | bytes 2097152 | tf_op jit(solution)/shard_map/pallas_call | solution.py:29
  18.0 0.5 %collective-permute-done.5.other_ref.refs_4_ = bf16[11,128,256]{2,1,0:T(8,128)(2,1)S(1)} collective-permute-done((bf16[11,128,256]{2,1,0:T(8,128)(2,1)S(1)}, bf16[11,128,256]{2,1,0:T(8,128)(2,1)S(1)}, u32[]{:S(2)}, u32[]{:S(2)}) %collective-permute-start.5) | collective-permute-done | bytes 720928 | tf_op jit(solution)/shard_map/ppermute | solution.py:41
  18.5 0.8 %shard_map.109 = (bf16[144,256]{1,0:T(8,128)(2,1)S(1)}, bf16[144,256]{1,0:T(8,128)(2,1)S(1)}) custom-call(bf16[4,144,256]{2,1,0:T(8,128)(2,1)S(1)} %get-tuple-element.43.query_ref.refs_0_, f32[2,2,1,256]{3,2,1,0:T(1,128)S(1)} %get-tuple-element.44.refs_1_, f32[2,2,1,256]{3,2,1,0:T(1,128)S(1)} %get-tuple-element.45.refs_2_, ...), custom_call_target="tpu_custom_call" | custom-call | flops 134217728 | bytes 2097152 | tf_op jit(solution)/shard_map/pallas_call | solution.py:29
  19.3 1.5 %collective-permute-start.7 = (bf16[144,256]{1,0:T(8,128)(2,1)S(1)}, bf16[144,256]{1,0:T(8,128)(2,1)S(1)}, u32[]{:S(2)}, u32[]{:S(2)}) collective-permute-start(bf16[144,256]{1,0:T(8,128)(2,1)S(1)} %get-tuple-element.47.refs_5_), channel_id=1, source_target_pairs={{0,16},{4,20},{8,24},{12,28},{16,0},{20,4},{24,8},{28,12},{1,17},{... | collective-permute-start | bytes 221192 | tf_op jit(solution)/shard_map/ppermute | solution.py:41
  20.8 1.4 %collective-permute-start.8 = (bf16[144,256]{1,0:T(8,128)(2,1)S(1)}, bf16[144,256]{1,0:T(8,128)(2,1)S(1)}, u32[]{:S(2)}, u32[]{:S(2)}) collective-permute-start(bf16[144,256]{1,0:T(8,128)(2,1)S(1)} %get-tuple-element.49), channel_id=1, source_target_pairs={{0,24},{4,28},{8,16},{12,20},{16,8},{20,12},{24,0},{28,4},{1,25},{... | collective-permute-start | bytes 221192 | tf_op jit(solution)/shard_map/ppermute | solution.py:41
  22.2 0.6 %shard_map.110 = (bf16[144,256]{1,0:T(8,128)(2,1)S(1)}, bf16[144,256]{1,0:T(8,128)(2,1)S(1)}) custom-call(bf16[4,144,256]{2,1,0:T(8,128)(2,1)S(1)} %get-tuple-element.43.query_ref.refs_0_, f32[2,2,1,256]{3,2,1,0:T(1,128)S(1)} %get-tuple-element.44.refs_1_, f32[2,2,1,256]{3,2,1,0:T(1,128)S(1)} %get-tuple-element.45.refs_2_, ...), custom_call_target="tpu_custom_call" | custom-call | flops 134217728 | bytes 2097152 | tf_op jit(solution)/shard_map/pallas_call | solution.py:29
  22.7 0.7 %collective-permute-start.9 = (bf16[144,256]{1,0:T(8,128)(2,1)S(1)}, bf16[144,256]{1,0:T(8,128)(2,1)S(1)}, u32[]{:S(2)}, u32[]{:S(2)}) collective-permute-start(bf16[144,256]{1,0:T(8,128)(2,1)S(1)} %get-tuple-element.50), channel_id=1, source_target_pairs={{0,8},{4,12},{8,0},{12,4},{16,24},{20,28},{24,16},{28,20},{1,9},{5... | collective-permute-start | bytes 221192 | tf_op jit(solution)/shard_map/ppermute | solution.py:41
  23.5 0.0 collective-permute-done.6.before_ref
  23.5 2.3 %shard_map.107 = bf16[128,1024]{1,0:T(8,128)(2,1)} custom-call(bf16[11,128,256]{2,1,0:T(8,128)(2,1)S(1)} %collective-permute-done.5.other_ref.refs_4_, bf16[11,128,256]{2,1,0:T(8,128)(2,1)S(1)} %get-tuple-element.37.mine_ref.key_value_ref, bf16[128,768]{1,0:T(8,128)(2,1)S(1)} %collective-permute-done.4.refs_5_.came_ref, ...), custom_call_target="tpu_custom_call" | custom-call | flops 536870912 | bytes 2097152 | tf_op jit(solution)/shard_map/pallas_call | solution.py:29
  25.8 1.3 %collective-permute-done.7.refs_1_ = bf16[144,256]{1,0:T(8,128)(2,1)S(1)} collective-permute-done((bf16[144,256]{1,0:T(8,128)(2,1)S(1)}, bf16[144,256]{1,0:T(8,128)(2,1)S(1)}, u32[]{:S(2)}, u32[]{:S(2)}) %collective-permute-start.7) | collective-permute-done | bytes 73760 | tf_op jit(solution)/shard_map/ppermute | solution.py:41
  27.1 0.0 collective-permute-done.8.refs_2_
  27.1 0.3 %collective-permute-done.9.refs_3_ = bf16[144,256]{1,0:T(8,128)(2,1)S(1)} collective-permute-done((bf16[144,256]{1,0:T(8,128)(2,1)S(1)}, bf16[144,256]{1,0:T(8,128)(2,1)S(1)}, u32[]{:S(2)}, u32[]{:S(2)}) %collective-permute-start.9) | collective-permute-done | bytes 73760 | tf_op jit(solution)/shard_map/ppermute | solution.py:41
  27.4 0.7 %shard_map.111 = (bf16[128,1024]{1,0:T(8,128)(2,1)}, f32[8,128]{1,0:T(8,128)}) custom-call(bf16[144,256]{1,0:T(8,128)(2,1)S(1)} %get-tuple-element.48.refs_0_, bf16[144,256]{1,0:T(8,128)(2,1)S(1)} %collective-permute-done.7.refs_1_, bf16[144,256]{1,0:T(8,128)(2,1)S(1)} %collective-permute-done.8.refs_2_, bf16[144,256]{1,0:T(8,128)(2,1)S(1)} %collective-permute-done.9.refs_3_), custom_call_target="tpu_custom_call" | custom-call | bytes 524288 | tf_op jit(solution)/shard_map/pallas_call | solution.py:29
Async XLA Ops:
  0.6 6.1 %copy-start = (bf16[3,128,1024]{2,1,0:T(8,128)(2,1)S(1)}, bf16[3,128,1024]{2,1,0:T(8,128)(2,1)}, u32[]{:S(2)}) copy-start(bf16[3,128,1024]{2,1,0:T(8,128)(2,1)} %gate_ref.1) | copy-start | bytes 2359300
  2.2 11.8 %collective-permute-start = (bf16[400,256]{1,0:T(8,128)(2,1)S(1)}, bf16[400,256]{1,0:T(8,128)(2,1)S(1)}, u32[]{:S(2)}, u32[]{:S(2)}) collective-permute-start(bf16[400,256]{1,0:T(8,128)(2,1)S(1)} %get-tuple-element.29), channel_id=1, source_target_pairs={{0,8},{4,12},{8,0},{12,4},{16,24},{20,28},{24,16},{28,20},{1,9},{5... | collective-permute-start | bytes 614408 | tf_op jit(solution)/shard_map/ppermute | solution.py:41
  5.2 10.9 %collective-permute-start.1 = (bf16[400,256]{1,0:T(8,128)(2,1)S(1)}, bf16[400,256]{1,0:T(8,128)(2,1)S(1)}, u32[]{:S(2)}, u32[]{:S(2)}) collective-permute-start(bf16[400,256]{1,0:T(8,128)(2,1)S(1)} %get-tuple-element.30), channel_id=1, source_target_pairs={{0,16},{4,20},{8,24},{12,28},{16,0},{20,4},{24,8},{28,12},{1,17},{... | collective-permute-start | bytes 614408 | tf_op jit(solution)/shard_map/ppermute | solution.py:41
  6.7 9.4 %collective-permute-start.2 = (bf16[400,256]{1,0:T(8,128)(2,1)S(1)}, bf16[400,256]{1,0:T(8,128)(2,1)S(1)}, u32[]{:S(2)}, u32[]{:S(2)}) collective-permute-start(bf16[400,256]{1,0:T(8,128)(2,1)S(1)} %get-tuple-element.31), channel_id=1, source_target_pairs={{0,24},{4,28},{8,16},{12,20},{16,8},{20,12},{24,0},{28,4},{1,25},{... | collective-permute-start | bytes 614408 | tf_op jit(solution)/shard_map/ppermute | solution.py:41
  6.9 7.1 %collective-permute-start.4 = (bf16[128,768]{1,0:T(8,128)(2,1)S(1)}, bf16[128,768]{1,0:T(8,128)(2,1)S(1)}, u32[]{:S(2)}, u32[]{:S(2)}) collective-permute-start(bf16[128,768]{1,0:T(8,128)(2,1)S(1)} %get-tuple-element.34), channel_id=1, source_target_pairs={{0,4},{1,5},{2,6},{3,7},{4,1},{5,0},{6,3},{7,2},{8,12},{9,13},{10,... | collective-permute-start | bytes 589832 | tf_op jit(solution)/shard_map/ppermute | solution.py:470
  7.0 7.1 %collective-permute-start.3 = (bf16[32,1024]{1,0:T(8,128)(2,1)S(1)}, bf16[32,1024]{1,0:T(8,128)(2,1)S(1)}, u32[]{:S(2)}, u32[]{:S(2)}) collective-permute-start(bf16[32,1024]{1,0:T(8,128)(2,1)S(1)} %get-tuple-element.33), channel_id=1, source_target_pairs={{0,3},{1,2},{2,1},{3,0},{4,6},{5,7},{6,4},{7,5},{8,11},{9,10},{10,... | collective-permute-start | bytes 196616 | tf_op jit(solution)/shard_map/ppermute | solution.py:469
  16.2 2.3 %collective-permute-start.5 = (bf16[11,128,256]{2,1,0:T(8,128)(2,1)S(1)}, bf16[11,128,256]{2,1,0:T(8,128)(2,1)S(1)}, u32[]{:S(2)}, u32[]{:S(2)}) collective-permute-start(bf16[11,128,256]{2,1,0:T(8,128)(2,1)S(1)} %get-tuple-element.37.mine_ref.key_value_ref), channel_id=1, source_target_pairs={{0,4},{4,0},{8,12},{12,8},{16,20},{20,16},{24,28},{28,24},{1,5},{5... | collective-permute-start | bytes 2162696 | tf_op jit(solution)/shard_map/ppermute | solution.py:41
  16.3 7.1 %collective-permute-start.6 = (bf16[128,1024]{1,0:T(8,128)(2,1)S(1)}, bf16[128,1024]{1,0:T(8,128)(2,1)S(1)}, u32[]{:S(2)}, u32[]{:S(2)}) collective-permute-start(bf16[128,1024]{1,0:T(8,128)(2,1)S(1)} %get-tuple-element.35.refs_6_.product_ref), channel_id=1, source_target_pairs={{4,8},{12,16},{20,24},{5,9},{13,17},{21,25},{6,10},{14,18},{22,26}... | collective-permute-start | bytes 786440 | tf_op jit(solution)/shard_map/ppermute | solution.py:471
  19.3 7.8 %collective-permute-start.7 = (bf16[144,256]{1,0:T(8,128)(2,1)S(1)}, bf16[144,256]{1,0:T(8,128)(2,1)S(1)}, u32[]{:S(2)}, u32[]{:S(2)}) collective-permute-start(bf16[144,256]{1,0:T(8,128)(2,1)S(1)} %get-tuple-element.47.refs_5_), channel_id=1, source_target_pairs={{0,16},{4,20},{8,24},{12,28},{16,0},{20,4},{24,8},{28,12},{1,17},{... | collective-permute-start | bytes 221192 | tf_op jit(solution)/shard_map/ppermute | solution.py:41
  20.8 6.3 %collective-permute-start.8 = (bf16[144,256]{1,0:T(8,128)(2,1)S(1)}, bf16[144,256]{1,0:T(8,128)(2,1)S(1)}, u32[]{:S(2)}, u32[]{:S(2)}) collective-permute-start(bf16[144,256]{1,0:T(8,128)(2,1)S(1)} %get-tuple-element.49), channel_id=1, source_target_pairs={{0,24},{4,28},{8,16},{12,20},{16,8},{20,12},{24,0},{28,4},{1,25},{... | collective-permute-start | bytes 221192 | tf_op jit(solution)/shard_map/ppermute | solution.py:41
  22.7 4.7 %collective-permute-start.9 = (bf16[144,256]{1,0:T(8,128)(2,1)S(1)}, bf16[144,256]{1,0:T(8,128)(2,1)S(1)}, u32[]{:S(2)}, u32[]{:S(2)}) collective-permute-start(bf16[144,256]{1,0:T(8,128)(2,1)S(1)} %get-tuple-element.50), channel_id=1, source_target_pairs={{0,8},{4,12},{8,0},{12,4},{16,24},{20,28},{24,16},{28,20},{1,9},{5... | collective-permute-start | bytes 221192 | tf_op jit(solution)/shard_map/ppermute | solution.py:41

commit v4 on v3

--- a/solution.py
+++ b/solution.py
@@ -468,7 +468,8 @@
     far_pairs, mixed_pairs = side_pairs(peers, lax.axis_size("tp"))
     far_taps = lax.ppermute(far_taps, axes, far_pairs)
     came = lax.ppermute(mixed_rows, axes, mixed_pairs)
-    before = lax.ppermute(product, "ctx", [(i, i + 1) for i in range(1, peers - 1, 2)])
+    halo_pairs = [pair for i in range(1, peers - 1, 2) for pair in ((i, i + 1), (i + 1, i))]
+    before = lax.ppermute(product, "ctx", halo_pairs)
     ahead, back = twiddles(rows)
     early, late, back, near_starts, skip = call(
         prepare,

time: 28.5 us -> 31.3 us (1.098)
  waiting for transfers between devices: 6.18 us -> 7.7 us
  starting transfers between devices: 13.1 us -> 14.5 us
    ppermute x7, waiting for transfers between devices: 4.29 us -> 5.81 us  [crossed(): lax.ppermute(array, axis, [(i, i ^ bits) for i in range(lax.axis_size(axi...]
    ppermute x7, starting transfers between devices: 8.25 us -> 9.64 us  [crossed(): lax.ppermute(array, axis, [(i, i ^ bits) for i in range(lax.axis_size(axi...]
  transfers between devices with their start and end apart: 10 -> 10, of which waited for: 5 -> 5; matrix products, arithmetic and copies ran while one was open for 0% -> 0% of each run, Pallas kernels for 20% -> 19%
where the time goes in v4:
time: 31.3 us; the launch traced here: 31.1 us
  starting transfers between devices  14.5 us (46%)
  Pallas kernels  8.17 us (26%)
  waiting for transfers between devices  7.7 us (25%)
  between operations  0.72 us (2%)
    ppermute x7, starting transfers between devices, crossed(): lax.ppermute(array, axis, [(i, i ^ bits) for i in range(lax.axis_size(axi...  9.64 us
    pallas_call x9, Pallas kernels, call(): pl.pallas_call(kernel, out_shape=out_shape, in_specs=specs or [vmem() for...  8.17 us
    ppermute x7, waiting for transfers between devices, crossed(): lax.ppermute(array, axis, [(i, i ^ bits) for i in range(lax.axis_size(axi...  5.81 us
    ppermute x1, starting transfers between devices, local(): far_taps = lax.ppermute(far_taps, axes, far_pairs)  4.12 us
    ppermute x1, waiting for transfers between devices, local(): far_taps = lax.ppermute(far_taps, axes, far_pairs)  1.88 us
    ppermute x1, starting transfers between devices, local(): before = lax.ppermute(product, 'ctx', halo_pairs)  0.68 us
  transfers between devices with their start and end apart: 10, of which 5 were waited for; matrix products, arithmetic and copies ran while one was open for 0% of the time, Pallas kernels for 19%

profile of v4, /device:TPU:0, one launch (start us, length us, event | category | flops | bytes accessed | tf_op | source)
XLA Modules:
  0.0 31.1 jit_solution(4733226091700321541)
XLA Ops:
  0.6 0.0 copy-start
  0.6 1.6 %shard_map.103 = (bf16[400,256]{1,0:T(8,128)(2,1)S(1)}, bf16[400,256]{1,0:T(8,128)(2,1)S(1)}, bf16[400,256]{1,0:T(8,128)(2,1)S(1)}, bf16[400,256]{1,0:T(8,128)(2,1)S(1)}, f32[3,32,1024]{2,1,0:T(8,128)S(1)}) custom-call(bf16[128,1024]{1,0:T(8,128)(2,1)} %queries_ref.1, bf16[2,128,1024]{2,1,0:T(8,128)(2,1)} %keys_values_ref.1, s32[1,128]{1,0:T(1,128)} %bitcast.3, ...), custom_call_target="tpu_custom_call" | custom-call | bytes 1572864 | tf_op jit(solution)/shard_map/pallas_call | solution.py:29
  2.2 3.0 %collective-permute-start = (bf16[400,256]{1,0:T(8,128)(2,1)S(1)}, bf16[400,256]{1,0:T(8,128)(2,1)S(1)}, u32[]{:S(2)}, u32[]{:S(2)}) collective-permute-start(bf16[400,256]{1,0:T(8,128)(2,1)S(1)} %get-tuple-element.29), channel_id=1, source_target_pairs={{0,8},{4,12},{8,0},{12,4},{16,24},{20,28},{24,16},{28,20},{1,9},{5... | collective-permute-start | bytes 614408 | tf_op jit(solution)/shard_map/ppermute | solution.py:41
  5.2 1.5 %collective-permute-start.1 = (bf16[400,256]{1,0:T(8,128)(2,1)S(1)}, bf16[400,256]{1,0:T(8,128)(2,1)S(1)}, u32[]{:S(2)}, u32[]{:S(2)}) collective-permute-start(bf16[400,256]{1,0:T(8,128)(2,1)S(1)} %get-tuple-element.30), channel_id=1, source_target_pairs={{0,16},{4,20},{8,24},{12,28},{16,0},{20,4},{24,8},{28,12},{1,17},{... | collective-permute-start | bytes 614408 | tf_op jit(solution)/shard_map/ppermute | solution.py:41
  6.7 0.0 collective-permute-start.2
  6.8 0.0 copy-done
  6.8 0.1 shard_map.104
  6.9 0.1 collective-permute-start.4
  7.0 4.1 %collective-permute-start.3 = (bf16[32,1024]{1,0:T(8,128)(2,1)S(1)}, bf16[32,1024]{1,0:T(8,128)(2,1)S(1)}, u32[]{:S(2)}, u32[]{:S(2)}) collective-permute-start(bf16[32,1024]{1,0:T(8,128)(2,1)S(1)} %get-tuple-element.33), channel_id=1, source_target_pairs={{0,3},{1,2},{2,1},{3,0},{4,6},{5,7},{6,4},{7,5},{8,11},{9,10},{10,... | collective-permute-start | bytes 196616 | tf_op jit(solution)/shard_map/ppermute | solution.py:469
  11.1 1.1 %shard_map.105 = (bf16[256,256]{1,0:T(8,128)(2,1)S(1)}, bf16[256,256]{1,0:T(8,128)(2,1)S(1)}, bf16[128,256]{1,0:T(8,128)(2,1)S(1)}, s32[1,128]{1,0:T(1,128)S(1)}, f32[1,1024]{1,0:T(1,128)S(1)}) custom-call(f32[256,256]{1,0:T(8,128)} %constant.4.clone.ahead_ref, f32[128,256]{1,0:T(8,128)} %constant.5.clone.back_ref, s32[1,128]{1,0:T(1,128)} %bitcast.4, ...), custom_call_target="tpu_custom_call" | custom-call | bytes 524288 | tf_op jit(solution)/shard_map/pallas_call | solution.py:29
  12.2 1.9 %collective-permute-done.3.refs_4_ = bf16[32,1024]{1,0:T(8,128)(2,1)S(1)} collective-permute-done((bf16[32,1024]{1,0:T(8,128)(2,1)S(1)}, bf16[32,1024]{1,0:T(8,128)(2,1)S(1)}, u32[]{:S(2)}, u32[]{:S(2)}) %collective-permute-start.3) | collective-permute-done | bytes 65568 | tf_op jit(solution)/shard_map/ppermute | solution.py:469
  14.0 0.0 collective-permute-done.4.refs_5_.came_ref
  14.0 0.0 collective-permute-done.refs_1_
  14.0 2.1 %collective-permute-done.1.refs_2_ = bf16[400,256]{1,0:T(8,128)(2,1)S(1)} collective-permute-done((bf16[400,256]{1,0:T(8,128)(2,1)S(1)}, bf16[400,256]{1,0:T(8,128)(2,1)S(1)}, u32[]{:S(2)}, u32[]{:S(2)}) %collective-permute-start.1) | collective-permute-done | bytes 204832 | tf_op jit(solution)/shard_map/ppermute | solution.py:41
  16.1 0.0 collective-permute-done.2.refs_3_
  16.1 0.1 shard_map.106
  16.2 0.1 collective-permute-start.5
  16.3 0.7 %collective-permute-start.6 = (bf16[128,1024]{1,0:T(8,128)(2,1)S(1)}, bf16[128,1024]{1,0:T(8,128)(2,1)S(1)}, u32[]{:S(2)}, u32[]{:S(2)}) collective-permute-start(bf16[128,1024]{1,0:T(8,128)(2,1)S(1)} %get-tuple-element.35.refs_6_.product_ref), channel_id=1, source_target_pairs={{4,8},{8,4},{12,16},{16,12},{20,24},{24,20},{5,9},{9,5},{13,17},{1... | collective-permute-start | bytes 786440 | tf_op jit(solution)/shard_map/ppermute | solution.py:472
  17.0 1.0 %shard_map.108 = (f32[2,2,1,256]{3,2,1,0:T(1,128)S(1)}, f32[2,2,1,256]{3,2,1,0:T(1,128)S(1)}, f32[2,2,128,256]{3,2,1,0:T(8,128)S(1)}) custom-call(bf16[4,144,256]{2,1,0:T(8,128)(2,1)S(1)} %get-tuple-element.43.query_ref.refs_0_, bf16[11,128,256]{2,1,0:T(8,128)(2,1)S(1)} %get-tuple-element.37.mine_ref.key_value_ref), custom_call_target="tpu_custom_call" | custom-call | flops 268435456 | bytes 2097152 | tf_op jit(solution)/shard_map/pallas_call | solution.py:29
  18.0 0.5 %collective-permute-done.5.other_ref.refs_4_ = bf16[11,128,256]{2,1,0:T(8,128)(2,1)S(1)} collective-permute-done((bf16[11,128,256]{2,1,0:T(8,128)(2,1)S(1)}, bf16[11,128,256]{2,1,0:T(8,128)(2,1)S(1)}, u32[]{:S(2)}, u32[]{:S(2)}) %collective-permute-start.5) | collective-permute-done | bytes 720928 | tf_op jit(solution)/shard_map/ppermute | solution.py:41
  18.5 0.8 %shard_map.109 = (bf16[144,256]{1,0:T(8,128)(2,1)S(1)}, bf16[144,256]{1,0:T(8,128)(2,1)S(1)}) custom-call(bf16[4,144,256]{2,1,0:T(8,128)(2,1)S(1)} %get-tuple-element.43.query_ref.refs_0_, f32[2,2,1,256]{3,2,1,0:T(1,128)S(1)} %get-tuple-element.44.refs_1_, f32[2,2,1,256]{3,2,1,0:T(1,128)S(1)} %get-tuple-element.45.refs_2_, ...), custom_call_target="tpu_custom_call" | custom-call | flops 134217728 | bytes 2097152 | tf_op jit(solution)/shard_map/pallas_call | solution.py:29
  19.3 3.4 %collective-permute-start.7 = (bf16[144,256]{1,0:T(8,128)(2,1)S(1)}, bf16[144,256]{1,0:T(8,128)(2,1)S(1)}, u32[]{:S(2)}, u32[]{:S(2)}) collective-permute-start(bf16[144,256]{1,0:T(8,128)(2,1)S(1)} %get-tuple-element.47.refs_5_), channel_id=1, source_target_pairs={{0,16},{4,20},{8,24},{12,28},{16,0},{20,4},{24,8},{28,12},{1,17},{... | collective-permute-start | bytes 221192 | tf_op jit(solution)/shard_map/ppermute | solution.py:41
  22.7 1.0 %collective-permute-start.8 = (bf16[144,256]{1,0:T(8,128)(2,1)S(1)}, bf16[144,256]{1,0:T(8,128)(2,1)S(1)}, u32[]{:S(2)}, u32[]{:S(2)}) collective-permute-start(bf16[144,256]{1,0:T(8,128)(2,1)S(1)} %get-tuple-element.49), channel_id=1, source_target_pairs={{0,24},{4,28},{8,16},{12,20},{16,8},{20,12},{24,0},{28,4},{1,25},{... | collective-permute-start | bytes 221192 | tf_op jit(solution)/shard_map/ppermute | solution.py:41
  23.7 0.6 %shard_map.110 = (bf16[144,256]{1,0:T(8,128)(2,1)S(1)}, bf16[144,256]{1,0:T(8,128)(2,1)S(1)}) custom-call(bf16[4,144,256]{2,1,0:T(8,128)(2,1)S(1)} %get-tuple-element.43.query_ref.refs_0_, f32[2,2,1,256]{3,2,1,0:T(1,128)S(1)} %get-tuple-element.44.refs_1_, f32[2,2,1,256]{3,2,1,0:T(1,128)S(1)} %get-tuple-element.45.refs_2_, ...), custom_call_target="tpu_custom_call" | custom-call | flops 134217728 | bytes 2097152 | tf_op jit(solution)/shard_map/pallas_call | solution.py:29
  24.2 0.6 %collective-permute-start.9 = (bf16[144,256]{1,0:T(8,128)(2,1)S(1)}, bf16[144,256]{1,0:T(8,128)(2,1)S(1)}, u32[]{:S(2)}, u32[]{:S(2)}) collective-permute-start(bf16[144,256]{1,0:T(8,128)(2,1)S(1)} %get-tuple-element.50), channel_id=1, source_target_pairs={{0,8},{4,12},{8,0},{12,4},{16,24},{20,28},{24,16},{28,20},{1,9},{5... | collective-permute-start | bytes 221192 | tf_op jit(solution)/shard_map/ppermute | solution.py:41
  24.9 0.0 collective-permute-done.6.before_ref
  24.9 2.3 %shard_map.107 = bf16[128,1024]{1,0:T(8,128)(2,1)} custom-call(bf16[11,128,256]{2,1,0:T(8,128)(2,1)S(1)} %collective-permute-done.5.other_ref.refs_4_, bf16[11,128,256]{2,1,0:T(8,128)(2,1)S(1)} %get-tuple-element.37.mine_ref.key_value_ref, bf16[128,768]{1,0:T(8,128)(2,1)S(1)} %collective-permute-done.4.refs_5_.came_ref, ...), custom_call_target="tpu_custom_call" | custom-call | flops 536870912 | bytes 2097152 | tf_op jit(solution)/shard_map/pallas_call | solution.py:29
  27.2 0.0 collective-permute-done.7.refs_1_
  27.2 1.4 %collective-permute-done.8.refs_2_ = bf16[144,256]{1,0:T(8,128)(2,1)S(1)} collective-permute-done((bf16[144,256]{1,0:T(8,128)(2,1)S(1)}, bf16[144,256]{1,0:T(8,128)(2,1)S(1)}, u32[]{:S(2)}, u32[]{:S(2)}) %collective-permute-start.8) | collective-permute-done | bytes 73760 | tf_op jit(solution)/shard_map/ppermute | solution.py:41
  28.5 1.8 %collective-permute-done.9.refs_3_ = bf16[144,256]{1,0:T(8,128)(2,1)S(1)} collective-permute-done((bf16[144,256]{1,0:T(8,128)(2,1)S(1)}, bf16[144,256]{1,0:T(8,128)(2,1)S(1)}, u32[]{:S(2)}, u32[]{:S(2)}) %collective-permute-start.9) | collective-permute-done | bytes 73760 | tf_op jit(solution)/shard_map/ppermute | solution.py:41
  30.3 0.7 %shard_map.111 = (bf16[128,1024]{1,0:T(8,128)(2,1)}, f32[8,128]{1,0:T(8,128)}) custom-call(bf16[144,256]{1,0:T(8,128)(2,1)S(1)} %get-tuple-element.48.refs_0_, bf16[144,256]{1,0:T(8,128)(2,1)S(1)} %collective-permute-done.7.refs_1_, bf16[144,256]{1,0:T(8,128)(2,1)S(1)} %collective-permute-done.8.refs_2_, bf16[144,256]{1,0:T(8,128)(2,1)S(1)} %collective-permute-done.9.refs_3_), custom_call_target="tpu_custom_call" | custom-call | bytes 524288 | tf_op jit(solution)/shard_map/pallas_call | solution.py:29
Async XLA Ops:
  0.6 6.1 %copy-start = (bf16[3,128,1024]{2,1,0:T(8,128)(2,1)S(1)}, bf16[3,128,1024]{2,1,0:T(8,128)(2,1)}, u32[]{:S(2)}) copy-start(bf16[3,128,1024]{2,1,0:T(8,128)(2,1)} %gate_ref.1) | copy-start | bytes 2359300
  2.2 11.8 %collective-permute-start = (bf16[400,256]{1,0:T(8,128)(2,1)S(1)}, bf16[400,256]{1,0:T(8,128)(2,1)S(1)}, u32[]{:S(2)}, u32[]{:S(2)}) collective-permute-start(bf16[400,256]{1,0:T(8,128)(2,1)S(1)} %get-tuple-element.29), channel_id=1, source_target_pairs={{0,8},{4,12},{8,0},{12,4},{16,24},{20,28},{24,16},{28,20},{1,9},{5... | collective-permute-start | bytes 614408 | tf_op jit(solution)/shard_map/ppermute | solution.py:41
  5.2 10.9 %collective-permute-start.1 = (bf16[400,256]{1,0:T(8,128)(2,1)S(1)}, bf16[400,256]{1,0:T(8,128)(2,1)S(1)}, u32[]{:S(2)}, u32[]{:S(2)}) collective-permute-start(bf16[400,256]{1,0:T(8,128)(2,1)S(1)} %get-tuple-element.30), channel_id=1, source_target_pairs={{0,16},{4,20},{8,24},{12,28},{16,0},{20,4},{24,8},{28,12},{1,17},{... | collective-permute-start | bytes 614408 | tf_op jit(solution)/shard_map/ppermute | solution.py:41
  6.7 9.4 %collective-permute-start.2 = (bf16[400,256]{1,0:T(8,128)(2,1)S(1)}, bf16[400,256]{1,0:T(8,128)(2,1)S(1)}, u32[]{:S(2)}, u32[]{:S(2)}) collective-permute-start(bf16[400,256]{1,0:T(8,128)(2,1)S(1)} %get-tuple-element.31), channel_id=1, source_target_pairs={{0,24},{4,28},{8,16},{12,20},{16,8},{20,12},{24,0},{28,4},{1,25},{... | collective-permute-start | bytes 614408 | tf_op jit(solution)/shard_map/ppermute | solution.py:41
  6.9 7.1 %collective-permute-start.4 = (bf16[128,768]{1,0:T(8,128)(2,1)S(1)}, bf16[128,768]{1,0:T(8,128)(2,1)S(1)}, u32[]{:S(2)}, u32[]{:S(2)}) collective-permute-start(bf16[128,768]{1,0:T(8,128)(2,1)S(1)} %get-tuple-element.34), channel_id=1, source_target_pairs={{0,4},{1,5},{2,6},{3,7},{4,1},{5,0},{6,3},{7,2},{8,12},{9,13},{10,... | collective-permute-start | bytes 589832 | tf_op jit(solution)/shard_map/ppermute | solution.py:470
  7.0 7.1 %collective-permute-start.3 = (bf16[32,1024]{1,0:T(8,128)(2,1)S(1)}, bf16[32,1024]{1,0:T(8,128)(2,1)S(1)}, u32[]{:S(2)}, u32[]{:S(2)}) collective-permute-start(bf16[32,1024]{1,0:T(8,128)(2,1)S(1)} %get-tuple-element.33), channel_id=1, source_target_pairs={{0,3},{1,2},{2,1},{3,0},{4,6},{5,7},{6,4},{7,5},{8,11},{9,10},{10,... | collective-permute-start | bytes 196616 | tf_op jit(solution)/shard_map/ppermute | solution.py:469
  16.2 2.3 %collective-permute-start.5 = (bf16[11,128,256]{2,1,0:T(8,128)(2,1)S(1)}, bf16[11,128,256]{2,1,0:T(8,128)(2,1)S(1)}, u32[]{:S(2)}, u32[]{:S(2)}) collective-permute-start(bf16[11,128,256]{2,1,0:T(8,128)(2,1)S(1)} %get-tuple-element.37.mine_ref.key_value_ref), channel_id=1, source_target_pairs={{0,4},{4,0},{8,12},{12,8},{16,20},{20,16},{24,28},{28,24},{1,5},{5... | collective-permute-start | bytes 2162696 | tf_op jit(solution)/shard_map/ppermute | solution.py:41
  16.3 8.5 %collective-permute-start.6 = (bf16[128,1024]{1,0:T(8,128)(2,1)S(1)}, bf16[128,1024]{1,0:T(8,128)(2,1)S(1)}, u32[]{:S(2)}, u32[]{:S(2)}) collective-permute-start(bf16[128,1024]{1,0:T(8,128)(2,1)S(1)} %get-tuple-element.35.refs_6_.product_ref), channel_id=1, source_target_pairs={{4,8},{8,4},{12,16},{16,12},{20,24},{24,20},{5,9},{9,5},{13,17},{1... | collective-permute-start | bytes 786440 | tf_op jit(solution)/shard_map/ppermute | solution.py:472
  19.3 7.9 %collective-permute-start.7 = (bf16[144,256]{1,0:T(8,128)(2,1)S(1)}, bf16[144,256]{1,0:T(8,128)(2,1)S(1)}, u32[]{:S(2)}, u32[]{:S(2)}) collective-permute-start(bf16[144,256]{1,0:T(8,128)(2,1)S(1)} %get-tuple-element.47.refs_5_), channel_id=1, source_target_pairs={{0,16},{4,20},{8,24},{12,28},{16,0},{20,4},{24,8},{28,12},{1,17},{... | collective-permute-start | bytes 221192 | tf_op jit(solution)/shard_map/ppermute | solution.py:41
  22.7 5.9 %collective-permute-start.8 = (bf16[144,256]{1,0:T(8,128)(2,1)S(1)}, bf16[144,256]{1,0:T(8,128)(2,1)S(1)}, u32[]{:S(2)}, u32[]{:S(2)}) collective-permute-start(bf16[144,256]{1,0:T(8,128)(2,1)S(1)} %get-tuple-element.49), channel_id=1, source_target_pairs={{0,24},{4,28},{8,16},{12,20},{16,8},{20,12},{24,0},{28,4},{1,25},{... | collective-permute-start | bytes 221192 | tf_op jit(solution)/shard_map/ppermute | solution.py:41
  24.2 6.1 %collective-permute-start.9 = (bf16[144,256]{1,0:T(8,128)(2,1)S(1)}, bf16[144,256]{1,0:T(8,128)(2,1)S(1)}, u32[]{:S(2)}, u32[]{:S(2)}) collective-permute-start(bf16[144,256]{1,0:T(8,128)(2,1)S(1)} %get-tuple-element.50), channel_id=1, source_target_pairs={{0,8},{4,12},{8,0},{12,4},{16,24},{20,28},{24,16},{28,20},{1,9},{5... | collective-permute-start | bytes 221192 | tf_op jit(solution)/shard_map/ppermute | solution.py:41

commit v5 on v3

--- a/solution.py
+++ b/solution.py
@@ -15,6 +15,7 @@
 NOTE_ROWS = 16
 MASKED = -1e30
 VMEM_LIMIT = 16 * 1024 * 1024
+LONG = 200
 
 
 def vmem():
@@ -56,12 +57,12 @@
     copies = []
     for step, out in enumerate(outs):
         columns = pl.ds(pl.multiple_of((pair ^ step) * (2 * HD), 2 * HD), 2 * HD)
-        for part, source in enumerate(
-            (queries_ref, keys_values_ref.at[0], keys_values_ref.at[1])
-        ):
+        for part, source in enumerate((queries_ref, keys_values_ref)):
             copies.append(
                 pltpu.make_async_copy(
-                    source.at[:, columns], out.at[pl.ds(part * rows, rows)], sem.at[step, part]
+                    source.at[:, columns],
+                    out.at[pl.ds(part * rows, source.shape[0])],
+                    sem.at[step, part],
                 )
             )
     width = taps_ref.shape[2]
@@ -443,14 +444,14 @@
     *packed, wide_taps = call(
         functools.partial(pack_heads, heads),
         (shape((3 * rows + NOTE_ROWS, 2 * HD), bf16),) * count + (shape((3, height, channels), f32),),
-        pinned(queries, keys_values, starts, filters),
+        pinned(queries, keys_values.reshape(2 * rows, heads * HD), starts, filters),
         0,
         4 * queries.size * 3,
         scratch=(
             pltpu.VMEM((1, rows), jnp.int32),
             pltpu.SemaphoreType.DMA,
             pltpu.SemaphoreType.DMA((3,)),
-            pltpu.SemaphoreType.DMA((count, 3)),
+            pltpu.SemaphoreType.DMA((count, 2)),
         ),
         specs=[hbm()] * 4,
     )
@@ -505,7 +506,7 @@
             shape((2, units, HD, UNIT * rows), f32),
         ),
         (query, key_value),
-        2 * (heads * rows) ** 2 * HD,
+        LONG * (heads * rows) ** 2 * HD,
         4 * queries.size * 4,
     )
     operands = [query, *partial, other]

time: 28.5 us -> 29.4 us (1.032)
  starting transfers between devices: 13.1 us -> 14.7 us
  waiting for transfers between devices: 6.18 us -> 5.65 us
    ppermute x7, starting transfers between devices: 8.25 us -> 9.84 us  [crossed(): lax.ppermute(array, axis, [(i, i ^ bits) for i in range(lax.axis_size(axi...]
    ppermute x7, waiting for transfers between devices: 4.29 us -> 3.77 us  [crossed(): lax.ppermute(array, axis, [(i, i ^ bits) for i in range(lax.axis_size(axi...]
where the time goes in v5:
time: 29.4 us; the launch traced here: 29.2 us
  starting transfers between devices  14.7 us (50%)
  Pallas kernels  8.16 us (28%)
  waiting for transfers between devices  5.65 us (19%)
  between operations  0.73 us (2%)
    ppermute x7, starting transfers between devices, crossed(): lax.ppermute(array, axis, [(i, i ^ bits) for i in range(lax.axis_size(axi...  9.84 us
    pallas_call x9, Pallas kernels, call(): pl.pallas_call(kernel, out_shape=out_shape, in_specs=specs or [vmem() for...  8.16 us
    ppermute x1, starting transfers between devices, local(): far_taps = lax.ppermute(far_taps, axes, far_pairs)  4.12 us
    ppermute x7, waiting for transfers between devices, crossed(): lax.ppermute(array, axis, [(i, i ^ bits) for i in range(lax.axis_size(axi...  3.77 us
    ppermute x1, waiting for transfers between devices, local(): far_taps = lax.ppermute(far_taps, axes, far_pairs)  1.88 us
    ppermute x1, starting transfers between devices, local(): lax.ppermute(product, 'ctx', [(i, i + 1) for i in range(1, peers - 1, 2)])  0.67 us
  transfers between devices with their start and end apart: 10, of which 5 were waited for; matrix products, arithmetic and copies ran while one was open for 0% of the time, Pallas kernels for 20%

profile of v5, /device:TPU:0, one launch (start us, length us, event | category | flops | bytes accessed | tf_op | source)
XLA Modules:
  0.0 29.2 jit_solution(14274993133978512627)
XLA Ops:
  0.6 0.0 copy-start
  0.6 1.5 %shard_map.103 = (bf16[400,256]{1,0:T(8,128)(2,1)S(1)}, bf16[400,256]{1,0:T(8,128)(2,1)S(1)}, bf16[400,256]{1,0:T(8,128)(2,1)S(1)}, bf16[400,256]{1,0:T(8,128)(2,1)S(1)}, f32[3,32,1024]{2,1,0:T(8,128)S(1)}) custom-call(bf16[128,1024]{1,0:T(8,128)(2,1)} %queries_ref.1, bf16[256,1024]{1,0:T(8,128)(2,1)} %bitcast.3, s32[1,128]{1,0:T(1,128)} %bitcast.5, ...), custom_call_target="tpu_custom_call" | custom-call | bytes 1572864 | tf_op jit(solution)/shard_map/pallas_call | solution.py:30
  2.2 3.0 %collective-permute-start = (bf16[400,256]{1,0:T(8,128)(2,1)S(1)}, bf16[400,256]{1,0:T(8,128)(2,1)S(1)}, u32[]{:S(2)}, u32[]{:S(2)}) collective-permute-start(bf16[400,256]{1,0:T(8,128)(2,1)S(1)} %get-tuple-element.29), channel_id=1, source_target_pairs={{0,8},{4,12},{8,0},{12,4},{16,24},{20,28},{24,16},{28,20},{1,9},{5... | collective-permute-start | bytes 614408 | tf_op jit(solution)/shard_map/ppermute | solution.py:42
  5.2 1.5 %collective-permute-start.1 = (bf16[400,256]{1,0:T(8,128)(2,1)S(1)}, bf16[400,256]{1,0:T(8,128)(2,1)S(1)}, u32[]{:S(2)}, u32[]{:S(2)}) collective-permute-start(bf16[400,256]{1,0:T(8,128)(2,1)S(1)} %get-tuple-element.30), channel_id=1, source_target_pairs={{0,16},{4,20},{8,24},{12,28},{16,0},{20,4},{24,8},{28,12},{1,17},{... | collective-permute-start | bytes 614408 | tf_op jit(solution)/shard_map/ppermute | solution.py:42
  6.7 0.0 collective-permute-start.2
  6.7 0.0 copy-done
  6.7 0.1 shard_map.104
  6.9 0.1 collective-permute-start.4
  6.9 4.1 %collective-permute-start.3 = (bf16[32,1024]{1,0:T(8,128)(2,1)S(1)}, bf16[32,1024]{1,0:T(8,128)(2,1)S(1)}, u32[]{:S(2)}, u32[]{:S(2)}) collective-permute-start(bf16[32,1024]{1,0:T(8,128)(2,1)S(1)} %get-tuple-element.33), channel_id=1, source_target_pairs={{0,3},{1,2},{2,1},{3,0},{4,6},{5,7},{6,4},{7,5},{8,11},{9,10},{10,... | collective-permute-start | bytes 196616 | tf_op jit(solution)/shard_map/ppermute | solution.py:470
  11.0 1.1 %shard_map.105 = (bf16[256,256]{1,0:T(8,128)(2,1)S(1)}, bf16[256,256]{1,0:T(8,128)(2,1)S(1)}, bf16[128,256]{1,0:T(8,128)(2,1)S(1)}, s32[1,128]{1,0:T(1,128)S(1)}, f32[1,1024]{1,0:T(1,128)S(1)}) custom-call(f32[256,256]{1,0:T(8,128)} %constant.4.clone.ahead_ref, f32[128,256]{1,0:T(8,128)} %constant.5.clone.back_ref, s32[1,128]{1,0:T(1,128)} %bitcast.6, ...), custom_call_target="tpu_custom_call" | custom-call | bytes 524288 | tf_op jit(solution)/shard_map/pallas_call | solution.py:30
  12.1 1.9 %collective-permute-done.3.refs_4_ = bf16[32,1024]{1,0:T(8,128)(2,1)S(1)} collective-permute-done((bf16[32,1024]{1,0:T(8,128)(2,1)S(1)}, bf16[32,1024]{1,0:T(8,128)(2,1)S(1)}, u32[]{:S(2)}, u32[]{:S(2)}) %collective-permute-start.3) | collective-permute-done | bytes 65568 | tf_op jit(solution)/shard_map/ppermute | solution.py:470
  14.0 0.7 %collective-permute-start.6 = (bf16[128,1024]{1,0:T(8,128)(2,1)S(1)}, bf16[128,1024]{1,0:T(8,128)(2,1)S(1)}, u32[]{:S(2)}, u32[]{:S(2)}) collective-permute-start(bf16[128,1024]{1,0:T(8,128)(2,1)S(1)} %get-tuple-element.35.refs_6_.product_ref), channel_id=1, source_target_pairs={{4,8},{12,16},{20,24},{5,9},{13,17},{21,25},{6,10},{14,18},{22,26}... | collective-permute-start | bytes 786440 | tf_op jit(solution)/shard_map/ppermute | solution.py:472
  14.7 0.0 collective-permute-done.4.refs_5_.came_ref
  14.7 0.0 collective-permute-done.refs_1_
  14.7 1.4 %collective-permute-done.1.refs_2_ = bf16[400,256]{1,0:T(8,128)(2,1)S(1)} collective-permute-done((bf16[400,256]{1,0:T(8,128)(2,1)S(1)}, bf16[400,256]{1,0:T(8,128)(2,1)S(1)}, u32[]{:S(2)}, u32[]{:S(2)}) %collective-permute-start.1) | collective-permute-done | bytes 204832 | tf_op jit(solution)/shard_map/ppermute | solution.py:42
  16.1 0.0 collective-permute-done.2.refs_3_
  16.1 0.1 shard_map.106
  16.2 1.7 %collective-permute-start.5 = (bf16[11,128,256]{2,1,0:T(8,128)(2,1)S(1)}, bf16[11,128,256]{2,1,0:T(8,128)(2,1)S(1)}, u32[]{:S(2)}, u32[]{:S(2)}) collective-permute-start(bf16[11,128,256]{2,1,0:T(8,128)(2,1)S(1)} %get-tuple-element.37.mine_ref.key_value_ref), channel_id=1, source_target_pairs={{0,4},{4,0},{8,12},{12,8},{16,20},{20,16},{24,28},{28,24},{1,5},{5... | collective-permute-start | bytes 2162696 | tf_op jit(solution)/shard_map/ppermute | solution.py:42
  17.9 1.0 %shard_map.108 = (f32[2,2,1,256]{3,2,1,0:T(1,128)S(1)}, f32[2,2,1,256]{3,2,1,0:T(1,128)S(1)}, f32[2,2,128,256]{3,2,1,0:T(8,128)S(1)}) custom-call(bf16[4,144,256]{2,1,0:T(8,128)(2,1)S(1)} %get-tuple-element.43.query_ref.refs_0_, bf16[11,128,256]{2,1,0:T(8,128)(2,1)S(1)} %get-tuple-element.37.mine_ref.key_value_ref), custom_call_target="tpu_custom_call" | custom-call | flops 26843545600 | bytes 2097152 | tf_op jit(solution)/shard_map/pallas_call | solution.py:30
  18.8 0.8 %collective-permute-done.5.other_ref.refs_4_ = bf16[11,128,256]{2,1,0:T(8,128)(2,1)S(1)} collective-permute-done((bf16[11,128,256]{2,1,0:T(8,128)(2,1)S(1)}, bf16[11,128,256]{2,1,0:T(8,128)(2,1)S(1)}, u32[]{:S(2)}, u32[]{:S(2)}) %collective-permute-start.5) | collective-permute-done | bytes 720928 | tf_op jit(solution)/shard_map/ppermute | solution.py:42
  19.7 0.8 %shard_map.109 = (bf16[144,256]{1,0:T(8,128)(2,1)S(1)}, bf16[144,256]{1,0:T(8,128)(2,1)S(1)}) custom-call(bf16[4,144,256]{2,1,0:T(8,128)(2,1)S(1)} %get-tuple-element.43.query_ref.refs_0_, f32[2,2,1,256]{3,2,1,0:T(1,128)S(1)} %get-tuple-element.44.refs_1_, f32[2,2,1,256]{3,2,1,0:T(1,128)S(1)} %get-tuple-element.45.refs_2_, ...), custom_call_target="tpu_custom_call" | custom-call | flops 134217728 | bytes 2097152 | tf_op jit(solution)/shard_map/pallas_call | solution.py:30
  20.4 1.4 %collective-permute-start.7 = (bf16[144,256]{1,0:T(8,128)(2,1)S(1)}, bf16[144,256]{1,0:T(8,128)(2,1)S(1)}, u32[]{:S(2)}, u32[]{:S(2)}) collective-permute-start(bf16[144,256]{1,0:T(8,128)(2,1)S(1)} %get-tuple-element.47.refs_5_), channel_id=1, source_target_pairs={{0,16},{4,20},{8,24},{12,28},{16,0},{20,4},{24,8},{28,12},{1,17},{... | collective-permute-start | bytes 221192 | tf_op jit(solution)/shard_map/ppermute | solution.py:42
  21.9 1.6 %collective-permute-start.8 = (bf16[144,256]{1,0:T(8,128)(2,1)S(1)}, bf16[144,256]{1,0:T(8,128)(2,1)S(1)}, u32[]{:S(2)}, u32[]{:S(2)}) collective-permute-start(bf16[144,256]{1,0:T(8,128)(2,1)S(1)} %get-tuple-element.49), channel_id=1, source_target_pairs={{0,24},{4,28},{8,16},{12,20},{16,8},{20,12},{24,0},{28,4},{1,25},{... | collective-permute-start | bytes 221192 | tf_op jit(solution)/shard_map/ppermute | solution.py:42
  23.5 0.6 %shard_map.110 = (bf16[144,256]{1,0:T(8,128)(2,1)S(1)}, bf16[144,256]{1,0:T(8,128)(2,1)S(1)}) custom-call(bf16[4,144,256]{2,1,0:T(8,128)(2,1)S(1)} %get-tuple-element.43.query_ref.refs_0_, f32[2,2,1,256]{3,2,1,0:T(1,128)S(1)} %get-tuple-element.44.refs_1_, f32[2,2,1,256]{3,2,1,0:T(1,128)S(1)} %get-tuple-element.45.refs_2_, ...), custom_call_target="tpu_custom_call" | custom-call | flops 134217728 | bytes 2097152 | tf_op jit(solution)/shard_map/pallas_call | solution.py:30
  24.1 0.6 %collective-permute-start.9 = (bf16[144,256]{1,0:T(8,128)(2,1)S(1)}, bf16[144,256]{1,0:T(8,128)(2,1)S(1)}, u32[]{:S(2)}, u32[]{:S(2)}) collective-permute-start(bf16[144,256]{1,0:T(8,128)(2,1)S(1)} %get-tuple-element.50), channel_id=1, source_target_pairs={{0,8},{4,12},{8,0},{12,4},{16,24},{20,28},{24,16},{28,20},{1,9},{5... | collective-permute-start | bytes 221192 | tf_op jit(solution)/shard_map/ppermute | solution.py:42
  24.7 0.0 collective-permute-done.6.before_ref
  24.7 2.3 %shard_map.107 = bf16[128,1024]{1,0:T(8,128)(2,1)} custom-call(bf16[11,128,256]{2,1,0:T(8,128)(2,1)S(1)} %collective-permute-done.5.other_ref.refs_4_, bf16[11,128,256]{2,1,0:T(8,128)(2,1)S(1)} %get-tuple-element.37.mine_ref.key_value_ref, bf16[128,768]{1,0:T(8,128)(2,1)S(1)} %collective-permute-done.4.refs_5_.came_ref, ...), custom_call_target="tpu_custom_call" | custom-call | flops 536870912 | bytes 2097152 | tf_op jit(solution)/shard_map/pallas_call | solution.py:30
  27.0 0.0 collective-permute-done.7.refs_1_
  27.0 0.7 %collective-permute-done.8.refs_2_ = bf16[144,256]{1,0:T(8,128)(2,1)S(1)} collective-permute-done((bf16[144,256]{1,0:T(8,128)(2,1)S(1)}, bf16[144,256]{1,0:T(8,128)(2,1)S(1)}, u32[]{:S(2)}, u32[]{:S(2)}) %collective-permute-start.8) | collective-permute-done | bytes 73760 | tf_op jit(solution)/shard_map/ppermute | solution.py:42
  27.7 0.8 %collective-permute-done.9.refs_3_ = bf16[144,256]{1,0:T(8,128)(2,1)S(1)} collective-permute-done((bf16[144,256]{1,0:T(8,128)(2,1)S(1)}, bf16[144,256]{1,0:T(8,128)(2,1)S(1)}, u32[]{:S(2)}, u32[]{:S(2)}) %collective-permute-start.9) | collective-permute-done | bytes 73760 | tf_op jit(solution)/shard_map/ppermute | solution.py:42
  28.5 0.7 %shard_map.111 = (bf16[128,1024]{1,0:T(8,128)(2,1)}, f32[8,128]{1,0:T(8,128)}) custom-call(bf16[144,256]{1,0:T(8,128)(2,1)S(1)} %get-tuple-element.48.refs_0_, bf16[144,256]{1,0:T(8,128)(2,1)S(1)} %collective-permute-done.7.refs_1_, bf16[144,256]{1,0:T(8,128)(2,1)S(1)} %collective-permute-done.8.refs_2_, bf16[144,256]{1,0:T(8,128)(2,1)S(1)} %collective-permute-done.9.refs_3_), custom_call_target="tpu_custom_call" | custom-call | bytes 524288 | tf_op jit(solution)/shard_map/pallas_call | solution.py:30
Async XLA Ops:
  0.6 6.1 %copy-start = (bf16[3,128,1024]{2,1,0:T(8,128)(2,1)S(1)}, bf16[3,128,1024]{2,1,0:T(8,128)(2,1)}, u32[]{:S(2)}) copy-start(bf16[3,128,1024]{2,1,0:T(8,128)(2,1)} %gate_ref.1) | copy-start | bytes 2359300
  2.2 12.5 %collective-permute-start = (bf16[400,256]{1,0:T(8,128)(2,1)S(1)}, bf16[400,256]{1,0:T(8,128)(2,1)S(1)}, u32[]{:S(2)}, u32[]{:S(2)}) collective-permute-start(bf16[400,256]{1,0:T(8,128)(2,1)S(1)} %get-tuple-element.29), channel_id=1, source_target_pairs={{0,8},{4,12},{8,0},{12,4},{16,24},{20,28},{24,16},{28,20},{1,9},{5... | collective-permute-start | bytes 614408 | tf_op jit(solution)/shard_map/ppermute | solution.py:42
  5.2 10.9 %collective-permute-start.1 = (bf16[400,256]{1,0:T(8,128)(2,1)S(1)}, bf16[400,256]{1,0:T(8,128)(2,1)S(1)}, u32[]{:S(2)}, u32[]{:S(2)}) collective-permute-start(bf16[400,256]{1,0:T(8,128)(2,1)S(1)} %get-tuple-element.30), channel_id=1, source_target_pairs={{0,16},{4,20},{8,24},{12,28},{16,0},{20,4},{24,8},{28,12},{1,17},{... | collective-permute-start | bytes 614408 | tf_op jit(solution)/shard_map/ppermute | solution.py:42
  6.7 9.4 %collective-permute-start.2 = (bf16[400,256]{1,0:T(8,128)(2,1)S(1)}, bf16[400,256]{1,0:T(8,128)(2,1)S(1)}, u32[]{:S(2)}, u32[]{:S(2)}) collective-permute-start(bf16[400,256]{1,0:T(8,128)(2,1)S(1)} %get-tuple-element.31), channel_id=1, source_target_pairs={{0,24},{4,28},{8,16},{12,20},{16,8},{20,12},{24,0},{28,4},{1,25},{... | collective-permute-start | bytes 614408 | tf_op jit(solution)/shard_map/ppermute | solution.py:42
  6.9 7.8 %collective-permute-start.4 = (bf16[128,768]{1,0:T(8,128)(2,1)S(1)}, bf16[128,768]{1,0:T(8,128)(2,1)S(1)}, u32[]{:S(2)}, u32[]{:S(2)}) collective-permute-start(bf16[128,768]{1,0:T(8,128)(2,1)S(1)} %get-tuple-element.34), channel_id=1, source_target_pairs={{0,4},{1,5},{2,6},{3,7},{4,1},{5,0},{6,3},{7,2},{8,12},{9,13},{10,... | collective-permute-start | bytes 589832 | tf_op jit(solution)/shard_map/ppermute | solution.py:471
  6.9 7.1 %collective-permute-start.3 = (bf16[32,1024]{1,0:T(8,128)(2,1)S(1)}, bf16[32,1024]{1,0:T(8,128)(2,1)S(1)}, u32[]{:S(2)}, u32[]{:S(2)}) collective-permute-start(bf16[32,1024]{1,0:T(8,128)(2,1)S(1)} %get-tuple-element.33), channel_id=1, source_target_pairs={{0,3},{1,2},{2,1},{3,0},{4,6},{5,7},{6,4},{7,5},{8,11},{9,10},{10,... | collective-permute-start | bytes 196616 | tf_op jit(solution)/shard_map/ppermute | solution.py:470
  14.0 10.7 %collective-permute-start.6 = (bf16[128,1024]{1,0:T(8,128)(2,1)S(1)}, bf16[128,1024]{1,0:T(8,128)(2,1)S(1)}, u32[]{:S(2)}, u32[]{:S(2)}) collective-permute-start(bf16[128,1024]{1,0:T(8,128)(2,1)S(1)} %get-tuple-element.35.refs_6_.product_ref), channel_id=1, source_target_pairs={{4,8},{12,16},{20,24},{5,9},{13,17},{21,25},{6,10},{14,18},{22,26}... | collective-permute-start | bytes 786440 | tf_op jit(solution)/shard_map/ppermute | solution.py:472
  16.2 3.5 %collective-permute-start.5 = (bf16[11,128,256]{2,1,0:T(8,128)(2,1)S(1)}, bf16[11,128,256]{2,1,0:T(8,128)(2,1)S(1)}, u32[]{:S(2)}, u32[]{:S(2)}) collective-permute-start(bf16[11,128,256]{2,1,0:T(8,128)(2,1)S(1)} %get-tuple-element.37.mine_ref.key_value_ref), channel_id=1, source_target_pairs={{0,4},{4,0},{8,12},{12,8},{16,20},{20,16},{24,28},{28,24},{1,5},{5... | collective-permute-start | bytes 2162696 | tf_op jit(solution)/shard_map/ppermute | solution.py:42
  20.4 6.5 %collective-permute-start.7 = (bf16[144,256]{1,0:T(8,128)(2,1)S(1)}, bf16[144,256]{1,0:T(8,128)(2,1)S(1)}, u32[]{:S(2)}, u32[]{:S(2)}) collective-permute-start(bf16[144,256]{1,0:T(8,128)(2,1)S(1)} %get-tuple-element.47.refs_5_), channel_id=1, source_target_pairs={{0,16},{4,20},{8,24},{12,28},{16,0},{20,4},{24,8},{28,12},{1,17},{... | collective-permute-start | bytes 221192 | tf_op jit(solution)/shard_map/ppermute | solution.py:42
  21.9 5.8 %collective-permute-start.8 = (bf16[144,256]{1,0:T(8,128)(2,1)S(1)}, bf16[144,256]{1,0:T(8,128)(2,1)S(1)}, u32[]{:S(2)}, u32[]{:S(2)}) collective-permute-start(bf16[144,256]{1,0:T(8,128)(2,1)S(1)} %get-tuple-element.49), channel_id=1, source_target_pairs={{0,24},{4,28},{8,16},{12,20},{16,8},{20,12},{24,0},{28,4},{1,25},{... | collective-permute-start | bytes 221192 | tf_op jit(solution)/shard_map/ppermute | solution.py:42
  24.1 4.4 %collective-permute-start.9 = (bf16[144,256]{1,0:T(8,128)(2,1)S(1)}, bf16[144,256]{1,0:T(8,128)(2,1)S(1)}, u32[]{:S(2)}, u32[]{:S(2)}) collective-permute-start(bf16[144,256]{1,0:T(8,128)(2,1)S(1)} %get-tuple-element.50), channel_id=1, source_target_pairs={{0,8},{4,12},{8,0},{12,4},{16,24},{20,28},{24,16},{28,20},{1,9},{5... | collective-permute-start | bytes 221192 | tf_op jit(solution)/shard_map/ppermute | solution.py:42

commit v6 on v3

--- a/solution.py
+++ b/solution.py
@@ -55,15 +55,16 @@
     first.start()
     copies = []
     for step, out in enumerate(outs):
-        columns = pl.ds(pl.multiple_of((pair ^ step) * (2 * HD), 2 * HD), 2 * HD)
-        for part, source in enumerate(
-            (queries_ref, keys_values_ref.at[0], keys_values_ref.at[1])
-        ):
-            copies.append(
-                pltpu.make_async_copy(
-                    source.at[:, columns], out.at[pl.ds(part * rows, rows)], sem.at[step, part]
+        for head in range(2):
+            columns = pl.ds(pl.multiple_of(((pair ^ step) * 2 + head) * HD, HD), HD)
+            first_row = head * 3 * rows
+            for part, source in enumerate((queries_ref, keys_values_ref)):
+                lines = pl.ds(first_row + part * rows, source.shape[0])
+                copies.append(
+                    pltpu.make_async_copy(
+                        source.at[:, columns], out.at[lines], sem.at[step, 2 * head + part]
+                    )
                 )
-            )
     width = taps_ref.shape[2]
     panel = lax.axis_index("tp")
     for index, target in enumerate((panel, panel ^ (3 - lax.rem(lax.axis_index("ctx"), 2)), panel ^ 1)):
@@ -82,8 +83,7 @@
     line = lax.broadcasted_iota(jnp.int32, (NOTE_ROWS, rows), 0)
     note = jnp.where(line == 0, high, jnp.where(line == 1, low, 0.0)).astype(jnp.bfloat16)
     for out in outs:
-        out[3 * rows :, :HD] = note
-        out[3 * rows :, HD:] = note
+        out[6 * rows :] = note
     for copy in copies:
         copy.wait()
 
@@ -146,14 +146,18 @@
     count = heads // 2
     far_ref, came_ref, product_ref = refs[count : count + 3]
     query_ref, side_ref = refs[-2:]
-    rows = (refs[0].shape[0] - NOTE_ROWS) // 3
+    rows = (refs[0].shape[0] - NOTE_ROWS) // 6
     _, pair, _ = place(heads)
     for step in range(count):
         source = pair ^ step
-        query_ref[source, :rows] = refs[step][:rows]
-        query_ref[source, rows:] = refs[step][3 * rows :]
-        side_ref[2 * source] = refs[step][rows : 2 * rows]
-        side_ref[2 * source + 1] = refs[step][2 * rows : 3 * rows]
+        query_ref[source, rows:, :HD] = refs[step][6 * rows :]
+        for head in range(2):
+            columns = slice(head * HD, (head + 1) * HD)
+            first = head * 3 * rows
+            query_ref[source, :rows, columns] = refs[step][first : first + rows]
+            for part in range(2):
+                line = first + (part + 1) * rows
+                side_ref[2 * source + part, :, columns] = refs[step][line : line + rows]
     height, width = far_ref.shape
     parts = width // (2 * HD)
     for part in range(parts):
@@ -286,8 +290,8 @@
         for head in range(2):
             tops.append(jnp.maximum(top_ref[head, unit], highest(held[head])))
         weights = [weigh(each, top) for each, top in zip(held, tops)]
+        notes = jnp.zeros((NOTE_ROWS, UNIT * rows), jnp.float32)
         for head, (total, rounded) in enumerate(weights):
-            columns = slice(head * HD, (head + 1) * HD)
             top = tops[head]
             scale = jnp.exp2((top_ref[head, unit] - top) * FACTOR)
             total = total_ref[head, unit] * scale + total
@@ -297,14 +301,17 @@
             high = logs.astype(jnp.bfloat16).astype(jnp.float32)
             middle = (logs - high).astype(jnp.bfloat16).astype(jnp.float32)
             low = logs - high - middle
-            line = lax.broadcasted_iota(jnp.int32, (NOTE_ROWS, UNIT * rows), 0)
-            note = jnp.where(
-                line == 0, high, jnp.where(line == 1, middle, jnp.where(line == 2, low, 0.0))
-            ).astype(jnp.bfloat16)
+            line = lax.broadcasted_iota(jnp.int32, (NOTE_ROWS, UNIT * rows), 0) - 3 * head
+            for index, part in enumerate((high, middle, low)):
+                notes = jnp.where(line == index, part, notes)
             for index in range(UNIT):
-                span = slice(index * rows, (index + 1) * rows)
-                held_ref[index, :rows, columns] = mixed[span]
-                held_ref[index, rows:, columns] = note[:, span]
+                held_ref[index, head * rows : (head + 1) * rows] = mixed[
+                    index * rows : (index + 1) * rows
+                ]
+        for index in range(UNIT):
+            held_ref[index, 2 * rows :] = notes[:, index * rows : (index + 1) * rows].astype(
+                jnp.bfloat16
+            )
 
     for unit in range(count // UNIT):
 
@@ -322,11 +329,12 @@
     _, pair, _ = place(heads)
     for step, source in zip(steps, sources):
         owner = pair ^ step
-        out_ref[:, pl.ds(pl.multiple_of(owner * (2 * HD), 2 * HD), 2 * HD)] = source[:rows]
-        note = source[rows:].astype(jnp.float32)
-        logs = note[0:1] + note[1:2] + note[2:3]
+        note = source[2 * rows :].astype(jnp.float32)
         for head in range(2):
-            logs_ref[pl.ds(owner * 2 + head, 1), :] = logs[:, head * HD : (head + 1) * HD]
+            columns = pl.ds(pl.multiple_of((owner * 2 + head) * HD, HD), HD)
+            out_ref[:, columns] = source[head * rows : (head + 1) * rows]
+            parts = [note[3 * head + index : 3 * head + index + 1] for index in range(3)]
+            logs_ref[pl.ds(owner * 2 + head, 1), :] = parts[0] + parts[1] + parts[2]
 
 
 def dot(left, right):
@@ -442,15 +450,15 @@
 
     *packed, wide_taps = call(
         functools.partial(pack_heads, heads),
-        (shape((3 * rows + NOTE_ROWS, 2 * HD), bf16),) * count + (shape((3, height, channels), f32),),
-        pinned(queries, keys_values, starts, filters),
+        (shape((6 * rows + NOTE_ROWS, HD), bf16),) * count + (shape((3, height, channels), f32),),
+        pinned(queries, keys_values.reshape(2 * rows, heads * HD), starts, filters),
         0,
         4 * queries.size * 3,
         scratch=(
             pltpu.VMEM((1, rows), jnp.int32),
             pltpu.SemaphoreType.DMA,
             pltpu.SemaphoreType.DMA((3,)),
-            pltpu.SemaphoreType.DMA((count, 3)),
+            pltpu.SemaphoreType.DMA((count, 4)),
         ),
         specs=[hbm()] * 4,
     )
@@ -513,7 +521,7 @@
         pairs = [(i, i + heads) for i in range(peers - heads)]
         operands += [lax.ppermute(each, "ctx", pairs) for each in (key_value, other)]
     assert count == 2 * UNIT
-    message = shape((rows + NOTE_ROWS, 2 * HD), bf16)
+    message = shape((2 * rows + NOTE_ROWS, HD), bf16)
 
     def second(mine, *more):
         return call(
@@ -522,7 +530,7 @@
             (*operands, *more),
             (heads * rows) ** 2 * HD,
             4 * queries.size * 4,
-            scratch=(pltpu.VMEM((UNIT, rows + NOTE_ROWS, 2 * HD), bf16),),
+            scratch=(pltpu.VMEM((UNIT, 2 * rows + NOTE_ROWS, HD), bf16),),
         )
 
     theirs = second(False)

time: 28.5 us -> 28.3 us (level)
  waiting for transfers between devices: 6.18 us -> 5.81 us
    ppermute x7, waiting for transfers between devices: 4.29 us -> 3.92 us  [crossed(): lax.ppermute(array, axis, [(i, i ^ bits) for i in range(lax.axis_size(axi...]
  transfers between devices with their start and end apart: 10 -> 10, of which waited for: 5 -> 5; matrix products, arithmetic and copies ran while one was open for 0% -> 0% of each run, Pallas kernels for 20% -> 21%
where the time goes in v6:
time: 28.3 us; the launch traced here: 28 us
  starting transfers between devices  13.1 us (46%)
  Pallas kernels  8.36 us (30%)
  waiting for transfers between devices  5.81 us (21%)
  between operations  0.72 us (3%)
    pallas_call x9, Pallas kernels, call(): pl.pallas_call(kernel, out_shape=out_shape, in_specs=specs or [vmem() for...  8.36 us
    ppermute x7, starting transfers between devices, crossed(): lax.ppermute(array, axis, [(i, i ^ bits) for i in range(lax.axis_size(axi...  8.22 us
    ppermute x1, starting transfers between devices, local(): far_taps = lax.ppermute(far_taps, axes, far_pairs)  4.12 us
    ppermute x7, waiting for transfers between devices, crossed(): lax.ppermute(array, axis, [(i, i ^ bits) for i in range(lax.axis_size(axi...  3.92 us
    ppermute x1, waiting for transfers between devices, local(): far_taps = lax.ppermute(far_taps, axes, far_pairs)  1.88 us
    ppermute x1, starting transfers between devices, local(): lax.ppermute(product, 'ctx', [(i, i + 1) for i in range(1, peers - 1, 2)])  0.68 us
  transfers between devices with their start and end apart: 10, of which 5 were waited for; matrix products, arithmetic and copies ran while one was open for 0% of the time, Pallas kernels for 21%

profile of v6, /device:TPU:0, one launch (start us, length us, event | category | flops | bytes accessed | tf_op | source)
XLA Modules:
  0.0 28.0 jit_solution(11961671750648915619)
XLA Ops:
  0.6 0.0 copy-start
  0.6 1.6 %shard_map.103 = (bf16[784,128]{1,0:T(8,128)(2,1)S(1)}, bf16[784,128]{1,0:T(8,128)(2,1)S(1)}, bf16[784,128]{1,0:T(8,128)(2,1)S(1)}, bf16[784,128]{1,0:T(8,128)(2,1)S(1)}, f32[3,32,1024]{2,1,0:T(8,128)S(1)}) custom-call(bf16[128,1024]{1,0:T(8,128)(2,1)} %queries_ref.1, bf16[256,1024]{1,0:T(8,128)(2,1)} %bitcast.3, s32[1,128]{1,0:T(1,128)} %bitcast.5, ...), custom_call_target="tpu_custom_call" | custom-call | bytes 1572864 | tf_op jit(solution)/shard_map/pallas_call | solution.py:29
  2.3 3.0 %collective-permute-start = (bf16[784,128]{1,0:T(8,128)(2,1)S(1)}, bf16[784,128]{1,0:T(8,128)(2,1)S(1)}, u32[]{:S(2)}, u32[]{:S(2)}) collective-permute-start(bf16[784,128]{1,0:T(8,128)(2,1)S(1)} %get-tuple-element.29), channel_id=1, source_target_pairs={{0,8},{4,12},{8,0},{12,4},{16,24},{20,28},{24,16},{28,20},{1,9},{5... | collective-permute-start | bytes 602120 | tf_op jit(solution)/shard_map/ppermute | solution.py:41
  5.3 1.5 %collective-permute-start.1 = (bf16[784,128]{1,0:T(8,128)(2,1)S(1)}, bf16[784,128]{1,0:T(8,128)(2,1)S(1)}, u32[]{:S(2)}, u32[]{:S(2)}) collective-permute-start(bf16[784,128]{1,0:T(8,128)(2,1)S(1)} %get-tuple-element.30), channel_id=1, source_target_pairs={{0,16},{4,20},{8,24},{12,28},{16,0},{20,4},{24,8},{28,12},{1,17},{... | collective-permute-start | bytes 602120 | tf_op jit(solution)/shard_map/ppermute | solution.py:41
  6.8 0.0 collective-permute-start.2
  6.8 0.0 copy-done
  6.8 0.1 shard_map.104
  6.9 0.1 collective-permute-start.4
  7.0 4.1 %collective-permute-start.3 = (bf16[32,1024]{1,0:T(8,128)(2,1)S(1)}, bf16[32,1024]{1,0:T(8,128)(2,1)S(1)}, u32[]{:S(2)}, u32[]{:S(2)}) collective-permute-start(bf16[32,1024]{1,0:T(8,128)(2,1)S(1)} %get-tuple-element.33), channel_id=1, source_target_pairs={{0,3},{1,2},{2,1},{3,0},{4,6},{5,7},{6,4},{7,5},{8,11},{9,10},{10,... | collective-permute-start | bytes 196616 | tf_op jit(solution)/shard_map/ppermute | solution.py:477
  11.1 1.1 %shard_map.105 = (bf16[256,256]{1,0:T(8,128)(2,1)S(1)}, bf16[256,256]{1,0:T(8,128)(2,1)S(1)}, bf16[128,256]{1,0:T(8,128)(2,1)S(1)}, s32[1,128]{1,0:T(1,128)S(1)}, f32[1,1024]{1,0:T(1,128)S(1)}) custom-call(f32[256,256]{1,0:T(8,128)} %constant.4.clone.ahead_ref, f32[128,256]{1,0:T(8,128)} %constant.5.clone.back_ref, s32[1,128]{1,0:T(1,128)} %bitcast.6, ...), custom_call_target="tpu_custom_call" | custom-call | bytes 524288 | tf_op jit(solution)/shard_map/pallas_call | solution.py:29
  12.2 1.9 %collective-permute-done.3.refs_4_ = bf16[32,1024]{1,0:T(8,128)(2,1)S(1)} collective-permute-done((bf16[32,1024]{1,0:T(8,128)(2,1)S(1)}, bf16[32,1024]{1,0:T(8,128)(2,1)S(1)}, u32[]{:S(2)}, u32[]{:S(2)}) %collective-permute-start.3) | collective-permute-done | bytes 65568 | tf_op jit(solution)/shard_map/ppermute | solution.py:477
  14.1 0.0 collective-permute-done.4.refs_5_.came_ref
  14.1 0.0 collective-permute-done.refs_1_
  14.1 1.9 %collective-permute-done.1.refs_2_ = bf16[784,128]{1,0:T(8,128)(2,1)S(1)} collective-permute-done((bf16[784,128]{1,0:T(8,128)(2,1)S(1)}, bf16[784,128]{1,0:T(8,128)(2,1)S(1)}, u32[]{:S(2)}, u32[]{:S(2)}) %collective-permute-start.1) | collective-permute-done | bytes 200736 | tf_op jit(solution)/shard_map/ppermute | solution.py:41
  16.0 0.0 collective-permute-done.2.refs_3_
  16.0 0.2 shard_map.106
  16.2 0.1 collective-permute-start.5
  16.3 0.7 %collective-permute-start.6 = (bf16[128,1024]{1,0:T(8,128)(2,1)S(1)}, bf16[128,1024]{1,0:T(8,128)(2,1)S(1)}, u32[]{:S(2)}, u32[]{:S(2)}) collective-permute-start(bf16[128,1024]{1,0:T(8,128)(2,1)S(1)} %get-tuple-element.35.refs_6_.product_ref), channel_id=1, source_target_pairs={{4,8},{12,16},{20,24},{5,9},{13,17},{21,25},{6,10},{14,18},{22,26}... | collective-permute-start | bytes 786440 | tf_op jit(solution)/shard_map/ppermute | solution.py:479
  16.9 1.0 %shard_map.108 = (f32[2,2,1,256]{3,2,1,0:T(1,128)S(1)}, f32[2,2,1,256]{3,2,1,0:T(1,128)S(1)}, f32[2,2,128,256]{3,2,1,0:T(8,128)S(1)}) custom-call(bf16[4,144,256]{2,1,0:T(8,128)(2,1)S(1)} %get-tuple-element.43.query_ref.refs_0_, bf16[11,128,256]{2,1,0:T(8,128)(2,1)S(1)} %get-tuple-element.37.mine_ref.key_value_ref), custom_call_target="tpu_custom_call" | custom-call | flops 268435456 | bytes 2097152 | tf_op jit(solution)/shard_map/pallas_call | solution.py:29
  17.9 0.5 %collective-permute-done.5.other_ref.refs_4_ = bf16[11,128,256]{2,1,0:T(8,128)(2,1)S(1)} collective-permute-done((bf16[11,128,256]{2,1,0:T(8,128)(2,1)S(1)}, bf16[11,128,256]{2,1,0:T(8,128)(2,1)S(1)}, u32[]{:S(2)}, u32[]{:S(2)}) %collective-permute-start.5) | collective-permute-done | bytes 720928 | tf_op jit(solution)/shard_map/ppermute | solution.py:41
  18.4 0.8 %shard_map.109 = (bf16[272,128]{1,0:T(8,128)(2,1)S(1)}, bf16[272,128]{1,0:T(8,128)(2,1)S(1)}) custom-call(bf16[4,144,256]{2,1,0:T(8,128)(2,1)S(1)} %get-tuple-element.43.query_ref.refs_0_, f32[2,2,1,256]{3,2,1,0:T(1,128)S(1)} %get-tuple-element.44.refs_1_, f32[2,2,1,256]{3,2,1,0:T(1,128)S(1)} %get-tuple-element.45.refs_2_, ...), custom_call_target="tpu_custom_call" | custom-call | flops 134217728 | bytes 2097152 | tf_op jit(solution)/shard_map/pallas_call | solution.py:29
  19.2 1.5 %collective-permute-start.7 = (bf16[272,128]{1,0:T(8,128)(2,1)S(1)}, bf16[272,128]{1,0:T(8,128)(2,1)S(1)}, u32[]{:S(2)}, u32[]{:S(2)}) collective-permute-start(bf16[272,128]{1,0:T(8,128)(2,1)S(1)} %get-tuple-element.47.refs_5_), channel_id=1, source_target_pairs={{0,16},{4,20},{8,24},{12,28},{16,0},{20,4},{24,8},{28,12},{1,17},{... | collective-permute-start | bytes 208904 | tf_op jit(solution)/shard_map/ppermute | solution.py:41
  20.7 1.4 %collective-permute-start.8 = (bf16[272,128]{1,0:T(8,128)(2,1)S(1)}, bf16[272,128]{1,0:T(8,128)(2,1)S(1)}, u32[]{:S(2)}, u32[]{:S(2)}) collective-permute-start(bf16[272,128]{1,0:T(8,128)(2,1)S(1)} %get-tuple-element.49), channel_id=1, source_target_pairs={{0,24},{4,28},{8,16},{12,20},{16,8},{20,12},{24,0},{28,4},{1,25},{... | collective-permute-start | bytes 208904 | tf_op jit(solution)/shard_map/ppermute | solution.py:41
  22.1 0.6 %shard_map.110 = (bf16[272,128]{1,0:T(8,128)(2,1)S(1)}, bf16[272,128]{1,0:T(8,128)(2,1)S(1)}) custom-call(bf16[4,144,256]{2,1,0:T(8,128)(2,1)S(1)} %get-tuple-element.43.query_ref.refs_0_, f32[2,2,1,256]{3,2,1,0:T(1,128)S(1)} %get-tuple-element.44.refs_1_, f32[2,2,1,256]{3,2,1,0:T(1,128)S(1)} %get-tuple-element.45.refs_2_, ...), custom_call_target="tpu_custom_call" | custom-call | flops 134217728 | bytes 2097152 | tf_op jit(solution)/shard_map/pallas_call | solution.py:29
  22.7 0.7 %collective-permute-start.9 = (bf16[272,128]{1,0:T(8,128)(2,1)S(1)}, bf16[272,128]{1,0:T(8,128)(2,1)S(1)}, u32[]{:S(2)}, u32[]{:S(2)}) collective-permute-start(bf16[272,128]{1,0:T(8,128)(2,1)S(1)} %get-tuple-element.50), channel_id=1, source_target_pairs={{0,8},{4,12},{8,0},{12,4},{16,24},{20,28},{24,16},{28,20},{1,9},{5... | collective-permute-start | bytes 208904 | tf_op jit(solution)/shard_map/ppermute | solution.py:41
  23.4 0.0 collective-permute-done.6.before_ref
  23.4 2.3 %shard_map.107 = bf16[128,1024]{1,0:T(8,128)(2,1)} custom-call(bf16[11,128,256]{2,1,0:T(8,128)(2,1)S(1)} %collective-permute-done.5.other_ref.refs_4_, bf16[11,128,256]{2,1,0:T(8,128)(2,1)S(1)} %get-tuple-element.37.mine_ref.key_value_ref, bf16[128,768]{1,0:T(8,128)(2,1)S(1)} %collective-permute-done.4.refs_5_.came_ref, ...), custom_call_target="tpu_custom_call" | custom-call | flops 536870912 | bytes 2097152 | tf_op jit(solution)/shard_map/pallas_call | solution.py:29
  25.7 1.1 %collective-permute-done.7.refs_1_ = bf16[272,128]{1,0:T(8,128)(2,1)S(1)} collective-permute-done((bf16[272,128]{1,0:T(8,128)(2,1)S(1)}, bf16[272,128]{1,0:T(8,128)(2,1)S(1)}, u32[]{:S(2)}, u32[]{:S(2)}) %collective-permute-start.7) | collective-permute-done | bytes 69664 | tf_op jit(solution)/shard_map/ppermute | solution.py:41
  26.9 0.0 collective-permute-done.8.refs_2_
  26.9 0.3 %collective-permute-done.9.refs_3_ = bf16[272,128]{1,0:T(8,128)(2,1)S(1)} collective-permute-done((bf16[272,128]{1,0:T(8,128)(2,1)S(1)}, bf16[272,128]{1,0:T(8,128)(2,1)S(1)}, u32[]{:S(2)}, u32[]{:S(2)}) %collective-permute-start.9) | collective-permute-done | bytes 69664 | tf_op jit(solution)/shard_map/ppermute | solution.py:41
  27.2 0.8 %shard_map.111 = (bf16[128,1024]{1,0:T(8,128)(2,1)}, f32[8,128]{1,0:T(8,128)}) custom-call(bf16[272,128]{1,0:T(8,128)(2,1)S(1)} %get-tuple-element.48.refs_0_, bf16[272,128]{1,0:T(8,128)(2,1)S(1)} %collective-permute-done.7.refs_1_, bf16[272,128]{1,0:T(8,128)(2,1)S(1)} %collective-permute-done.8.refs_2_, bf16[272,128]{1,0:T(8,128)(2,1)S(1)} %collective-permute-done.9.refs_3_), custom_call_target="tpu_custom_call" | custom-call | bytes 524288 | tf_op jit(solution)/shard_map/pallas_call | solution.py:29
Async XLA Ops:
  0.6 6.2 %copy-start = (bf16[3,128,1024]{2,1,0:T(8,128)(2,1)S(1)}, bf16[3,128,1024]{2,1,0:T(8,128)(2,1)}, u32[]{:S(2)}) copy-start(bf16[3,128,1024]{2,1,0:T(8,128)(2,1)} %gate_ref.1) | copy-start | bytes 2359300
  2.3 11.8 %collective-permute-start = (bf16[784,128]{1,0:T(8,128)(2,1)S(1)}, bf16[784,128]{1,0:T(8,128)(2,1)S(1)}, u32[]{:S(2)}, u32[]{:S(2)}) collective-permute-start(bf16[784,128]{1,0:T(8,128)(2,1)S(1)} %get-tuple-element.29), channel_id=1, source_target_pairs={{0,8},{4,12},{8,0},{12,4},{16,24},{20,28},{24,16},{28,20},{1,9},{5... | collective-permute-start | bytes 602120 | tf_op jit(solution)/shard_map/ppermute | solution.py:41
  5.3 10.8 %collective-permute-start.1 = (bf16[784,128]{1,0:T(8,128)(2,1)S(1)}, bf16[784,128]{1,0:T(8,128)(2,1)S(1)}, u32[]{:S(2)}, u32[]{:S(2)}) collective-permute-start(bf16[784,128]{1,0:T(8,128)(2,1)S(1)} %get-tuple-element.30), channel_id=1, source_target_pairs={{0,16},{4,20},{8,24},{12,28},{16,0},{20,4},{24,8},{28,12},{1,17},{... | collective-permute-start | bytes 602120 | tf_op jit(solution)/shard_map/ppermute | solution.py:41
  6.8 9.2 %collective-permute-start.2 = (bf16[784,128]{1,0:T(8,128)(2,1)S(1)}, bf16[784,128]{1,0:T(8,128)(2,1)S(1)}, u32[]{:S(2)}, u32[]{:S(2)}) collective-permute-start(bf16[784,128]{1,0:T(8,128)(2,1)S(1)} %get-tuple-element.31), channel_id=1, source_target_pairs={{0,24},{4,28},{8,16},{12,20},{16,8},{20,12},{24,0},{28,4},{1,25},{... | collective-permute-start | bytes 602120 | tf_op jit(solution)/shard_map/ppermute | solution.py:41
  6.9 7.1 %collective-permute-start.4 = (bf16[128,768]{1,0:T(8,128)(2,1)S(1)}, bf16[128,768]{1,0:T(8,128)(2,1)S(1)}, u32[]{:S(2)}, u32[]{:S(2)}) collective-permute-start(bf16[128,768]{1,0:T(8,128)(2,1)S(1)} %get-tuple-element.34), channel_id=1, source_target_pairs={{0,4},{1,5},{2,6},{3,7},{4,1},{5,0},{6,3},{7,2},{8,12},{9,13},{10,... | collective-permute-start | bytes 589832 | tf_op jit(solution)/shard_map/ppermute | solution.py:478
  7.0 7.1 %collective-permute-start.3 = (bf16[32,1024]{1,0:T(8,128)(2,1)S(1)}, bf16[32,1024]{1,0:T(8,128)(2,1)S(1)}, u32[]{:S(2)}, u32[]{:S(2)}) collective-permute-start(bf16[32,1024]{1,0:T(8,128)(2,1)S(1)} %get-tuple-element.33), channel_id=1, source_target_pairs={{0,3},{1,2},{2,1},{3,0},{4,6},{5,7},{6,4},{7,5},{8,11},{9,10},{10,... | collective-permute-start | bytes 196616 | tf_op jit(solution)/shard_map/ppermute | solution.py:477
  16.2 2.3 %collective-permute-start.5 = (bf16[11,128,256]{2,1,0:T(8,128)(2,1)S(1)}, bf16[11,128,256]{2,1,0:T(8,128)(2,1)S(1)}, u32[]{:S(2)}, u32[]{:S(2)}) collective-permute-start(bf16[11,128,256]{2,1,0:T(8,128)(2,1)S(1)} %get-tuple-element.37.mine_ref.key_value_ref), channel_id=1, source_target_pairs={{0,4},{4,0},{8,12},{12,8},{16,20},{20,16},{24,28},{28,24},{1,5},{5... | collective-permute-start | bytes 2162696 | tf_op jit(solution)/shard_map/ppermute | solution.py:41
  16.3 7.1 %collective-permute-start.6 = (bf16[128,1024]{1,0:T(8,128)(2,1)S(1)}, bf16[128,1024]{1,0:T(8,128)(2,1)S(1)}, u32[]{:S(2)}, u32[]{:S(2)}) collective-permute-start(bf16[128,1024]{1,0:T(8,128)(2,1)S(1)} %get-tuple-element.35.refs_6_.product_ref), channel_id=1, source_target_pairs={{4,8},{12,16},{20,24},{5,9},{13,17},{21,25},{6,10},{14,18},{22,26}... | collective-permute-start | bytes 786440 | tf_op jit(solution)/shard_map/ppermute | solution.py:479
  19.2 7.6 %collective-permute-start.7 = (bf16[272,128]{1,0:T(8,128)(2,1)S(1)}, bf16[272,128]{1,0:T(8,128)(2,1)S(1)}, u32[]{:S(2)}, u32[]{:S(2)}) collective-permute-start(bf16[272,128]{1,0:T(8,128)(2,1)S(1)} %get-tuple-element.47.refs_5_), channel_id=1, source_target_pairs={{0,16},{4,20},{8,24},{12,28},{16,0},{20,4},{24,8},{28,12},{1,17},{... | collective-permute-start | bytes 208904 | tf_op jit(solution)/shard_map/ppermute | solution.py:41
  20.7 6.1 %collective-permute-start.8 = (bf16[272,128]{1,0:T(8,128)(2,1)S(1)}, bf16[272,128]{1,0:T(8,128)(2,1)S(1)}, u32[]{:S(2)}, u32[]{:S(2)}) collective-permute-start(bf16[272,128]{1,0:T(8,128)(2,1)S(1)} %get-tuple-element.49), channel_id=1, source_target_pairs={{0,24},{4,28},{8,16},{12,20},{16,8},{20,12},{24,0},{28,4},{1,25},{... | collective-permute-start | bytes 208904 | tf_op jit(solution)/shard_map/ppermute | solution.py:41
  22.7 4.5 %collective-permute-start.9 = (bf16[272,128]{1,0:T(8,128)(2,1)S(1)}, bf16[272,128]{1,0:T(8,128)(2,1)S(1)}, u32[]{:S(2)}, u32[]{:S(2)}) collective-permute-start(bf16[272,128]{1,0:T(8,128)(2,1)S(1)} %get-tuple-element.50), channel_id=1, source_target_pairs={{0,8},{4,12},{8,0},{12,4},{16,24},{20,28},{24,16},{28,20},{1,9},{5... | collective-permute-start | bytes 208904 | tf_op jit(solution)/shard_map/ppermute | solution.py:41

commit v7 on v6

--- a/solution.py
+++ b/solution.py
@@ -15,6 +15,7 @@
 NOTE_ROWS = 16
 MASKED = -1e30
 VMEM_LIMIT = 16 * 1024 * 1024
+LONG = 200
 
 
 def vmem():
@@ -94,21 +95,12 @@
     return jnp.concatenate([high, low], axis=1)
 
 
-def pack_hyena(hyena_ref, taps_ref, product_ref, own_ref, far_ref, mixed_ref):
+def pack_hyena(hyena_ref, taps_ref, product_ref, own_ref, far_ref, near_ref):
     product_ref[...] = (hyena_ref[1].astype(jnp.float32) * hyena_ref[2].astype(jnp.float32)).astype(
         jnp.bfloat16
     )
-    own_ref[...] = taps_ref[0].astype(jnp.bfloat16)
-    far_ref[...] = taps_ref[1].astype(jnp.bfloat16)
-    height, width = own_ref.shape
-    whole = mixed_ref.shape[1]
-    mixed_ref[...] = product_ref[:, :whole]
-
-    @pl.when(lax.rem(lax.axis_index("ctx"), 2) == 1)
-    def _():
-        near = taps_ref[2].astype(jnp.bfloat16)
-        mixed_ref[:height] = near[:, :whole]
-        mixed_ref[height : 2 * height, : width - whole] = near[:, whole:]
+    for index, out in enumerate((own_ref, far_ref, near_ref)):
+        out[...] = taps_ref[index].astype(jnp.bfloat16)
 
 
 def prepare(
@@ -136,15 +128,9 @@
     return ref[rows, index * 2 * HD : (index + 1) * 2 * HD]
 
 
-def near_strip(came_ref, height, part):
-    parts = came_ref.shape[1] // (2 * HD)
-    line = part // parts
-    return columns_of(came_ref, slice(line * height, (line + 1) * height), part % parts)
-
-
 def sort_heads(heads, *refs):
     count = heads // 2
-    far_ref, came_ref, product_ref = refs[count : count + 3]
+    near_ref, far_ref = refs[count : count + 2]
     query_ref, side_ref = refs[-2:]
     rows = (refs[0].shape[0] - NOTE_ROWS) // 6
     _, pair, _ = place(heads)
@@ -163,8 +149,7 @@
     for part in range(parts):
         line = slice(part * height, (part + 1) * height)
         side_ref[heads, line] = columns_of(far_ref, slice(None), part)
-        side_ref[heads + 1, line] = near_strip(came_ref, height, part)
-    side_ref[heads + 2] = columns_of(product_ref, slice(None), parts - 1)
+        side_ref[heads + 1, line] = columns_of(near_ref, slice(None), part)
 
 
 UNIT = 2
@@ -359,8 +344,8 @@
 
 
 def convolve(
-    heads, other_ref, mine_ref, came_ref, before_ref, own_taps_ref, starts_ref, product_ref, gate_ref, skip_ref,
-    early_ref, late_ref, back_ref, out_ref, taps_ref, halo_ref, filter_ref, sum_ref,
+    heads, other_ref, mine_ref, before_ref, own_taps_ref, starts_ref, product_ref, gate_ref, skip_ref,
+    early_ref, late_ref, back_ref, out_ref, taps_ref, filter_ref, sum_ref,
 ):
     rows = product_ref.shape[0]
     height, width = own_taps_ref.shape
@@ -377,21 +362,16 @@
         line = slice(part * height, (part + 1) * height)
         mine_far, other_far = mine_ref[heads, line], other_ref[heads, line]
         store(0, part, columns_of(own_taps_ref, everything, part))
-        store(1, part, jnp.where(even, near_strip(came_ref, height, part), other_ref[heads + 1, line]))
+        store(1, part, jnp.where(even, other_ref[heads + 1, line], mine_ref[heads + 1, line]))
         store(2, part, jnp.where(even, other_far, mine_far))
         store(3, part, jnp.where(even, mine_far, other_far))
-        halo_ref[:, part * 2 * HD : (part + 1) * 2 * HD] = jnp.where(
-            even,
-            columns_of(before_ref, everything, part),
-            other_ref[heads + 2] if part == parts - 1 else columns_of(came_ref, everything, part),
-        )
     filter_ref[...] = dot(early_ref[...], twice(taps_ref[...]))
     starts = document_starts(starts_ref, rows)
     line = lax.broadcasted_iota(jnp.int32, (rows, 1), 0)
     zero = jnp.zeros((), jnp.bfloat16)
 
     begin = jnp.min(starts)
-    past = jnp.where(line - rows >= begin, halo_ref[...], zero)
+    past = jnp.where(line - rows >= begin, before_ref[...], zero)
     here = jnp.where(line >= begin, product_ref[...], zero)
     spectrum = dot(early_ref[...], twice(past)) + dot(late_ref[...], twice(here))
     sum_ref[...] = filtered(spectrum, filter_ref, back_ref)
@@ -419,18 +399,16 @@
     return jnp.asarray(ahead, jnp.float32), jnp.asarray(back, jnp.float32)
 
 
-def side_pairs(peers, panels):
+def taps_pairs(peers, panels):
     assert panels == 4
-    far, mixed = [], []
+    near, far = [], []
     for peer in range(peers):
         for panel in range(panels):
             here = peer * panels + panel
             far.append((here, peer * panels + (panel ^ (3 - peer % 2))))
-            if peer % 2 == 0:
-                mixed.append((here, here + panels))
-            else:
-                mixed.append((here, (peer - 1) * panels + (panel ^ 1)))
-    return far, mixed
+            if peer % 2 == 1:
+                near.append((here, peer * panels + (panel ^ 1)))
+    return near, far
 
 
 def local(hyena_inputs, filters, skip_bias, queries, keys_values, doc_start):
@@ -463,20 +441,18 @@
         specs=[hbm()] * 4,
     )
     arrived = [packed[0]] + [crossed(packed[step], "ctx", 2 * step) for step in range(1, count)]
-    product, own_taps, far_taps, mixed_rows = call(
+    product, own_taps, far_taps, near_taps = call(
         pack_hyena,
-        (shape((rows, channels), bf16),)
-        + (shape((height, channels), bf16),) * 2
-        + (shape((rows, channels - 2 * HD), bf16),),
+        (shape((rows, channels), bf16),) + (shape((height, channels), bf16),) * 3,
         (hyena_inputs, wide_taps),
         0,
         4 * queries.size * 3,
     )
     axes = ("ctx", "tp")
-    far_pairs, mixed_pairs = side_pairs(peers, lax.axis_size("tp"))
+    near_pairs, far_pairs = taps_pairs(peers, lax.axis_size("tp"))
+    near_taps = lax.ppermute(near_taps, axes, near_pairs)
     far_taps = lax.ppermute(far_taps, axes, far_pairs)
-    came = lax.ppermute(mixed_rows, axes, mixed_pairs)
-    before = lax.ppermute(product, "ctx", [(i, i + 1) for i in range(1, peers - 1, 2)])
+    before = lax.ppermute(product, "ctx", [(i, i + 1) for i in range(peers - 1)])
     ahead, back = twiddles(rows)
     early, late, back, near_starts, skip = call(
         prepare,
@@ -497,9 +473,9 @@
         functools.partial(sort_heads, heads),
         (
             shape((count, rows + NOTE_ROWS, 2 * HD), bf16),
-            shape((heads + 3, rows, 2 * HD), bf16),
+            shape((heads + 2, rows, 2 * HD), bf16),
         ),
-        (*arrived, far_taps, came, product, skip),
+        (*arrived, near_taps, far_taps, skip),
         0,
         4 * queries.size * 3,
     )
@@ -513,7 +489,7 @@
             shape((2, units, HD, UNIT * rows), f32),
         ),
         (query, key_value),
-        2 * (heads * rows) ** 2 * HD,
+        LONG * (heads * rows) ** 2 * HD,
         4 * queries.size * 4,
     )
     operands = [query, *partial, other]
@@ -541,14 +517,13 @@
         functools.partial(convolve, heads),
         shape((rows, channels), bf16),
         (
-            other, key_value, came, before, own_taps, near_starts, product, hyena_inputs,
+            other, key_value, before, own_taps, near_starts, product, hyena_inputs,
             skip, early, late, back,
         ),
         2 * 4 * 256 * 256 * channels,
         4 * queries.size * 4,
         scratch=(
             pltpu.VMEM((FLEN, channels), bf16),
-            pltpu.VMEM((rows, channels), bf16),
             pltpu.VMEM((2 * rows, channels), f32),
             pltpu.VMEM((rows, channels), f32),
         ),

time: 28.3 us -> 28.5 us (level)
  the two profiles are of different devices: /device:TPU:0 before, /device:TPU:24 now
where the time goes in v7:
time: 28.5 us; the launch traced here: 28.3 us
  starting transfers between devices  14.5 us (51%)
  Pallas kernels  8.27 us (29%)
  waiting for transfers between devices  4.78 us (17%)
  between operations  0.73 us (3%)
    ppermute x7, starting transfers between devices, crossed(): lax.ppermute(array, axis, [(i, i ^ bits) for i in range(lax.axis_size(axi...  9.43 us
    pallas_call x9, Pallas kernels, call(): pl.pallas_call(kernel, out_shape=out_shape, in_specs=specs or [vmem() for...  8.27 us
    ppermute x1, starting transfers between devices, local(): lax.ppermute(product, 'ctx', [(i, i + 1) for i in range(peers - 1)])  4.38 us
    ppermute x7, waiting for transfers between devices, crossed(): lax.ppermute(array, axis, [(i, i ^ bits) for i in range(lax.axis_size(axi...  3.94 us
    ppermute x1, waiting for transfers between devices, local(): far_taps = lax.ppermute(far_taps, axes, far_pairs)  0.84 us
    ppermute x1, starting transfers between devices, local(): near_taps = lax.ppermute(near_taps, axes, near_pairs)  0.66 us
  transfers between devices with their start and end apart: 10, of which 4 were waited for; matrix products, arithmetic and copies ran while one was open for 0% of the time, Pallas kernels for 21%

profile of v7, /device:TPU:24, one launch (start us, length us, event | category | flops | bytes accessed | tf_op | source)
XLA Modules:
  0.0 28.3 jit_solution(328798250794155836)
XLA Ops:
  0.6 0.0 copy-start
  0.6 1.6 %shard_map.103 = (bf16[784,128]{1,0:T(8,128)(2,1)S(1)}, bf16[784,128]{1,0:T(8,128)(2,1)S(1)}, bf16[784,128]{1,0:T(8,128)(2,1)S(1)}, bf16[784,128]{1,0:T(8,128)(2,1)S(1)}, f32[3,32,1024]{2,1,0:T(8,128)S(1)}) custom-call(bf16[128,1024]{1,0:T(8,128)(2,1)} %queries_ref.1, bf16[256,1024]{1,0:T(8,128)(2,1)} %bitcast.3, s32[1,128]{1,0:T(1,128)} %bitcast.5, ...), custom_call_target="tpu_custom_call" | custom-call | bytes 1572864 | tf_op jit(solution)/shard_map/pallas_call | solution.py:30
  2.3 1.6 %collective-permute-start = (bf16[784,128]{1,0:T(8,128)(2,1)S(1)}, bf16[784,128]{1,0:T(8,128)(2,1)S(1)}, u32[]{:S(2)}, u32[]{:S(2)}) collective-permute-start(bf16[784,128]{1,0:T(8,128)(2,1)S(1)} %get-tuple-element.29), channel_id=1, source_target_pairs={{0,8},{4,12},{8,0},{12,4},{16,24},{20,28},{24,16},{28,20},{1,9},{5... | collective-permute-start | bytes 602120 | tf_op jit(solution)/shard_map/ppermute | solution.py:42
  3.8 1.5 %collective-permute-start.1 = (bf16[784,128]{1,0:T(8,128)(2,1)S(1)}, bf16[784,128]{1,0:T(8,128)(2,1)S(1)}, u32[]{:S(2)}, u32[]{:S(2)}) collective-permute-start(bf16[784,128]{1,0:T(8,128)(2,1)S(1)} %get-tuple-element.30), channel_id=1, source_target_pairs={{0,16},{4,20},{8,24},{12,28},{16,0},{20,4},{24,8},{28,12},{1,17},{... | collective-permute-start | bytes 602120 | tf_op jit(solution)/shard_map/ppermute | solution.py:42
  5.3 0.5 %collective-permute-start.2 = (bf16[784,128]{1,0:T(8,128)(2,1)S(1)}, bf16[784,128]{1,0:T(8,128)(2,1)S(1)}, u32[]{:S(2)}, u32[]{:S(2)}) collective-permute-start(bf16[784,128]{1,0:T(8,128)(2,1)S(1)} %get-tuple-element.31), channel_id=1, source_target_pairs={{0,24},{4,28},{8,16},{12,20},{16,8},{20,12},{24,0},{28,4},{1,25},{... | collective-permute-start | bytes 602120 | tf_op jit(solution)/shard_map/ppermute | solution.py:42
  5.8 0.0 copy-done
  5.8 0.1 shard_map.104
  5.9 0.7 %collective-permute-start.3 = (bf16[32,1024]{1,0:T(8,128)(2,1)S(1)}, bf16[32,1024]{1,0:T(8,128)(2,1)S(1)}, u32[]{:S(2)}, u32[]{:S(2)}) collective-permute-start(bf16[32,1024]{1,0:T(8,128)(2,1)S(1)} %get-tuple-element.33), channel_id=1, source_target_pairs={{4,5},{5,4},{6,7},{7,6},{12,13},{13,12},{14,15},{15,14},{20,21},{2... | collective-permute-start | bytes 196616 | tf_op jit(solution)/shard_map/ppermute | solution.py:453
  6.6 0.1 collective-permute-start.4
  6.6 1.1 %shard_map.105 = (bf16[256,256]{1,0:T(8,128)(2,1)S(1)}, bf16[256,256]{1,0:T(8,128)(2,1)S(1)}, bf16[128,256]{1,0:T(8,128)(2,1)S(1)}, s32[1,128]{1,0:T(1,128)S(1)}, f32[1,1024]{1,0:T(1,128)S(1)}) custom-call(f32[256,256]{1,0:T(8,128)} %constant.4.clone.ahead_ref, f32[128,256]{1,0:T(8,128)} %constant.5.clone.back_ref, s32[1,128]{1,0:T(1,128)} %bitcast.6, ...), custom_call_target="tpu_custom_call" | custom-call | bytes 524288 | tf_op jit(solution)/shard_map/pallas_call | solution.py:30
  7.7 0.0 collective-permute-done.3.refs_4_
  7.7 4.4 %collective-permute-start.6 = (bf16[128,1024]{1,0:T(8,128)(2,1)S(1)}, bf16[128,1024]{1,0:T(8,128)(2,1)S(1)}, u32[]{:S(2)}, u32[]{:S(2)}) collective-permute-start(bf16[128,1024]{1,0:T(8,128)(2,1)S(1)} %get-tuple-element.37.product_ref), channel_id=1, source_target_pairs={{0,4},{4,8},{8,12},{12,16},{16,20},{20,24},{24,28},{1,5},{5,9},{9,... | collective-permute-start | bytes 786440 | tf_op jit(solution)/shard_map/ppermute | solution.py:455
  12.1 0.8 %collective-permute-done.4.refs_5_ = bf16[32,1024]{1,0:T(8,128)(2,1)S(1)} collective-permute-done((bf16[32,1024]{1,0:T(8,128)(2,1)S(1)}, bf16[32,1024]{1,0:T(8,128)(2,1)S(1)}, u32[]{:S(2)}, u32[]{:S(2)}) %collective-permute-start.4) | collective-permute-done | bytes 65568 | tf_op jit(solution)/shard_map/ppermute | solution.py:454
  13.0 0.0 collective-permute-done.refs_1_
  13.0 1.6 %collective-permute-done.1.refs_2_ = bf16[784,128]{1,0:T(8,128)(2,1)S(1)} collective-permute-done((bf16[784,128]{1,0:T(8,128)(2,1)S(1)}, bf16[784,128]{1,0:T(8,128)(2,1)S(1)}, u32[]{:S(2)}, u32[]{:S(2)}) %collective-permute-start.1) | collective-permute-done | bytes 200736 | tf_op jit(solution)/shard_map/ppermute | solution.py:42
  14.6 0.0 collective-permute-done.2.refs_3_
  14.6 0.2 shard_map.106
  14.7 0.1 collective-permute-start.5
  14.8 1.0 %shard_map.108 = (f32[2,2,1,256]{3,2,1,0:T(1,128)S(1)}, f32[2,2,1,256]{3,2,1,0:T(1,128)S(1)}, f32[2,2,128,256]{3,2,1,0:T(8,128)S(1)}) custom-call(bf16[4,144,256]{2,1,0:T(8,128)(2,1)S(1)} %get-tuple-element.43.query_ref.refs_0_, bf16[10,128,256]{2,1,0:T(8,128)(2,1)S(1)} %get-tuple-element.36.mine_ref.key_value_ref), custom_call_target="tpu_custom_call" | custom-call | flops 26843545600 | bytes 2097152 | tf_op jit(solution)/shard_map/pallas_call | solution.py:30
  15.8 1.1 %collective-permute-done.5.other_ref.refs_4_ = bf16[10,128,256]{2,1,0:T(8,128)(2,1)S(1)} collective-permute-done((bf16[10,128,256]{2,1,0:T(8,128)(2,1)S(1)}, bf16[10,128,256]{2,1,0:T(8,128)(2,1)S(1)}, u32[]{:S(2)}, u32[]{:S(2)}) %collective-permute-start.5) | collective-permute-done | bytes 655392 | tf_op jit(solution)/shard_map/ppermute | solution.py:42
  16.9 0.8 %shard_map.109 = (bf16[272,128]{1,0:T(8,128)(2,1)S(1)}, bf16[272,128]{1,0:T(8,128)(2,1)S(1)}) custom-call(bf16[4,144,256]{2,1,0:T(8,128)(2,1)S(1)} %get-tuple-element.43.query_ref.refs_0_, f32[2,2,1,256]{3,2,1,0:T(1,128)S(1)} %get-tuple-element.44.refs_1_, f32[2,2,1,256]{3,2,1,0:T(1,128)S(1)} %get-tuple-element.45.refs_2_, ...), custom_call_target="tpu_custom_call" | custom-call | flops 134217728 | bytes 2097152 | tf_op jit(solution)/shard_map/pallas_call | solution.py:30
  17.7 4.2 %collective-permute-start.7 = (bf16[272,128]{1,0:T(8,128)(2,1)S(1)}, bf16[272,128]{1,0:T(8,128)(2,1)S(1)}, u32[]{:S(2)}, u32[]{:S(2)}) collective-permute-start(bf16[272,128]{1,0:T(8,128)(2,1)S(1)} %get-tuple-element.47.refs_5_), channel_id=1, source_target_pairs={{0,16},{4,20},{8,24},{12,28},{16,0},{20,4},{24,8},{28,12},{1,17},{... | collective-permute-start | bytes 208904 | tf_op jit(solution)/shard_map/ppermute | solution.py:42
  21.9 0.0 collective-permute-start.8
  21.9 0.6 %shard_map.110 = (bf16[272,128]{1,0:T(8,128)(2,1)S(1)}, bf16[272,128]{1,0:T(8,128)(2,1)S(1)}) custom-call(bf16[4,144,256]{2,1,0:T(8,128)(2,1)S(1)} %get-tuple-element.43.query_ref.refs_0_, f32[2,2,1,256]{3,2,1,0:T(1,128)S(1)} %get-tuple-element.44.refs_1_, f32[2,2,1,256]{3,2,1,0:T(1,128)S(1)} %get-tuple-element.45.refs_2_, ...), custom_call_target="tpu_custom_call" | custom-call | flops 134217728 | bytes 2097152 | tf_op jit(solution)/shard_map/pallas_call | solution.py:30
  22.5 1.6 %collective-permute-start.9 = (bf16[272,128]{1,0:T(8,128)(2,1)S(1)}, bf16[272,128]{1,0:T(8,128)(2,1)S(1)}, u32[]{:S(2)}, u32[]{:S(2)}) collective-permute-start(bf16[272,128]{1,0:T(8,128)(2,1)S(1)} %get-tuple-element.50), channel_id=1, source_target_pairs={{0,8},{4,12},{8,0},{12,4},{16,24},{20,28},{24,16},{28,20},{1,9},{5... | collective-permute-start | bytes 208904 | tf_op jit(solution)/shard_map/ppermute | solution.py:42
  24.1 0.0 collective-permute-done.6.before_ref
  24.1 2.3 %shard_map.107 = bf16[128,1024]{1,0:T(8,128)(2,1)} custom-call(bf16[10,128,256]{2,1,0:T(8,128)(2,1)S(1)} %collective-permute-done.5.other_ref.refs_4_, bf16[10,128,256]{2,1,0:T(8,128)(2,1)S(1)} %get-tuple-element.36.mine_ref.key_value_ref, bf16[128,1024]{1,0:T(8,128)(2,1)S(1)} %collective-permute-done.6.before_ref, ...), custom_call_target="tpu_custom_call" | custom-call | flops 536870912 | bytes 2097152 | tf_op jit(solution)/shard_map/pallas_call | solution.py:30
  26.3 0.0 collective-permute-done.7.refs_1_
  26.3 1.2 %collective-permute-done.8.refs_2_ = bf16[272,128]{1,0:T(8,128)(2,1)S(1)} collective-permute-done((bf16[272,128]{1,0:T(8,128)(2,1)S(1)}, bf16[272,128]{1,0:T(8,128)(2,1)S(1)}, u32[]{:S(2)}, u32[]{:S(2)}) %collective-permute-start.8) | collective-permute-done | bytes 69664 | tf_op jit(solution)/shard_map/ppermute | solution.py:42
  27.5 0.0 collective-permute-done.9.refs_3_
  27.5 0.8 %shard_map.111 = (bf16[128,1024]{1,0:T(8,128)(2,1)}, f32[8,128]{1,0:T(8,128)}) custom-call(bf16[272,128]{1,0:T(8,128)(2,1)S(1)} %get-tuple-element.48.refs_0_, bf16[272,128]{1,0:T(8,128)(2,1)S(1)} %collective-permute-done.7.refs_1_, bf16[272,128]{1,0:T(8,128)(2,1)S(1)} %collective-permute-done.8.refs_2_, bf16[272,128]{1,0:T(8,128)(2,1)S(1)} %collective-permute-done.9.refs_3_), custom_call_target="tpu_custom_call" | custom-call | bytes 524288 | tf_op jit(solution)/shard_map/pallas_call | solution.py:30
Async XLA Ops:
  0.6 5.2 %copy-start = (bf16[3,128,1024]{2,1,0:T(8,128)(2,1)S(1)}, bf16[3,128,1024]{2,1,0:T(8,128)(2,1)}, u32[]{:S(2)}) copy-start(bf16[3,128,1024]{2,1,0:T(8,128)(2,1)} %gate_ref.1) | copy-start | bytes 2359300
  2.3 10.7 %collective-permute-start = (bf16[784,128]{1,0:T(8,128)(2,1)S(1)}, bf16[784,128]{1,0:T(8,128)(2,1)S(1)}, u32[]{:S(2)}, u32[]{:S(2)}) collective-permute-start(bf16[784,128]{1,0:T(8,128)(2,1)S(1)} %get-tuple-element.29), channel_id=1, source_target_pairs={{0,8},{4,12},{8,0},{12,4},{16,24},{20,28},{24,16},{28,20},{1,9},{5... | collective-permute-start | bytes 602120 | tf_op jit(solution)/shard_map/ppermute | solution.py:42
  3.8 10.8 %collective-permute-start.1 = (bf16[784,128]{1,0:T(8,128)(2,1)S(1)}, bf16[784,128]{1,0:T(8,128)(2,1)S(1)}, u32[]{:S(2)}, u32[]{:S(2)}) collective-permute-start(bf16[784,128]{1,0:T(8,128)(2,1)S(1)} %get-tuple-element.30), channel_id=1, source_target_pairs={{0,16},{4,20},{8,24},{12,28},{16,0},{20,4},{24,8},{28,12},{1,17},{... | collective-permute-start | bytes 602120 | tf_op jit(solution)/shard_map/ppermute | solution.py:42
  5.3 9.2 %collective-permute-start.2 = (bf16[784,128]{1,0:T(8,128)(2,1)S(1)}, bf16[784,128]{1,0:T(8,128)(2,1)S(1)}, u32[]{:S(2)}, u32[]{:S(2)}) collective-permute-start(bf16[784,128]{1,0:T(8,128)(2,1)S(1)} %get-tuple-element.31), channel_id=1, source_target_pairs={{0,24},{4,28},{8,16},{12,20},{16,8},{20,12},{24,0},{28,4},{1,25},{... | collective-permute-start | bytes 602120 | tf_op jit(solution)/shard_map/ppermute | solution.py:42
  5.9 1.8 %collective-permute-start.3 = (bf16[32,1024]{1,0:T(8,128)(2,1)S(1)}, bf16[32,1024]{1,0:T(8,128)(2,1)S(1)}, u32[]{:S(2)}, u32[]{:S(2)}) collective-permute-start(bf16[32,1024]{1,0:T(8,128)(2,1)S(1)} %get-tuple-element.33), channel_id=1, source_target_pairs={{4,5},{5,4},{6,7},{7,6},{12,13},{13,12},{14,15},{15,14},{20,21},{2... | collective-permute-start | bytes 196616 | tf_op jit(solution)/shard_map/ppermute | solution.py:453
  6.6 6.4 %collective-permute-start.4 = (bf16[32,1024]{1,0:T(8,128)(2,1)S(1)}, bf16[32,1024]{1,0:T(8,128)(2,1)S(1)}, u32[]{:S(2)}, u32[]{:S(2)}) collective-permute-start(bf16[32,1024]{1,0:T(8,128)(2,1)S(1)} %get-tuple-element.34), channel_id=1, source_target_pairs={{0,3},{1,2},{2,1},{3,0},{4,6},{5,7},{6,4},{7,5},{8,11},{9,10},{10,... | collective-permute-start | bytes 196616 | tf_op jit(solution)/shard_map/ppermute | solution.py:454
  7.7 16.3 %collective-permute-start.6 = (bf16[128,1024]{1,0:T(8,128)(2,1)S(1)}, bf16[128,1024]{1,0:T(8,128)(2,1)S(1)}, u32[]{:S(2)}, u32[]{:S(2)}) collective-permute-start(bf16[128,1024]{1,0:T(8,128)(2,1)S(1)} %get-tuple-element.37.product_ref), channel_id=1, source_target_pairs={{0,4},{4,8},{8,12},{12,16},{16,20},{20,24},{24,28},{1,5},{5,9},{9,... | collective-permute-start | bytes 786440 | tf_op jit(solution)/shard_map/ppermute | solution.py:455
  14.7 2.2 %collective-permute-start.5 = (bf16[10,128,256]{2,1,0:T(8,128)(2,1)S(1)}, bf16[10,128,256]{2,1,0:T(8,128)(2,1)S(1)}, u32[]{:S(2)}, u32[]{:S(2)}) collective-permute-start(bf16[10,128,256]{2,1,0:T(8,128)(2,1)S(1)} %get-tuple-element.36.mine_ref.key_value_ref), channel_id=1, source_target_pairs={{0,4},{4,0},{8,12},{12,8},{16,20},{20,16},{24,28},{28,24},{1,5},{5... | collective-permute-start | bytes 1966088 | tf_op jit(solution)/shard_map/ppermute | solution.py:42
  17.7 8.7 %collective-permute-start.7 = (bf16[272,128]{1,0:T(8,128)(2,1)S(1)}, bf16[272,128]{1,0:T(8,128)(2,1)S(1)}, u32[]{:S(2)}, u32[]{:S(2)}) collective-permute-start(bf16[272,128]{1,0:T(8,128)(2,1)S(1)} %get-tuple-element.47.refs_5_), channel_id=1, source_target_pairs={{0,16},{4,20},{8,24},{12,28},{16,0},{20,4},{24,8},{28,12},{1,17},{... | collective-permute-start | bytes 208904 | tf_op jit(solution)/shard_map/ppermute | solution.py:42
  21.9 5.7 %collective-permute-start.8 = (bf16[272,128]{1,0:T(8,128)(2,1)S(1)}, bf16[272,128]{1,0:T(8,128)(2,1)S(1)}, u32[]{:S(2)}, u32[]{:S(2)}) collective-permute-start(bf16[272,128]{1,0:T(8,128)(2,1)S(1)} %get-tuple-element.49), channel_id=1, source_target_pairs={{0,24},{4,28},{8,16},{12,20},{16,8},{20,12},{24,0},{28,4},{1,25},{... | collective-permute-start | bytes 208904 | tf_op jit(solution)/shard_map/ppermute | solution.py:42
  22.5 5.1 %collective-permute-start.9 = (bf16[272,128]{1,0:T(8,128)(2,1)S(1)}, bf16[272,128]{1,0:T(8,128)(2,1)S(1)}, u32[]{:S(2)}, u32[]{:S(2)}) collective-permute-start(bf16[272,128]{1,0:T(8,128)(2,1)S(1)} %get-tuple-element.50), channel_id=1, source_target_pairs={{0,8},{4,12},{8,0},{12,4},{16,24},{20,28},{24,16},{28,20},{1,9},{5... | collective-permute-start | bytes 208904 | tf_op jit(solution)/shard_map/ppermute | solution.py:42

commit v8 on v7

--- a/solution.py
+++ b/solution.py
@@ -42,6 +42,9 @@
     return lax.ppermute(array, axis, [(i, i ^ bits) for i in range(lax.axis_size(axis))])
 
 
+STEPS = (0, 2, 1, 3)
+
+
 def place(heads):
     index = lax.axis_index("ctx")
     member = lax.rem(index, heads)
@@ -55,7 +58,7 @@
     first = pltpu.make_async_copy(starts_ref, held_ref, start_sem)
     first.start()
     copies = []
-    for step, out in enumerate(outs):
+    for step, out in zip(STEPS, outs):
         for head in range(2):
             columns = pl.ds(pl.multiple_of(((pair ^ step) * 2 + head) * HD, HD), HD)
             first_row = head * 3 * rows
@@ -134,16 +137,16 @@
     query_ref, side_ref = refs[-2:]
     rows = (refs[0].shape[0] - NOTE_ROWS) // 6
     _, pair, _ = place(heads)
-    for step in range(count):
+    for step, ref in zip(STEPS, refs):
         source = pair ^ step
-        query_ref[source, rows:, :HD] = refs[step][6 * rows :]
+        query_ref[source, rows:, :HD] = ref[6 * rows :]
         for head in range(2):
             columns = slice(head * HD, (head + 1) * HD)
             first = head * 3 * rows
-            query_ref[source, :rows, columns] = refs[step][first : first + rows]
+            query_ref[source, :rows, columns] = ref[first : first + rows]
             for part in range(2):
                 line = first + (part + 1) * rows
-                side_ref[2 * source + part, :, columns] = refs[step][line : line + rows]
+                side_ref[2 * source + part, :, columns] = ref[line : line + rows]
     height, width = far_ref.shape
     parts = width // (2 * HD)
     for part in range(parts):
@@ -440,7 +443,8 @@
         ),
         specs=[hbm()] * 4,
     )
-    arrived = [packed[0]] + [crossed(packed[step], "ctx", 2 * step) for step in range(1, count)]
+    assert count == len(STEPS)
+    arrived = [packed[0]] + [crossed(packed[i], "ctx", 2 * STEPS[i]) for i in range(1, count)]
     product, own_taps, far_taps, near_taps = call(
         pack_hyena,
         (shape((rows, channels), bf16),) + (shape((height, channels), bf16),) * 3,

time: 28.5 us -> 28 us (0.982)
  the two profiles are of different devices: /device:TPU:24 before, /device:TPU:0 now
where the time goes in v8:
time: 28 us; the launch traced here: 27.8 us
  starting transfers between devices  15.7 us (56%)
  Pallas kernels  8.26 us (30%)
  waiting for transfers between devices  3.16 us (11%)
  between operations  0.74 us (3%)
    ppermute x7, starting transfers between devices, crossed(): lax.ppermute(array, axis, [(i, i ^ bits) for i in range(lax.axis_size(axi...  8.76 us
    pallas_call x9, Pallas kernels, call(): pl.pallas_call(kernel, out_shape=out_shape, in_specs=specs or [vmem() for...  8.26 us
    ppermute x1, starting transfers between devices, local(): far_taps = lax.ppermute(far_taps, axes, far_pairs)  4.09 us
    ppermute x7, waiting for transfers between devices, crossed(): lax.ppermute(array, axis, [(i, i ^ bits) for i in range(lax.axis_size(axi...  3.15 us
    ppermute x1, starting transfers between devices, local(): lax.ppermute(product, 'ctx', [(i, i + 1) for i in range(peers - 1)])  2.16 us
    ppermute x1, starting transfers between devices, local(): near_taps = lax.ppermute(near_taps, axes, near_pairs)  0.66 us
  transfers between devices with their start and end apart: 10, of which 4 were waited for; matrix products, arithmetic and copies ran while one was open for 0% of the time, Pallas kernels for 21%

profile of v8, /device:TPU:0, one launch (start us, length us, event | category | flops | bytes accessed | tf_op | source)
XLA Modules:
  0.0 27.8 jit_solution(14485244038374827565)
XLA Ops:
  0.6 0.0 copy-start
  0.6 1.6 %shard_map.103 = (bf16[784,128]{1,0:T(8,128)(2,1)S(1)}, bf16[784,128]{1,0:T(8,128)(2,1)S(1)}, bf16[784,128]{1,0:T(8,128)(2,1)S(1)}, bf16[784,128]{1,0:T(8,128)(2,1)S(1)}, f32[3,32,1024]{2,1,0:T(8,128)S(1)}) custom-call(bf16[128,1024]{1,0:T(8,128)(2,1)} %queries_ref.1, bf16[256,1024]{1,0:T(8,128)(2,1)} %bitcast.3, s32[1,128]{1,0:T(1,128)} %bitcast.5, ...), custom_call_target="tpu_custom_call" | custom-call | bytes 1572864 | tf_op jit(solution)/shard_map/pallas_call | solution.py:30
  2.3 3.0 %collective-permute-start = (bf16[784,128]{1,0:T(8,128)(2,1)S(1)}, bf16[784,128]{1,0:T(8,128)(2,1)S(1)}, u32[]{:S(2)}, u32[]{:S(2)}) collective-permute-start(bf16[784,128]{1,0:T(8,128)(2,1)S(1)} %get-tuple-element.29), channel_id=1, source_target_pairs={{0,16},{4,20},{8,24},{12,28},{16,0},{20,4},{24,8},{28,12},{1,17},{... | collective-permute-start | bytes 602120 | tf_op jit(solution)/shard_map/ppermute | solution.py:42
  5.3 1.5 %collective-permute-start.1 = (bf16[784,128]{1,0:T(8,128)(2,1)S(1)}, bf16[784,128]{1,0:T(8,128)(2,1)S(1)}, u32[]{:S(2)}, u32[]{:S(2)}) collective-permute-start(bf16[784,128]{1,0:T(8,128)(2,1)S(1)} %get-tuple-element.30), channel_id=1, source_target_pairs={{0,8},{4,12},{8,0},{12,4},{16,24},{20,28},{24,16},{28,20},{1,9},{5... | collective-permute-start | bytes 602120 | tf_op jit(solution)/shard_map/ppermute | solution.py:42
  6.8 0.0 collective-permute-start.2
  6.8 0.0 copy-done
  6.8 0.1 shard_map.104
  6.9 0.7 %collective-permute-start.3 = (bf16[32,1024]{1,0:T(8,128)(2,1)S(1)}, bf16[32,1024]{1,0:T(8,128)(2,1)S(1)}, u32[]{:S(2)}, u32[]{:S(2)}) collective-permute-start(bf16[32,1024]{1,0:T(8,128)(2,1)S(1)} %get-tuple-element.33), channel_id=1, source_target_pairs={{4,5},{5,4},{6,7},{7,6},{12,13},{13,12},{14,15},{15,14},{20,21},{2... | collective-permute-start | bytes 196616 | tf_op jit(solution)/shard_map/ppermute | solution.py:457
  7.6 4.1 %collective-permute-start.4 = (bf16[32,1024]{1,0:T(8,128)(2,1)S(1)}, bf16[32,1024]{1,0:T(8,128)(2,1)S(1)}, u32[]{:S(2)}, u32[]{:S(2)}) collective-permute-start(bf16[32,1024]{1,0:T(8,128)(2,1)S(1)} %get-tuple-element.34), channel_id=1, source_target_pairs={{0,3},{1,2},{2,1},{3,0},{4,6},{5,7},{6,4},{7,5},{8,11},{9,10},{10,... | collective-permute-start | bytes 196616 | tf_op jit(solution)/shard_map/ppermute | solution.py:458
  11.7 1.1 %shard_map.105 = (bf16[256,256]{1,0:T(8,128)(2,1)S(1)}, bf16[256,256]{1,0:T(8,128)(2,1)S(1)}, bf16[128,256]{1,0:T(8,128)(2,1)S(1)}, s32[1,128]{1,0:T(1,128)S(1)}, f32[1,1024]{1,0:T(1,128)S(1)}) custom-call(f32[256,256]{1,0:T(8,128)} %constant.4.clone.ahead_ref, f32[128,256]{1,0:T(8,128)} %constant.5.clone.back_ref, s32[1,128]{1,0:T(1,128)} %bitcast.6, ...), custom_call_target="tpu_custom_call" | custom-call | bytes 524288 | tf_op jit(solution)/shard_map/pallas_call | solution.py:30
  12.7 0.0 collective-permute-done.3.refs_4_
  12.8 2.2 %collective-permute-start.6 = (bf16[128,1024]{1,0:T(8,128)(2,1)S(1)}, bf16[128,1024]{1,0:T(8,128)(2,1)S(1)}, u32[]{:S(2)}, u32[]{:S(2)}) collective-permute-start(bf16[128,1024]{1,0:T(8,128)(2,1)S(1)} %get-tuple-element.37.product_ref), channel_id=1, source_target_pairs={{0,4},{4,8},{8,12},{12,16},{16,20},{20,24},{24,28},{1,5},{5,9},{9,... | collective-permute-start | bytes 786440 | tf_op jit(solution)/shard_map/ppermute | solution.py:459
  14.9 0.0 collective-permute-done.4.refs_5_
  14.9 0.0 collective-permute-done.refs_1_
  15.0 0.0 collective-permute-done.1.refs_2_
  15.0 0.9 %collective-permute-done.2.refs_3_ = bf16[784,128]{1,0:T(8,128)(2,1)S(1)} collective-permute-done((bf16[784,128]{1,0:T(8,128)(2,1)S(1)}, bf16[784,128]{1,0:T(8,128)(2,1)S(1)}, u32[]{:S(2)}, u32[]{:S(2)}) %collective-permute-start.2) | collective-permute-done | bytes 200736 | tf_op jit(solution)/shard_map/ppermute | solution.py:42
  15.8 0.2 shard_map.106
  16.0 0.6 %collective-permute-start.5 = (bf16[10,128,256]{2,1,0:T(8,128)(2,1)S(1)}, bf16[10,128,256]{2,1,0:T(8,128)(2,1)S(1)}, u32[]{:S(2)}, u32[]{:S(2)}) collective-permute-start(bf16[10,128,256]{2,1,0:T(8,128)(2,1)S(1)} %get-tuple-element.36.mine_ref.key_value_ref), channel_id=1, source_target_pairs={{0,4},{4,0},{8,12},{12,8},{16,20},{20,16},{24,28},{28,24},{1,5},{5... | collective-permute-start | bytes 1966088 | tf_op jit(solution)/shard_map/ppermute | solution.py:42
  16.6 1.0 %shard_map.108 = (f32[2,2,1,256]{3,2,1,0:T(1,128)S(1)}, f32[2,2,1,256]{3,2,1,0:T(1,128)S(1)}, f32[2,2,128,256]{3,2,1,0:T(8,128)S(1)}) custom-call(bf16[4,144,256]{2,1,0:T(8,128)(2,1)S(1)} %get-tuple-element.43.query_ref.refs_0_, bf16[10,128,256]{2,1,0:T(8,128)(2,1)S(1)} %get-tuple-element.36.mine_ref.key_value_ref), custom_call_target="tpu_custom_call" | custom-call | flops 26843545600 | bytes 2097152 | tf_op jit(solution)/shard_map/pallas_call | solution.py:30
  17.5 0.8 %collective-permute-done.5.other_ref.refs_4_ = bf16[10,128,256]{2,1,0:T(8,128)(2,1)S(1)} collective-permute-done((bf16[10,128,256]{2,1,0:T(8,128)(2,1)S(1)}, bf16[10,128,256]{2,1,0:T(8,128)(2,1)S(1)}, u32[]{:S(2)}, u32[]{:S(2)}) %collective-permute-start.5) | collective-permute-done | bytes 655392 | tf_op jit(solution)/shard_map/ppermute | solution.py:42
  18.3 0.8 %shard_map.109 = (bf16[272,128]{1,0:T(8,128)(2,1)S(1)}, bf16[272,128]{1,0:T(8,128)(2,1)S(1)}) custom-call(bf16[4,144,256]{2,1,0:T(8,128)(2,1)S(1)} %get-tuple-element.43.query_ref.refs_0_, f32[2,2,1,256]{3,2,1,0:T(1,128)S(1)} %get-tuple-element.44.refs_1_, f32[2,2,1,256]{3,2,1,0:T(1,128)S(1)} %get-tuple-element.45.refs_2_, ...), custom_call_target="tpu_custom_call" | custom-call | flops 134217728 | bytes 2097152 | tf_op jit(solution)/shard_map/pallas_call | solution.py:30
  19.0 1.4 %collective-permute-start.7 = (bf16[272,128]{1,0:T(8,128)(2,1)S(1)}, bf16[272,128]{1,0:T(8,128)(2,1)S(1)}, u32[]{:S(2)}, u32[]{:S(2)}) collective-permute-start(bf16[272,128]{1,0:T(8,128)(2,1)S(1)} %get-tuple-element.47.refs_5_), channel_id=1, source_target_pairs={{0,16},{4,20},{8,24},{12,28},{16,0},{20,4},{24,8},{28,12},{1,17},{... | collective-permute-start | bytes 208904 | tf_op jit(solution)/shard_map/ppermute | solution.py:42
  20.5 1.6 %collective-permute-start.8 = (bf16[272,128]{1,0:T(8,128)(2,1)S(1)}, bf16[272,128]{1,0:T(8,128)(2,1)S(1)}, u32[]{:S(2)}, u32[]{:S(2)}) collective-permute-start(bf16[272,128]{1,0:T(8,128)(2,1)S(1)} %get-tuple-element.49), channel_id=1, source_target_pairs={{0,24},{4,28},{8,16},{12,20},{16,8},{20,12},{24,0},{28,4},{1,25},{... | collective-permute-start | bytes 208904 | tf_op jit(solution)/shard_map/ppermute | solution.py:42
  22.1 0.6 %shard_map.110 = (bf16[272,128]{1,0:T(8,128)(2,1)S(1)}, bf16[272,128]{1,0:T(8,128)(2,1)S(1)}) custom-call(bf16[4,144,256]{2,1,0:T(8,128)(2,1)S(1)} %get-tuple-element.43.query_ref.refs_0_, f32[2,2,1,256]{3,2,1,0:T(1,128)S(1)} %get-tuple-element.44.refs_1_, f32[2,2,1,256]{3,2,1,0:T(1,128)S(1)} %get-tuple-element.45.refs_2_, ...), custom_call_target="tpu_custom_call" | custom-call | flops 134217728 | bytes 2097152 | tf_op jit(solution)/shard_map/pallas_call | solution.py:30
  22.7 0.6 %collective-permute-start.9 = (bf16[272,128]{1,0:T(8,128)(2,1)S(1)}, bf16[272,128]{1,0:T(8,128)(2,1)S(1)}, u32[]{:S(2)}, u32[]{:S(2)}) collective-permute-start(bf16[272,128]{1,0:T(8,128)(2,1)S(1)} %get-tuple-element.50), channel_id=1, source_target_pairs={{0,8},{4,12},{8,0},{12,4},{16,24},{20,28},{24,16},{28,20},{1,9},{5... | collective-permute-start | bytes 208904 | tf_op jit(solution)/shard_map/ppermute | solution.py:42
  23.3 0.0 collective-permute-done.6.before_ref
  23.3 2.3 %shard_map.107 = bf16[128,1024]{1,0:T(8,128)(2,1)} custom-call(bf16[10,128,256]{2,1,0:T(8,128)(2,1)S(1)} %collective-permute-done.5.other_ref.refs_4_, bf16[10,128,256]{2,1,0:T(8,128)(2,1)S(1)} %get-tuple-element.36.mine_ref.key_value_ref, bf16[128,1024]{1,0:T(8,128)(2,1)S(1)} %collective-permute-done.6.before_ref, ...), custom_call_target="tpu_custom_call" | custom-call | flops 536870912 | bytes 2097152 | tf_op jit(solution)/shard_map/pallas_call | solution.py:30
  25.5 0.0 collective-permute-done.7.refs_1_
  25.5 0.1 collective-permute-done.8.refs_2_
  25.7 1.4 %collective-permute-done.9.refs_3_ = bf16[272,128]{1,0:T(8,128)(2,1)S(1)} collective-permute-done((bf16[272,128]{1,0:T(8,128)(2,1)S(1)}, bf16[272,128]{1,0:T(8,128)(2,1)S(1)}, u32[]{:S(2)}, u32[]{:S(2)}) %collective-permute-start.9) | collective-permute-done | bytes 69664 | tf_op jit(solution)/shard_map/ppermute | solution.py:42
  27.1 0.8 %shard_map.111 = (bf16[128,1024]{1,0:T(8,128)(2,1)}, f32[8,128]{1,0:T(8,128)}) custom-call(bf16[272,128]{1,0:T(8,128)(2,1)S(1)} %get-tuple-element.48.refs_0_, bf16[272,128]{1,0:T(8,128)(2,1)S(1)} %collective-permute-done.7.refs_1_, bf16[272,128]{1,0:T(8,128)(2,1)S(1)} %collective-permute-done.8.refs_2_, bf16[272,128]{1,0:T(8,128)(2,1)S(1)} %collective-permute-done.9.refs_3_), custom_call_target="tpu_custom_call" | custom-call | bytes 524288 | tf_op jit(solution)/shard_map/pallas_call | solution.py:30
Async XLA Ops:
  0.6 6.2 %copy-start = (bf16[3,128,1024]{2,1,0:T(8,128)(2,1)S(1)}, bf16[3,128,1024]{2,1,0:T(8,128)(2,1)}, u32[]{:S(2)}) copy-start(bf16[3,128,1024]{2,1,0:T(8,128)(2,1)} %gate_ref.1) | copy-start | bytes 2359300
  2.3 12.7 %collective-permute-start = (bf16[784,128]{1,0:T(8,128)(2,1)S(1)}, bf16[784,128]{1,0:T(8,128)(2,1)S(1)}, u32[]{:S(2)}, u32[]{:S(2)}) collective-permute-start(bf16[784,128]{1,0:T(8,128)(2,1)S(1)} %get-tuple-element.29), channel_id=1, source_target_pairs={{0,16},{4,20},{8,24},{12,28},{16,0},{20,4},{24,8},{28,12},{1,17},{... | collective-permute-start | bytes 602120 | tf_op jit(solution)/shard_map/ppermute | solution.py:42
  5.3 9.7 %collective-permute-start.1 = (bf16[784,128]{1,0:T(8,128)(2,1)S(1)}, bf16[784,128]{1,0:T(8,128)(2,1)S(1)}, u32[]{:S(2)}, u32[]{:S(2)}) collective-permute-start(bf16[784,128]{1,0:T(8,128)(2,1)S(1)} %get-tuple-element.30), channel_id=1, source_target_pairs={{0,8},{4,12},{8,0},{12,4},{16,24},{20,28},{24,16},{28,20},{1,9},{5... | collective-permute-start | bytes 602120 | tf_op jit(solution)/shard_map/ppermute | solution.py:42
  6.8 9.1 %collective-permute-start.2 = (bf16[784,128]{1,0:T(8,128)(2,1)S(1)}, bf16[784,128]{1,0:T(8,128)(2,1)S(1)}, u32[]{:S(2)}, u32[]{:S(2)}) collective-permute-start(bf16[784,128]{1,0:T(8,128)(2,1)S(1)} %get-tuple-element.31), channel_id=1, source_target_pairs={{0,24},{4,28},{8,16},{12,20},{16,8},{20,12},{24,0},{28,4},{1,25},{... | collective-permute-start | bytes 602120 | tf_op jit(solution)/shard_map/ppermute | solution.py:42
  6.9 5.8 %collective-permute-start.3 = (bf16[32,1024]{1,0:T(8,128)(2,1)S(1)}, bf16[32,1024]{1,0:T(8,128)(2,1)S(1)}, u32[]{:S(2)}, u32[]{:S(2)}) collective-permute-start(bf16[32,1024]{1,0:T(8,128)(2,1)S(1)} %get-tuple-element.33), channel_id=1, source_target_pairs={{4,5},{5,4},{6,7},{7,6},{12,13},{13,12},{14,15},{15,14},{20,21},{2... | collective-permute-start | bytes 196616 | tf_op jit(solution)/shard_map/ppermute | solution.py:457
  7.6 7.3 %collective-permute-start.4 = (bf16[32,1024]{1,0:T(8,128)(2,1)S(1)}, bf16[32,1024]{1,0:T(8,128)(2,1)S(1)}, u32[]{:S(2)}, u32[]{:S(2)}) collective-permute-start(bf16[32,1024]{1,0:T(8,128)(2,1)S(1)} %get-tuple-element.34), channel_id=1, source_target_pairs={{0,3},{1,2},{2,1},{3,0},{4,6},{5,7},{6,4},{7,5},{8,11},{9,10},{10,... | collective-permute-start | bytes 196616 | tf_op jit(solution)/shard_map/ppermute | solution.py:458
  12.8 10.5 %collective-permute-start.6 = (bf16[128,1024]{1,0:T(8,128)(2,1)S(1)}, bf16[128,1024]{1,0:T(8,128)(2,1)S(1)}, u32[]{:S(2)}, u32[]{:S(2)}) collective-permute-start(bf16[128,1024]{1,0:T(8,128)(2,1)S(1)} %get-tuple-element.37.product_ref), channel_id=1, source_target_pairs={{0,4},{4,8},{8,12},{12,16},{16,20},{20,24},{24,28},{1,5},{5,9},{9,... | collective-permute-start | bytes 786440 | tf_op jit(solution)/shard_map/ppermute | solution.py:459
  16.0 2.3 %collective-permute-start.5 = (bf16[10,128,256]{2,1,0:T(8,128)(2,1)S(1)}, bf16[10,128,256]{2,1,0:T(8,128)(2,1)S(1)}, u32[]{:S(2)}, u32[]{:S(2)}) collective-permute-start(bf16[10,128,256]{2,1,0:T(8,128)(2,1)S(1)} %get-tuple-element.36.mine_ref.key_value_ref), channel_id=1, source_target_pairs={{0,4},{4,0},{8,12},{12,8},{16,20},{20,16},{24,28},{28,24},{1,5},{5... | collective-permute-start | bytes 1966088 | tf_op jit(solution)/shard_map/ppermute | solution.py:42
  19.0 6.5 %collective-permute-start.7 = (bf16[272,128]{1,0:T(8,128)(2,1)S(1)}, bf16[272,128]{1,0:T(8,128)(2,1)S(1)}, u32[]{:S(2)}, u32[]{:S(2)}) collective-permute-start(bf16[272,128]{1,0:T(8,128)(2,1)S(1)} %get-tuple-element.47.refs_5_), channel_id=1, source_target_pairs={{0,16},{4,20},{8,24},{12,28},{16,0},{20,4},{24,8},{28,12},{1,17},{... | collective-permute-start | bytes 208904 | tf_op jit(solution)/shard_map/ppermute | solution.py:42
  20.5 5.2 %collective-permute-start.8 = (bf16[272,128]{1,0:T(8,128)(2,1)S(1)}, bf16[272,128]{1,0:T(8,128)(2,1)S(1)}, u32[]{:S(2)}, u32[]{:S(2)}) collective-permute-start(bf16[272,128]{1,0:T(8,128)(2,1)S(1)} %get-tuple-element.49), channel_id=1, source_target_pairs={{0,24},{4,28},{8,16},{12,20},{16,8},{20,12},{24,0},{28,4},{1,25},{... | collective-permute-start | bytes 208904 | tf_op jit(solution)/shard_map/ppermute | solution.py:42
  22.7 4.4 %collective-permute-start.9 = (bf16[272,128]{1,0:T(8,128)(2,1)S(1)}, bf16[272,128]{1,0:T(8,128)(2,1)S(1)}, u32[]{:S(2)}, u32[]{:S(2)}) collective-permute-start(bf16[272,128]{1,0:T(8,128)(2,1)S(1)} %get-tuple-element.50), channel_id=1, source_target_pairs={{0,8},{4,12},{8,0},{12,4},{16,24},{20,28},{24,16},{28,20},{1,9},{5... | collective-permute-start | bytes 208904 | tf_op jit(solution)/shard_map/ppermute | solution.py:42

commit v9 on v8

--- a/solution.py
+++ b/solution.py
@@ -26,12 +26,13 @@
     return pl.BlockSpec(memory_space=pltpu.HBM)
 
 
-def call(kernel, out_shape, args, flops, nbytes, scratch=(), specs=None):
+def call(kernel, out_shape, args, flops, nbytes, scratch=(), specs=None, out_specs=None, aliases=None):
     return pl.pallas_call(
         kernel,
         out_shape=out_shape,
         in_specs=specs or [vmem() for _ in args],
-        out_specs=jax.tree.map(lambda _: vmem(), out_shape),
+        out_specs=out_specs or jax.tree.map(lambda _: vmem(), out_shape),
+        input_output_aliases=aliases or {},
         scratch_shapes=list(scratch),
         compiler_params=pltpu.CompilerParams(vmem_limit_bytes=VMEM_LIMIT),
         cost_estimate=pl.CostEstimate(flops=flops, bytes_accessed=nbytes, transcendentals=0),
@@ -256,14 +257,12 @@
             mixed_ref[head, unit] = mix(sets[head], rounded)
 
 
-def attend_second(heads, mine, *refs):
+def attend_second(heads, *refs):
     count = heads // 2
-    query_ref, top_ref, total_ref, mixed_ref, other_ref, *more = refs[: -UNIT - 1]
-    outs, held_ref = refs[-UNIT - 1 : -1], refs[-1]
-    more = more[: len(more) // 2 * 2]
+    query_ref, top_ref, total_ref, mixed_ref, other_ref, *more = refs[: -count - 1]
+    outs, held_ref = refs[-count - 1 : -1], refs[-1]
     rows = query_ref.shape[1] - NOTE_ROWS
     _, pair, parity = place(heads)
-    here = pair // UNIT
 
     def one_unit(unit):
         begin = unit * UNIT
@@ -293,36 +292,53 @@
             for index, part in enumerate((high, middle, low)):
                 notes = jnp.where(line == index, part, notes)
             for index in range(UNIT):
-                held_ref[index, head * rows : (head + 1) * rows] = mixed[
+                held_ref[begin + index, head * rows : (head + 1) * rows] = mixed[
                     index * rows : (index + 1) * rows
                 ]
         for index in range(UNIT):
-            held_ref[index, 2 * rows :] = notes[:, index * rows : (index + 1) * rows].astype(
+            held_ref[begin + index, 2 * rows :] = notes[:, index * rows : (index + 1) * rows].astype(
                 jnp.bfloat16
             )
 
     for unit in range(count // UNIT):
-
-        @pl.when((here == unit) if mine else (here != unit))
-        def _():
-            one_unit(unit)
-
+        one_unit(unit)
     for step, out in enumerate(outs):
-        out[...] = held_ref[lax.rem(pair, UNIT) ^ step]
-
-
-def unpack_heads(heads, steps, *refs):
-    *sources, out_ref, logs_ref = refs
+        out[...] = held_ref[pair ^ step]
+
+
+def send_columns(heads, sources, out_ref, held_ref, sem):
+    rows = out_ref.shape[0]
+    _, pair, _ = place(heads)
+    copies = []
+    for index, (step, source) in enumerate(sources):
+        for head in range(2):
+            held_ref[index, :, head * HD : (head + 1) * HD] = source[head * rows : (head + 1) * rows]
+        columns = pl.ds(pl.multiple_of((pair ^ step) * (2 * HD), 2 * HD), 2 * HD)
+        copies.append(
+            pltpu.make_async_copy(held_ref.at[index], out_ref.at[:, columns], sem.at[index])
+        )
+        copies[-1].start()
+    return copies
+
+
+def unpack_early(heads, steps, *refs):
+    *sources, out_ref, held_ref, sem = refs
+    for copy in send_columns(heads, list(zip(steps, sources)), out_ref, held_ref, sem):
+        copy.wait()
+
+
+def unpack_late(heads, steps, *refs):
+    *sources, _, out_ref, logs_ref, held_ref, sem = refs
+    copies = send_columns(heads, [(steps[-1], sources[-1])], out_ref, held_ref, sem)
     rows = out_ref.shape[0]
     _, pair, _ = place(heads)
     for step, source in zip(steps, sources):
-        owner = pair ^ step
         note = source[2 * rows :].astype(jnp.float32)
         for head in range(2):
-            columns = pl.ds(pl.multiple_of((owner * 2 + head) * HD, HD), HD)
-            out_ref[:, columns] = source[head * rows : (head + 1) * rows]
             parts = [note[3 * head + index : 3 * head + index + 1] for index in range(3)]
-            logs_ref[pl.ds(owner * 2 + head, 1), :] = parts[0] + parts[1] + parts[2]
+            logs_ref[pl.ds((pair ^ step) * 2 + head, 1), :] = parts[0] + parts[1] + parts[2]
+    for copy in copies:
+        copy.wait()
 
 
 def dot(left, right):
@@ -503,20 +519,15 @@
     assert count == 2 * UNIT
     message = shape((2 * rows + NOTE_ROWS, HD), bf16)
 
-    def second(mine, *more):
-        return call(
-            functools.partial(attend_second, heads, mine),
-            (message,) * UNIT,
-            (*operands, *more),
-            (heads * rows) ** 2 * HD,
-            4 * queries.size * 4,
-            scratch=(pltpu.VMEM((UNIT, 2 * rows + NOTE_ROWS, HD), bf16),),
-        )
-
-    theirs = second(False)
-    own = second(True, theirs[0])
-    returned = [own[0], crossed(theirs[0], "ctx", 4), crossed(theirs[1], "ctx", 6)]
-    returned.append(crossed(own[1], "ctx", 2))
+    mixed = call(
+        functools.partial(attend_second, heads),
+        (message,) * count,
+        operands,
+        2 * (heads * rows) ** 2 * HD,
+        4 * queries.size * 4,
+        scratch=(pltpu.VMEM((count, 2 * rows + NOTE_ROWS, HD), bf16),),
+    )
+    own, *returned = [mixed[0]] + [crossed(mixed[step], "ctx", 2 * step) for step in (2, 3, 1)]
     hyena_out = call(
         functools.partial(convolve, heads),
         shape((rows, channels), bf16),
@@ -532,12 +543,26 @@
             pltpu.VMEM((rows, channels), f32),
         ),
     )
-    attention_out, log_totals = call(
-        functools.partial(unpack_heads, heads, (0, 2, 3, 1)),
-        (shape((rows, heads * HD), bf16), shape((heads, rows), f32)),
-        returned,
+    order = (0, 2, 3, 1)
+    early_out = call(
+        functools.partial(unpack_early, heads, order[:-1]),
+        shape((rows, heads * HD), bf16),
+        (own, *returned[:-1]),
         0,
         4 * queries.size,
+        scratch=(pltpu.VMEM((count - 1, rows, 2 * HD), bf16), pltpu.SemaphoreType.DMA((count - 1,))),
+        out_specs=hbm(),
+    )
+    attention_out, log_totals = call(
+        functools.partial(unpack_late, heads, order),
+        (shape((rows, heads * HD), bf16), shape((heads, rows), f32)),
+        (own, *returned, early_out),
+        0,
+        4 * queries.size,
+        scratch=(pltpu.VMEM((1, rows, 2 * HD), bf16), pltpu.SemaphoreType.DMA((1,))),
+        specs=[vmem()] * count + [hbm()],
+        out_specs=(hbm(), vmem()),
+        aliases={count: 0},
     )
     return (hyena_out, attention_out, log_totals)
 

time: 28 us -> 29 us (1.036)
  Pallas kernels: 8.26 us -> 9.22 us
    pallas_call x9, Pallas kernels: 8.26 us -> 9.22 us  [call(): pl.pallas_call(kernel, out_shape=out_shape, in_specs=specs or [vmem() for...]
  transfers between devices with their start and end apart: 10 -> 10, of which waited for: 4 -> 3; matrix products, arithmetic and copies ran while one was open for 0% -> 0% of each run, Pallas kernels for 21% -> 22%
where the time goes in v9:
time: 29 us; the launch traced here: 28.9 us
  starting transfers between devices  15.6 us (54%)
  Pallas kernels  9.22 us (32%)
  waiting for transfers between devices  3.26 us (11%)
  between operations  0.74 us (3%)
    pallas_call x9, Pallas kernels, call(): pl.pallas_call(kernel, out_shape=out_shape, in_specs=specs or [vmem() for...  9.22 us
    ppermute x7, starting transfers between devices, crossed(): lax.ppermute(array, axis, [(i, i ^ bits) for i in range(lax.axis_size(axi...  8.7 us
    ppermute x1, starting transfers between devices, local(): far_taps = lax.ppermute(far_taps, axes, far_pairs)  4.09 us
    ppermute x7, waiting for transfers between devices, crossed(): lax.ppermute(array, axis, [(i, i ^ bits) for i in range(lax.axis_size(axi...  3.25 us
    ppermute x1, starting transfers between devices, local(): lax.ppermute(product, 'ctx', [(i, i + 1) for i in range(peers - 1)])  2.16 us
    ppermute x1, starting transfers between devices, local(): near_taps = lax.ppermute(near_taps, axes, near_pairs)  0.66 us
  transfers between devices with their start and end apart: 10, of which 3 were waited for; matrix products, arithmetic and copies ran while one was open for 0% of the time, Pallas kernels for 22%

profile of v9, /device:TPU:0, one launch (start us, length us, event | category | flops | bytes accessed | tf_op | source)
XLA Modules:
  0.0 28.9 jit_solution(17254899482661262215)
XLA Ops:
  0.6 0.0 copy-start
  0.6 1.6 %shard_map.103 = (bf16[784,128]{1,0:T(8,128)(2,1)S(1)}, bf16[784,128]{1,0:T(8,128)(2,1)S(1)}, bf16[784,128]{1,0:T(8,128)(2,1)S(1)}, bf16[784,128]{1,0:T(8,128)(2,1)S(1)}, f32[3,32,1024]{2,1,0:T(8,128)S(1)}) custom-call(bf16[128,1024]{1,0:T(8,128)(2,1)} %queries_ref.1, bf16[256,1024]{1,0:T(8,128)(2,1)} %bitcast.3, s32[1,128]{1,0:T(1,128)} %bitcast.5, ...), custom_call_target="tpu_custom_call" | custom-call | bytes 1572864 | tf_op jit(solution)/shard_map/pallas_call | solution.py:30
  2.3 3.0 %collective-permute-start = (bf16[784,128]{1,0:T(8,128)(2,1)S(1)}, bf16[784,128]{1,0:T(8,128)(2,1)S(1)}, u32[]{:S(2)}, u32[]{:S(2)}) collective-permute-start(bf16[784,128]{1,0:T(8,128)(2,1)S(1)} %get-tuple-element.29), channel_id=1, source_target_pairs={{0,16},{4,20},{8,24},{12,28},{16,0},{20,4},{24,8},{28,12},{1,17},{... | collective-permute-start | bytes 602120 | tf_op jit(solution)/shard_map/ppermute | solution.py:43
  5.3 1.5 %collective-permute-start.1 = (bf16[784,128]{1,0:T(8,128)(2,1)S(1)}, bf16[784,128]{1,0:T(8,128)(2,1)S(1)}, u32[]{:S(2)}, u32[]{:S(2)}) collective-permute-start(bf16[784,128]{1,0:T(8,128)(2,1)S(1)} %get-tuple-element.30), channel_id=1, source_target_pairs={{0,8},{4,12},{8,0},{12,4},{16,24},{20,28},{24,16},{28,20},{1,9},{5... | collective-permute-start | bytes 602120 | tf_op jit(solution)/shard_map/ppermute | solution.py:43
  6.8 0.0 collective-permute-start.2
  6.8 0.0 copy-done
  6.8 0.1 shard_map.104
  6.9 0.7 %collective-permute-start.3 = (bf16[32,1024]{1,0:T(8,128)(2,1)S(1)}, bf16[32,1024]{1,0:T(8,128)(2,1)S(1)}, u32[]{:S(2)}, u32[]{:S(2)}) collective-permute-start(bf16[32,1024]{1,0:T(8,128)(2,1)S(1)} %get-tuple-element.33), channel_id=1, source_target_pairs={{4,5},{5,4},{6,7},{7,6},{12,13},{13,12},{14,15},{15,14},{20,21},{2... | collective-permute-start | bytes 196616 | tf_op jit(solution)/shard_map/ppermute | solution.py:473
  7.6 4.1 %collective-permute-start.4 = (bf16[32,1024]{1,0:T(8,128)(2,1)S(1)}, bf16[32,1024]{1,0:T(8,128)(2,1)S(1)}, u32[]{:S(2)}, u32[]{:S(2)}) collective-permute-start(bf16[32,1024]{1,0:T(8,128)(2,1)S(1)} %get-tuple-element.34), channel_id=1, source_target_pairs={{0,3},{1,2},{2,1},{3,0},{4,6},{5,7},{6,4},{7,5},{8,11},{9,10},{10,... | collective-permute-start | bytes 196616 | tf_op jit(solution)/shard_map/ppermute | solution.py:474
  11.7 1.1 %shard_map.105 = (bf16[256,256]{1,0:T(8,128)(2,1)S(1)}, bf16[256,256]{1,0:T(8,128)(2,1)S(1)}, bf16[128,256]{1,0:T(8,128)(2,1)S(1)}, s32[1,128]{1,0:T(1,128)S(1)}, f32[1,1024]{1,0:T(1,128)S(1)}) custom-call(f32[256,256]{1,0:T(8,128)} %constant.4.clone.ahead_ref, f32[128,256]{1,0:T(8,128)} %constant.5.clone.back_ref, s32[1,128]{1,0:T(1,128)} %bitcast.6, ...), custom_call_target="tpu_custom_call" | custom-call | bytes 524288 | tf_op jit(solution)/shard_map/pallas_call | solution.py:30
  12.7 0.0 collective-permute-done.3.refs_4_
  12.8 2.2 %collective-permute-start.6 = (bf16[128,1024]{1,0:T(8,128)(2,1)S(1)}, bf16[128,1024]{1,0:T(8,128)(2,1)S(1)}, u32[]{:S(2)}, u32[]{:S(2)}) collective-permute-start(bf16[128,1024]{1,0:T(8,128)(2,1)S(1)} %get-tuple-element.37.product_ref), channel_id=1, source_target_pairs={{0,4},{4,8},{8,12},{12,16},{16,20},{20,24},{24,28},{1,5},{5,9},{9,... | collective-permute-start | bytes 786440 | tf_op jit(solution)/shard_map/ppermute | solution.py:475
  14.9 0.0 collective-permute-done.4.refs_5_
  14.9 0.0 collective-permute-done.refs_1_
  15.0 0.0 collective-permute-done.1.refs_2_
  15.0 0.9 %collective-permute-done.2.refs_3_ = bf16[784,128]{1,0:T(8,128)(2,1)S(1)} collective-permute-done((bf16[784,128]{1,0:T(8,128)(2,1)S(1)}, bf16[784,128]{1,0:T(8,128)(2,1)S(1)}, u32[]{:S(2)}, u32[]{:S(2)}) %collective-permute-start.2) | collective-permute-done | bytes 200736 | tf_op jit(solution)/shard_map/ppermute | solution.py:43
  15.8 0.2 shard_map.106
  16.0 0.6 %collective-permute-start.5 = (bf16[10,128,256]{2,1,0:T(8,128)(2,1)S(1)}, bf16[10,128,256]{2,1,0:T(8,128)(2,1)S(1)}, u32[]{:S(2)}, u32[]{:S(2)}) collective-permute-start(bf16[10,128,256]{2,1,0:T(8,128)(2,1)S(1)} %get-tuple-element.36.mine_ref.key_value_ref), channel_id=1, source_target_pairs={{0,4},{4,0},{8,12},{12,8},{16,20},{20,16},{24,28},{28,24},{1,5},{5... | collective-permute-start | bytes 1966088 | tf_op jit(solution)/shard_map/ppermute | solution.py:43
  16.6 1.0 %shard_map.108 = (f32[2,2,1,256]{3,2,1,0:T(1,128)S(1)}, f32[2,2,1,256]{3,2,1,0:T(1,128)S(1)}, f32[2,2,128,256]{3,2,1,0:T(8,128)S(1)}) custom-call(bf16[4,144,256]{2,1,0:T(8,128)(2,1)S(1)} %get-tuple-element.43.query_ref.refs_0_, bf16[10,128,256]{2,1,0:T(8,128)(2,1)S(1)} %get-tuple-element.36.mine_ref.key_value_ref), custom_call_target="tpu_custom_call" | custom-call | flops 26843545600 | bytes 2097152 | tf_op jit(solution)/shard_map/pallas_call | solution.py:30
  17.5 0.8 %collective-permute-done.5.other_ref.refs_4_ = bf16[10,128,256]{2,1,0:T(8,128)(2,1)S(1)} collective-permute-done((bf16[10,128,256]{2,1,0:T(8,128)(2,1)S(1)}, bf16[10,128,256]{2,1,0:T(8,128)(2,1)S(1)}, u32[]{:S(2)}, u32[]{:S(2)}) %collective-permute-start.5) | collective-permute-done | bytes 655392 | tf_op jit(solution)/shard_map/ppermute | solution.py:43
  18.3 1.1 %shard_map.109 = (bf16[272,128]{1,0:T(8,128)(2,1)S(1)}, bf16[272,128]{1,0:T(8,128)(2,1)S(1)}, bf16[272,128]{1,0:T(8,128)(2,1)S(1)}, bf16[272,128]{1,0:T(8,128)(2,1)S(1)}) custom-call(bf16[4,144,256]{2,1,0:T(8,128)(2,1)S(1)} %get-tuple-element.43.query_ref.refs_0_, f32[2,2,1,256]{3,2,1,0:T(1,128)S(1)} %get-tuple-element.44.refs_1_, ...), custom_call_target="tpu_custom_call" | custom-call | flops 268435456 | bytes 2097152 | tf_op jit(solution)/shard_map/pallas_call | solution.py:30
  19.4 1.6 %collective-permute-start.7 = (bf16[272,128]{1,0:T(8,128)(2,1)S(1)}, bf16[272,128]{1,0:T(8,128)(2,1)S(1)}, u32[]{:S(2)}, u32[]{:S(2)}) collective-permute-start(bf16[272,128]{1,0:T(8,128)(2,1)S(1)} %get-tuple-element.48), channel_id=1, source_target_pairs={{0,16},{4,20},{8,24},{12,28},{16,0},{20,4},{24,8},{28,12},{1,17},{... | collective-permute-start | bytes 208904 | tf_op jit(solution)/shard_map/ppermute | solution.py:43
  21.0 1.4 %collective-permute-start.8 = (bf16[272,128]{1,0:T(8,128)(2,1)S(1)}, bf16[272,128]{1,0:T(8,128)(2,1)S(1)}, u32[]{:S(2)}, u32[]{:S(2)}) collective-permute-start(bf16[272,128]{1,0:T(8,128)(2,1)S(1)} %get-tuple-element.49), channel_id=1, source_target_pairs={{0,24},{4,28},{8,16},{12,20},{16,8},{20,12},{24,0},{28,4},{1,25},{... | collective-permute-start | bytes 208904 | tf_op jit(solution)/shard_map/ppermute | solution.py:43
  22.4 0.5 %collective-permute-start.9 = (bf16[272,128]{1,0:T(8,128)(2,1)S(1)}, bf16[272,128]{1,0:T(8,128)(2,1)S(1)}, u32[]{:S(2)}, u32[]{:S(2)}) collective-permute-start(bf16[272,128]{1,0:T(8,128)(2,1)S(1)} %get-tuple-element.50), channel_id=1, source_target_pairs={{0,8},{4,12},{8,0},{12,4},{16,24},{20,28},{24,16},{28,20},{1,9},{5... | collective-permute-start | bytes 208904 | tf_op jit(solution)/shard_map/ppermute | solution.py:43
  22.9 0.0 collective-permute-done.6.before_ref
  23.0 2.3 %shard_map.107 = bf16[128,1024]{1,0:T(8,128)(2,1)} custom-call(bf16[10,128,256]{2,1,0:T(8,128)(2,1)S(1)} %collective-permute-done.5.other_ref.refs_4_, bf16[10,128,256]{2,1,0:T(8,128)(2,1)S(1)} %get-tuple-element.36.mine_ref.key_value_ref, bf16[128,1024]{1,0:T(8,128)(2,1)S(1)} %collective-permute-done.6.before_ref, ...), custom_call_target="tpu_custom_call" | custom-call | flops 536870912 | bytes 2097152 | tf_op jit(solution)/shard_map/pallas_call | solution.py:30
  25.2 0.0 collective-permute-done.7.refs_1_
  25.2 1.6 %collective-permute-done.8.refs_2_ = bf16[272,128]{1,0:T(8,128)(2,1)S(1)} collective-permute-done((bf16[272,128]{1,0:T(8,128)(2,1)S(1)}, bf16[272,128]{1,0:T(8,128)(2,1)S(1)}, u32[]{:S(2)}, u32[]{:S(2)}) %collective-permute-start.8) | collective-permute-done | bytes 69664 | tf_op jit(solution)/shard_map/ppermute | solution.py:43
  26.9 0.7 %shard_map.110.refs_4_ = bf16[128,1024]{1,0:T(8,128)(2,1)} custom-call(bf16[272,128]{1,0:T(8,128)(2,1)S(1)} %get-tuple-element.47.refs_0_, bf16[272,128]{1,0:T(8,128)(2,1)S(1)} %collective-permute-done.7.refs_1_, bf16[272,128]{1,0:T(8,128)(2,1)S(1)} %collective-permute-done.8.refs_2_), custom_call_target="tpu_custom_call" | custom-call | bytes 524288 | tf_op jit(solution)/shard_map/pallas_call | solution.py:30
  27.6 0.0 collective-permute-done.9.refs_3_
  27.6 1.3 %shard_map.111 = (bf16[128,1024]{1,0:T(8,128)(2,1)}, f32[8,128]{1,0:T(8,128)}) custom-call(bf16[272,128]{1,0:T(8,128)(2,1)S(1)} %get-tuple-element.47.refs_0_, bf16[272,128]{1,0:T(8,128)(2,1)S(1)} %collective-permute-done.7.refs_1_, bf16[272,128]{1,0:T(8,128)(2,1)S(1)} %collective-permute-done.8.refs_2_, ...), custom_call_target="tpu_custom_call", output_to_operand_aliasing={{0}: (4, {})} | custom-call | bytes 524288 | tf_op jit(solution)/shard_map/pallas_call | solution.py:30
Async XLA Ops:
  0.6 6.2 %copy-start = (bf16[3,128,1024]{2,1,0:T(8,128)(2,1)S(1)}, bf16[3,128,1024]{2,1,0:T(8,128)(2,1)}, u32[]{:S(2)}) copy-start(bf16[3,128,1024]{2,1,0:T(8,128)(2,1)} %gate_ref.1) | copy-start | bytes 2359300
  2.3 12.7 %collective-permute-start = (bf16[784,128]{1,0:T(8,128)(2,1)S(1)}, bf16[784,128]{1,0:T(8,128)(2,1)S(1)}, u32[]{:S(2)}, u32[]{:S(2)}) collective-permute-start(bf16[784,128]{1,0:T(8,128)(2,1)S(1)} %get-tuple-element.29), channel_id=1, source_target_pairs={{0,16},{4,20},{8,24},{12,28},{16,0},{20,4},{24,8},{28,12},{1,17},{... | collective-permute-start | bytes 602120 | tf_op jit(solution)/shard_map/ppermute | solution.py:43
  5.3 9.7 %collective-permute-start.1 = (bf16[784,128]{1,0:T(8,128)(2,1)S(1)}, bf16[784,128]{1,0:T(8,128)(2,1)S(1)}, u32[]{:S(2)}, u32[]{:S(2)}) collective-permute-start(bf16[784,128]{1,0:T(8,128)(2,1)S(1)} %get-tuple-element.30), channel_id=1, source_target_pairs={{0,8},{4,12},{8,0},{12,4},{16,24},{20,28},{24,16},{28,20},{1,9},{5... | collective-permute-start | bytes 602120 | tf_op jit(solution)/shard_map/ppermute | solution.py:43
  6.8 9.1 %collective-permute-start.2 = (bf16[784,128]{1,0:T(8,128)(2,1)S(1)}, bf16[784,128]{1,0:T(8,128)(2,1)S(1)}, u32[]{:S(2)}, u32[]{:S(2)}) collective-permute-start(bf16[784,128]{1,0:T(8,128)(2,1)S(1)} %get-tuple-element.31), channel_id=1, source_target_pairs={{0,24},{4,28},{8,16},{12,20},{16,8},{20,12},{24,0},{28,4},{1,25},{... | collective-permute-start | bytes 602120 | tf_op jit(solution)/shard_map/ppermute | solution.py:43
  6.9 5.8 %collective-permute-start.3 = (bf16[32,1024]{1,0:T(8,128)(2,1)S(1)}, bf16[32,1024]{1,0:T(8,128)(2,1)S(1)}, u32[]{:S(2)}, u32[]{:S(2)}) collective-permute-start(bf16[32,1024]{1,0:T(8,128)(2,1)S(1)} %get-tuple-element.33), channel_id=1, source_target_pairs={{4,5},{5,4},{6,7},{7,6},{12,13},{13,12},{14,15},{15,14},{20,21},{2... | collective-permute-start | bytes 196616 | tf_op jit(solution)/shard_map/ppermute | solution.py:473
  7.6 7.3 %collective-permute-start.4 = (bf16[32,1024]{1,0:T(8,128)(2,1)S(1)}, bf16[32,1024]{1,0:T(8,128)(2,1)S(1)}, u32[]{:S(2)}, u32[]{:S(2)}) collective-permute-start(bf16[32,1024]{1,0:T(8,128)(2,1)S(1)} %get-tuple-element.34), channel_id=1, source_target_pairs={{0,3},{1,2},{2,1},{3,0},{4,6},{5,7},{6,4},{7,5},{8,11},{9,10},{10,... | collective-permute-start | bytes 196616 | tf_op jit(solution)/shard_map/ppermute | solution.py:474
  12.8 10.2 %collective-permute-start.6 = (bf16[128,1024]{1,0:T(8,128)(2,1)S(1)}, bf16[128,1024]{1,0:T(8,128)(2,1)S(1)}, u32[]{:S(2)}, u32[]{:S(2)}) collective-permute-start(bf16[128,1024]{1,0:T(8,128)(2,1)S(1)} %get-tuple-element.37.product_ref), channel_id=1, source_target_pairs={{0,4},{4,8},{8,12},{12,16},{16,20},{20,24},{24,28},{1,5},{5,9},{9,... | collective-permute-start | bytes 786440 | tf_op jit(solution)/shard_map/ppermute | solution.py:475
  16.0 2.3 %collective-permute-start.5 = (bf16[10,128,256]{2,1,0:T(8,128)(2,1)S(1)}, bf16[10,128,256]{2,1,0:T(8,128)(2,1)S(1)}, u32[]{:S(2)}, u32[]{:S(2)}) collective-permute-start(bf16[10,128,256]{2,1,0:T(8,128)(2,1)S(1)} %get-tuple-element.36.mine_ref.key_value_ref), channel_id=1, source_target_pairs={{0,4},{4,0},{8,12},{12,8},{16,20},{20,16},{24,28},{28,24},{1,5},{5... | collective-permute-start | bytes 1966088 | tf_op jit(solution)/shard_map/ppermute | solution.py:43
  19.4 5.9 %collective-permute-start.7 = (bf16[272,128]{1,0:T(8,128)(2,1)S(1)}, bf16[272,128]{1,0:T(8,128)(2,1)S(1)}, u32[]{:S(2)}, u32[]{:S(2)}) collective-permute-start(bf16[272,128]{1,0:T(8,128)(2,1)S(1)} %get-tuple-element.48), channel_id=1, source_target_pairs={{0,16},{4,20},{8,24},{12,28},{16,0},{20,4},{24,8},{28,12},{1,17},{... | collective-permute-start | bytes 208904 | tf_op jit(solution)/shard_map/ppermute | solution.py:43
  21.0 5.9 %collective-permute-start.8 = (bf16[272,128]{1,0:T(8,128)(2,1)S(1)}, bf16[272,128]{1,0:T(8,128)(2,1)S(1)}, u32[]{:S(2)}, u32[]{:S(2)}) collective-permute-start(bf16[272,128]{1,0:T(8,128)(2,1)S(1)} %get-tuple-element.49), channel_id=1, source_target_pairs={{0,24},{4,28},{8,16},{12,20},{16,8},{20,12},{24,0},{28,4},{1,25},{... | collective-permute-start | bytes 208904 | tf_op jit(solution)/shard_map/ppermute | solution.py:43
  22.4 5.2 %collective-permute-start.9 = (bf16[272,128]{1,0:T(8,128)(2,1)S(1)}, bf16[272,128]{1,0:T(8,128)(2,1)S(1)}, u32[]{:S(2)}, u32[]{:S(2)}) collective-permute-start(bf16[272,128]{1,0:T(8,128)(2,1)S(1)} %get-tuple-element.50), channel_id=1, source_target_pairs={{0,8},{4,12},{8,0},{12,4},{16,24},{20,28},{24,16},{28,20},{1,9},{5... | collective-permute-start | bytes 208904 | tf_op jit(solution)/shard_map/ppermute | solution.py:43

commit v10 on v8

--- a/solution.py
+++ b/solution.py
@@ -51,8 +51,8 @@
     return index // heads, member // 2, lax.rem(member, 2)
 
 
-def pack_heads(heads, queries_ref, keys_values_ref, starts_ref, filters_ref, *refs):
-    *outs, taps_ref, held_ref, start_sem, taps_sem, sem = refs
+def pack_heads(heads, queries_ref, keys_values_ref, starts_ref, *refs):
+    *outs, held_ref, start_sem, sem = refs
     rows = queries_ref.shape[0]
     _, pair, _ = place(heads)
     first = pltpu.make_async_copy(starts_ref, held_ref, start_sem)
@@ -69,15 +69,6 @@
                         source.at[:, columns], out.at[lines], sem.at[step, 2 * head + part]
                     )
                 )
-    width = taps_ref.shape[2]
-    panel = lax.axis_index("tp")
-    for index, target in enumerate((panel, panel ^ (3 - lax.rem(lax.axis_index("ctx"), 2)), panel ^ 1)):
-        columns = pl.ds(pl.multiple_of(target * width, width), width)
-        copies.append(
-            pltpu.make_async_copy(
-                filters_ref.at[:, columns], taps_ref.at[index], taps_sem.at[index]
-            )
-        )
     for copy in copies:
         copy.start()
     first.wait()
@@ -98,33 +89,25 @@
     return jnp.concatenate([high, low], axis=1)
 
 
-def pack_hyena(hyena_ref, taps_ref, product_ref, own_ref, far_ref, near_ref):
+def pack_hyena(hyena_ref, filters_ref, product_ref, own_ref, far_ref, near_ref, taps_ref, sem):
+    width = own_ref.shape[1]
+    panel = lax.axis_index("tp")
+    parity = lax.rem(lax.axis_index("ctx"), 2)
+    copies = []
+    for index, target in enumerate((panel, panel ^ (3 - parity), panel ^ 1)):
+        columns = pl.ds(pl.multiple_of(target * width, width), width)
+        copies.append(
+            pltpu.make_async_copy(filters_ref.at[:, columns], taps_ref.at[index], sem.at[index])
+        )
+    for copy in copies:
+        copy.start()
     product_ref[...] = (hyena_ref[1].astype(jnp.float32) * hyena_ref[2].astype(jnp.float32)).astype(
         jnp.bfloat16
     )
+    for copy in copies:
+        copy.wait()
     for index, out in enumerate((own_ref, far_ref, near_ref)):
         out[...] = taps_ref[index].astype(jnp.bfloat16)
-
-
-def prepare(
-    ahead_ref, back_ref, starts_ref, skip_ref, early_ref, late_ref, back_out, starts_out, skip_out,
-    ahead_held, back_held, sem,
-):
-    pairs = (
-        (ahead_ref, ahead_held), (back_ref, back_held), (starts_ref, starts_out), (skip_ref, skip_out)
-    )
-    copies = [
-        pltpu.make_async_copy(source, out, sem.at[index])
-        for index, (source, out) in enumerate(pairs)
-    ]
-    for copy in copies:
-        copy.start()
-    for copy in copies:
-        copy.wait()
-    rows = back_out.shape[0]
-    early_ref[...] = split(ahead_held[:, :rows])
-    late_ref[...] = split(ahead_held[:, rows:])
-    back_out[...] = back_held[...].astype(jnp.bfloat16)
 
 
 def columns_of(ref, rows, index):
@@ -348,9 +331,12 @@
 
 def convolve(
     heads, other_ref, mine_ref, before_ref, own_taps_ref, starts_ref, product_ref, gate_ref, skip_ref,
-    early_ref, late_ref, back_ref, out_ref, taps_ref, filter_ref, sum_ref,
+    ahead_ref, wide_back_ref, out_ref, taps_ref, filter_ref, sum_ref, early_ref, late_ref, back_ref,
 ):
     rows = product_ref.shape[0]
+    early_ref[...] = split(ahead_ref[:, :rows])
+    late_ref[...] = split(ahead_ref[:, rows:])
+    back_ref[...] = wide_back_ref[...].astype(jnp.bfloat16)
     height, width = own_taps_ref.shape
     panel = lax.axis_index("tp")
     even = lax.rem(lax.axis_index("ctx"), 2) == 0
@@ -429,57 +415,42 @@
     def pinned(*arrays):
         return [pltpu.with_memory_space_constraint(x, pltpu.HBM) for x in arrays]
 
-    *packed, wide_taps = call(
+    packed = call(
         functools.partial(pack_heads, heads),
-        (shape((6 * rows + NOTE_ROWS, HD), bf16),) * count + (shape((3, height, channels), f32),),
-        pinned(queries, keys_values.reshape(2 * rows, heads * HD), starts, filters),
+        (shape((6 * rows + NOTE_ROWS, HD), bf16),) * count,
+        pinned(queries, keys_values.reshape(2 * rows, heads * HD), starts),
         0,
         4 * queries.size * 3,
         scratch=(
             pltpu.VMEM((1, rows), jnp.int32),
             pltpu.SemaphoreType.DMA,
-            pltpu.SemaphoreType.DMA((3,)),
             pltpu.SemaphoreType.DMA((count, 4)),
         ),
-        specs=[hbm()] * 4,
+        specs=[hbm()] * 3,
     )
     assert count == len(STEPS)
     arrived = [packed[0]] + [crossed(packed[i], "ctx", 2 * STEPS[i]) for i in range(1, count)]
     product, own_taps, far_taps, near_taps = call(
         pack_hyena,
         (shape((rows, channels), bf16),) + (shape((height, channels), bf16),) * 3,
-        (hyena_inputs, wide_taps),
+        (hyena_inputs, *pinned(filters)),
         0,
         4 * queries.size * 3,
+        scratch=(pltpu.VMEM((3, height, channels), f32), pltpu.SemaphoreType.DMA((3,))),
+        specs=[vmem(), hbm()],
     )
     axes = ("ctx", "tp")
     near_pairs, far_pairs = taps_pairs(peers, lax.axis_size("tp"))
     near_taps = lax.ppermute(near_taps, axes, near_pairs)
     far_taps = lax.ppermute(far_taps, axes, far_pairs)
     before = lax.ppermute(product, "ctx", [(i, i + 1) for i in range(peers - 1)])
-    ahead, back = twiddles(rows)
-    early, late, back, near_starts, skip = call(
-        prepare,
-        (shape((2 * rows, 2 * rows), bf16),) * 2
-        + (shape((rows, 2 * rows), bf16), shape((1, rows), jnp.int32), shape((1, channels), f32)),
-        pinned(ahead, back, starts, skip_bias.reshape(1, channels)),
-        0,
-        4 * queries.size,
-        scratch=(
-            pltpu.VMEM((2 * rows, 2 * rows), f32),
-            pltpu.VMEM((rows, 2 * rows), f32),
-            pltpu.SemaphoreType.DMA((4,)),
-        ),
-        specs=[hbm()] * 4,
-    )
-
     query, key_value = call(
         functools.partial(sort_heads, heads),
         (
             shape((count, rows + NOTE_ROWS, 2 * HD), bf16),
             shape((heads + 2, rows, 2 * HD), bf16),
         ),
-        (*arrived, near_taps, far_taps, skip),
+        (*arrived, near_taps, far_taps),
         0,
         4 * queries.size * 3,
     )
@@ -521,8 +492,8 @@
         functools.partial(convolve, heads),
         shape((rows, channels), bf16),
         (
-            other, key_value, before, own_taps, near_starts, product, hyena_inputs,
-            skip, early, late, back,
+            other, key_value, before, own_taps, starts, product, hyena_inputs,
+            skip_bias.reshape(1, channels), *twiddles(rows),
         ),
         2 * 4 * 256 * 256 * channels,
         4 * queries.size * 4,
@@ -530,6 +501,9 @@
             pltpu.VMEM((FLEN, channels), bf16),
             pltpu.VMEM((2 * rows, channels), f32),
             pltpu.VMEM((rows, channels), f32),
+            pltpu.VMEM((2 * rows, 2 * rows), bf16),
+            pltpu.VMEM((2 * rows, 2 * rows), bf16),
+            pltpu.VMEM((rows, 2 * rows), bf16),
         ),
     )
     attention_out, log_totals = call(

time: 28 us -> 27.9 us (level)
  local copies, waits for them, and re-layouts: 0.01 us -> 0.66 us
  waiting for transfers between devices: 3.16 us -> 2.61 us
    ppermute x7, waiting for transfers between devices: 3.15 us -> 1.91 us  [crossed(): lax.ppermute(array, axis, [(i, i ^ bits) for i in range(lax.axis_size(axi...]
    ppermute x1, waiting for transfers between devices: 0.01 us -> 0.7 us  [local(): far_taps = lax.ppermute(far_taps, axes, far_pairs)]
    unnamed x2 -> x10, local copies, waits for them, and re-layouts: 0.01 us -> 0.66 us
    pallas_call x9 -> x8, Pallas kernels: 8.26 us -> 8.01 us  [call(): pl.pallas_call(kernel, out_shape=out_shape, in_specs=specs or [vmem() for...]
where the time goes in v10:
time: 27.9 us; the launch traced here: 27.7 us
  starting transfers between devices  15.7 us (56%)
  Pallas kernels  8.01 us (29%)
  waiting for transfers between devices  2.61 us (9%)
  between operations  0.72 us (3%)
  local copies, waits for them, and re-layouts  0.66 us (2%)
    ppermute x7, starting transfers between devices, crossed(): lax.ppermute(array, axis, [(i, i ^ bits) for i in range(lax.axis_size(axi...  8.74 us
    pallas_call x8, Pallas kernels, call(): pl.pallas_call(kernel, out_shape=out_shape, in_specs=specs or [vmem() for...  8.01 us
    ppermute x1, starting transfers between devices, local(): far_taps = lax.ppermute(far_taps, axes, far_pairs)  4.09 us
    ppermute x1, starting transfers between devices, local(): lax.ppermute(product, 'ctx', [(i, i + 1) for i in range(peers - 1)])  2.15 us
    ppermute x7, waiting for transfers between devices, crossed(): lax.ppermute(array, axis, [(i, i ^ bits) for i in range(lax.axis_size(axi...  1.91 us
    ppermute x1, waiting for transfers between devices, local(): far_taps = lax.ppermute(far_taps, axes, far_pairs)  0.7 us
    ppermute x1, starting transfers between devices, local(): near_taps = lax.ppermute(near_taps, axes, near_pairs)  0.66 us
    unnamed x10, local copies, waits for them, and re-layouts  0.66 us
  transfers between devices with their start and end apart: 10, of which 4 were waited for; matrix products, arithmetic and copies ran while one was open for 0% of the time, Pallas kernels for 21%

profile of v10, /device:TPU:0, one launch (start us, length us, event | category | flops | bytes accessed | tf_op | source)
XLA Modules:
  0.0 27.7 jit_solution(9183858138327194014)
XLA Ops:
  0.6 1.4 %shard_map.103 = (bf16[784,128]{1,0:T(8,128)(2,1)S(1)}, bf16[784,128]{1,0:T(8,128)(2,1)S(1)}, bf16[784,128]{1,0:T(8,128)(2,1)S(1)}, bf16[784,128]{1,0:T(8,128)(2,1)S(1)}) custom-call(bf16[128,1024]{1,0:T(8,128)(2,1)} %queries_ref.1, bf16[256,1024]{1,0:T(8,128)(2,1)} %bitcast.6, s32[1,128]{1,0:T(1,128)} %bitcast.4), custom_call_target="tpu_custom_call" | custom-call | bytes 1572864 | tf_op jit(solution)/shard_map/pallas_call | solution.py:30
  2.1 3.0 %collective-permute-start = (bf16[784,128]{1,0:T(8,128)(2,1)S(1)}, bf16[784,128]{1,0:T(8,128)(2,1)S(1)}, u32[]{:S(2)}, u32[]{:S(2)}) collective-permute-start(bf16[784,128]{1,0:T(8,128)(2,1)S(1)} %get-tuple-element.23), channel_id=1, source_target_pairs={{0,16},{4,20},{8,24},{12,28},{16,0},{20,4},{24,8},{28,12},{1,17},{... | collective-permute-start | bytes 602120 | tf_op jit(solution)/shard_map/ppermute | solution.py:42
  5.1 1.5 %collective-permute-start.1 = (bf16[784,128]{1,0:T(8,128)(2,1)S(1)}, bf16[784,128]{1,0:T(8,128)(2,1)S(1)}, u32[]{:S(2)}, u32[]{:S(2)}) collective-permute-start(bf16[784,128]{1,0:T(8,128)(2,1)S(1)} %get-tuple-element.24), channel_id=1, source_target_pairs={{0,8},{4,12},{8,0},{12,4},{16,24},{20,28},{24,16},{28,20},{1,9},{5... | collective-permute-start | bytes 602120 | tf_op jit(solution)/shard_map/ppermute | solution.py:42
  6.6 0.0 collective-permute-start.2
  6.6 1.1 %shard_map.104 = (bf16[128,1024]{1,0:T(8,128)(2,1)S(1)}, bf16[32,1024]{1,0:T(8,128)(2,1)S(1)}, bf16[32,1024]{1,0:T(8,128)(2,1)S(1)}, bf16[32,1024]{1,0:T(8,128)(2,1)S(1)}) custom-call(bf16[3,128,1024]{2,1,0:T(8,128)(2,1)S(1)} %copy-done, f32[32,4096]{1,0:T(8,128)} %filters_ref.1), custom_call_target="tpu_custom_call" | custom-call | bytes 1572864 | tf_op jit(solution)/shard_map/pallas_call | solution.py:30
  7.7 0.7 %collective-permute-start.3 = (bf16[32,1024]{1,0:T(8,128)(2,1)S(1)}, bf16[32,1024]{1,0:T(8,128)(2,1)S(1)}, u32[]{:S(2)}, u32[]{:S(2)}) collective-permute-start(bf16[32,1024]{1,0:T(8,128)(2,1)S(1)} %get-tuple-element.26), channel_id=1, source_target_pairs={{4,5},{5,4},{6,7},{7,6},{12,13},{13,12},{14,15},{15,14},{20,21},{2... | collective-permute-start | bytes 196616 | tf_op jit(solution)/shard_map/ppermute | solution.py:444
  8.4 4.1 %collective-permute-start.4 = (bf16[32,1024]{1,0:T(8,128)(2,1)S(1)}, bf16[32,1024]{1,0:T(8,128)(2,1)S(1)}, u32[]{:S(2)}, u32[]{:S(2)}) collective-permute-start(bf16[32,1024]{1,0:T(8,128)(2,1)S(1)} %get-tuple-element.27), channel_id=1, source_target_pairs={{0,3},{1,2},{2,1},{3,0},{4,6},{5,7},{6,4},{7,5},{8,11},{9,10},{10,... | collective-permute-start | bytes 196616 | tf_op jit(solution)/shard_map/ppermute | solution.py:445
  12.5 0.0 collective-permute-done.3.refs_4_
  12.5 2.2 %collective-permute-start.6 = (bf16[128,1024]{1,0:T(8,128)(2,1)S(1)}, bf16[128,1024]{1,0:T(8,128)(2,1)S(1)}, u32[]{:S(2)}, u32[]{:S(2)}) collective-permute-start(bf16[128,1024]{1,0:T(8,128)(2,1)S(1)} %get-tuple-element.29.product_ref), channel_id=1, source_target_pairs={{0,4},{4,8},{8,12},{12,16},{16,20},{20,24},{24,28},{1,5},{5,9},{9,... | collective-permute-start | bytes 786440 | tf_op jit(solution)/shard_map/ppermute | solution.py:446
  14.7 0.7 %collective-permute-done.4.refs_5_ = bf16[32,1024]{1,0:T(8,128)(2,1)S(1)} collective-permute-done((bf16[32,1024]{1,0:T(8,128)(2,1)S(1)}, bf16[32,1024]{1,0:T(8,128)(2,1)S(1)}, u32[]{:S(2)}, u32[]{:S(2)}) %collective-permute-start.4) | collective-permute-done | bytes 65568 | tf_op jit(solution)/shard_map/ppermute | solution.py:445
  15.4 0.0 collective-permute-done.refs_1_
  15.4 0.0 collective-permute-done.1.refs_2_
  15.4 0.3 collective-permute-done.2.refs_3_
  15.6 0.2 shard_map.105
  15.8 0.5 %collective-permute-start.5 = (bf16[10,128,256]{2,1,0:T(8,128)(2,1)S(1)}, bf16[10,128,256]{2,1,0:T(8,128)(2,1)S(1)}, u32[]{:S(2)}, u32[]{:S(2)}) collective-permute-start(bf16[10,128,256]{2,1,0:T(8,128)(2,1)S(1)} %get-tuple-element.28.mine_ref.key_value_ref), channel_id=1, source_target_pairs={{0,4},{4,0},{8,12},{12,8},{16,20},{20,16},{24,28},{28,24},{1,5},{5... | collective-permute-start | bytes 1966088 | tf_op jit(solution)/shard_map/ppermute | solution.py:42
  16.3 1.0 %shard_map.107 = (f32[2,2,1,256]{3,2,1,0:T(1,128)S(1)}, f32[2,2,1,256]{3,2,1,0:T(1,128)S(1)}, f32[2,2,128,256]{3,2,1,0:T(8,128)S(1)}) custom-call(bf16[4,144,256]{2,1,0:T(8,128)(2,1)S(1)} %get-tuple-element.31.query_ref.refs_0_, bf16[10,128,256]{2,1,0:T(8,128)(2,1)S(1)} %get-tuple-element.28.mine_ref.key_value_ref), custom_call_target="tpu_custom_call" | custom-call | flops 26843545600 | bytes 2097152 | tf_op jit(solution)/shard_map/pallas_call | solution.py:30
  17.3 0.8 %collective-permute-done.5.other_ref.refs_4_ = bf16[10,128,256]{2,1,0:T(8,128)(2,1)S(1)} collective-permute-done((bf16[10,128,256]{2,1,0:T(8,128)(2,1)S(1)}, bf16[10,128,256]{2,1,0:T(8,128)(2,1)S(1)}, u32[]{:S(2)}, u32[]{:S(2)}) %collective-permute-start.5) | collective-permute-done | bytes 655392 | tf_op jit(solution)/shard_map/ppermute | solution.py:42
  18.1 0.8 %shard_map.108 = (bf16[272,128]{1,0:T(8,128)(2,1)S(1)}, bf16[272,128]{1,0:T(8,128)(2,1)S(1)}) custom-call(bf16[4,144,256]{2,1,0:T(8,128)(2,1)S(1)} %get-tuple-element.31.query_ref.refs_0_, f32[2,2,1,256]{3,2,1,0:T(1,128)S(1)} %get-tuple-element.32.refs_1_, f32[2,2,1,256]{3,2,1,0:T(1,128)S(1)} %get-tuple-element.33.refs_2_, ...), custom_call_target="tpu_custom_call" | custom-call | flops 134217728 | bytes 2097152 | tf_op jit(solution)/shard_map/pallas_call | solution.py:30
  18.8 1.4 %collective-permute-start.7 = (bf16[272,128]{1,0:T(8,128)(2,1)S(1)}, bf16[272,128]{1,0:T(8,128)(2,1)S(1)}, u32[]{:S(2)}, u32[]{:S(2)}) collective-permute-start(bf16[272,128]{1,0:T(8,128)(2,1)S(1)} %get-tuple-element.35.refs_5_), channel_id=1, source_target_pairs={{0,16},{4,20},{8,24},{12,28},{16,0},{20,4},{24,8},{28,12},{1,17},{... | collective-permute-start | bytes 208904 | tf_op jit(solution)/shard_map/ppermute | solution.py:42
  20.3 1.6 %collective-permute-start.8 = (bf16[272,128]{1,0:T(8,128)(2,1)S(1)}, bf16[272,128]{1,0:T(8,128)(2,1)S(1)}, u32[]{:S(2)}, u32[]{:S(2)}) collective-permute-start(bf16[272,128]{1,0:T(8,128)(2,1)S(1)} %get-tuple-element.37), channel_id=1, source_target_pairs={{0,24},{4,28},{8,16},{12,20},{16,8},{20,12},{24,0},{28,4},{1,25},{... | collective-permute-start | bytes 208904 | tf_op jit(solution)/shard_map/ppermute | solution.py:42
  21.9 0.6 %shard_map.109 = (bf16[272,128]{1,0:T(8,128)(2,1)S(1)}, bf16[272,128]{1,0:T(8,128)(2,1)S(1)}) custom-call(bf16[4,144,256]{2,1,0:T(8,128)(2,1)S(1)} %get-tuple-element.31.query_ref.refs_0_, f32[2,2,1,256]{3,2,1,0:T(1,128)S(1)} %get-tuple-element.32.refs_1_, f32[2,2,1,256]{3,2,1,0:T(1,128)S(1)} %get-tuple-element.33.refs_2_, ...), custom_call_target="tpu_custom_call" | custom-call | flops 134217728 | bytes 2097152 | tf_op jit(solution)/shard_map/pallas_call | solution.py:30
  22.5 0.0 copy-start.3
  22.5 0.6 %collective-permute-start.9 = (bf16[272,128]{1,0:T(8,128)(2,1)S(1)}, bf16[272,128]{1,0:T(8,128)(2,1)S(1)}, u32[]{:S(2)}, u32[]{:S(2)}) collective-permute-start(bf16[272,128]{1,0:T(8,128)(2,1)S(1)} %get-tuple-element.38), channel_id=1, source_target_pairs={{0,8},{4,12},{8,0},{12,4},{16,24},{20,28},{24,16},{28,20},{1,9},{5... | collective-permute-start | bytes 208904 | tf_op jit(solution)/shard_map/ppermute | solution.py:42
  23.1 0.0 collective-permute-done.6.before_ref
  23.1 0.0 copy-done.2
  23.1 0.1 copy-done.3
  23.2 0.5 %copy-done.4 = s32[128]{0:T(128)S(1)} copy-done((s32[128]{0:T(128)S(1)}, s32[128]{0:T(128)}, u32[]{:S(2)}) %copy-start.4) | copy-done | bytes 536
  23.7 2.3 %shard_map.106 = bf16[128,1024]{1,0:T(8,128)(2,1)} custom-call(bf16[10,128,256]{2,1,0:T(8,128)(2,1)S(1)} %collective-permute-done.5.other_ref.refs_4_, bf16[10,128,256]{2,1,0:T(8,128)(2,1)S(1)} %get-tuple-element.28.mine_ref.key_value_ref, bf16[128,1024]{1,0:T(8,128)(2,1)S(1)} %collective-permute-done.6.before_ref, ...), custom_call_target="tpu_custom_call" | custom-call | flops 536870912 | bytes 2097152 | tf_op jit(solution)/shard_map/pallas_call | solution.py:30
  26.0 0.0 collective-permute-done.7.refs_1_
  26.0 0.0 collective-permute-done.8.refs_2_
  26.0 0.9 %collective-permute-done.9.refs_3_ = bf16[272,128]{1,0:T(8,128)(2,1)S(1)} collective-permute-done((bf16[272,128]{1,0:T(8,128)(2,1)S(1)}, bf16[272,128]{1,0:T(8,128)(2,1)S(1)}, u32[]{:S(2)}, u32[]{:S(2)}) %collective-permute-start.9) | collective-permute-done | bytes 69664 | tf_op jit(solution)/shard_map/ppermute | solution.py:42
  26.9 0.8 %shard_map.110 = (bf16[128,1024]{1,0:T(8,128)(2,1)}, f32[8,128]{1,0:T(8,128)}) custom-call(bf16[272,128]{1,0:T(8,128)(2,1)S(1)} %get-tuple-element.36.refs_0_, bf16[272,128]{1,0:T(8,128)(2,1)S(1)} %collective-permute-done.7.refs_1_, bf16[272,128]{1,0:T(8,128)(2,1)S(1)} %collective-permute-done.8.refs_2_, bf16[272,128]{1,0:T(8,128)(2,1)S(1)} %collective-permute-done.9.refs_3_), custom_call_target="tpu_custom_call" | custom-call | bytes 524288 | tf_op jit(solution)/shard_map/pallas_call | solution.py:30
  (6 shorter events, 0.0 us)
Async XLA Ops:
  0.6 6.0 %copy-start = (bf16[3,128,1024]{2,1,0:T(8,128)(2,1)S(1)}, bf16[3,128,1024]{2,1,0:T(8,128)(2,1)}, u32[]{:S(2)}) copy-start(bf16[3,128,1024]{2,1,0:T(8,128)(2,1)} %gate_ref.1) | copy-start | bytes 2359300
  2.1 13.3 %collective-permute-start = (bf16[784,128]{1,0:T(8,128)(2,1)S(1)}, bf16[784,128]{1,0:T(8,128)(2,1)S(1)}, u32[]{:S(2)}, u32[]{:S(2)}) collective-permute-start(bf16[784,128]{1,0:T(8,128)(2,1)S(1)} %get-tuple-element.23), channel_id=1, source_target_pairs={{0,16},{4,20},{8,24},{12,28},{16,0},{20,4},{24,8},{28,12},{1,17},{... | collective-permute-start | bytes 602120 | tf_op jit(solution)/shard_map/ppermute | solution.py:42
  5.1 10.3 %collective-permute-start.1 = (bf16[784,128]{1,0:T(8,128)(2,1)S(1)}, bf16[784,128]{1,0:T(8,128)(2,1)S(1)}, u32[]{:S(2)}, u32[]{:S(2)}) collective-permute-start(bf16[784,128]{1,0:T(8,128)(2,1)S(1)} %get-tuple-element.24), channel_id=1, source_target_pairs={{0,8},{4,12},{8,0},{12,4},{16,24},{20,28},{24,16},{28,20},{1,9},{5... | collective-permute-start | bytes 602120 | tf_op jit(solution)/shard_map/ppermute | solution.py:42
  6.6 9.1 %collective-permute-start.2 = (bf16[784,128]{1,0:T(8,128)(2,1)S(1)}, bf16[784,128]{1,0:T(8,128)(2,1)S(1)}, u32[]{:S(2)}, u32[]{:S(2)}) collective-permute-start(bf16[784,128]{1,0:T(8,128)(2,1)S(1)} %get-tuple-element.25), channel_id=1, source_target_pairs={{0,24},{4,28},{8,16},{12,20},{16,8},{20,12},{24,0},{28,4},{1,25},{... | collective-permute-start | bytes 602120 | tf_op jit(solution)/shard_map/ppermute | solution.py:42
  7.7 4.8 %collective-permute-start.3 = (bf16[32,1024]{1,0:T(8,128)(2,1)S(1)}, bf16[32,1024]{1,0:T(8,128)(2,1)S(1)}, u32[]{:S(2)}, u32[]{:S(2)}) collective-permute-start(bf16[32,1024]{1,0:T(8,128)(2,1)S(1)} %get-tuple-element.26), channel_id=1, source_target_pairs={{4,5},{5,4},{6,7},{7,6},{12,13},{13,12},{14,15},{15,14},{20,21},{2... | collective-permute-start | bytes 196616 | tf_op jit(solution)/shard_map/ppermute | solution.py:444
  8.4 7.0 %collective-permute-start.4 = (bf16[32,1024]{1,0:T(8,128)(2,1)S(1)}, bf16[32,1024]{1,0:T(8,128)(2,1)S(1)}, u32[]{:S(2)}, u32[]{:S(2)}) collective-permute-start(bf16[32,1024]{1,0:T(8,128)(2,1)S(1)} %get-tuple-element.27), channel_id=1, source_target_pairs={{0,3},{1,2},{2,1},{3,0},{4,6},{5,7},{6,4},{7,5},{8,11},{9,10},{10,... | collective-permute-start | bytes 196616 | tf_op jit(solution)/shard_map/ppermute | solution.py:445
  12.5 10.6 %collective-permute-start.6 = (bf16[128,1024]{1,0:T(8,128)(2,1)S(1)}, bf16[128,1024]{1,0:T(8,128)(2,1)S(1)}, u32[]{:S(2)}, u32[]{:S(2)}) collective-permute-start(bf16[128,1024]{1,0:T(8,128)(2,1)S(1)} %get-tuple-element.29.product_ref), channel_id=1, source_target_pairs={{0,4},{4,8},{8,12},{12,16},{16,20},{20,24},{24,28},{1,5},{5,9},{9,... | collective-permute-start | bytes 786440 | tf_op jit(solution)/shard_map/ppermute | solution.py:446
  15.8 2.3 %collective-permute-start.5 = (bf16[10,128,256]{2,1,0:T(8,128)(2,1)S(1)}, bf16[10,128,256]{2,1,0:T(8,128)(2,1)S(1)}, u32[]{:S(2)}, u32[]{:S(2)}) collective-permute-start(bf16[10,128,256]{2,1,0:T(8,128)(2,1)S(1)} %get-tuple-element.28.mine_ref.key_value_ref), channel_id=1, source_target_pairs={{0,4},{4,0},{8,12},{12,8},{16,20},{20,16},{24,28},{28,24},{1,5},{5... | collective-permute-start | bytes 1966088 | tf_op jit(solution)/shard_map/ppermute | solution.py:42
  18.8 7.2 %collective-permute-start.7 = (bf16[272,128]{1,0:T(8,128)(2,1)S(1)}, bf16[272,128]{1,0:T(8,128)(2,1)S(1)}, u32[]{:S(2)}, u32[]{:S(2)}) collective-permute-start(bf16[272,128]{1,0:T(8,128)(2,1)S(1)} %get-tuple-element.35.refs_5_), channel_id=1, source_target_pairs={{0,16},{4,20},{8,24},{12,28},{16,0},{20,4},{24,8},{28,12},{1,17},{... | collective-permute-start | bytes 208904 | tf_op jit(solution)/shard_map/ppermute | solution.py:42
  20.3 2.8 %copy-start.1 = (f32[256,256]{1,0:T(8,128)S(1)}, f32[256,256]{1,0:T(8,128)}, u32[]{:S(2)}) copy-start(f32[256,256]{1,0:T(8,128)} %constant.4.clone.ahead_ref) | copy-start | bytes 786436
  20.3 2.8 %copy-start.2 = (f32[128,256]{1,0:T(8,128)S(1)}, f32[128,256]{1,0:T(8,128)}, u32[]{:S(2)}) copy-start(f32[128,256]{1,0:T(8,128)} %constant.5.clone.wide_back_ref) | copy-start | bytes 393220
  20.3 5.7 %collective-permute-start.8 = (bf16[272,128]{1,0:T(8,128)(2,1)S(1)}, bf16[272,128]{1,0:T(8,128)(2,1)S(1)}, u32[]{:S(2)}, u32[]{:S(2)}) collective-permute-start(bf16[272,128]{1,0:T(8,128)(2,1)S(1)} %get-tuple-element.37), channel_id=1, source_target_pairs={{0,24},{4,28},{8,16},{12,20},{16,8},{20,12},{24,0},{28,4},{1,25},{... | collective-permute-start | bytes 208904 | tf_op jit(solution)/shard_map/ppermute | solution.py:42
  22.5 0.7 %copy-start.3 = (f32[1024]{0:T(1024)S(1)}, f32[1024]{0:T(1024)}, u32[]{:S(2)}) copy-start(f32[1024]{0:T(1024)} %param.10) | copy-start | bytes 12292
  22.5 4.4 %collective-permute-start.9 = (bf16[272,128]{1,0:T(8,128)(2,1)S(1)}, bf16[272,128]{1,0:T(8,128)(2,1)S(1)}, u32[]{:S(2)}, u32[]{:S(2)}) collective-permute-start(bf16[272,128]{1,0:T(8,128)(2,1)S(1)} %get-tuple-element.38), channel_id=1, source_target_pairs={{0,8},{4,12},{8,0},{12,4},{16,24},{20,28},{24,16},{28,20},{1,9},{5... | collective-permute-start | bytes 208904 | tf_op jit(solution)/shard_map/ppermute | solution.py:42
  23.1 0.7 %copy-start.4 = (s32[128]{0:T(128)S(1)}, s32[128]{0:T(128)}, u32[]{:S(2)}) copy-start(s32[128]{0:T(128)} %param.13) | copy-start | bytes 1540

commit v11 on v10

--- a/solution.py
+++ b/solution.py
@@ -239,14 +239,12 @@
             mixed_ref[head, unit] = mix(sets[head], rounded)
 
 
-def attend_second(heads, mine, *refs):
+def attend_second(heads, *refs):
     count = heads // 2
-    query_ref, top_ref, total_ref, mixed_ref, other_ref, *more = refs[: -UNIT - 1]
-    outs, held_ref = refs[-UNIT - 1 : -1], refs[-1]
-    more = more[: len(more) // 2 * 2]
+    query_ref, top_ref, total_ref, mixed_ref, other_ref, *more = refs[: -count - 1]
+    outs, held_ref = refs[-count - 1 : -1], refs[-1]
     rows = query_ref.shape[1] - NOTE_ROWS
     _, pair, parity = place(heads)
-    here = pair // UNIT
 
     def one_unit(unit):
         begin = unit * UNIT
@@ -276,22 +274,18 @@
             for index, part in enumerate((high, middle, low)):
                 notes = jnp.where(line == index, part, notes)
             for index in range(UNIT):
-                held_ref[index, head * rows : (head + 1) * rows] = mixed[
+                held_ref[begin + index, head * rows : (head + 1) * rows] = mixed[
                     index * rows : (index + 1) * rows
                 ]
         for index in range(UNIT):
-            held_ref[index, 2 * rows :] = notes[:, index * rows : (index + 1) * rows].astype(
+            held_ref[begin + index, 2 * rows :] = notes[:, index * rows : (index + 1) * rows].astype(
                 jnp.bfloat16
             )
 
     for unit in range(count // UNIT):
-
-        @pl.when((here == unit) if mine else (here != unit))
-        def _():
-            one_unit(unit)
-
+        one_unit(unit)
     for step, out in enumerate(outs):
-        out[...] = held_ref[lax.rem(pair, UNIT) ^ step]
+        out[...] = held_ref[pair ^ step]
 
 
 def unpack_heads(heads, steps, *refs):
@@ -415,17 +409,13 @@
     def pinned(*arrays):
         return [pltpu.with_memory_space_constraint(x, pltpu.HBM) for x in arrays]
 
-    packed = call(
+    *packed, near_starts = call(
         functools.partial(pack_heads, heads),
-        (shape((6 * rows + NOTE_ROWS, HD), bf16),) * count,
+        (shape((6 * rows + NOTE_ROWS, HD), bf16),) * count + (shape((1, rows), jnp.int32),),
         pinned(queries, keys_values.reshape(2 * rows, heads * HD), starts),
         0,
         4 * queries.size * 3,
-        scratch=(
-            pltpu.VMEM((1, rows), jnp.int32),
-            pltpu.SemaphoreType.DMA,
-            pltpu.SemaphoreType.DMA((count, 4)),
-        ),
+        scratch=(pltpu.SemaphoreType.DMA, pltpu.SemaphoreType.DMA((count, 4))),
         specs=[hbm()] * 3,
     )
     assert count == len(STEPS)
@@ -474,25 +464,20 @@
     assert count == 2 * UNIT
     message = shape((2 * rows + NOTE_ROWS, HD), bf16)
 
-    def second(mine, *more):
-        return call(
-            functools.partial(attend_second, heads, mine),
-            (message,) * UNIT,
-            (*operands, *more),
-            (heads * rows) ** 2 * HD,
-            4 * queries.size * 4,
-            scratch=(pltpu.VMEM((UNIT, 2 * rows + NOTE_ROWS, HD), bf16),),
-        )
-
-    theirs = second(False)
-    own = second(True, theirs[0])
-    returned = [own[0], crossed(theirs[0], "ctx", 4), crossed(theirs[1], "ctx", 6)]
-    returned.append(crossed(own[1], "ctx", 2))
+    mixed = call(
+        functools.partial(attend_second, heads),
+        (message,) * count,
+        operands,
+        2 * (heads * rows) ** 2 * HD,
+        4 * queries.size * 4,
+        scratch=(pltpu.VMEM((count, 2 * rows + NOTE_ROWS, HD), bf16),),
+    )
+    returned = [mixed[0]] + [crossed(mixed[step], "ctx", 2 * step) for step in (2, 3, 1)]
     hyena_out = call(
         functools.partial(convolve, heads),
         shape((rows, channels), bf16),
         (
-            other, key_value, before, own_taps, starts, product, hyena_inputs,
+            other, key_value, before, own_taps, near_starts, product, hyena_inputs,
             skip_bias.reshape(1, channels), *twiddles(rows),
         ),
         2 * 4 * 256 * 256 * channels,

time: 27.9 us -> 27.5 us (0.986)
  local copies, waits for them, and re-layouts: 0.66 us -> 0.02 us
  Pallas kernels: 8.01 us -> 8.31 us
    unnamed x10 -> x8, local copies, waits for them, and re-layouts: 0.66 us -> 0.02 us
    pallas_call x8 -> x7, Pallas kernels: 8.01 us -> 8.31 us  [call(): pl.pallas_call(kernel, out_shape=out_shape, in_specs=specs or [vmem() for...]
  transfers between devices with their start and end apart: 10 -> 10, of which waited for: 4 -> 5; matrix products, arithmetic and copies ran while one was open for 0% -> 0% of each run, Pallas kernels for 21% -> 22%
where the time goes in v11:
time: 27.5 us; the launch traced here: 27.3 us
  starting transfers between devices  15.6 us (57%)
  Pallas kernels  8.31 us (30%)
  waiting for transfers between devices  2.69 us (10%)
  between operations  0.71 us (3%)
    ppermute x7, starting transfers between devices, crossed(): lax.ppermute(array, axis, [(i, i ^ bits) for i in range(lax.axis_size(axi...  8.69 us
    pallas_call x7, Pallas kernels, call(): pl.pallas_call(kernel, out_shape=out_shape, in_specs=specs or [vmem() for...  8.31 us
    ppermute x1, starting transfers between devices, local(): far_taps = lax.ppermute(far_taps, axes, far_pairs)  4.09 us
    ppermute x1, starting transfers between devices, local(): lax.ppermute(product, 'ctx', [(i, i + 1) for i in range(peers - 1)])  2.15 us
    ppermute x7, waiting for transfers between devices, crossed(): lax.ppermute(array, axis, [(i, i ^ bits) for i in range(lax.axis_size(axi...  1.99 us
    ppermute x1, waiting for transfers between devices, local(): far_taps = lax.ppermute(far_taps, axes, far_pairs)  0.7 us
    ppermute x1, starting transfers between devices, local(): near_taps = lax.ppermute(near_taps, axes, near_pairs)  0.66 us
  transfers between devices with their start and end apart: 10, of which 5 were waited for; matrix products, arithmetic and copies ran while one was open for 0% of the time, Pallas kernels for 22%

profile of v11, /device:TPU:0, one launch (start us, length us, event | category | flops | bytes accessed | tf_op | source)
XLA Modules:
  0.0 27.3 jit_solution(5903797005972723185)
XLA Ops:
  0.6 0.0 copy-start
  0.6 1.4 %shard_map.103 = (bf16[784,128]{1,0:T(8,128)(2,1)S(1)}, bf16[784,128]{1,0:T(8,128)(2,1)S(1)}, bf16[784,128]{1,0:T(8,128)(2,1)S(1)}, bf16[784,128]{1,0:T(8,128)(2,1)S(1)}, s32[1,128]{1,0:T(1,128)S(1)}) custom-call(bf16[128,1024]{1,0:T(8,128)(2,1)} %queries_ref.1, bf16[256,1024]{1,0:T(8,128)(2,1)} %bitcast.4, s32[1,128]{1,0:T(1,128)} %bitcast.5), custom_call_target="tpu_custom_call" | custom-call | bytes 1572864 | tf_op jit(solution)/shard_map/pallas_call | solution.py:30
  2.1 3.0 %collective-permute-start = (bf16[784,128]{1,0:T(8,128)(2,1)S(1)}, bf16[784,128]{1,0:T(8,128)(2,1)S(1)}, u32[]{:S(2)}, u32[]{:S(2)}) collective-permute-start(bf16[784,128]{1,0:T(8,128)(2,1)S(1)} %get-tuple-element.24), channel_id=1, source_target_pairs={{0,16},{4,20},{8,24},{12,28},{16,0},{20,4},{24,8},{28,12},{1,17},{... | collective-permute-start | bytes 602120 | tf_op jit(solution)/shard_map/ppermute | solution.py:42
  5.1 1.5 %collective-permute-start.1 = (bf16[784,128]{1,0:T(8,128)(2,1)S(1)}, bf16[784,128]{1,0:T(8,128)(2,1)S(1)}, u32[]{:S(2)}, u32[]{:S(2)}) collective-permute-start(bf16[784,128]{1,0:T(8,128)(2,1)S(1)} %get-tuple-element.25), channel_id=1, source_target_pairs={{0,8},{4,12},{8,0},{12,4},{16,24},{20,28},{24,16},{28,20},{1,9},{5... | collective-permute-start | bytes 602120 | tf_op jit(solution)/shard_map/ppermute | solution.py:42
  6.6 0.0 collective-permute-start.2
  6.6 0.0 copy-done
  6.6 1.1 %shard_map.104 = (bf16[128,1024]{1,0:T(8,128)(2,1)S(1)}, bf16[32,1024]{1,0:T(8,128)(2,1)S(1)}, bf16[32,1024]{1,0:T(8,128)(2,1)S(1)}, bf16[32,1024]{1,0:T(8,128)(2,1)S(1)}) custom-call(bf16[3,128,1024]{2,1,0:T(8,128)(2,1)S(1)} %copy-done, f32[32,4096]{1,0:T(8,128)} %filters_ref.1), custom_call_target="tpu_custom_call" | custom-call | bytes 1572864 | tf_op jit(solution)/shard_map/pallas_call | solution.py:30
  7.7 0.7 %collective-permute-start.3 = (bf16[32,1024]{1,0:T(8,128)(2,1)S(1)}, bf16[32,1024]{1,0:T(8,128)(2,1)S(1)}, u32[]{:S(2)}, u32[]{:S(2)}) collective-permute-start(bf16[32,1024]{1,0:T(8,128)(2,1)S(1)} %get-tuple-element.27), channel_id=1, source_target_pairs={{4,5},{5,4},{6,7},{7,6},{12,13},{13,12},{14,15},{15,14},{20,21},{2... | collective-permute-start | bytes 196616 | tf_op jit(solution)/shard_map/ppermute | solution.py:434
  8.4 4.1 %collective-permute-start.4 = (bf16[32,1024]{1,0:T(8,128)(2,1)S(1)}, bf16[32,1024]{1,0:T(8,128)(2,1)S(1)}, u32[]{:S(2)}, u32[]{:S(2)}) collective-permute-start(bf16[32,1024]{1,0:T(8,128)(2,1)S(1)} %get-tuple-element.28), channel_id=1, source_target_pairs={{0,3},{1,2},{2,1},{3,0},{4,6},{5,7},{6,4},{7,5},{8,11},{9,10},{10,... | collective-permute-start | bytes 196616 | tf_op jit(solution)/shard_map/ppermute | solution.py:435
  12.5 0.0 collective-permute-done.3.refs_4_
  12.5 2.2 %collective-permute-start.6 = (bf16[128,1024]{1,0:T(8,128)(2,1)S(1)}, bf16[128,1024]{1,0:T(8,128)(2,1)S(1)}, u32[]{:S(2)}, u32[]{:S(2)}) collective-permute-start(bf16[128,1024]{1,0:T(8,128)(2,1)S(1)} %get-tuple-element.30.product_ref), channel_id=1, source_target_pairs={{0,4},{4,8},{8,12},{12,16},{16,20},{20,24},{24,28},{1,5},{5,9},{9,... | collective-permute-start | bytes 786440 | tf_op jit(solution)/shard_map/ppermute | solution.py:436
  14.7 0.7 %collective-permute-done.4.refs_5_ = bf16[32,1024]{1,0:T(8,128)(2,1)S(1)} collective-permute-done((bf16[32,1024]{1,0:T(8,128)(2,1)S(1)}, bf16[32,1024]{1,0:T(8,128)(2,1)S(1)}, u32[]{:S(2)}, u32[]{:S(2)}) %collective-permute-start.4) | collective-permute-done | bytes 65568 | tf_op jit(solution)/shard_map/ppermute | solution.py:435
  15.4 0.0 collective-permute-done.refs_1_
  15.4 0.0 collective-permute-done.1.refs_2_
  15.4 0.3 collective-permute-done.2.refs_3_
  15.6 0.2 shard_map.105
  15.8 0.5 %collective-permute-start.5 = (bf16[10,128,256]{2,1,0:T(8,128)(2,1)S(1)}, bf16[10,128,256]{2,1,0:T(8,128)(2,1)S(1)}, u32[]{:S(2)}, u32[]{:S(2)}) collective-permute-start(bf16[10,128,256]{2,1,0:T(8,128)(2,1)S(1)} %get-tuple-element.29.mine_ref.key_value_ref), channel_id=1, source_target_pairs={{0,4},{4,0},{8,12},{12,8},{16,20},{20,16},{24,28},{28,24},{1,5},{5... | collective-permute-start | bytes 1966088 | tf_op jit(solution)/shard_map/ppermute | solution.py:42
  16.4 1.0 %shard_map.107 = (f32[2,2,1,256]{3,2,1,0:T(1,128)S(1)}, f32[2,2,1,256]{3,2,1,0:T(1,128)S(1)}, f32[2,2,128,256]{3,2,1,0:T(8,128)S(1)}) custom-call(bf16[4,144,256]{2,1,0:T(8,128)(2,1)S(1)} %get-tuple-element.33.query_ref.refs_0_, bf16[10,128,256]{2,1,0:T(8,128)(2,1)S(1)} %get-tuple-element.29.mine_ref.key_value_ref), custom_call_target="tpu_custom_call" | custom-call | flops 26843545600 | bytes 2097152 | tf_op jit(solution)/shard_map/pallas_call | solution.py:30
  17.3 0.8 %collective-permute-done.5.other_ref.refs_4_ = bf16[10,128,256]{2,1,0:T(8,128)(2,1)S(1)} collective-permute-done((bf16[10,128,256]{2,1,0:T(8,128)(2,1)S(1)}, bf16[10,128,256]{2,1,0:T(8,128)(2,1)S(1)}, u32[]{:S(2)}, u32[]{:S(2)}) %collective-permute-start.5) | collective-permute-done | bytes 655392 | tf_op jit(solution)/shard_map/ppermute | solution.py:42
  18.1 1.1 %shard_map.108 = (bf16[272,128]{1,0:T(8,128)(2,1)S(1)}, bf16[272,128]{1,0:T(8,128)(2,1)S(1)}, bf16[272,128]{1,0:T(8,128)(2,1)S(1)}, bf16[272,128]{1,0:T(8,128)(2,1)S(1)}) custom-call(bf16[4,144,256]{2,1,0:T(8,128)(2,1)S(1)} %get-tuple-element.33.query_ref.refs_0_, f32[2,2,1,256]{3,2,1,0:T(1,128)S(1)} %get-tuple-element.34.refs_1_, ...), custom_call_target="tpu_custom_call" | custom-call | flops 268435456 | bytes 2097152 | tf_op jit(solution)/shard_map/pallas_call | solution.py:30
  19.2 1.6 %collective-permute-start.7 = (bf16[272,128]{1,0:T(8,128)(2,1)S(1)}, bf16[272,128]{1,0:T(8,128)(2,1)S(1)}, u32[]{:S(2)}, u32[]{:S(2)}) collective-permute-start(bf16[272,128]{1,0:T(8,128)(2,1)S(1)} %get-tuple-element.38), channel_id=1, source_target_pairs={{0,16},{4,20},{8,24},{12,28},{16,0},{20,4},{24,8},{28,12},{1,17},{... | collective-permute-start | bytes 208904 | tf_op jit(solution)/shard_map/ppermute | solution.py:42
  20.8 1.4 %collective-permute-start.8 = (bf16[272,128]{1,0:T(8,128)(2,1)S(1)}, bf16[272,128]{1,0:T(8,128)(2,1)S(1)}, u32[]{:S(2)}, u32[]{:S(2)}) collective-permute-start(bf16[272,128]{1,0:T(8,128)(2,1)S(1)} %get-tuple-element.39), channel_id=1, source_target_pairs={{0,24},{4,28},{8,16},{12,20},{16,8},{20,12},{24,0},{28,4},{1,25},{... | collective-permute-start | bytes 208904 | tf_op jit(solution)/shard_map/ppermute | solution.py:42
  22.2 0.5 %collective-permute-start.9 = (bf16[272,128]{1,0:T(8,128)(2,1)S(1)}, bf16[272,128]{1,0:T(8,128)(2,1)S(1)}, u32[]{:S(2)}, u32[]{:S(2)}) collective-permute-start(bf16[272,128]{1,0:T(8,128)(2,1)S(1)} %get-tuple-element.40), channel_id=1, source_target_pairs={{0,8},{4,12},{8,0},{12,4},{16,24},{20,28},{24,16},{28,20},{1,9},{5... | collective-permute-start | bytes 208904 | tf_op jit(solution)/shard_map/ppermute | solution.py:42
  22.7 0.0 collective-permute-done.6.before_ref
  22.7 0.0 copy-done.1
  22.7 0.0 copy-done.2
  22.8 0.0 copy-done.3
  22.8 2.8 %shard_map.106 = bf16[128,1024]{1,0:T(8,128)(2,1)} custom-call(bf16[10,128,256]{2,1,0:T(8,128)(2,1)S(1)} %collective-permute-done.5.other_ref.refs_4_, bf16[10,128,256]{2,1,0:T(8,128)(2,1)S(1)} %get-tuple-element.29.mine_ref.key_value_ref, bf16[128,1024]{1,0:T(8,128)(2,1)S(1)} %collective-permute-done.6.before_ref, ...), custom_call_target="tpu_custom_call" | custom-call | flops 536870912 | bytes 2097152 | tf_op jit(solution)/shard_map/pallas_call | solution.py:30
  25.6 0.0 collective-permute-done.7.refs_1_
  25.6 0.9 %collective-permute-done.8.refs_2_ = bf16[272,128]{1,0:T(8,128)(2,1)S(1)} collective-permute-done((bf16[272,128]{1,0:T(8,128)(2,1)S(1)}, bf16[272,128]{1,0:T(8,128)(2,1)S(1)}, u32[]{:S(2)}, u32[]{:S(2)}) %collective-permute-start.8) | collective-permute-done | bytes 69664 | tf_op jit(solution)/shard_map/ppermute | solution.py:42
  26.5 0.1 collective-permute-done.9.refs_3_
  26.5 0.8 %shard_map.109 = (bf16[128,1024]{1,0:T(8,128)(2,1)}, f32[8,128]{1,0:T(8,128)}) custom-call(bf16[272,128]{1,0:T(8,128)(2,1)S(1)} %get-tuple-element.37.refs_0_, bf16[272,128]{1,0:T(8,128)(2,1)S(1)} %collective-permute-done.7.refs_1_, bf16[272,128]{1,0:T(8,128)(2,1)S(1)} %collective-permute-done.8.refs_2_, bf16[272,128]{1,0:T(8,128)(2,1)S(1)} %collective-permute-done.9.refs_3_), custom_call_target="tpu_custom_call" | custom-call | bytes 524288 | tf_op jit(solution)/shard_map/pallas_call | solution.py:30
  (3 shorter events, 0.0 us)
Async XLA Ops:
  0.6 6.0 %copy-start = (bf16[3,128,1024]{2,1,0:T(8,128)(2,1)S(1)}, bf16[3,128,1024]{2,1,0:T(8,128)(2,1)}, u32[]{:S(2)}) copy-start(bf16[3,128,1024]{2,1,0:T(8,128)(2,1)} %gate_ref.1) | copy-start | bytes 2359300
  2.1 13.3 %collective-permute-start = (bf16[784,128]{1,0:T(8,128)(2,1)S(1)}, bf16[784,128]{1,0:T(8,128)(2,1)S(1)}, u32[]{:S(2)}, u32[]{:S(2)}) collective-permute-start(bf16[784,128]{1,0:T(8,128)(2,1)S(1)} %get-tuple-element.24), channel_id=1, source_target_pairs={{0,16},{4,20},{8,24},{12,28},{16,0},{20,4},{24,8},{28,12},{1,17},{... | collective-permute-start | bytes 602120 | tf_op jit(solution)/shard_map/ppermute | solution.py:42
  5.1 10.3 %collective-permute-start.1 = (bf16[784,128]{1,0:T(8,128)(2,1)S(1)}, bf16[784,128]{1,0:T(8,128)(2,1)S(1)}, u32[]{:S(2)}, u32[]{:S(2)}) collective-permute-start(bf16[784,128]{1,0:T(8,128)(2,1)S(1)} %get-tuple-element.25), channel_id=1, source_target_pairs={{0,8},{4,12},{8,0},{12,4},{16,24},{20,28},{24,16},{28,20},{1,9},{5... | collective-permute-start | bytes 602120 | tf_op jit(solution)/shard_map/ppermute | solution.py:42
  6.6 9.1 %collective-permute-start.2 = (bf16[784,128]{1,0:T(8,128)(2,1)S(1)}, bf16[784,128]{1,0:T(8,128)(2,1)S(1)}, u32[]{:S(2)}, u32[]{:S(2)}) collective-permute-start(bf16[784,128]{1,0:T(8,128)(2,1)S(1)} %get-tuple-element.26), channel_id=1, source_target_pairs={{0,24},{4,28},{8,16},{12,20},{16,8},{20,12},{24,0},{28,4},{1,25},{... | collective-permute-start | bytes 602120 | tf_op jit(solution)/shard_map/ppermute | solution.py:42
  7.7 4.8 %collective-permute-start.3 = (bf16[32,1024]{1,0:T(8,128)(2,1)S(1)}, bf16[32,1024]{1,0:T(8,128)(2,1)S(1)}, u32[]{:S(2)}, u32[]{:S(2)}) collective-permute-start(bf16[32,1024]{1,0:T(8,128)(2,1)S(1)} %get-tuple-element.27), channel_id=1, source_target_pairs={{4,5},{5,4},{6,7},{7,6},{12,13},{13,12},{14,15},{15,14},{20,21},{2... | collective-permute-start | bytes 196616 | tf_op jit(solution)/shard_map/ppermute | solution.py:434
  8.4 7.0 %collective-permute-start.4 = (bf16[32,1024]{1,0:T(8,128)(2,1)S(1)}, bf16[32,1024]{1,0:T(8,128)(2,1)S(1)}, u32[]{:S(2)}, u32[]{:S(2)}) collective-permute-start(bf16[32,1024]{1,0:T(8,128)(2,1)S(1)} %get-tuple-element.28), channel_id=1, source_target_pairs={{0,3},{1,2},{2,1},{3,0},{4,6},{5,7},{6,4},{7,5},{8,11},{9,10},{10,... | collective-permute-start | bytes 196616 | tf_op jit(solution)/shard_map/ppermute | solution.py:435
  12.5 10.2 %collective-permute-start.6 = (bf16[128,1024]{1,0:T(8,128)(2,1)S(1)}, bf16[128,1024]{1,0:T(8,128)(2,1)S(1)}, u32[]{:S(2)}, u32[]{:S(2)}) collective-permute-start(bf16[128,1024]{1,0:T(8,128)(2,1)S(1)} %get-tuple-element.30.product_ref), channel_id=1, source_target_pairs={{0,4},{4,8},{8,12},{12,16},{16,20},{20,24},{24,28},{1,5},{5,9},{9,... | collective-permute-start | bytes 786440 | tf_op jit(solution)/shard_map/ppermute | solution.py:436
  15.8 2.3 %collective-permute-start.5 = (bf16[10,128,256]{2,1,0:T(8,128)(2,1)S(1)}, bf16[10,128,256]{2,1,0:T(8,128)(2,1)S(1)}, u32[]{:S(2)}, u32[]{:S(2)}) collective-permute-start(bf16[10,128,256]{2,1,0:T(8,128)(2,1)S(1)} %get-tuple-element.29.mine_ref.key_value_ref), channel_id=1, source_target_pairs={{0,4},{4,0},{8,12},{12,8},{16,20},{20,16},{24,28},{28,24},{1,5},{5... | collective-permute-start | bytes 1966088 | tf_op jit(solution)/shard_map/ppermute | solution.py:42
  18.1 4.7 %copy-start.1 = (f32[256,256]{1,0:T(8,128)S(1)}, f32[256,256]{1,0:T(8,128)}, u32[]{:S(2)}) copy-start(f32[256,256]{1,0:T(8,128)} %constant.4.clone.ahead_ref) | copy-start | bytes 786436
  18.1 4.7 %copy-start.2 = (f32[128,256]{1,0:T(8,128)S(1)}, f32[128,256]{1,0:T(8,128)}, u32[]{:S(2)}) copy-start(f32[128,256]{1,0:T(8,128)} %constant.5.clone.wide_back_ref) | copy-start | bytes 393220
  19.2 6.4 %collective-permute-start.7 = (bf16[272,128]{1,0:T(8,128)(2,1)S(1)}, bf16[272,128]{1,0:T(8,128)(2,1)S(1)}, u32[]{:S(2)}, u32[]{:S(2)}) collective-permute-start(bf16[272,128]{1,0:T(8,128)(2,1)S(1)} %get-tuple-element.38), channel_id=1, source_target_pairs={{0,16},{4,20},{8,24},{12,28},{16,0},{20,4},{24,8},{28,12},{1,17},{... | collective-permute-start | bytes 208904 | tf_op jit(solution)/shard_map/ppermute | solution.py:42
  20.8 2.0 %copy-start.3 = (f32[1024]{0:T(1024)S(1)}, f32[1024]{0:T(1024)}, u32[]{:S(2)}) copy-start(f32[1024]{0:T(1024)} %param.10) | copy-start | bytes 12292
  20.8 5.7 %collective-permute-start.8 = (bf16[272,128]{1,0:T(8,128)(2,1)S(1)}, bf16[272,128]{1,0:T(8,128)(2,1)S(1)}, u32[]{:S(2)}, u32[]{:S(2)}) collective-permute-start(bf16[272,128]{1,0:T(8,128)(2,1)S(1)} %get-tuple-element.39), channel_id=1, source_target_pairs={{0,24},{4,28},{8,16},{12,20},{16,8},{20,12},{24,0},{28,4},{1,25},{... | collective-permute-start | bytes 208904 | tf_op jit(solution)/shard_map/ppermute | solution.py:42
  22.2 4.3 %collective-permute-start.9 = (bf16[272,128]{1,0:T(8,128)(2,1)S(1)}, bf16[272,128]{1,0:T(8,128)(2,1)S(1)}, u32[]{:S(2)}, u32[]{:S(2)}) collective-permute-start(bf16[272,128]{1,0:T(8,128)(2,1)S(1)} %get-tuple-element.40), channel_id=1, source_target_pairs={{0,8},{4,12},{8,0},{12,4},{16,24},{20,28},{24,16},{28,20},{1,9},{5... | collective-permute-start | bytes 208904 | tf_op jit(solution)/shard_map/ppermute | solution.py:42

commit v12 on v10

--- a/solution.py
+++ b/solution.py
@@ -149,12 +149,10 @@
     return key, value, [(2 * block + parity) * rows + origin for block in range(blocks)], causal
 
 
-def masked_scores(sets, query, start, own, begin):
+def masked_scores(sets, turned, start, own, begin):
     held = [[] for _ in range(UNIT)]
     for key, _, firsts, causal in sets:
-        scores = lax.dot_general(
-            key, query, (((1,), (1,)), ((), ())), preferred_element_type=jnp.float32
-        )
+        scores = dot(key, turned)
         rows = key.shape[0] // len(firsts)
         line = lax.broadcasted_iota(jnp.int32, (rows, rows), 0)
         for block, first in enumerate(firsts):
@@ -221,15 +219,16 @@
 FACTOR = math.log2(math.e) / math.sqrt(HD)
 
 
-def attend_first(heads, query_ref, key_value_ref, top_ref, total_ref, mixed_ref):
+def attend_first(heads, query_ref, key_value_ref, top_ref, total_ref, mixed_ref, turned_ref):
     _, _, parity = place(heads)
     for unit in range(heads // 2 // UNIT):
         begin = unit * UNIT
         start, own = unit_rows(heads, query_ref, begin)
         sets = [[key_set(key_value_ref, begin + UNIT, head, 0, parity, True)] for head in range(2)]
+        for head in range(2):
+            turned_ref[head, unit] = unit_queries(query_ref, head, begin).T
         held = [
-            masked_scores(sets[head], unit_queries(query_ref, head, begin), start, own, begin)
-            for head in range(2)
+            masked_scores(sets[head], turned_ref[head, unit], start, own, begin) for head in range(2)
         ]
         tops = [highest(each) for each in held]
         weights = [weigh(each, top) for each, top in zip(held, tops)]
@@ -241,7 +240,7 @@
 
 def attend_second(heads, mine, *refs):
     count = heads // 2
-    query_ref, top_ref, total_ref, mixed_ref, other_ref, *more = refs[: -UNIT - 1]
+    query_ref, top_ref, total_ref, mixed_ref, turned_ref, other_ref, *more = refs[: -UNIT - 1]
     outs, held_ref = refs[-UNIT - 1 : -1], refs[-1]
     more = more[: len(more) // 2 * 2]
     rows = query_ref.shape[1] - NOTE_ROWS
@@ -256,8 +255,7 @@
             sets.append([key_set(other_ref, begin + UNIT, head, 0, 1 - parity, True)])
             for ref, side in zip(more, (parity, 1 - parity)):
                 sets[head].append(key_set(ref, count, head, -heads * rows, side, False))
-            query = unit_queries(query_ref, head, begin)
-            held.append(masked_scores(sets[head], query, start, own, begin))
+            held.append(masked_scores(sets[head], turned_ref[head, unit], start, own, begin))
         for head in range(2):
             tops.append(jnp.maximum(top_ref[head, unit], highest(held[head])))
         weights = [weigh(each, top) for each, top in zip(held, tops)]
@@ -415,17 +413,13 @@
     def pinned(*arrays):
         return [pltpu.with_memory_space_constraint(x, pltpu.HBM) for x in arrays]
 
-    packed = call(
+    *packed, near_starts = call(
         functools.partial(pack_heads, heads),
-        (shape((6 * rows + NOTE_ROWS, HD), bf16),) * count,
+        (shape((6 * rows + NOTE_ROWS, HD), bf16),) * count + (shape((1, rows), jnp.int32),),
         pinned(queries, keys_values.reshape(2 * rows, heads * HD), starts),
         0,
         4 * queries.size * 3,
-        scratch=(
-            pltpu.VMEM((1, rows), jnp.int32),
-            pltpu.SemaphoreType.DMA,
-            pltpu.SemaphoreType.DMA((count, 4)),
-        ),
+        scratch=(pltpu.SemaphoreType.DMA, pltpu.SemaphoreType.DMA((count, 4))),
         specs=[hbm()] * 3,
     )
     assert count == len(STEPS)
@@ -462,6 +456,7 @@
             shape((2, units, 1, UNIT * rows), f32),
             shape((2, units, 1, UNIT * rows), f32),
             shape((2, units, HD, UNIT * rows), f32),
+            shape((2, units, HD, UNIT * rows), bf16),
         ),
         (query, key_value),
         LONG * (heads * rows) ** 2 * HD,
@@ -492,7 +487,7 @@
         functools.partial(convolve, heads),
         shape((rows, channels), bf16),
         (
-            other, key_value, before, own_taps, starts, product, hyena_inputs,
+            other, key_value, before, own_taps, near_starts, product, hyena_inputs,
             skip_bias.reshape(1, channels), *twiddles(rows),
         ),
         2 * 4 * 256 * 256 * channels,

time: 27.9 us -> 28.7 us (1.029)
  waiting for transfers between devices: 2.61 us -> 4.09 us
  local copies, waits for them, and re-layouts: 0.66 us -> 0.02 us
    ppermute x7, waiting for transfers between devices: 1.91 us -> 3.39 us  [crossed(): lax.ppermute(array, axis, [(i, i ^ bits) for i in range(lax.axis_size(axi...]
    unnamed x10 -> x8, local copies, waits for them, and re-layouts: 0.66 us -> 0.02 us
  transfers between devices with their start and end apart: 10 -> 10, of which waited for: 4 -> 5; matrix products, arithmetic and copies ran while one was open for 0% -> 0% of each run, Pallas kernels for 21% -> 20%
where the time goes in v12:
time: 28.7 us; the launch traced here: 28.5 us
  starting transfers between devices  15.6 us (54%)
  Pallas kernels  8.03 us (28%)
  waiting for transfers between devices  4.09 us (14%)
  between operations  0.74 us (3%)
    ppermute x7, starting transfers between devices, crossed(): lax.ppermute(array, axis, [(i, i ^ bits) for i in range(lax.axis_size(axi...  8.69 us
    pallas_call x8, Pallas kernels, call(): pl.pallas_call(kernel, out_shape=out_shape, in_specs=specs or [vmem() for...  8.03 us
    ppermute x1, starting transfers between devices, local(): far_taps = lax.ppermute(far_taps, axes, far_pairs)  4.09 us
    ppermute x7, waiting for transfers between devices, crossed(): lax.ppermute(array, axis, [(i, i ^ bits) for i in range(lax.axis_size(axi...  3.39 us
    ppermute x1, starting transfers between devices, local(): lax.ppermute(product, 'ctx', [(i, i + 1) for i in range(peers - 1)])  2.15 us
    ppermute x1, waiting for transfers between devices, local(): far_taps = lax.ppermute(far_taps, axes, far_pairs)  0.7 us
    ppermute x1, starting transfers between devices, local(): near_taps = lax.ppermute(near_taps, axes, near_pairs)  0.66 us
  transfers between devices with their start and end apart: 10, of which 5 were waited for; matrix products, arithmetic and copies ran while one was open for 0% of the time, Pallas kernels for 20%

profile of v12, /device:TPU:0, one launch (start us, length us, event | category | flops | bytes accessed | tf_op | source)
XLA Modules:
  0.0 28.5 jit_solution(8668823065054910258)
XLA Ops:
  0.6 1.4 %shard_map.103 = (bf16[784,128]{1,0:T(8,128)(2,1)S(1)}, bf16[784,128]{1,0:T(8,128)(2,1)S(1)}, bf16[784,128]{1,0:T(8,128)(2,1)S(1)}, bf16[784,128]{1,0:T(8,128)(2,1)S(1)}, s32[1,128]{1,0:T(1,128)S(1)}) custom-call(bf16[128,1024]{1,0:T(8,128)(2,1)} %queries_ref.1, bf16[256,1024]{1,0:T(8,128)(2,1)} %bitcast.4, s32[1,128]{1,0:T(1,128)} %bitcast.5), custom_call_target="tpu_custom_call" | custom-call | bytes 1572864 | tf_op jit(solution)/shard_map/pallas_call | solution.py:30
  2.1 3.0 %collective-permute-start = (bf16[784,128]{1,0:T(8,128)(2,1)S(1)}, bf16[784,128]{1,0:T(8,128)(2,1)S(1)}, u32[]{:S(2)}, u32[]{:S(2)}) collective-permute-start(bf16[784,128]{1,0:T(8,128)(2,1)S(1)} %get-tuple-element.25), channel_id=1, source_target_pairs={{0,16},{4,20},{8,24},{12,28},{16,0},{20,4},{24,8},{28,12},{1,17},{... | collective-permute-start | bytes 602120 | tf_op jit(solution)/shard_map/ppermute | solution.py:42
  5.1 1.5 %collective-permute-start.1 = (bf16[784,128]{1,0:T(8,128)(2,1)S(1)}, bf16[784,128]{1,0:T(8,128)(2,1)S(1)}, u32[]{:S(2)}, u32[]{:S(2)}) collective-permute-start(bf16[784,128]{1,0:T(8,128)(2,1)S(1)} %get-tuple-element.26), channel_id=1, source_target_pairs={{0,8},{4,12},{8,0},{12,4},{16,24},{20,28},{24,16},{28,20},{1,9},{5... | collective-permute-start | bytes 602120 | tf_op jit(solution)/shard_map/ppermute | solution.py:42
  6.6 0.0 collective-permute-start.2
  6.6 1.1 %shard_map.104 = (bf16[128,1024]{1,0:T(8,128)(2,1)S(1)}, bf16[32,1024]{1,0:T(8,128)(2,1)S(1)}, bf16[32,1024]{1,0:T(8,128)(2,1)S(1)}, bf16[32,1024]{1,0:T(8,128)(2,1)S(1)}) custom-call(bf16[3,128,1024]{2,1,0:T(8,128)(2,1)S(1)} %copy-done, f32[32,4096]{1,0:T(8,128)} %filters_ref.1), custom_call_target="tpu_custom_call" | custom-call | bytes 1572864 | tf_op jit(solution)/shard_map/pallas_call | solution.py:30
  7.7 0.7 %collective-permute-start.3 = (bf16[32,1024]{1,0:T(8,128)(2,1)S(1)}, bf16[32,1024]{1,0:T(8,128)(2,1)S(1)}, u32[]{:S(2)}, u32[]{:S(2)}) collective-permute-start(bf16[32,1024]{1,0:T(8,128)(2,1)S(1)} %get-tuple-element.28), channel_id=1, source_target_pairs={{4,5},{5,4},{6,7},{7,6},{12,13},{13,12},{14,15},{15,14},{20,21},{2... | collective-permute-start | bytes 196616 | tf_op jit(solution)/shard_map/ppermute | solution.py:438
  8.4 4.1 %collective-permute-start.4 = (bf16[32,1024]{1,0:T(8,128)(2,1)S(1)}, bf16[32,1024]{1,0:T(8,128)(2,1)S(1)}, u32[]{:S(2)}, u32[]{:S(2)}) collective-permute-start(bf16[32,1024]{1,0:T(8,128)(2,1)S(1)} %get-tuple-element.29), channel_id=1, source_target_pairs={{0,3},{1,2},{2,1},{3,0},{4,6},{5,7},{6,4},{7,5},{8,11},{9,10},{10,... | collective-permute-start | bytes 196616 | tf_op jit(solution)/shard_map/ppermute | solution.py:439
  12.5 0.0 collective-permute-done.3.refs_4_
  12.5 2.2 %collective-permute-start.6 = (bf16[128,1024]{1,0:T(8,128)(2,1)S(1)}, bf16[128,1024]{1,0:T(8,128)(2,1)S(1)}, u32[]{:S(2)}, u32[]{:S(2)}) collective-permute-start(bf16[128,1024]{1,0:T(8,128)(2,1)S(1)} %get-tuple-element.31.product_ref), channel_id=1, source_target_pairs={{0,4},{4,8},{8,12},{12,16},{16,20},{20,24},{24,28},{1,5},{5,9},{9,... | collective-permute-start | bytes 786440 | tf_op jit(solution)/shard_map/ppermute | solution.py:440
  14.7 0.7 %collective-permute-done.4.refs_5_ = bf16[32,1024]{1,0:T(8,128)(2,1)S(1)} collective-permute-done((bf16[32,1024]{1,0:T(8,128)(2,1)S(1)}, bf16[32,1024]{1,0:T(8,128)(2,1)S(1)}, u32[]{:S(2)}, u32[]{:S(2)}) %collective-permute-start.4) | collective-permute-done | bytes 65568 | tf_op jit(solution)/shard_map/ppermute | solution.py:439
  15.4 0.0 collective-permute-done.refs_1_
  15.4 0.0 collective-permute-done.1.refs_2_
  15.4 0.3 collective-permute-done.2.refs_3_
  15.6 0.2 shard_map.105
  15.8 0.5 %collective-permute-start.5 = (bf16[10,128,256]{2,1,0:T(8,128)(2,1)S(1)}, bf16[10,128,256]{2,1,0:T(8,128)(2,1)S(1)}, u32[]{:S(2)}, u32[]{:S(2)}) collective-permute-start(bf16[10,128,256]{2,1,0:T(8,128)(2,1)S(1)} %get-tuple-element.30.mine_ref.key_value_ref), channel_id=1, source_target_pairs={{0,4},{4,0},{8,12},{12,8},{16,20},{20,16},{24,28},{28,24},{1,5},{5... | collective-permute-start | bytes 1966088 | tf_op jit(solution)/shard_map/ppermute | solution.py:42
  16.4 1.0 %shard_map.107 = (f32[2,2,1,256]{3,2,1,0:T(1,128)S(1)}, f32[2,2,1,256]{3,2,1,0:T(1,128)S(1)}, f32[2,2,128,256]{3,2,1,0:T(8,128)S(1)}, bf16[2,2,128,256]{3,2,1,0:T(8,128)(2,1)S(1)}) custom-call(bf16[4,144,256]{2,1,0:T(8,128)(2,1)S(1)} %get-tuple-element.34.query_ref.refs_0_, bf16[10,128,256]{2,1,0:T(8,128)(2,1)S(1)} %get-tuple-element.30.mine_ref.key_value_ref), custom_call_target="tpu_custom_call" | custom-call | flops 26843545600 | bytes 2097152 | tf_op jit(solution)/shard_map/pallas_call | solution.py:30
  17.3 0.7 %collective-permute-done.5.other_ref.refs_5_ = bf16[10,128,256]{2,1,0:T(8,128)(2,1)S(1)} collective-permute-done((bf16[10,128,256]{2,1,0:T(8,128)(2,1)S(1)}, bf16[10,128,256]{2,1,0:T(8,128)(2,1)S(1)}, u32[]{:S(2)}, u32[]{:S(2)}) %collective-permute-start.5) | collective-permute-done | bytes 655392 | tf_op jit(solution)/shard_map/ppermute | solution.py:42
  18.1 0.7 %shard_map.108 = (bf16[272,128]{1,0:T(8,128)(2,1)S(1)}, bf16[272,128]{1,0:T(8,128)(2,1)S(1)}) custom-call(bf16[4,144,256]{2,1,0:T(8,128)(2,1)S(1)} %get-tuple-element.34.query_ref.refs_0_, f32[2,2,1,256]{3,2,1,0:T(1,128)S(1)} %get-tuple-element.35.refs_1_, f32[2,2,1,256]{3,2,1,0:T(1,128)S(1)} %get-tuple-element.36.refs_2_, ...), custom_call_target="tpu_custom_call" | custom-call | flops 134217728 | bytes 2097152 | tf_op jit(solution)/shard_map/pallas_call | solution.py:30
  18.8 0.0 copy-start.1
  18.8 0.0 copy-start.2
  18.9 0.6 %shard_map.109 = (bf16[272,128]{1,0:T(8,128)(2,1)S(1)}, bf16[272,128]{1,0:T(8,128)(2,1)S(1)}) custom-call(bf16[4,144,256]{2,1,0:T(8,128)(2,1)S(1)} %get-tuple-element.34.query_ref.refs_0_, f32[2,2,1,256]{3,2,1,0:T(1,128)S(1)} %get-tuple-element.35.refs_1_, f32[2,2,1,256]{3,2,1,0:T(1,128)S(1)} %get-tuple-element.36.refs_2_, ...), custom_call_target="tpu_custom_call" | custom-call | flops 134217728 | bytes 2097152 | tf_op jit(solution)/shard_map/pallas_call | solution.py:30
  19.4 0.0 copy-start.3
  19.5 1.6 %collective-permute-start.9 = (bf16[272,128]{1,0:T(8,128)(2,1)S(1)}, bf16[272,128]{1,0:T(8,128)(2,1)S(1)}, u32[]{:S(2)}, u32[]{:S(2)}) collective-permute-start(bf16[272,128]{1,0:T(8,128)(2,1)S(1)} %get-tuple-element.42), channel_id=1, source_target_pairs={{0,8},{4,12},{8,0},{12,4},{16,24},{20,28},{24,16},{28,20},{1,9},{5... | collective-permute-start | bytes 208904 | tf_op jit(solution)/shard_map/ppermute | solution.py:42
  21.1 1.5 %collective-permute-start.8 = (bf16[272,128]{1,0:T(8,128)(2,1)S(1)}, bf16[272,128]{1,0:T(8,128)(2,1)S(1)}, u32[]{:S(2)}, u32[]{:S(2)}) collective-permute-start(bf16[272,128]{1,0:T(8,128)(2,1)S(1)} %get-tuple-element.41), channel_id=1, source_target_pairs={{0,24},{4,28},{8,16},{12,20},{16,8},{20,12},{24,0},{28,4},{1,25},{... | collective-permute-start | bytes 208904 | tf_op jit(solution)/shard_map/ppermute | solution.py:42
  22.5 0.5 %collective-permute-start.7 = (bf16[272,128]{1,0:T(8,128)(2,1)S(1)}, bf16[272,128]{1,0:T(8,128)(2,1)S(1)}, u32[]{:S(2)}, u32[]{:S(2)}) collective-permute-start(bf16[272,128]{1,0:T(8,128)(2,1)S(1)} %get-tuple-element.39.refs_6_), channel_id=1, source_target_pairs={{0,16},{4,20},{8,24},{12,28},{16,0},{20,4},{24,8},{28,12},{1,17},{... | collective-permute-start | bytes 208904 | tf_op jit(solution)/shard_map/ppermute | solution.py:42
  23.0 0.0 collective-permute-done.6.before_ref
  23.0 0.0 copy-done.2
  23.0 2.3 %shard_map.106 = bf16[128,1024]{1,0:T(8,128)(2,1)} custom-call(bf16[10,128,256]{2,1,0:T(8,128)(2,1)S(1)} %collective-permute-done.5.other_ref.refs_5_, bf16[10,128,256]{2,1,0:T(8,128)(2,1)S(1)} %get-tuple-element.30.mine_ref.key_value_ref, bf16[128,1024]{1,0:T(8,128)(2,1)S(1)} %collective-permute-done.6.before_ref, ...), custom_call_target="tpu_custom_call" | custom-call | flops 536870912 | bytes 2097152 | tf_op jit(solution)/shard_map/pallas_call | solution.py:30
  25.3 0.0 collective-permute-done.9.refs_3_
  25.3 1.2 %collective-permute-done.8.refs_2_ = bf16[272,128]{1,0:T(8,128)(2,1)S(1)} collective-permute-done((bf16[272,128]{1,0:T(8,128)(2,1)S(1)}, bf16[272,128]{1,0:T(8,128)(2,1)S(1)}, u32[]{:S(2)}, u32[]{:S(2)}) %collective-permute-start.8) | collective-permute-done | bytes 69664 | tf_op jit(solution)/shard_map/ppermute | solution.py:42
  26.5 1.2 %collective-permute-done.7.refs_1_ = bf16[272,128]{1,0:T(8,128)(2,1)S(1)} collective-permute-done((bf16[272,128]{1,0:T(8,128)(2,1)S(1)}, bf16[272,128]{1,0:T(8,128)(2,1)S(1)}, u32[]{:S(2)}, u32[]{:S(2)}) %collective-permute-start.7) | collective-permute-done | bytes 69664 | tf_op jit(solution)/shard_map/ppermute | solution.py:42
  27.7 0.8 %shard_map.110 = (bf16[128,1024]{1,0:T(8,128)(2,1)}, f32[8,128]{1,0:T(8,128)}) custom-call(bf16[272,128]{1,0:T(8,128)(2,1)S(1)} %get-tuple-element.40.refs_0_, bf16[272,128]{1,0:T(8,128)(2,1)S(1)} %collective-permute-done.7.refs_1_, bf16[272,128]{1,0:T(8,128)(2,1)S(1)} %collective-permute-done.8.refs_2_, bf16[272,128]{1,0:T(8,128)(2,1)S(1)} %collective-permute-done.9.refs_3_), custom_call_target="tpu_custom_call" | custom-call | bytes 524288 | tf_op jit(solution)/shard_map/pallas_call | solution.py:30
  (4 shorter events, 0.0 us)
Async XLA Ops:
  0.6 6.0 %copy-start = (bf16[3,128,1024]{2,1,0:T(8,128)(2,1)S(1)}, bf16[3,128,1024]{2,1,0:T(8,128)(2,1)}, u32[]{:S(2)}) copy-start(bf16[3,128,1024]{2,1,0:T(8,128)(2,1)} %gate_ref.1) | copy-start | bytes 2359300
  2.1 13.3 %collective-permute-start = (bf16[784,128]{1,0:T(8,128)(2,1)S(1)}, bf16[784,128]{1,0:T(8,128)(2,1)S(1)}, u32[]{:S(2)}, u32[]{:S(2)}) collective-permute-start(bf16[784,128]{1,0:T(8,128)(2,1)S(1)} %get-tuple-element.25), channel_id=1, source_target_pairs={{0,16},{4,20},{8,24},{12,28},{16,0},{20,4},{24,8},{28,12},{1,17},{... | collective-permute-start | bytes 602120 | tf_op jit(solution)/shard_map/ppermute | solution.py:42
  5.1 10.3 %collective-permute-start.1 = (bf16[784,128]{1,0:T(8,128)(2,1)S(1)}, bf16[784,128]{1,0:T(8,128)(2,1)S(1)}, u32[]{:S(2)}, u32[]{:S(2)}) collective-permute-start(bf16[784,128]{1,0:T(8,128)(2,1)S(1)} %get-tuple-element.26), channel_id=1, source_target_pairs={{0,8},{4,12},{8,0},{12,4},{16,24},{20,28},{24,16},{28,20},{1,9},{5... | collective-permute-start | bytes 602120 | tf_op jit(solution)/shard_map/ppermute | solution.py:42
  6.6 9.1 %collective-permute-start.2 = (bf16[784,128]{1,0:T(8,128)(2,1)S(1)}, bf16[784,128]{1,0:T(8,128)(2,1)S(1)}, u32[]{:S(2)}, u32[]{:S(2)}) collective-permute-start(bf16[784,128]{1,0:T(8,128)(2,1)S(1)} %get-tuple-element.27), channel_id=1, source_target_pairs={{0,24},{4,28},{8,16},{12,20},{16,8},{20,12},{24,0},{28,4},{1,25},{... | collective-permute-start | bytes 602120 | tf_op jit(solution)/shard_map/ppermute | solution.py:42
  7.7 4.8 %collective-permute-start.3 = (bf16[32,1024]{1,0:T(8,128)(2,1)S(1)}, bf16[32,1024]{1,0:T(8,128)(2,1)S(1)}, u32[]{:S(2)}, u32[]{:S(2)}) collective-permute-start(bf16[32,1024]{1,0:T(8,128)(2,1)S(1)} %get-tuple-element.28), channel_id=1, source_target_pairs={{4,5},{5,4},{6,7},{7,6},{12,13},{13,12},{14,15},{15,14},{20,21},{2... | collective-permute-start | bytes 196616 | tf_op jit(solution)/shard_map/ppermute | solution.py:438
  8.4 7.0 %collective-permute-start.4 = (bf16[32,1024]{1,0:T(8,128)(2,1)S(1)}, bf16[32,1024]{1,0:T(8,128)(2,1)S(1)}, u32[]{:S(2)}, u32[]{:S(2)}) collective-permute-start(bf16[32,1024]{1,0:T(8,128)(2,1)S(1)} %get-tuple-element.29), channel_id=1, source_target_pairs={{0,3},{1,2},{2,1},{3,0},{4,6},{5,7},{6,4},{7,5},{8,11},{9,10},{10,... | collective-permute-start | bytes 196616 | tf_op jit(solution)/shard_map/ppermute | solution.py:439
  12.5 10.5 %collective-permute-start.6 = (bf16[128,1024]{1,0:T(8,128)(2,1)S(1)}, bf16[128,1024]{1,0:T(8,128)(2,1)S(1)}, u32[]{:S(2)}, u32[]{:S(2)}) collective-permute-start(bf16[128,1024]{1,0:T(8,128)(2,1)S(1)} %get-tuple-element.31.product_ref), channel_id=1, source_target_pairs={{0,4},{4,8},{8,12},{12,16},{16,20},{20,24},{24,28},{1,5},{5,9},{9,... | collective-permute-start | bytes 786440 | tf_op jit(solution)/shard_map/ppermute | solution.py:440
  15.8 2.3 %collective-permute-start.5 = (bf16[10,128,256]{2,1,0:T(8,128)(2,1)S(1)}, bf16[10,128,256]{2,1,0:T(8,128)(2,1)S(1)}, u32[]{:S(2)}, u32[]{:S(2)}) collective-permute-start(bf16[10,128,256]{2,1,0:T(8,128)(2,1)S(1)} %get-tuple-element.30.mine_ref.key_value_ref), channel_id=1, source_target_pairs={{0,4},{4,0},{8,12},{12,8},{16,20},{20,16},{24,28},{28,24},{1,5},{5... | collective-permute-start | bytes 1966088 | tf_op jit(solution)/shard_map/ppermute | solution.py:42
  18.8 4.2 %copy-start.1 = (f32[256,256]{1,0:T(8,128)S(1)}, f32[256,256]{1,0:T(8,128)}, u32[]{:S(2)}) copy-start(f32[256,256]{1,0:T(8,128)} %constant.4.clone.ahead_ref) | copy-start | bytes 786436
  18.8 4.2 %copy-start.2 = (f32[128,256]{1,0:T(8,128)S(1)}, f32[128,256]{1,0:T(8,128)}, u32[]{:S(2)}) copy-start(f32[128,256]{1,0:T(8,128)} %constant.5.clone.wide_back_ref) | copy-start | bytes 393220
  19.4 3.6 %copy-start.3 = (f32[1024]{0:T(1024)S(1)}, f32[1024]{0:T(1024)}, u32[]{:S(2)}) copy-start(f32[1024]{0:T(1024)} %param.10) | copy-start | bytes 12292
  19.5 5.9 %collective-permute-start.9 = (bf16[272,128]{1,0:T(8,128)(2,1)S(1)}, bf16[272,128]{1,0:T(8,128)(2,1)S(1)}, u32[]{:S(2)}, u32[]{:S(2)}) collective-permute-start(bf16[272,128]{1,0:T(8,128)(2,1)S(1)} %get-tuple-element.42), channel_id=1, source_target_pairs={{0,8},{4,12},{8,0},{12,4},{16,24},{20,28},{24,16},{28,20},{1,9},{5... | collective-permute-start | bytes 208904 | tf_op jit(solution)/shard_map/ppermute | solution.py:42
  21.1 5.5 %collective-permute-start.8 = (bf16[272,128]{1,0:T(8,128)(2,1)S(1)}, bf16[272,128]{1,0:T(8,128)(2,1)S(1)}, u32[]{:S(2)}, u32[]{:S(2)}) collective-permute-start(bf16[272,128]{1,0:T(8,128)(2,1)S(1)} %get-tuple-element.41), channel_id=1, source_target_pairs={{0,24},{4,28},{8,16},{12,20},{16,8},{20,12},{24,0},{28,4},{1,25},{... | collective-permute-start | bytes 208904 | tf_op jit(solution)/shard_map/ppermute | solution.py:42
  22.5 5.2 %collective-permute-start.7 = (bf16[272,128]{1,0:T(8,128)(2,1)S(1)}, bf16[272,128]{1,0:T(8,128)(2,1)S(1)}, u32[]{:S(2)}, u32[]{:S(2)}) collective-permute-start(bf16[272,128]{1,0:T(8,128)(2,1)S(1)} %get-tuple-element.39.refs_6_), channel_id=1, source_target_pairs={{0,16},{4,20},{8,24},{12,28},{16,0},{20,4},{24,8},{28,12},{1,17},{... | collective-permute-start | bytes 208904 | tf_op jit(solution)/shard_map/ppermute | solution.py:42

commit v13 on v10

--- a/solution.py
+++ b/solution.py
@@ -94,7 +94,7 @@
     panel = lax.axis_index("tp")
     parity = lax.rem(lax.axis_index("ctx"), 2)
     copies = []
-    for index, target in enumerate((panel, panel ^ (3 - parity), panel ^ 1)):
+    for index, target in enumerate((panel, panel ^ (2 + parity), panel ^ 1)):
         columns = pl.ds(pl.multiple_of(target * width, width), width)
         copies.append(
             pltpu.make_async_copy(filters_ref.at[:, columns], taps_ref.at[index], sem.at[index])
@@ -351,9 +351,9 @@
         line = slice(part * height, (part + 1) * height)
         mine_far, other_far = mine_ref[heads, line], other_ref[heads, line]
         store(0, part, columns_of(own_taps_ref, everything, part))
-        store(1, part, jnp.where(even, other_ref[heads + 1, line], mine_ref[heads + 1, line]))
-        store(2, part, jnp.where(even, other_far, mine_far))
-        store(3, part, jnp.where(even, mine_far, other_far))
+        store(1, part, jnp.where(even, mine_ref[heads + 1, line], other_ref[heads + 1, line]))
+        store(2, part, jnp.where(even, mine_far, other_far))
+        store(3, part, jnp.where(even, other_far, mine_far))
     filter_ref[...] = dot(early_ref[...], twice(taps_ref[...]))
     starts = document_starts(starts_ref, rows)
     line = lax.broadcasted_iota(jnp.int32, (rows, 1), 0)
@@ -394,8 +394,8 @@
     for peer in range(peers):
         for panel in range(panels):
             here = peer * panels + panel
-            far.append((here, peer * panels + (panel ^ (3 - peer % 2))))
-            if peer % 2 == 1:
+            far.append((here, peer * panels + (panel ^ (2 + peer % 2))))
+            if peer % 2 == 0:
                 near.append((here, peer * panels + (panel ^ 1)))
     return near, far
 

time: 27.9 us -> 29.7 us (1.065)
  waiting for transfers between devices: 2.61 us -> 3.67 us
  starting transfers between devices: 15.7 us -> 16.4 us
    ppermute x1, starting transfers between devices: 0.66 us -> 3.91 us  [local(): near_taps = lax.ppermute(near_taps, axes, near_pairs)]
    ppermute x1, starting transfers between devices: 4.09 us -> 2.65 us  [local(): far_taps = lax.ppermute(far_taps, axes, far_pairs)]
    ppermute x1, waiting for transfers between devices: 0.7 us -> 1.97 us  [local(): far_taps = lax.ppermute(far_taps, axes, far_pairs)]
    ppermute x1, starting transfers between devices: 2.15 us -> 1.29 us  [local(): lax.ppermute(product, 'ctx', [(i, i + 1) for i in range(peers - 1)])]
  transfers between devices with their start and end apart: 10 -> 10, of which waited for: 4 -> 3; matrix products, arithmetic and copies ran while one was open for 0% -> 0% of each run, Pallas kernels for 21% -> 20%
where the time goes in v13:
time: 29.7 us; the launch traced here: 29.5 us
  starting transfers between devices  16.4 us (55%)
  Pallas kernels  8.01 us (27%)
  waiting for transfers between devices  3.67 us (12%)
  between operations  0.72 us (2%)
  local copies, waits for them, and re-layouts  0.66 us (2%)
    ppermute x7, starting transfers between devices, crossed(): lax.ppermute(array, axis, [(i, i ^ bits) for i in range(lax.axis_size(axi...  8.53 us
    pallas_call x8, Pallas kernels, call(): pl.pallas_call(kernel, out_shape=out_shape, in_specs=specs or [vmem() for...  8.01 us
    ppermute x1, starting transfers between devices, local(): near_taps = lax.ppermute(near_taps, axes, near_pairs)  3.91 us
    ppermute x1, starting transfers between devices, local(): far_taps = lax.ppermute(far_taps, axes, far_pairs)  2.65 us
    ppermute x1, waiting for transfers between devices, local(): far_taps = lax.ppermute(far_taps, axes, far_pairs)  1.97 us
    ppermute x7, waiting for transfers between devices, crossed(): lax.ppermute(array, axis, [(i, i ^ bits) for i in range(lax.axis_size(axi...  1.69 us
    ppermute x1, starting transfers between devices, local(): lax.ppermute(product, 'ctx', [(i, i + 1) for i in range(peers - 1)])  1.29 us
    unnamed x10, local copies, waits for them, and re-layouts  0.66 us
  transfers between devices with their start and end apart: 10, of which 3 were waited for; matrix products, arithmetic and copies ran while one was open for 0% of the time, Pallas kernels for 20%

profile of v13, /device:TPU:0, one launch (start us, length us, event | category | flops | bytes accessed | tf_op | source)
XLA Modules:
  0.0 29.5 jit_solution(18231699668741147931)
XLA Ops:
  0.6 1.4 %shard_map.103 = (bf16[784,128]{1,0:T(8,128)(2,1)S(1)}, bf16[784,128]{1,0:T(8,128)(2,1)S(1)}, bf16[784,128]{1,0:T(8,128)(2,1)S(1)}, bf16[784,128]{1,0:T(8,128)(2,1)S(1)}) custom-call(bf16[128,1024]{1,0:T(8,128)(2,1)} %queries_ref.1, bf16[256,1024]{1,0:T(8,128)(2,1)} %bitcast.6, s32[1,128]{1,0:T(1,128)} %bitcast.4), custom_call_target="tpu_custom_call" | custom-call | bytes 1572864 | tf_op jit(solution)/shard_map/pallas_call | solution.py:30
  2.1 3.0 %collective-permute-start = (bf16[784,128]{1,0:T(8,128)(2,1)S(1)}, bf16[784,128]{1,0:T(8,128)(2,1)S(1)}, u32[]{:S(2)}, u32[]{:S(2)}) collective-permute-start(bf16[784,128]{1,0:T(8,128)(2,1)S(1)} %get-tuple-element.23), channel_id=1, source_target_pairs={{0,16},{4,20},{8,24},{12,28},{16,0},{20,4},{24,8},{28,12},{1,17},{... | collective-permute-start | bytes 602120 | tf_op jit(solution)/shard_map/ppermute | solution.py:42
  5.1 1.5 %collective-permute-start.1 = (bf16[784,128]{1,0:T(8,128)(2,1)S(1)}, bf16[784,128]{1,0:T(8,128)(2,1)S(1)}, u32[]{:S(2)}, u32[]{:S(2)}) collective-permute-start(bf16[784,128]{1,0:T(8,128)(2,1)S(1)} %get-tuple-element.24), channel_id=1, source_target_pairs={{0,8},{4,12},{8,0},{12,4},{16,24},{20,28},{24,16},{28,20},{1,9},{5... | collective-permute-start | bytes 602120 | tf_op jit(solution)/shard_map/ppermute | solution.py:42
  6.6 0.0 collective-permute-start.2
  6.6 1.1 %shard_map.104 = (bf16[128,1024]{1,0:T(8,128)(2,1)S(1)}, bf16[32,1024]{1,0:T(8,128)(2,1)S(1)}, bf16[32,1024]{1,0:T(8,128)(2,1)S(1)}, bf16[32,1024]{1,0:T(8,128)(2,1)S(1)}) custom-call(bf16[3,128,1024]{2,1,0:T(8,128)(2,1)S(1)} %copy-done, f32[32,4096]{1,0:T(8,128)} %filters_ref.1), custom_call_target="tpu_custom_call" | custom-call | bytes 1572864 | tf_op jit(solution)/shard_map/pallas_call | solution.py:30
  7.7 3.9 %collective-permute-start.3 = (bf16[32,1024]{1,0:T(8,128)(2,1)S(1)}, bf16[32,1024]{1,0:T(8,128)(2,1)S(1)}, u32[]{:S(2)}, u32[]{:S(2)}) collective-permute-start(bf16[32,1024]{1,0:T(8,128)(2,1)S(1)} %get-tuple-element.26), channel_id=1, source_target_pairs={{0,1},{1,0},{2,3},{3,2},{8,9},{9,8},{10,11},{11,10},{16,17},{17,16... | collective-permute-start | bytes 196616 | tf_op jit(solution)/shard_map/ppermute | solution.py:444
  11.7 2.7 %collective-permute-start.4 = (bf16[32,1024]{1,0:T(8,128)(2,1)S(1)}, bf16[32,1024]{1,0:T(8,128)(2,1)S(1)}, u32[]{:S(2)}, u32[]{:S(2)}) collective-permute-start(bf16[32,1024]{1,0:T(8,128)(2,1)S(1)} %get-tuple-element.27), channel_id=1, source_target_pairs={{0,2},{1,3},{2,0},{3,1},{4,7},{5,6},{6,5},{7,4},{8,10},{9,11},{10,... | collective-permute-start | bytes 196616 | tf_op jit(solution)/shard_map/ppermute | solution.py:445
  14.3 0.0 collective-permute-done.3.refs_4_
  14.3 1.3 %collective-permute-start.6 = (bf16[128,1024]{1,0:T(8,128)(2,1)S(1)}, bf16[128,1024]{1,0:T(8,128)(2,1)S(1)}, u32[]{:S(2)}, u32[]{:S(2)}) collective-permute-start(bf16[128,1024]{1,0:T(8,128)(2,1)S(1)} %get-tuple-element.29.product_ref), channel_id=1, source_target_pairs={{0,4},{4,8},{8,12},{12,16},{16,20},{20,24},{24,28},{1,5},{5,9},{9,... | collective-permute-start | bytes 786440 | tf_op jit(solution)/shard_map/ppermute | solution.py:446
  15.6 2.0 %collective-permute-done.4.refs_5_ = bf16[32,1024]{1,0:T(8,128)(2,1)S(1)} collective-permute-done((bf16[32,1024]{1,0:T(8,128)(2,1)S(1)}, bf16[32,1024]{1,0:T(8,128)(2,1)S(1)}, u32[]{:S(2)}, u32[]{:S(2)}) %collective-permute-start.4) | collective-permute-done | bytes 65568 | tf_op jit(solution)/shard_map/ppermute | solution.py:445
  17.6 0.0 collective-permute-done.refs_1_
  17.6 0.0 collective-permute-done.1.refs_2_
  17.6 0.0 collective-permute-done.2.refs_3_
  17.6 0.2 shard_map.105
  17.8 0.3 %collective-permute-start.5 = (bf16[10,128,256]{2,1,0:T(8,128)(2,1)S(1)}, bf16[10,128,256]{2,1,0:T(8,128)(2,1)S(1)}, u32[]{:S(2)}, u32[]{:S(2)}) collective-permute-start(bf16[10,128,256]{2,1,0:T(8,128)(2,1)S(1)} %get-tuple-element.28.mine_ref.key_value_ref), channel_id=1, source_target_pairs={{0,4},{4,0},{8,12},{12,8},{16,20},{20,16},{24,28},{28,24},{1,5},{5... | collective-permute-start | bytes 1966088 | tf_op jit(solution)/shard_map/ppermute | solution.py:42
  18.1 1.0 %shard_map.107 = (f32[2,2,1,256]{3,2,1,0:T(1,128)S(1)}, f32[2,2,1,256]{3,2,1,0:T(1,128)S(1)}, f32[2,2,128,256]{3,2,1,0:T(8,128)S(1)}) custom-call(bf16[4,144,256]{2,1,0:T(8,128)(2,1)S(1)} %get-tuple-element.31.query_ref.refs_0_, bf16[10,128,256]{2,1,0:T(8,128)(2,1)S(1)} %get-tuple-element.28.mine_ref.key_value_ref), custom_call_target="tpu_custom_call" | custom-call | flops 26843545600 | bytes 2097152 | tf_op jit(solution)/shard_map/pallas_call | solution.py:30
  19.1 0.9 %collective-permute-done.5.other_ref.refs_4_ = bf16[10,128,256]{2,1,0:T(8,128)(2,1)S(1)} collective-permute-done((bf16[10,128,256]{2,1,0:T(8,128)(2,1)S(1)}, bf16[10,128,256]{2,1,0:T(8,128)(2,1)S(1)}, u32[]{:S(2)}, u32[]{:S(2)}) %collective-permute-start.5) | collective-permute-done | bytes 655392 | tf_op jit(solution)/shard_map/ppermute | solution.py:42
  19.9 0.8 %shard_map.108 = (bf16[272,128]{1,0:T(8,128)(2,1)S(1)}, bf16[272,128]{1,0:T(8,128)(2,1)S(1)}) custom-call(bf16[4,144,256]{2,1,0:T(8,128)(2,1)S(1)} %get-tuple-element.31.query_ref.refs_0_, f32[2,2,1,256]{3,2,1,0:T(1,128)S(1)} %get-tuple-element.32.refs_1_, f32[2,2,1,256]{3,2,1,0:T(1,128)S(1)} %get-tuple-element.33.refs_2_, ...), custom_call_target="tpu_custom_call" | custom-call | flops 134217728 | bytes 2097152 | tf_op jit(solution)/shard_map/pallas_call | solution.py:30
  20.7 1.4 %collective-permute-start.7 = (bf16[272,128]{1,0:T(8,128)(2,1)S(1)}, bf16[272,128]{1,0:T(8,128)(2,1)S(1)}, u32[]{:S(2)}, u32[]{:S(2)}) collective-permute-start(bf16[272,128]{1,0:T(8,128)(2,1)S(1)} %get-tuple-element.35.refs_5_), channel_id=1, source_target_pairs={{0,16},{4,20},{8,24},{12,28},{16,0},{20,4},{24,8},{28,12},{1,17},{... | collective-permute-start | bytes 208904 | tf_op jit(solution)/shard_map/ppermute | solution.py:42
  22.1 1.6 %collective-permute-start.8 = (bf16[272,128]{1,0:T(8,128)(2,1)S(1)}, bf16[272,128]{1,0:T(8,128)(2,1)S(1)}, u32[]{:S(2)}, u32[]{:S(2)}) collective-permute-start(bf16[272,128]{1,0:T(8,128)(2,1)S(1)} %get-tuple-element.37), channel_id=1, source_target_pairs={{0,24},{4,28},{8,16},{12,20},{16,8},{20,12},{24,0},{28,4},{1,25},{... | collective-permute-start | bytes 208904 | tf_op jit(solution)/shard_map/ppermute | solution.py:42
  23.7 0.6 %shard_map.109 = (bf16[272,128]{1,0:T(8,128)(2,1)S(1)}, bf16[272,128]{1,0:T(8,128)(2,1)S(1)}) custom-call(bf16[4,144,256]{2,1,0:T(8,128)(2,1)S(1)} %get-tuple-element.31.query_ref.refs_0_, f32[2,2,1,256]{3,2,1,0:T(1,128)S(1)} %get-tuple-element.32.refs_1_, f32[2,2,1,256]{3,2,1,0:T(1,128)S(1)} %get-tuple-element.33.refs_2_, ...), custom_call_target="tpu_custom_call" | custom-call | flops 134217728 | bytes 2097152 | tf_op jit(solution)/shard_map/pallas_call | solution.py:30
  24.3 0.0 copy-start.3
  24.3 0.6 %collective-permute-start.9 = (bf16[272,128]{1,0:T(8,128)(2,1)S(1)}, bf16[272,128]{1,0:T(8,128)(2,1)S(1)}, u32[]{:S(2)}, u32[]{:S(2)}) collective-permute-start(bf16[272,128]{1,0:T(8,128)(2,1)S(1)} %get-tuple-element.38), channel_id=1, source_target_pairs={{0,8},{4,12},{8,0},{12,4},{16,24},{20,28},{24,16},{28,20},{1,9},{5... | collective-permute-start | bytes 208904 | tf_op jit(solution)/shard_map/ppermute | solution.py:42
  24.9 0.0 collective-permute-done.6.before_ref
  24.9 0.0 copy-done.1
  24.9 0.1 copy-done.3
  25.0 0.6 %copy-done.4 = s32[128]{0:T(128)S(1)} copy-done((s32[128]{0:T(128)S(1)}, s32[128]{0:T(128)}, u32[]{:S(2)}) %copy-start.4) | copy-done | bytes 536
  25.6 2.3 %shard_map.106 = bf16[128,1024]{1,0:T(8,128)(2,1)} custom-call(bf16[10,128,256]{2,1,0:T(8,128)(2,1)S(1)} %collective-permute-done.5.other_ref.refs_4_, bf16[10,128,256]{2,1,0:T(8,128)(2,1)S(1)} %get-tuple-element.28.mine_ref.key_value_ref, bf16[128,1024]{1,0:T(8,128)(2,1)S(1)} %collective-permute-done.6.before_ref, ...), custom_call_target="tpu_custom_call" | custom-call | flops 536870912 | bytes 2097152 | tf_op jit(solution)/shard_map/pallas_call | solution.py:30
  27.8 0.0 collective-permute-done.7.refs_1_
  27.8 0.0 collective-permute-done.8.refs_2_
  27.8 0.8 %collective-permute-done.9.refs_3_ = bf16[272,128]{1,0:T(8,128)(2,1)S(1)} collective-permute-done((bf16[272,128]{1,0:T(8,128)(2,1)S(1)}, bf16[272,128]{1,0:T(8,128)(2,1)S(1)}, u32[]{:S(2)}, u32[]{:S(2)}) %collective-permute-start.9) | collective-permute-done | bytes 69664 | tf_op jit(solution)/shard_map/ppermute | solution.py:42
  28.7 0.8 %shard_map.110 = (bf16[128,1024]{1,0:T(8,128)(2,1)}, f32[8,128]{1,0:T(8,128)}) custom-call(bf16[272,128]{1,0:T(8,128)(2,1)S(1)} %get-tuple-element.36.refs_0_, bf16[272,128]{1,0:T(8,128)(2,1)S(1)} %collective-permute-done.7.refs_1_, bf16[272,128]{1,0:T(8,128)(2,1)S(1)} %collective-permute-done.8.refs_2_, bf16[272,128]{1,0:T(8,128)(2,1)S(1)} %collective-permute-done.9.refs_3_), custom_call_target="tpu_custom_call" | custom-call | bytes 524288 | tf_op jit(solution)/shard_map/pallas_call | solution.py:30
  (6 shorter events, 0.0 us)
Async XLA Ops:
  0.6 6.0 %copy-start = (bf16[3,128,1024]{2,1,0:T(8,128)(2,1)S(1)}, bf16[3,128,1024]{2,1,0:T(8,128)(2,1)}, u32[]{:S(2)}) copy-start(bf16[3,128,1024]{2,1,0:T(8,128)(2,1)} %gate_ref.1) | copy-start | bytes 2359300
  2.1 15.5 %collective-permute-start = (bf16[784,128]{1,0:T(8,128)(2,1)S(1)}, bf16[784,128]{1,0:T(8,128)(2,1)S(1)}, u32[]{:S(2)}, u32[]{:S(2)}) collective-permute-start(bf16[784,128]{1,0:T(8,128)(2,1)S(1)} %get-tuple-element.23), channel_id=1, source_target_pairs={{0,16},{4,20},{8,24},{12,28},{16,0},{20,4},{24,8},{28,12},{1,17},{... | collective-permute-start | bytes 602120 | tf_op jit(solution)/shard_map/ppermute | solution.py:42
  5.1 12.5 %collective-permute-start.1 = (bf16[784,128]{1,0:T(8,128)(2,1)S(1)}, bf16[784,128]{1,0:T(8,128)(2,1)S(1)}, u32[]{:S(2)}, u32[]{:S(2)}) collective-permute-start(bf16[784,128]{1,0:T(8,128)(2,1)S(1)} %get-tuple-element.24), channel_id=1, source_target_pairs={{0,8},{4,12},{8,0},{12,4},{16,24},{20,28},{24,16},{28,20},{1,9},{5... | collective-permute-start | bytes 602120 | tf_op jit(solution)/shard_map/ppermute | solution.py:42
  6.6 11.0 %collective-permute-start.2 = (bf16[784,128]{1,0:T(8,128)(2,1)S(1)}, bf16[784,128]{1,0:T(8,128)(2,1)S(1)}, u32[]{:S(2)}, u32[]{:S(2)}) collective-permute-start(bf16[784,128]{1,0:T(8,128)(2,1)S(1)} %get-tuple-element.25), channel_id=1, source_target_pairs={{0,24},{4,28},{8,16},{12,20},{16,8},{20,12},{24,0},{28,4},{1,25},{... | collective-permute-start | bytes 602120 | tf_op jit(solution)/shard_map/ppermute | solution.py:42
  7.7 6.6 %collective-permute-start.3 = (bf16[32,1024]{1,0:T(8,128)(2,1)S(1)}, bf16[32,1024]{1,0:T(8,128)(2,1)S(1)}, u32[]{:S(2)}, u32[]{:S(2)}) collective-permute-start(bf16[32,1024]{1,0:T(8,128)(2,1)S(1)} %get-tuple-element.26), channel_id=1, source_target_pairs={{0,1},{1,0},{2,3},{3,2},{8,9},{9,8},{10,11},{11,10},{16,17},{17,16... | collective-permute-start | bytes 196616 | tf_op jit(solution)/shard_map/ppermute | solution.py:444
  11.7 5.9 %collective-permute-start.4 = (bf16[32,1024]{1,0:T(8,128)(2,1)S(1)}, bf16[32,1024]{1,0:T(8,128)(2,1)S(1)}, u32[]{:S(2)}, u32[]{:S(2)}) collective-permute-start(bf16[32,1024]{1,0:T(8,128)(2,1)S(1)} %get-tuple-element.27), channel_id=1, source_target_pairs={{0,2},{1,3},{2,0},{3,1},{4,7},{5,6},{6,5},{7,4},{8,10},{9,11},{10,... | collective-permute-start | bytes 196616 | tf_op jit(solution)/shard_map/ppermute | solution.py:445
  14.3 10.6 %collective-permute-start.6 = (bf16[128,1024]{1,0:T(8,128)(2,1)S(1)}, bf16[128,1024]{1,0:T(8,128)(2,1)S(1)}, u32[]{:S(2)}, u32[]{:S(2)}) collective-permute-start(bf16[128,1024]{1,0:T(8,128)(2,1)S(1)} %get-tuple-element.29.product_ref), channel_id=1, source_target_pairs={{0,4},{4,8},{8,12},{12,16},{16,20},{20,24},{24,28},{1,5},{5,9},{9,... | collective-permute-start | bytes 786440 | tf_op jit(solution)/shard_map/ppermute | solution.py:446
  17.8 2.2 %collective-permute-start.5 = (bf16[10,128,256]{2,1,0:T(8,128)(2,1)S(1)}, bf16[10,128,256]{2,1,0:T(8,128)(2,1)S(1)}, u32[]{:S(2)}, u32[]{:S(2)}) collective-permute-start(bf16[10,128,256]{2,1,0:T(8,128)(2,1)S(1)} %get-tuple-element.28.mine_ref.key_value_ref), channel_id=1, source_target_pairs={{0,4},{4,0},{8,12},{12,8},{16,20},{20,16},{24,28},{28,24},{1,5},{5... | collective-permute-start | bytes 1966088 | tf_op jit(solution)/shard_map/ppermute | solution.py:42
  20.7 7.1 %collective-permute-start.7 = (bf16[272,128]{1,0:T(8,128)(2,1)S(1)}, bf16[272,128]{1,0:T(8,128)(2,1)S(1)}, u32[]{:S(2)}, u32[]{:S(2)}) collective-permute-start(bf16[272,128]{1,0:T(8,128)(2,1)S(1)} %get-tuple-element.35.refs_5_), channel_id=1, source_target_pairs={{0,16},{4,20},{8,24},{12,28},{16,0},{20,4},{24,8},{28,12},{1,17},{... | collective-permute-start | bytes 208904 | tf_op jit(solution)/shard_map/ppermute | solution.py:42
  22.1 2.8 %copy-start.1 = (f32[256,256]{1,0:T(8,128)S(1)}, f32[256,256]{1,0:T(8,128)}, u32[]{:S(2)}) copy-start(f32[256,256]{1,0:T(8,128)} %constant.4.clone.ahead_ref) | copy-start | bytes 786436
  22.1 2.8 %copy-start.2 = (f32[128,256]{1,0:T(8,128)S(1)}, f32[128,256]{1,0:T(8,128)}, u32[]{:S(2)}) copy-start(f32[128,256]{1,0:T(8,128)} %constant.5.clone.wide_back_ref) | copy-start | bytes 393220
  22.1 5.8 %collective-permute-start.8 = (bf16[272,128]{1,0:T(8,128)(2,1)S(1)}, bf16[272,128]{1,0:T(8,128)(2,1)S(1)}, u32[]{:S(2)}, u32[]{:S(2)}) collective-permute-start(bf16[272,128]{1,0:T(8,128)(2,1)S(1)} %get-tuple-element.37), channel_id=1, source_target_pairs={{0,24},{4,28},{8,16},{12,20},{16,8},{20,12},{24,0},{28,4},{1,25},{... | collective-permute-start | bytes 208904 | tf_op jit(solution)/shard_map/ppermute | solution.py:42
  24.3 0.7 %copy-start.3 = (f32[1024]{0:T(1024)S(1)}, f32[1024]{0:T(1024)}, u32[]{:S(2)}) copy-start(f32[1024]{0:T(1024)} %param.10) | copy-start | bytes 12292
  24.3 4.4 %collective-permute-start.9 = (bf16[272,128]{1,0:T(8,128)(2,1)S(1)}, bf16[272,128]{1,0:T(8,128)(2,1)S(1)}, u32[]{:S(2)}, u32[]{:S(2)}) collective-permute-start(bf16[272,128]{1,0:T(8,128)(2,1)S(1)} %get-tuple-element.38), channel_id=1, source_target_pairs={{0,8},{4,12},{8,0},{12,4},{16,24},{20,28},{24,16},{28,20},{1,9},{5... | collective-permute-start | bytes 208904 | tf_op jit(solution)/shard_map/ppermute | solution.py:42
  24.9 0.7 %copy-start.4 = (s32[128]{0:T(128)S(1)}, s32[128]{0:T(128)}, u32[]{:S(2)}) copy-start(s32[128]{0:T(128)} %param.13) | copy-start | bytes 1540

commit v14 on v10

--- a/solution.py
+++ b/solution.py
@@ -415,17 +415,13 @@
     def pinned(*arrays):
         return [pltpu.with_memory_space_constraint(x, pltpu.HBM) for x in arrays]
 
-    packed = call(
+    *packed, near_starts = call(
         functools.partial(pack_heads, heads),
-        (shape((6 * rows + NOTE_ROWS, HD), bf16),) * count,
+        (shape((6 * rows + NOTE_ROWS, HD), bf16),) * count + (shape((1, rows), jnp.int32),),
         pinned(queries, keys_values.reshape(2 * rows, heads * HD), starts),
         0,
         4 * queries.size * 3,
-        scratch=(
-            pltpu.VMEM((1, rows), jnp.int32),
-            pltpu.SemaphoreType.DMA,
-            pltpu.SemaphoreType.DMA((count, 4)),
-        ),
+        scratch=(pltpu.SemaphoreType.DMA, pltpu.SemaphoreType.DMA((count, 4))),
         specs=[hbm()] * 3,
     )
     assert count == len(STEPS)
@@ -492,7 +488,7 @@
         functools.partial(convolve, heads),
         shape((rows, channels), bf16),
         (
-            other, key_value, before, own_taps, starts, product, hyena_inputs,
+            other, key_value, before, own_taps, near_starts, product, hyena_inputs,
             skip_bias.reshape(1, channels), *twiddles(rows),
         ),
         2 * 4 * 256 * 256 * channels,

time: 27.9 us -> 27.9 us (level)
  local copies, waits for them, and re-layouts: 0.66 us -> 0.12 us
  waiting for transfers between devices: 2.61 us -> 3.15 us
    ppermute x7, waiting for transfers between devices: 1.91 us -> 2.45 us  [crossed(): lax.ppermute(array, axis, [(i, i ^ bits) for i in range(lax.axis_size(axi...]
    unnamed x10 -> x8, local copies, waits for them, and re-layouts: 0.66 us -> 0.12 us
where the time goes in v14:
time: 27.9 us; the launch traced here: 27.7 us
  starting transfers between devices  15.6 us (56%)
  Pallas kernels  8.02 us (29%)
  waiting for transfers between devices  3.15 us (11%)
  between operations  0.72 us (3%)
    ppermute x7, starting transfers between devices, crossed(): lax.ppermute(array, axis, [(i, i ^ bits) for i in range(lax.axis_size(axi...  8.74 us
    pallas_call x8, Pallas kernels, call(): pl.pallas_call(kernel, out_shape=out_shape, in_specs=specs or [vmem() for...  8.02 us
    ppermute x1, starting transfers between devices, local(): far_taps = lax.ppermute(far_taps, axes, far_pairs)  4.09 us
    ppermute x7, waiting for transfers between devices, crossed(): lax.ppermute(array, axis, [(i, i ^ bits) for i in range(lax.axis_size(axi...  2.45 us
    ppermute x1, starting transfers between devices, local(): lax.ppermute(product, 'ctx', [(i, i + 1) for i in range(peers - 1)])  2.15 us
    ppermute x1, waiting for transfers between devices, local(): far_taps = lax.ppermute(far_taps, axes, far_pairs)  0.7 us
    ppermute x1, starting transfers between devices, local(): near_taps = lax.ppermute(near_taps, axes, near_pairs)  0.66 us
  transfers between devices with their start and end apart: 10, of which 4 were waited for; matrix products, arithmetic and copies ran while one was open for 0% of the time, Pallas kernels for 21%

profile of v14, /device:TPU:0, one launch (start us, length us, event | category | flops | bytes accessed | tf_op | source)
XLA Modules:
  0.0 27.7 jit_solution(5690672188624972133)
XLA Ops:
  0.6 0.0 copy-start
  0.6 1.4 %shard_map.103 = (bf16[784,128]{1,0:T(8,128)(2,1)S(1)}, bf16[784,128]{1,0:T(8,128)(2,1)S(1)}, bf16[784,128]{1,0:T(8,128)(2,1)S(1)}, bf16[784,128]{1,0:T(8,128)(2,1)S(1)}, s32[1,128]{1,0:T(1,128)S(1)}) custom-call(bf16[128,1024]{1,0:T(8,128)(2,1)} %queries_ref.1, bf16[256,1024]{1,0:T(8,128)(2,1)} %bitcast.4, s32[1,128]{1,0:T(1,128)} %bitcast.5), custom_call_target="tpu_custom_call" | custom-call | bytes 1572864 | tf_op jit(solution)/shard_map/pallas_call | solution.py:30
  2.1 3.0 %collective-permute-start = (bf16[784,128]{1,0:T(8,128)(2,1)S(1)}, bf16[784,128]{1,0:T(8,128)(2,1)S(1)}, u32[]{:S(2)}, u32[]{:S(2)}) collective-permute-start(bf16[784,128]{1,0:T(8,128)(2,1)S(1)} %get-tuple-element.24), channel_id=1, source_target_pairs={{0,16},{4,20},{8,24},{12,28},{16,0},{20,4},{24,8},{28,12},{1,17},{... | collective-permute-start | bytes 602120 | tf_op jit(solution)/shard_map/ppermute | solution.py:42
  5.1 1.5 %collective-permute-start.1 = (bf16[784,128]{1,0:T(8,128)(2,1)S(1)}, bf16[784,128]{1,0:T(8,128)(2,1)S(1)}, u32[]{:S(2)}, u32[]{:S(2)}) collective-permute-start(bf16[784,128]{1,0:T(8,128)(2,1)S(1)} %get-tuple-element.25), channel_id=1, source_target_pairs={{0,8},{4,12},{8,0},{12,4},{16,24},{20,28},{24,16},{28,20},{1,9},{5... | collective-permute-start | bytes 602120 | tf_op jit(solution)/shard_map/ppermute | solution.py:42
  6.6 0.0 collective-permute-start.2
  6.6 1.1 %shard_map.104 = (bf16[128,1024]{1,0:T(8,128)(2,1)S(1)}, bf16[32,1024]{1,0:T(8,128)(2,1)S(1)}, bf16[32,1024]{1,0:T(8,128)(2,1)S(1)}, bf16[32,1024]{1,0:T(8,128)(2,1)S(1)}) custom-call(bf16[3,128,1024]{2,1,0:T(8,128)(2,1)S(1)} %copy-done, f32[32,4096]{1,0:T(8,128)} %filters_ref.1), custom_call_target="tpu_custom_call" | custom-call | bytes 1572864 | tf_op jit(solution)/shard_map/pallas_call | solution.py:30
  7.7 0.7 %collective-permute-start.3 = (bf16[32,1024]{1,0:T(8,128)(2,1)S(1)}, bf16[32,1024]{1,0:T(8,128)(2,1)S(1)}, u32[]{:S(2)}, u32[]{:S(2)}) collective-permute-start(bf16[32,1024]{1,0:T(8,128)(2,1)S(1)} %get-tuple-element.27), channel_id=1, source_target_pairs={{4,5},{5,4},{6,7},{7,6},{12,13},{13,12},{14,15},{15,14},{20,21},{2... | collective-permute-start | bytes 196616 | tf_op jit(solution)/shard_map/ppermute | solution.py:440
  8.4 4.1 %collective-permute-start.4 = (bf16[32,1024]{1,0:T(8,128)(2,1)S(1)}, bf16[32,1024]{1,0:T(8,128)(2,1)S(1)}, u32[]{:S(2)}, u32[]{:S(2)}) collective-permute-start(bf16[32,1024]{1,0:T(8,128)(2,1)S(1)} %get-tuple-element.28), channel_id=1, source_target_pairs={{0,3},{1,2},{2,1},{3,0},{4,6},{5,7},{6,4},{7,5},{8,11},{9,10},{10,... | collective-permute-start | bytes 196616 | tf_op jit(solution)/shard_map/ppermute | solution.py:441
  12.5 0.0 collective-permute-done.3.refs_4_
  12.5 2.2 %collective-permute-start.6 = (bf16[128,1024]{1,0:T(8,128)(2,1)S(1)}, bf16[128,1024]{1,0:T(8,128)(2,1)S(1)}, u32[]{:S(2)}, u32[]{:S(2)}) collective-permute-start(bf16[128,1024]{1,0:T(8,128)(2,1)S(1)} %get-tuple-element.30.product_ref), channel_id=1, source_target_pairs={{0,4},{4,8},{8,12},{12,16},{16,20},{20,24},{24,28},{1,5},{5,9},{9,... | collective-permute-start | bytes 786440 | tf_op jit(solution)/shard_map/ppermute | solution.py:442
  14.7 0.7 %collective-permute-done.4.refs_5_ = bf16[32,1024]{1,0:T(8,128)(2,1)S(1)} collective-permute-done((bf16[32,1024]{1,0:T(8,128)(2,1)S(1)}, bf16[32,1024]{1,0:T(8,128)(2,1)S(1)}, u32[]{:S(2)}, u32[]{:S(2)}) %collective-permute-start.4) | collective-permute-done | bytes 65568 | tf_op jit(solution)/shard_map/ppermute | solution.py:441
  15.4 0.0 collective-permute-done.refs_1_
  15.4 0.0 collective-permute-done.1.refs_2_
  15.4 0.3 collective-permute-done.2.refs_3_
  15.6 0.2 shard_map.105
  15.8 0.5 %collective-permute-start.5 = (bf16[10,128,256]{2,1,0:T(8,128)(2,1)S(1)}, bf16[10,128,256]{2,1,0:T(8,128)(2,1)S(1)}, u32[]{:S(2)}, u32[]{:S(2)}) collective-permute-start(bf16[10,128,256]{2,1,0:T(8,128)(2,1)S(1)} %get-tuple-element.29.mine_ref.key_value_ref), channel_id=1, source_target_pairs={{0,4},{4,0},{8,12},{12,8},{16,20},{20,16},{24,28},{28,24},{1,5},{5... | collective-permute-start | bytes 1966088 | tf_op jit(solution)/shard_map/ppermute | solution.py:42
  16.4 1.0 %shard_map.107 = (f32[2,2,1,256]{3,2,1,0:T(1,128)S(1)}, f32[2,2,1,256]{3,2,1,0:T(1,128)S(1)}, f32[2,2,128,256]{3,2,1,0:T(8,128)S(1)}) custom-call(bf16[4,144,256]{2,1,0:T(8,128)(2,1)S(1)} %get-tuple-element.33.query_ref.refs_0_, bf16[10,128,256]{2,1,0:T(8,128)(2,1)S(1)} %get-tuple-element.29.mine_ref.key_value_ref), custom_call_target="tpu_custom_call" | custom-call | flops 26843545600 | bytes 2097152 | tf_op jit(solution)/shard_map/pallas_call | solution.py:30
  17.3 0.8 %collective-permute-done.5.other_ref.refs_4_ = bf16[10,128,256]{2,1,0:T(8,128)(2,1)S(1)} collective-permute-done((bf16[10,128,256]{2,1,0:T(8,128)(2,1)S(1)}, bf16[10,128,256]{2,1,0:T(8,128)(2,1)S(1)}, u32[]{:S(2)}, u32[]{:S(2)}) %collective-permute-start.5) | collective-permute-done | bytes 655392 | tf_op jit(solution)/shard_map/ppermute | solution.py:42
  18.1 0.8 %shard_map.108 = (bf16[272,128]{1,0:T(8,128)(2,1)S(1)}, bf16[272,128]{1,0:T(8,128)(2,1)S(1)}) custom-call(bf16[4,144,256]{2,1,0:T(8,128)(2,1)S(1)} %get-tuple-element.33.query_ref.refs_0_, f32[2,2,1,256]{3,2,1,0:T(1,128)S(1)} %get-tuple-element.34.refs_1_, f32[2,2,1,256]{3,2,1,0:T(1,128)S(1)} %get-tuple-element.35.refs_2_, ...), custom_call_target="tpu_custom_call" | custom-call | flops 134217728 | bytes 2097152 | tf_op jit(solution)/shard_map/pallas_call | solution.py:30
  18.8 1.4 %collective-permute-start.7 = (bf16[272,128]{1,0:T(8,128)(2,1)S(1)}, bf16[272,128]{1,0:T(8,128)(2,1)S(1)}, u32[]{:S(2)}, u32[]{:S(2)}) collective-permute-start(bf16[272,128]{1,0:T(8,128)(2,1)S(1)} %get-tuple-element.37.refs_5_), channel_id=1, source_target_pairs={{0,16},{4,20},{8,24},{12,28},{16,0},{20,4},{24,8},{28,12},{1,17},{... | collective-permute-start | bytes 208904 | tf_op jit(solution)/shard_map/ppermute | solution.py:42
  20.3 1.6 %collective-permute-start.8 = (bf16[272,128]{1,0:T(8,128)(2,1)S(1)}, bf16[272,128]{1,0:T(8,128)(2,1)S(1)}, u32[]{:S(2)}, u32[]{:S(2)}) collective-permute-start(bf16[272,128]{1,0:T(8,128)(2,1)S(1)} %get-tuple-element.39), channel_id=1, source_target_pairs={{0,24},{4,28},{8,16},{12,20},{16,8},{20,12},{24,0},{28,4},{1,25},{... | collective-permute-start | bytes 208904 | tf_op jit(solution)/shard_map/ppermute | solution.py:42
  21.9 0.6 %shard_map.109 = (bf16[272,128]{1,0:T(8,128)(2,1)S(1)}, bf16[272,128]{1,0:T(8,128)(2,1)S(1)}) custom-call(bf16[4,144,256]{2,1,0:T(8,128)(2,1)S(1)} %get-tuple-element.33.query_ref.refs_0_, f32[2,2,1,256]{3,2,1,0:T(1,128)S(1)} %get-tuple-element.34.refs_1_, f32[2,2,1,256]{3,2,1,0:T(1,128)S(1)} %get-tuple-element.35.refs_2_, ...), custom_call_target="tpu_custom_call" | custom-call | flops 134217728 | bytes 2097152 | tf_op jit(solution)/shard_map/pallas_call | solution.py:30
  22.5 0.0 copy-start.3
  22.5 0.6 %collective-permute-start.9 = (bf16[272,128]{1,0:T(8,128)(2,1)S(1)}, bf16[272,128]{1,0:T(8,128)(2,1)S(1)}, u32[]{:S(2)}, u32[]{:S(2)}) collective-permute-start(bf16[272,128]{1,0:T(8,128)(2,1)S(1)} %get-tuple-element.40), channel_id=1, source_target_pairs={{0,8},{4,12},{8,0},{12,4},{16,24},{20,28},{24,16},{28,20},{1,9},{5... | collective-permute-start | bytes 208904 | tf_op jit(solution)/shard_map/ppermute | solution.py:42
  23.1 0.0 collective-permute-done.6.before_ref
  23.1 0.0 copy-done.2
  23.1 0.1 copy-done.3
  23.2 2.3 %shard_map.106 = bf16[128,1024]{1,0:T(8,128)(2,1)} custom-call(bf16[10,128,256]{2,1,0:T(8,128)(2,1)S(1)} %collective-permute-done.5.other_ref.refs_4_, bf16[10,128,256]{2,1,0:T(8,128)(2,1)S(1)} %get-tuple-element.29.mine_ref.key_value_ref, bf16[128,1024]{1,0:T(8,128)(2,1)S(1)} %collective-permute-done.6.before_ref, ...), custom_call_target="tpu_custom_call" | custom-call | flops 536870912 | bytes 2097152 | tf_op jit(solution)/shard_map/pallas_call | solution.py:30
  25.5 0.0 collective-permute-done.7.refs_1_
  25.5 0.0 collective-permute-done.8.refs_2_
  25.5 1.4 %collective-permute-done.9.refs_3_ = bf16[272,128]{1,0:T(8,128)(2,1)S(1)} collective-permute-done((bf16[272,128]{1,0:T(8,128)(2,1)S(1)}, bf16[272,128]{1,0:T(8,128)(2,1)S(1)}, u32[]{:S(2)}, u32[]{:S(2)}) %collective-permute-start.9) | collective-permute-done | bytes 69664 | tf_op jit(solution)/shard_map/ppermute | solution.py:42
  26.9 0.8 %shard_map.110 = (bf16[128,1024]{1,0:T(8,128)(2,1)}, f32[8,128]{1,0:T(8,128)}) custom-call(bf16[272,128]{1,0:T(8,128)(2,1)S(1)} %get-tuple-element.38.refs_0_, bf16[272,128]{1,0:T(8,128)(2,1)S(1)} %collective-permute-done.7.refs_1_, bf16[272,128]{1,0:T(8,128)(2,1)S(1)} %collective-permute-done.8.refs_2_, bf16[272,128]{1,0:T(8,128)(2,1)S(1)} %collective-permute-done.9.refs_3_), custom_call_target="tpu_custom_call" | custom-call | bytes 524288 | tf_op jit(solution)/shard_map/pallas_call | solution.py:30
  (4 shorter events, 0.0 us)
Async XLA Ops:
  0.6 6.0 %copy-start = (bf16[3,128,1024]{2,1,0:T(8,128)(2,1)S(1)}, bf16[3,128,1024]{2,1,0:T(8,128)(2,1)}, u32[]{:S(2)}) copy-start(bf16[3,128,1024]{2,1,0:T(8,128)(2,1)} %gate_ref.1) | copy-start | bytes 2359300
  2.1 13.3 %collective-permute-start = (bf16[784,128]{1,0:T(8,128)(2,1)S(1)}, bf16[784,128]{1,0:T(8,128)(2,1)S(1)}, u32[]{:S(2)}, u32[]{:S(2)}) collective-permute-start(bf16[784,128]{1,0:T(8,128)(2,1)S(1)} %get-tuple-element.24), channel_id=1, source_target_pairs={{0,16},{4,20},{8,24},{12,28},{16,0},{20,4},{24,8},{28,12},{1,17},{... | collective-permute-start | bytes 602120 | tf_op jit(solution)/shard_map/ppermute | solution.py:42
  5.1 10.3 %collective-permute-start.1 = (bf16[784,128]{1,0:T(8,128)(2,1)S(1)}, bf16[784,128]{1,0:T(8,128)(2,1)S(1)}, u32[]{:S(2)}, u32[]{:S(2)}) collective-permute-start(bf16[784,128]{1,0:T(8,128)(2,1)S(1)} %get-tuple-element.25), channel_id=1, source_target_pairs={{0,8},{4,12},{8,0},{12,4},{16,24},{20,28},{24,16},{28,20},{1,9},{5... | collective-permute-start | bytes 602120 | tf_op jit(solution)/shard_map/ppermute | solution.py:42
  6.6 9.1 %collective-permute-start.2 = (bf16[784,128]{1,0:T(8,128)(2,1)S(1)}, bf16[784,128]{1,0:T(8,128)(2,1)S(1)}, u32[]{:S(2)}, u32[]{:S(2)}) collective-permute-start(bf16[784,128]{1,0:T(8,128)(2,1)S(1)} %get-tuple-element.26), channel_id=1, source_target_pairs={{0,24},{4,28},{8,16},{12,20},{16,8},{20,12},{24,0},{28,4},{1,25},{... | collective-permute-start | bytes 602120 | tf_op jit(solution)/shard_map/ppermute | solution.py:42
  7.7 4.8 %collective-permute-start.3 = (bf16[32,1024]{1,0:T(8,128)(2,1)S(1)}, bf16[32,1024]{1,0:T(8,128)(2,1)S(1)}, u32[]{:S(2)}, u32[]{:S(2)}) collective-permute-start(bf16[32,1024]{1,0:T(8,128)(2,1)S(1)} %get-tuple-element.27), channel_id=1, source_target_pairs={{4,5},{5,4},{6,7},{7,6},{12,13},{13,12},{14,15},{15,14},{20,21},{2... | collective-permute-start | bytes 196616 | tf_op jit(solution)/shard_map/ppermute | solution.py:440
  8.4 7.0 %collective-permute-start.4 = (bf16[32,1024]{1,0:T(8,128)(2,1)S(1)}, bf16[32,1024]{1,0:T(8,128)(2,1)S(1)}, u32[]{:S(2)}, u32[]{:S(2)}) collective-permute-start(bf16[32,1024]{1,0:T(8,128)(2,1)S(1)} %get-tuple-element.28), channel_id=1, source_target_pairs={{0,3},{1,2},{2,1},{3,0},{4,6},{5,7},{6,4},{7,5},{8,11},{9,10},{10,... | collective-permute-start | bytes 196616 | tf_op jit(solution)/shard_map/ppermute | solution.py:441
  12.5 10.6 %collective-permute-start.6 = (bf16[128,1024]{1,0:T(8,128)(2,1)S(1)}, bf16[128,1024]{1,0:T(8,128)(2,1)S(1)}, u32[]{:S(2)}, u32[]{:S(2)}) collective-permute-start(bf16[128,1024]{1,0:T(8,128)(2,1)S(1)} %get-tuple-element.30.product_ref), channel_id=1, source_target_pairs={{0,4},{4,8},{8,12},{12,16},{16,20},{20,24},{24,28},{1,5},{5,9},{9,... | collective-permute-start | bytes 786440 | tf_op jit(solution)/shard_map/ppermute | solution.py:442
  15.8 2.3 %collective-permute-start.5 = (bf16[10,128,256]{2,1,0:T(8,128)(2,1)S(1)}, bf16[10,128,256]{2,1,0:T(8,128)(2,1)S(1)}, u32[]{:S(2)}, u32[]{:S(2)}) collective-permute-start(bf16[10,128,256]{2,1,0:T(8,128)(2,1)S(1)} %get-tuple-element.29.mine_ref.key_value_ref), channel_id=1, source_target_pairs={{0,4},{4,0},{8,12},{12,8},{16,20},{20,16},{24,28},{28,24},{1,5},{5... | collective-permute-start | bytes 1966088 | tf_op jit(solution)/shard_map/ppermute | solution.py:42
  18.8 6.6 %collective-permute-start.7 = (bf16[272,128]{1,0:T(8,128)(2,1)S(1)}, bf16[272,128]{1,0:T(8,128)(2,1)S(1)}, u32[]{:S(2)}, u32[]{:S(2)}) collective-permute-start(bf16[272,128]{1,0:T(8,128)(2,1)S(1)} %get-tuple-element.37.refs_5_), channel_id=1, source_target_pairs={{0,16},{4,20},{8,24},{12,28},{16,0},{20,4},{24,8},{28,12},{1,17},{... | collective-permute-start | bytes 208904 | tf_op jit(solution)/shard_map/ppermute | solution.py:42
  20.3 2.8 %copy-start.1 = (f32[256,256]{1,0:T(8,128)S(1)}, f32[256,256]{1,0:T(8,128)}, u32[]{:S(2)}) copy-start(f32[256,256]{1,0:T(8,128)} %constant.4.clone.ahead_ref) | copy-start | bytes 786436
  20.3 2.8 %copy-start.2 = (f32[128,256]{1,0:T(8,128)S(1)}, f32[128,256]{1,0:T(8,128)}, u32[]{:S(2)}) copy-start(f32[128,256]{1,0:T(8,128)} %constant.5.clone.wide_back_ref) | copy-start | bytes 393220
  20.3 5.2 %collective-permute-start.8 = (bf16[272,128]{1,0:T(8,128)(2,1)S(1)}, bf16[272,128]{1,0:T(8,128)(2,1)S(1)}, u32[]{:S(2)}, u32[]{:S(2)}) collective-permute-start(bf16[272,128]{1,0:T(8,128)(2,1)S(1)} %get-tuple-element.39), channel_id=1, source_target_pairs={{0,24},{4,28},{8,16},{12,20},{16,8},{20,12},{24,0},{28,4},{1,25},{... | collective-permute-start | bytes 208904 | tf_op jit(solution)/shard_map/ppermute | solution.py:42
  22.5 0.7 %copy-start.3 = (f32[1024]{0:T(1024)S(1)}, f32[1024]{0:T(1024)}, u32[]{:S(2)}) copy-start(f32[1024]{0:T(1024)} %param.10) | copy-start | bytes 12292
  22.5 4.4 %collective-permute-start.9 = (bf16[272,128]{1,0:T(8,128)(2,1)S(1)}, bf16[272,128]{1,0:T(8,128)(2,1)S(1)}, u32[]{:S(2)}, u32[]{:S(2)}) collective-permute-start(bf16[272,128]{1,0:T(8,128)(2,1)S(1)} %get-tuple-element.40), channel_id=1, source_target_pairs={{0,8},{4,12},{8,0},{12,4},{16,24},{20,28},{24,16},{28,20},{1,9},{5... | collective-permute-start | bytes 208904 | tf_op jit(solution)/shard_map/ppermute | solution.py:42

commit v15 on v11

--- a/solution.py
+++ b/solution.py
@@ -472,7 +472,7 @@
         4 * queries.size * 4,
         scratch=(pltpu.VMEM((count, 2 * rows + NOTE_ROWS, HD), bf16),),
     )
-    returned = [mixed[0]] + [crossed(mixed[step], "ctx", 2 * step) for step in (2, 3, 1)]
+    returned = [mixed[0]] + [crossed(mixed[step], "ctx", 2 * step) for step in (3, 2, 1)]
     hyena_out = call(
         functools.partial(convolve, heads),
         shape((rows, channels), bf16),
@@ -492,7 +492,7 @@
         ),
     )
     attention_out, log_totals = call(
-        functools.partial(unpack_heads, heads, (0, 2, 3, 1)),
+        functools.partial(unpack_heads, heads, (0, 3, 2, 1)),
         (shape((rows, heads * HD), bf16), shape((heads, rows), f32)),
         returned,
         0,

time: 27.5 us -> 27.5 us (level)
  waiting for transfers between devices: 2.69 us -> 2.15 us
  Pallas kernels: 8.31 us -> 8.85 us
    ppermute x7, waiting for transfers between devices: 1.99 us -> 1.45 us  [crossed(): lax.ppermute(array, axis, [(i, i ^ bits) for i in range(lax.axis_size(axi...]
    pallas_call x7, Pallas kernels: 8.31 us -> 8.85 us  [call(): pl.pallas_call(kernel, out_shape=out_shape, in_specs=specs or [vmem() for...]
  transfers between devices with their start and end apart: 10 -> 10, of which waited for: 5 -> 4; matrix products, arithmetic and copies ran while one was open for 0% -> 0% of each run, Pallas kernels for 22% -> 24%
where the time goes in v15:
time: 27.5 us; the launch traced here: 27.3 us
  starting transfers between devices  15.6 us (57%)
  Pallas kernels  8.85 us (32%)
  waiting for transfers between devices  2.15 us (8%)
  between operations  0.71 us (3%)
    pallas_call x7, Pallas kernels, call(): pl.pallas_call(kernel, out_shape=out_shape, in_specs=specs or [vmem() for...  8.85 us
    ppermute x7, starting transfers between devices, crossed(): lax.ppermute(array, axis, [(i, i ^ bits) for i in range(lax.axis_size(axi...  8.69 us
    ppermute x1, starting transfers between devices, local(): far_taps = lax.ppermute(far_taps, axes, far_pairs)  4.09 us
    ppermute x1, starting transfers between devices, local(): lax.ppermute(product, 'ctx', [(i, i + 1) for i in range(peers - 1)])  2.15 us
    ppermute x7, waiting for transfers between devices, crossed(): lax.ppermute(array, axis, [(i, i ^ bits) for i in range(lax.axis_size(axi...  1.45 us
    ppermute x1, waiting for transfers between devices, local(): far_taps = lax.ppermute(far_taps, axes, far_pairs)  0.7 us
    ppermute x1, starting transfers between devices, local(): near_taps = lax.ppermute(near_taps, axes, near_pairs)  0.66 us
  transfers between devices with their start and end apart: 10, of which 4 were waited for; matrix products, arithmetic and copies ran while one was open for 0% of the time, Pallas kernels for 24%

profile of v15, /device:TPU:0, one launch (start us, length us, event | category | flops | bytes accessed | tf_op | source)
XLA Modules:
  0.0 27.3 jit_solution(4724404961068047395)
XLA Ops:
  0.6 0.0 copy-start
  0.6 1.4 %shard_map.103 = (bf16[784,128]{1,0:T(8,128)(2,1)S(1)}, bf16[784,128]{1,0:T(8,128)(2,1)S(1)}, bf16[784,128]{1,0:T(8,128)(2,1)S(1)}, bf16[784,128]{1,0:T(8,128)(2,1)S(1)}, s32[1,128]{1,0:T(1,128)S(1)}) custom-call(bf16[128,1024]{1,0:T(8,128)(2,1)} %queries_ref.1, bf16[256,1024]{1,0:T(8,128)(2,1)} %bitcast.4, s32[1,128]{1,0:T(1,128)} %bitcast.5), custom_call_target="tpu_custom_call" | custom-call | bytes 1572864 | tf_op jit(solution)/shard_map/pallas_call | solution.py:30
  2.1 3.0 %collective-permute-start = (bf16[784,128]{1,0:T(8,128)(2,1)S(1)}, bf16[784,128]{1,0:T(8,128)(2,1)S(1)}, u32[]{:S(2)}, u32[]{:S(2)}) collective-permute-start(bf16[784,128]{1,0:T(8,128)(2,1)S(1)} %get-tuple-element.24), channel_id=1, source_target_pairs={{0,16},{4,20},{8,24},{12,28},{16,0},{20,4},{24,8},{28,12},{1,17},{... | collective-permute-start | bytes 602120 | tf_op jit(solution)/shard_map/ppermute | solution.py:42
  5.1 1.5 %collective-permute-start.1 = (bf16[784,128]{1,0:T(8,128)(2,1)S(1)}, bf16[784,128]{1,0:T(8,128)(2,1)S(1)}, u32[]{:S(2)}, u32[]{:S(2)}) collective-permute-start(bf16[784,128]{1,0:T(8,128)(2,1)S(1)} %get-tuple-element.25), channel_id=1, source_target_pairs={{0,8},{4,12},{8,0},{12,4},{16,24},{20,28},{24,16},{28,20},{1,9},{5... | collective-permute-start | bytes 602120 | tf_op jit(solution)/shard_map/ppermute | solution.py:42
  6.6 0.0 collective-permute-start.2
  6.6 0.0 copy-done
  6.6 1.1 %shard_map.104 = (bf16[128,1024]{1,0:T(8,128)(2,1)S(1)}, bf16[32,1024]{1,0:T(8,128)(2,1)S(1)}, bf16[32,1024]{1,0:T(8,128)(2,1)S(1)}, bf16[32,1024]{1,0:T(8,128)(2,1)S(1)}) custom-call(bf16[3,128,1024]{2,1,0:T(8,128)(2,1)S(1)} %copy-done, f32[32,4096]{1,0:T(8,128)} %filters_ref.1), custom_call_target="tpu_custom_call" | custom-call | bytes 1572864 | tf_op jit(solution)/shard_map/pallas_call | solution.py:30
  7.7 0.7 %collective-permute-start.3 = (bf16[32,1024]{1,0:T(8,128)(2,1)S(1)}, bf16[32,1024]{1,0:T(8,128)(2,1)S(1)}, u32[]{:S(2)}, u32[]{:S(2)}) collective-permute-start(bf16[32,1024]{1,0:T(8,128)(2,1)S(1)} %get-tuple-element.27), channel_id=1, source_target_pairs={{4,5},{5,4},{6,7},{7,6},{12,13},{13,12},{14,15},{15,14},{20,21},{2... | collective-permute-start | bytes 196616 | tf_op jit(solution)/shard_map/ppermute | solution.py:434
  8.4 4.1 %collective-permute-start.4 = (bf16[32,1024]{1,0:T(8,128)(2,1)S(1)}, bf16[32,1024]{1,0:T(8,128)(2,1)S(1)}, u32[]{:S(2)}, u32[]{:S(2)}) collective-permute-start(bf16[32,1024]{1,0:T(8,128)(2,1)S(1)} %get-tuple-element.28), channel_id=1, source_target_pairs={{0,3},{1,2},{2,1},{3,0},{4,6},{5,7},{6,4},{7,5},{8,11},{9,10},{10,... | collective-permute-start | bytes 196616 | tf_op jit(solution)/shard_map/ppermute | solution.py:435
  12.5 0.0 collective-permute-done.3.refs_4_
  12.5 2.2 %collective-permute-start.6 = (bf16[128,1024]{1,0:T(8,128)(2,1)S(1)}, bf16[128,1024]{1,0:T(8,128)(2,1)S(1)}, u32[]{:S(2)}, u32[]{:S(2)}) collective-permute-start(bf16[128,1024]{1,0:T(8,128)(2,1)S(1)} %get-tuple-element.30.product_ref), channel_id=1, source_target_pairs={{0,4},{4,8},{8,12},{12,16},{16,20},{20,24},{24,28},{1,5},{5,9},{9,... | collective-permute-start | bytes 786440 | tf_op jit(solution)/shard_map/ppermute | solution.py:436
  14.7 0.7 %collective-permute-done.4.refs_5_ = bf16[32,1024]{1,0:T(8,128)(2,1)S(1)} collective-permute-done((bf16[32,1024]{1,0:T(8,128)(2,1)S(1)}, bf16[32,1024]{1,0:T(8,128)(2,1)S(1)}, u32[]{:S(2)}, u32[]{:S(2)}) %collective-permute-start.4) | collective-permute-done | bytes 65568 | tf_op jit(solution)/shard_map/ppermute | solution.py:435
  15.4 0.0 collective-permute-done.refs_1_
  15.4 0.0 collective-permute-done.1.refs_2_
  15.4 0.3 collective-permute-done.2.refs_3_
  15.6 0.2 shard_map.105
  15.8 0.5 %collective-permute-start.5 = (bf16[10,128,256]{2,1,0:T(8,128)(2,1)S(1)}, bf16[10,128,256]{2,1,0:T(8,128)(2,1)S(1)}, u32[]{:S(2)}, u32[]{:S(2)}) collective-permute-start(bf16[10,128,256]{2,1,0:T(8,128)(2,1)S(1)} %get-tuple-element.29.mine_ref.key_value_ref), channel_id=1, source_target_pairs={{0,4},{4,0},{8,12},{12,8},{16,20},{20,16},{24,28},{28,24},{1,5},{5... | collective-permute-start | bytes 1966088 | tf_op jit(solution)/shard_map/ppermute | solution.py:42
  16.4 1.0 %shard_map.107 = (f32[2,2,1,256]{3,2,1,0:T(1,128)S(1)}, f32[2,2,1,256]{3,2,1,0:T(1,128)S(1)}, f32[2,2,128,256]{3,2,1,0:T(8,128)S(1)}) custom-call(bf16[4,144,256]{2,1,0:T(8,128)(2,1)S(1)} %get-tuple-element.33.query_ref.refs_0_, bf16[10,128,256]{2,1,0:T(8,128)(2,1)S(1)} %get-tuple-element.29.mine_ref.key_value_ref), custom_call_target="tpu_custom_call" | custom-call | flops 26843545600 | bytes 2097152 | tf_op jit(solution)/shard_map/pallas_call | solution.py:30
  17.3 0.8 %collective-permute-done.5.other_ref.refs_4_ = bf16[10,128,256]{2,1,0:T(8,128)(2,1)S(1)} collective-permute-done((bf16[10,128,256]{2,1,0:T(8,128)(2,1)S(1)}, bf16[10,128,256]{2,1,0:T(8,128)(2,1)S(1)}, u32[]{:S(2)}, u32[]{:S(2)}) %collective-permute-start.5) | collective-permute-done | bytes 655392 | tf_op jit(solution)/shard_map/ppermute | solution.py:42
  18.1 1.1 %shard_map.108 = (bf16[272,128]{1,0:T(8,128)(2,1)S(1)}, bf16[272,128]{1,0:T(8,128)(2,1)S(1)}, bf16[272,128]{1,0:T(8,128)(2,1)S(1)}, bf16[272,128]{1,0:T(8,128)(2,1)S(1)}) custom-call(bf16[4,144,256]{2,1,0:T(8,128)(2,1)S(1)} %get-tuple-element.33.query_ref.refs_0_, f32[2,2,1,256]{3,2,1,0:T(1,128)S(1)} %get-tuple-element.34.refs_1_, ...), custom_call_target="tpu_custom_call" | custom-call | flops 268435456 | bytes 2097152 | tf_op jit(solution)/shard_map/pallas_call | solution.py:30
  19.2 2.6 %collective-permute-start.7 = (bf16[272,128]{1,0:T(8,128)(2,1)S(1)}, bf16[272,128]{1,0:T(8,128)(2,1)S(1)}, u32[]{:S(2)}, u32[]{:S(2)}) collective-permute-start(bf16[272,128]{1,0:T(8,128)(2,1)S(1)} %get-tuple-element.38), channel_id=1, source_target_pairs={{0,24},{4,28},{8,16},{12,20},{16,8},{20,12},{24,0},{28,4},{1,25},{... | collective-permute-start | bytes 208904 | tf_op jit(solution)/shard_map/ppermute | solution.py:42
  21.7 0.5 %collective-permute-start.8 = (bf16[272,128]{1,0:T(8,128)(2,1)S(1)}, bf16[272,128]{1,0:T(8,128)(2,1)S(1)}, u32[]{:S(2)}, u32[]{:S(2)}) collective-permute-start(bf16[272,128]{1,0:T(8,128)(2,1)S(1)} %get-tuple-element.39), channel_id=1, source_target_pairs={{0,16},{4,20},{8,24},{12,28},{16,0},{20,4},{24,8},{28,12},{1,17},{... | collective-permute-start | bytes 208904 | tf_op jit(solution)/shard_map/ppermute | solution.py:42
  22.2 0.5 %collective-permute-start.9 = (bf16[272,128]{1,0:T(8,128)(2,1)S(1)}, bf16[272,128]{1,0:T(8,128)(2,1)S(1)}, u32[]{:S(2)}, u32[]{:S(2)}) collective-permute-start(bf16[272,128]{1,0:T(8,128)(2,1)S(1)} %get-tuple-element.40), channel_id=1, source_target_pairs={{0,8},{4,12},{8,0},{12,4},{16,24},{20,28},{24,16},{28,20},{1,9},{5... | collective-permute-start | bytes 208904 | tf_op jit(solution)/shard_map/ppermute | solution.py:42
  22.7 0.0 collective-permute-done.6.before_ref
  22.7 0.0 copy-done.1
  22.7 0.0 copy-done.2
  22.8 0.0 copy-done.3
  22.8 3.4 %shard_map.106 = bf16[128,1024]{1,0:T(8,128)(2,1)} custom-call(bf16[10,128,256]{2,1,0:T(8,128)(2,1)S(1)} %collective-permute-done.5.other_ref.refs_4_, bf16[10,128,256]{2,1,0:T(8,128)(2,1)S(1)} %get-tuple-element.29.mine_ref.key_value_ref, bf16[128,1024]{1,0:T(8,128)(2,1)S(1)} %collective-permute-done.6.before_ref, ...), custom_call_target="tpu_custom_call" | custom-call | flops 536870912 | bytes 2097152 | tf_op jit(solution)/shard_map/pallas_call | solution.py:30
  26.1 0.0 collective-permute-done.7.refs_1_
  26.1 0.0 collective-permute-done.8.refs_2_
  26.1 0.4 %collective-permute-done.9.refs_3_ = bf16[272,128]{1,0:T(8,128)(2,1)S(1)} collective-permute-done((bf16[272,128]{1,0:T(8,128)(2,1)S(1)}, bf16[272,128]{1,0:T(8,128)(2,1)S(1)}, u32[]{:S(2)}, u32[]{:S(2)}) %collective-permute-start.9) | collective-permute-done | bytes 69664 | tf_op jit(solution)/shard_map/ppermute | solution.py:42
  26.5 0.8 %shard_map.109 = (bf16[128,1024]{1,0:T(8,128)(2,1)}, f32[8,128]{1,0:T(8,128)}) custom-call(bf16[272,128]{1,0:T(8,128)(2,1)S(1)} %get-tuple-element.37.refs_0_, bf16[272,128]{1,0:T(8,128)(2,1)S(1)} %collective-permute-done.7.refs_1_, bf16[272,128]{1,0:T(8,128)(2,1)S(1)} %collective-permute-done.8.refs_2_, bf16[272,128]{1,0:T(8,128)(2,1)S(1)} %collective-permute-done.9.refs_3_), custom_call_target="tpu_custom_call" | custom-call | bytes 524288 | tf_op jit(solution)/shard_map/pallas_call | solution.py:30
  (3 shorter events, 0.0 us)
Async XLA Ops:
  0.6 6.0 %copy-start = (bf16[3,128,1024]{2,1,0:T(8,128)(2,1)S(1)}, bf16[3,128,1024]{2,1,0:T(8,128)(2,1)}, u32[]{:S(2)}) copy-start(bf16[3,128,1024]{2,1,0:T(8,128)(2,1)} %gate_ref.1) | copy-start | bytes 2359300
  2.1 13.3 %collective-permute-start = (bf16[784,128]{1,0:T(8,128)(2,1)S(1)}, bf16[784,128]{1,0:T(8,128)(2,1)S(1)}, u32[]{:S(2)}, u32[]{:S(2)}) collective-permute-start(bf16[784,128]{1,0:T(8,128)(2,1)S(1)} %get-tuple-element.24), channel_id=1, source_target_pairs={{0,16},{4,20},{8,24},{12,28},{16,0},{20,4},{24,8},{28,12},{1,17},{... | collective-permute-start | bytes 602120 | tf_op jit(solution)/shard_map/ppermute | solution.py:42
  5.1 10.3 %collective-permute-start.1 = (bf16[784,128]{1,0:T(8,128)(2,1)S(1)}, bf16[784,128]{1,0:T(8,128)(2,1)S(1)}, u32[]{:S(2)}, u32[]{:S(2)}) collective-permute-start(bf16[784,128]{1,0:T(8,128)(2,1)S(1)} %get-tuple-element.25), channel_id=1, source_target_pairs={{0,8},{4,12},{8,0},{12,4},{16,24},{20,28},{24,16},{28,20},{1,9},{5... | collective-permute-start | bytes 602120 | tf_op jit(solution)/shard_map/ppermute | solution.py:42
  6.6 9.1 %collective-permute-start.2 = (bf16[784,128]{1,0:T(8,128)(2,1)S(1)}, bf16[784,128]{1,0:T(8,128)(2,1)S(1)}, u32[]{:S(2)}, u32[]{:S(2)}) collective-permute-start(bf16[784,128]{1,0:T(8,128)(2,1)S(1)} %get-tuple-element.26), channel_id=1, source_target_pairs={{0,24},{4,28},{8,16},{12,20},{16,8},{20,12},{24,0},{28,4},{1,25},{... | collective-permute-start | bytes 602120 | tf_op jit(solution)/shard_map/ppermute | solution.py:42
  7.7 4.8 %collective-permute-start.3 = (bf16[32,1024]{1,0:T(8,128)(2,1)S(1)}, bf16[32,1024]{1,0:T(8,128)(2,1)S(1)}, u32[]{:S(2)}, u32[]{:S(2)}) collective-permute-start(bf16[32,1024]{1,0:T(8,128)(2,1)S(1)} %get-tuple-element.27), channel_id=1, source_target_pairs={{4,5},{5,4},{6,7},{7,6},{12,13},{13,12},{14,15},{15,14},{20,21},{2... | collective-permute-start | bytes 196616 | tf_op jit(solution)/shard_map/ppermute | solution.py:434
  8.4 7.0 %collective-permute-start.4 = (bf16[32,1024]{1,0:T(8,128)(2,1)S(1)}, bf16[32,1024]{1,0:T(8,128)(2,1)S(1)}, u32[]{:S(2)}, u32[]{:S(2)}) collective-permute-start(bf16[32,1024]{1,0:T(8,128)(2,1)S(1)} %get-tuple-element.28), channel_id=1, source_target_pairs={{0,3},{1,2},{2,1},{3,0},{4,6},{5,7},{6,4},{7,5},{8,11},{9,10},{10,... | collective-permute-start | bytes 196616 | tf_op jit(solution)/shard_map/ppermute | solution.py:435
  12.5 10.2 %collective-permute-start.6 = (bf16[128,1024]{1,0:T(8,128)(2,1)S(1)}, bf16[128,1024]{1,0:T(8,128)(2,1)S(1)}, u32[]{:S(2)}, u32[]{:S(2)}) collective-permute-start(bf16[128,1024]{1,0:T(8,128)(2,1)S(1)} %get-tuple-element.30.product_ref), channel_id=1, source_target_pairs={{0,4},{4,8},{8,12},{12,16},{16,20},{20,24},{24,28},{1,5},{5,9},{9,... | collective-permute-start | bytes 786440 | tf_op jit(solution)/shard_map/ppermute | solution.py:436
  15.8 2.3 %collective-permute-start.5 = (bf16[10,128,256]{2,1,0:T(8,128)(2,1)S(1)}, bf16[10,128,256]{2,1,0:T(8,128)(2,1)S(1)}, u32[]{:S(2)}, u32[]{:S(2)}) collective-permute-start(bf16[10,128,256]{2,1,0:T(8,128)(2,1)S(1)} %get-tuple-element.29.mine_ref.key_value_ref), channel_id=1, source_target_pairs={{0,4},{4,0},{8,12},{12,8},{16,20},{20,16},{24,28},{28,24},{1,5},{5... | collective-permute-start | bytes 1966088 | tf_op jit(solution)/shard_map/ppermute | solution.py:42
  18.1 4.7 %copy-start.1 = (f32[256,256]{1,0:T(8,128)S(1)}, f32[256,256]{1,0:T(8,128)}, u32[]{:S(2)}) copy-start(f32[256,256]{1,0:T(8,128)} %constant.4.clone.ahead_ref) | copy-start | bytes 786436
  18.1 4.7 %copy-start.2 = (f32[128,256]{1,0:T(8,128)S(1)}, f32[128,256]{1,0:T(8,128)}, u32[]{:S(2)}) copy-start(f32[128,256]{1,0:T(8,128)} %constant.5.clone.wide_back_ref) | copy-start | bytes 393220
  19.2 7.0 %collective-permute-start.7 = (bf16[272,128]{1,0:T(8,128)(2,1)S(1)}, bf16[272,128]{1,0:T(8,128)(2,1)S(1)}, u32[]{:S(2)}, u32[]{:S(2)}) collective-permute-start(bf16[272,128]{1,0:T(8,128)(2,1)S(1)} %get-tuple-element.38), channel_id=1, source_target_pairs={{0,24},{4,28},{8,16},{12,20},{16,8},{20,12},{24,0},{28,4},{1,25},{... | collective-permute-start | bytes 208904 | tf_op jit(solution)/shard_map/ppermute | solution.py:42
  21.7 1.0 %copy-start.3 = (f32[1024]{0:T(1024)S(1)}, f32[1024]{0:T(1024)}, u32[]{:S(2)}) copy-start(f32[1024]{0:T(1024)} %param.10) | copy-start | bytes 12292
  21.7 4.4 %collective-permute-start.8 = (bf16[272,128]{1,0:T(8,128)(2,1)S(1)}, bf16[272,128]{1,0:T(8,128)(2,1)S(1)}, u32[]{:S(2)}, u32[]{:S(2)}) collective-permute-start(bf16[272,128]{1,0:T(8,128)(2,1)S(1)} %get-tuple-element.39), channel_id=1, source_target_pairs={{0,16},{4,20},{8,24},{12,28},{16,0},{20,4},{24,8},{28,12},{1,17},{... | collective-permute-start | bytes 208904 | tf_op jit(solution)/shard_map/ppermute | solution.py:42
  22.2 4.3 %collective-permute-start.9 = (bf16[272,128]{1,0:T(8,128)(2,1)S(1)}, bf16[272,128]{1,0:T(8,128)(2,1)S(1)}, u32[]{:S(2)}, u32[]{:S(2)}) collective-permute-start(bf16[272,128]{1,0:T(8,128)(2,1)S(1)} %get-tuple-element.40), channel_id=1, source_target_pairs={{0,8},{4,12},{8,0},{12,4},{16,24},{20,28},{24,16},{28,20},{1,9},{5... | collective-permute-start | bytes 208904 | tf_op jit(solution)/shard_map/ppermute | solution.py:42

commit v16 on v15

--- a/solution.py
+++ b/solution.py
@@ -472,7 +472,7 @@
         4 * queries.size * 4,
         scratch=(pltpu.VMEM((count, 2 * rows + NOTE_ROWS, HD), bf16),),
     )
-    returned = [mixed[0]] + [crossed(mixed[step], "ctx", 2 * step) for step in (3, 2, 1)]
+    returned = [mixed[0]] + [crossed(mixed[step], "ctx", 2 * step) for step in (3, 1, 2)]
     hyena_out = call(
         functools.partial(convolve, heads),
         shape((rows, channels), bf16),
@@ -492,7 +492,7 @@
         ),
     )
     attention_out, log_totals = call(
-        functools.partial(unpack_heads, heads, (0, 3, 2, 1)),
+        functools.partial(unpack_heads, heads, (0, 3, 1, 2)),
         (shape((rows, heads * HD), bf16), shape((heads, rows), f32)),
         returned,
         0,

time: 27.5 us -> 27.6 us (level)
  waiting for transfers between devices: 2.15 us -> 3.26 us
  Pallas kernels: 8.85 us -> 7.77 us
    ppermute x7, waiting for transfers between devices: 1.45 us -> 2.56 us  [crossed(): lax.ppermute(array, axis, [(i, i ^ bits) for i in range(lax.axis_size(axi...]
    pallas_call x7, Pallas kernels: 8.85 us -> 7.77 us  [call(): pl.pallas_call(kernel, out_shape=out_shape, in_specs=specs or [vmem() for...]
  transfers between devices with their start and end apart: 10 -> 10, of which waited for: 4 -> 5; matrix products, arithmetic and copies ran while one was open for 0% -> 0% of each run, Pallas kernels for 24% -> 20%
where the time goes in v16:
time: 27.6 us; the launch traced here: 27.4 us
  starting transfers between devices  15.6 us (57%)
  Pallas kernels  7.77 us (28%)
  waiting for transfers between devices  3.26 us (12%)
  between operations  0.71 us (3%)
    ppermute x7, starting transfers between devices, crossed(): lax.ppermute(array, axis, [(i, i ^ bits) for i in range(lax.axis_size(axi...  8.69 us
    pallas_call x7, Pallas kernels, call(): pl.pallas_call(kernel, out_shape=out_shape, in_specs=specs or [vmem() for...  7.77 us
    ppermute x1, starting transfers between devices, local(): far_taps = lax.ppermute(far_taps, axes, far_pairs)  4.09 us
    ppermute x7, waiting for transfers between devices, crossed(): lax.ppermute(array, axis, [(i, i ^ bits) for i in range(lax.axis_size(axi...  2.56 us
    ppermute x1, starting transfers between devices, local(): lax.ppermute(product, 'ctx', [(i, i + 1) for i in range(peers - 1)])  2.15 us
    ppermute x1, waiting for transfers between devices, local(): far_taps = lax.ppermute(far_taps, axes, far_pairs)  0.7 us
    ppermute x1, starting transfers between devices, local(): near_taps = lax.ppermute(near_taps, axes, near_pairs)  0.66 us
  transfers between devices with their start and end apart: 10, of which 5 were waited for; matrix products, arithmetic and copies ran while one was open for 0% of the time, Pallas kernels for 20%

profile of v16, /device:TPU:0, one launch (start us, length us, event | category | flops | bytes accessed | tf_op | source)
XLA Modules:
  0.0 27.4 jit_solution(5078439674959304214)
XLA Ops:
  0.6 0.0 copy-start
  0.6 1.4 %shard_map.103 = (bf16[784,128]{1,0:T(8,128)(2,1)S(1)}, bf16[784,128]{1,0:T(8,128)(2,1)S(1)}, bf16[784,128]{1,0:T(8,128)(2,1)S(1)}, bf16[784,128]{1,0:T(8,128)(2,1)S(1)}, s32[1,128]{1,0:T(1,128)S(1)}) custom-call(bf16[128,1024]{1,0:T(8,128)(2,1)} %queries_ref.1, bf16[256,1024]{1,0:T(8,128)(2,1)} %bitcast.4, s32[1,128]{1,0:T(1,128)} %bitcast.5), custom_call_target="tpu_custom_call" | custom-call | bytes 1572864 | tf_op jit(solution)/shard_map/pallas_call | solution.py:30
  2.1 3.0 %collective-permute-start = (bf16[784,128]{1,0:T(8,128)(2,1)S(1)}, bf16[784,128]{1,0:T(8,128)(2,1)S(1)}, u32[]{:S(2)}, u32[]{:S(2)}) collective-permute-start(bf16[784,128]{1,0:T(8,128)(2,1)S(1)} %get-tuple-element.24), channel_id=1, source_target_pairs={{0,16},{4,20},{8,24},{12,28},{16,0},{20,4},{24,8},{28,12},{1,17},{... | collective-permute-start | bytes 602120 | tf_op jit(solution)/shard_map/ppermute | solution.py:42
  5.1 1.5 %collective-permute-start.1 = (bf16[784,128]{1,0:T(8,128)(2,1)S(1)}, bf16[784,128]{1,0:T(8,128)(2,1)S(1)}, u32[]{:S(2)}, u32[]{:S(2)}) collective-permute-start(bf16[784,128]{1,0:T(8,128)(2,1)S(1)} %get-tuple-element.25), channel_id=1, source_target_pairs={{0,8},{4,12},{8,0},{12,4},{16,24},{20,28},{24,16},{28,20},{1,9},{5... | collective-permute-start | bytes 602120 | tf_op jit(solution)/shard_map/ppermute | solution.py:42
  6.6 0.0 collective-permute-start.2
  6.6 0.0 copy-done
  6.6 1.1 %shard_map.104 = (bf16[128,1024]{1,0:T(8,128)(2,1)S(1)}, bf16[32,1024]{1,0:T(8,128)(2,1)S(1)}, bf16[32,1024]{1,0:T(8,128)(2,1)S(1)}, bf16[32,1024]{1,0:T(8,128)(2,1)S(1)}) custom-call(bf16[3,128,1024]{2,1,0:T(8,128)(2,1)S(1)} %copy-done, f32[32,4096]{1,0:T(8,128)} %filters_ref.1), custom_call_target="tpu_custom_call" | custom-call | bytes 1572864 | tf_op jit(solution)/shard_map/pallas_call | solution.py:30
  7.7 0.7 %collective-permute-start.3 = (bf16[32,1024]{1,0:T(8,128)(2,1)S(1)}, bf16[32,1024]{1,0:T(8,128)(2,1)S(1)}, u32[]{:S(2)}, u32[]{:S(2)}) collective-permute-start(bf16[32,1024]{1,0:T(8,128)(2,1)S(1)} %get-tuple-element.27), channel_id=1, source_target_pairs={{4,5},{5,4},{6,7},{7,6},{12,13},{13,12},{14,15},{15,14},{20,21},{2... | collective-permute-start | bytes 196616 | tf_op jit(solution)/shard_map/ppermute | solution.py:434
  8.4 4.1 %collective-permute-start.4 = (bf16[32,1024]{1,0:T(8,128)(2,1)S(1)}, bf16[32,1024]{1,0:T(8,128)(2,1)S(1)}, u32[]{:S(2)}, u32[]{:S(2)}) collective-permute-start(bf16[32,1024]{1,0:T(8,128)(2,1)S(1)} %get-tuple-element.28), channel_id=1, source_target_pairs={{0,3},{1,2},{2,1},{3,0},{4,6},{5,7},{6,4},{7,5},{8,11},{9,10},{10,... | collective-permute-start | bytes 196616 | tf_op jit(solution)/shard_map/ppermute | solution.py:435
  12.5 0.0 collective-permute-done.3.refs_4_
  12.5 2.2 %collective-permute-start.6 = (bf16[128,1024]{1,0:T(8,128)(2,1)S(1)}, bf16[128,1024]{1,0:T(8,128)(2,1)S(1)}, u32[]{:S(2)}, u32[]{:S(2)}) collective-permute-start(bf16[128,1024]{1,0:T(8,128)(2,1)S(1)} %get-tuple-element.30.product_ref), channel_id=1, source_target_pairs={{0,4},{4,8},{8,12},{12,16},{16,20},{20,24},{24,28},{1,5},{5,9},{9,... | collective-permute-start | bytes 786440 | tf_op jit(solution)/shard_map/ppermute | solution.py:436
  14.7 0.7 %collective-permute-done.4.refs_5_ = bf16[32,1024]{1,0:T(8,128)(2,1)S(1)} collective-permute-done((bf16[32,1024]{1,0:T(8,128)(2,1)S(1)}, bf16[32,1024]{1,0:T(8,128)(2,1)S(1)}, u32[]{:S(2)}, u32[]{:S(2)}) %collective-permute-start.4) | collective-permute-done | bytes 65568 | tf_op jit(solution)/shard_map/ppermute | solution.py:435
  15.4 0.0 collective-permute-done.refs_1_
  15.4 0.0 collective-permute-done.1.refs_2_
  15.4 0.3 collective-permute-done.2.refs_3_
  15.6 0.2 shard_map.105
  15.8 0.5 %collective-permute-start.5 = (bf16[10,128,256]{2,1,0:T(8,128)(2,1)S(1)}, bf16[10,128,256]{2,1,0:T(8,128)(2,1)S(1)}, u32[]{:S(2)}, u32[]{:S(2)}) collective-permute-start(bf16[10,128,256]{2,1,0:T(8,128)(2,1)S(1)} %get-tuple-element.29.mine_ref.key_value_ref), channel_id=1, source_target_pairs={{0,4},{4,0},{8,12},{12,8},{16,20},{20,16},{24,28},{28,24},{1,5},{5... | collective-permute-start | bytes 1966088 | tf_op jit(solution)/shard_map/ppermute | solution.py:42
  16.4 1.0 %shard_map.107 = (f32[2,2,1,256]{3,2,1,0:T(1,128)S(1)}, f32[2,2,1,256]{3,2,1,0:T(1,128)S(1)}, f32[2,2,128,256]{3,2,1,0:T(8,128)S(1)}) custom-call(bf16[4,144,256]{2,1,0:T(8,128)(2,1)S(1)} %get-tuple-element.33.query_ref.refs_0_, bf16[10,128,256]{2,1,0:T(8,128)(2,1)S(1)} %get-tuple-element.29.mine_ref.key_value_ref), custom_call_target="tpu_custom_call" | custom-call | flops 26843545600 | bytes 2097152 | tf_op jit(solution)/shard_map/pallas_call | solution.py:30
  17.3 0.8 %collective-permute-done.5.other_ref.refs_4_ = bf16[10,128,256]{2,1,0:T(8,128)(2,1)S(1)} collective-permute-done((bf16[10,128,256]{2,1,0:T(8,128)(2,1)S(1)}, bf16[10,128,256]{2,1,0:T(8,128)(2,1)S(1)}, u32[]{:S(2)}, u32[]{:S(2)}) %collective-permute-start.5) | collective-permute-done | bytes 655392 | tf_op jit(solution)/shard_map/ppermute | solution.py:42
  18.1 1.1 %shard_map.108 = (bf16[272,128]{1,0:T(8,128)(2,1)S(1)}, bf16[272,128]{1,0:T(8,128)(2,1)S(1)}, bf16[272,128]{1,0:T(8,128)(2,1)S(1)}, bf16[272,128]{1,0:T(8,128)(2,1)S(1)}) custom-call(bf16[4,144,256]{2,1,0:T(8,128)(2,1)S(1)} %get-tuple-element.33.query_ref.refs_0_, f32[2,2,1,256]{3,2,1,0:T(1,128)S(1)} %get-tuple-element.34.refs_1_, ...), custom_call_target="tpu_custom_call" | custom-call | flops 268435456 | bytes 2097152 | tf_op jit(solution)/shard_map/pallas_call | solution.py:30
  19.2 2.6 %collective-permute-start.7 = (bf16[272,128]{1,0:T(8,128)(2,1)S(1)}, bf16[272,128]{1,0:T(8,128)(2,1)S(1)}, u32[]{:S(2)}, u32[]{:S(2)}) collective-permute-start(bf16[272,128]{1,0:T(8,128)(2,1)S(1)} %get-tuple-element.38), channel_id=1, source_target_pairs={{0,24},{4,28},{8,16},{12,20},{16,8},{20,12},{24,0},{28,4},{1,25},{... | collective-permute-start | bytes 208904 | tf_op jit(solution)/shard_map/ppermute | solution.py:42
  21.7 0.5 %collective-permute-start.8 = (bf16[272,128]{1,0:T(8,128)(2,1)S(1)}, bf16[272,128]{1,0:T(8,128)(2,1)S(1)}, u32[]{:S(2)}, u32[]{:S(2)}) collective-permute-start(bf16[272,128]{1,0:T(8,128)(2,1)S(1)} %get-tuple-element.39), channel_id=1, source_target_pairs={{0,8},{4,12},{8,0},{12,4},{16,24},{20,28},{24,16},{28,20},{1,9},{5... | collective-permute-start | bytes 208904 | tf_op jit(solution)/shard_map/ppermute | solution.py:42
  22.3 0.5 %collective-permute-start.9 = (bf16[272,128]{1,0:T(8,128)(2,1)S(1)}, bf16[272,128]{1,0:T(8,128)(2,1)S(1)}, u32[]{:S(2)}, u32[]{:S(2)}) collective-permute-start(bf16[272,128]{1,0:T(8,128)(2,1)S(1)} %get-tuple-element.40), channel_id=1, source_target_pairs={{0,16},{4,20},{8,24},{12,28},{16,0},{20,4},{24,8},{28,12},{1,17},{... | collective-permute-start | bytes 208904 | tf_op jit(solution)/shard_map/ppermute | solution.py:42
  22.7 0.0 collective-permute-done.6.before_ref
  22.7 0.0 copy-done.1
  22.7 0.0 copy-done.2
  22.8 0.0 copy-done.3
  22.8 2.3 %shard_map.106 = bf16[128,1024]{1,0:T(8,128)(2,1)} custom-call(bf16[10,128,256]{2,1,0:T(8,128)(2,1)S(1)} %collective-permute-done.5.other_ref.refs_4_, bf16[10,128,256]{2,1,0:T(8,128)(2,1)S(1)} %get-tuple-element.29.mine_ref.key_value_ref, bf16[128,1024]{1,0:T(8,128)(2,1)S(1)} %collective-permute-done.6.before_ref, ...), custom_call_target="tpu_custom_call" | custom-call | flops 536870912 | bytes 2097152 | tf_op jit(solution)/shard_map/pallas_call | solution.py:30
  25.1 0.0 collective-permute-done.7.refs_1_
  25.1 1.1 %collective-permute-done.8.refs_2_ = bf16[272,128]{1,0:T(8,128)(2,1)S(1)} collective-permute-done((bf16[272,128]{1,0:T(8,128)(2,1)S(1)}, bf16[272,128]{1,0:T(8,128)(2,1)S(1)}, u32[]{:S(2)}, u32[]{:S(2)}) %collective-permute-start.8) | collective-permute-done | bytes 69664 | tf_op jit(solution)/shard_map/ppermute | solution.py:42
  26.1 0.4 %collective-permute-done.9.refs_3_ = bf16[272,128]{1,0:T(8,128)(2,1)S(1)} collective-permute-done((bf16[272,128]{1,0:T(8,128)(2,1)S(1)}, bf16[272,128]{1,0:T(8,128)(2,1)S(1)}, u32[]{:S(2)}, u32[]{:S(2)}) %collective-permute-start.9) | collective-permute-done | bytes 69664 | tf_op jit(solution)/shard_map/ppermute | solution.py:42
  26.6 0.8 %shard_map.109 = (bf16[128,1024]{1,0:T(8,128)(2,1)}, f32[8,128]{1,0:T(8,128)}) custom-call(bf16[272,128]{1,0:T(8,128)(2,1)S(1)} %get-tuple-element.37.refs_0_, bf16[272,128]{1,0:T(8,128)(2,1)S(1)} %collective-permute-done.7.refs_1_, bf16[272,128]{1,0:T(8,128)(2,1)S(1)} %collective-permute-done.8.refs_2_, bf16[272,128]{1,0:T(8,128)(2,1)S(1)} %collective-permute-done.9.refs_3_), custom_call_target="tpu_custom_call" | custom-call | bytes 524288 | tf_op jit(solution)/shard_map/pallas_call | solution.py:30
  (3 shorter events, 0.0 us)
Async XLA Ops:
  0.6 6.0 %copy-start = (bf16[3,128,1024]{2,1,0:T(8,128)(2,1)S(1)}, bf16[3,128,1024]{2,1,0:T(8,128)(2,1)}, u32[]{:S(2)}) copy-start(bf16[3,128,1024]{2,1,0:T(8,128)(2,1)} %gate_ref.1) | copy-start | bytes 2359300
  2.1 13.3 %collective-permute-start = (bf16[784,128]{1,0:T(8,128)(2,1)S(1)}, bf16[784,128]{1,0:T(8,128)(2,1)S(1)}, u32[]{:S(2)}, u32[]{:S(2)}) collective-permute-start(bf16[784,128]{1,0:T(8,128)(2,1)S(1)} %get-tuple-element.24), channel_id=1, source_target_pairs={{0,16},{4,20},{8,24},{12,28},{16,0},{20,4},{24,8},{28,12},{1,17},{... | collective-permute-start | bytes 602120 | tf_op jit(solution)/shard_map/ppermute | solution.py:42
  5.1 10.3 %collective-permute-start.1 = (bf16[784,128]{1,0:T(8,128)(2,1)S(1)}, bf16[784,128]{1,0:T(8,128)(2,1)S(1)}, u32[]{:S(2)}, u32[]{:S(2)}) collective-permute-start(bf16[784,128]{1,0:T(8,128)(2,1)S(1)} %get-tuple-element.25), channel_id=1, source_target_pairs={{0,8},{4,12},{8,0},{12,4},{16,24},{20,28},{24,16},{28,20},{1,9},{5... | collective-permute-start | bytes 602120 | tf_op jit(solution)/shard_map/ppermute | solution.py:42
  6.6 9.1 %collective-permute-start.2 = (bf16[784,128]{1,0:T(8,128)(2,1)S(1)}, bf16[784,128]{1,0:T(8,128)(2,1)S(1)}, u32[]{:S(2)}, u32[]{:S(2)}) collective-permute-start(bf16[784,128]{1,0:T(8,128)(2,1)S(1)} %get-tuple-element.26), channel_id=1, source_target_pairs={{0,24},{4,28},{8,16},{12,20},{16,8},{20,12},{24,0},{28,4},{1,25},{... | collective-permute-start | bytes 602120 | tf_op jit(solution)/shard_map/ppermute | solution.py:42
  7.7 4.8 %collective-permute-start.3 = (bf16[32,1024]{1,0:T(8,128)(2,1)S(1)}, bf16[32,1024]{1,0:T(8,128)(2,1)S(1)}, u32[]{:S(2)}, u32[]{:S(2)}) collective-permute-start(bf16[32,1024]{1,0:T(8,128)(2,1)S(1)} %get-tuple-element.27), channel_id=1, source_target_pairs={{4,5},{5,4},{6,7},{7,6},{12,13},{13,12},{14,15},{15,14},{20,21},{2... | collective-permute-start | bytes 196616 | tf_op jit(solution)/shard_map/ppermute | solution.py:434
  8.4 7.0 %collective-permute-start.4 = (bf16[32,1024]{1,0:T(8,128)(2,1)S(1)}, bf16[32,1024]{1,0:T(8,128)(2,1)S(1)}, u32[]{:S(2)}, u32[]{:S(2)}) collective-permute-start(bf16[32,1024]{1,0:T(8,128)(2,1)S(1)} %get-tuple-element.28), channel_id=1, source_target_pairs={{0,3},{1,2},{2,1},{3,0},{4,6},{5,7},{6,4},{7,5},{8,11},{9,10},{10,... | collective-permute-start | bytes 196616 | tf_op jit(solution)/shard_map/ppermute | solution.py:435
  12.5 10.2 %collective-permute-start.6 = (bf16[128,1024]{1,0:T(8,128)(2,1)S(1)}, bf16[128,1024]{1,0:T(8,128)(2,1)S(1)}, u32[]{:S(2)}, u32[]{:S(2)}) collective-permute-start(bf16[128,1024]{1,0:T(8,128)(2,1)S(1)} %get-tuple-element.30.product_ref), channel_id=1, source_target_pairs={{0,4},{4,8},{8,12},{12,16},{16,20},{20,24},{24,28},{1,5},{5,9},{9,... | collective-permute-start | bytes 786440 | tf_op jit(solution)/shard_map/ppermute | solution.py:436
  15.8 2.3 %collective-permute-start.5 = (bf16[10,128,256]{2,1,0:T(8,128)(2,1)S(1)}, bf16[10,128,256]{2,1,0:T(8,128)(2,1)S(1)}, u32[]{:S(2)}, u32[]{:S(2)}) collective-permute-start(bf16[10,128,256]{2,1,0:T(8,128)(2,1)S(1)} %get-tuple-element.29.mine_ref.key_value_ref), channel_id=1, source_target_pairs={{0,4},{4,0},{8,12},{12,8},{16,20},{20,16},{24,28},{28,24},{1,5},{5... | collective-permute-start | bytes 1966088 | tf_op jit(solution)/shard_map/ppermute | solution.py:42
  18.1 4.7 %copy-start.1 = (f32[256,256]{1,0:T(8,128)S(1)}, f32[256,256]{1,0:T(8,128)}, u32[]{:S(2)}) copy-start(f32[256,256]{1,0:T(8,128)} %constant.4.clone.ahead_ref) | copy-start | bytes 786436
  18.1 4.7 %copy-start.2 = (f32[128,256]{1,0:T(8,128)S(1)}, f32[128,256]{1,0:T(8,128)}, u32[]{:S(2)}) copy-start(f32[128,256]{1,0:T(8,128)} %constant.5.clone.wide_back_ref) | copy-start | bytes 393220
  19.2 5.9 %collective-permute-start.7 = (bf16[272,128]{1,0:T(8,128)(2,1)S(1)}, bf16[272,128]{1,0:T(8,128)(2,1)S(1)}, u32[]{:S(2)}, u32[]{:S(2)}) collective-permute-start(bf16[272,128]{1,0:T(8,128)(2,1)S(1)} %get-tuple-element.38), channel_id=1, source_target_pairs={{0,24},{4,28},{8,16},{12,20},{16,8},{20,12},{24,0},{28,4},{1,25},{... | collective-permute-start | bytes 208904 | tf_op jit(solution)/shard_map/ppermute | solution.py:42
  21.7 1.0 %copy-start.3 = (f32[1024]{0:T(1024)S(1)}, f32[1024]{0:T(1024)}, u32[]{:S(2)}) copy-start(f32[1024]{0:T(1024)} %param.10) | copy-start | bytes 12292
  21.7 4.4 %collective-permute-start.8 = (bf16[272,128]{1,0:T(8,128)(2,1)S(1)}, bf16[272,128]{1,0:T(8,128)(2,1)S(1)}, u32[]{:S(2)}, u32[]{:S(2)}) collective-permute-start(bf16[272,128]{1,0:T(8,128)(2,1)S(1)} %get-tuple-element.39), channel_id=1, source_target_pairs={{0,8},{4,12},{8,0},{12,4},{16,24},{20,28},{24,16},{28,20},{1,9},{5... | collective-permute-start | bytes 208904 | tf_op jit(solution)/shard_map/ppermute | solution.py:42
  22.3 4.3 %collective-permute-start.9 = (bf16[272,128]{1,0:T(8,128)(2,1)S(1)}, bf16[272,128]{1,0:T(8,128)(2,1)S(1)}, u32[]{:S(2)}, u32[]{:S(2)}) collective-permute-start(bf16[272,128]{1,0:T(8,128)(2,1)S(1)} %get-tuple-element.40), channel_id=1, source_target_pairs={{0,16},{4,20},{8,24},{12,28},{16,0},{20,4},{24,8},{28,12},{1,17},{... | collective-permute-start | bytes 208904 | tf_op jit(solution)/shard_map/ppermute | solution.py:42
